TPU v7x, 256 devices: a whole 4x4x8 slice. The times are simulated.
256 devices in a mesh: row: 16 (over z, x_lo), col: 16 (over x_hi, y, core).
Axes of the slice: x: 4 (x_hi: 2, x_lo: 2; x = x_hi * 2 + x_lo), y: 4, z: 8, core: 2. Of those that a mesh axis runs over, the one named last changes fastest.
Arguments:
- embedding: float32 [32768, 256], P(('row', 'col')), may hold values from -6 to 6
- tiles: bfloat16 [16, 16, 64, 128, 128], P('row', 'col')
- tile_rows: int32 [16, 16, 64], P('row', 'col'), may hold values from 0 to 15
- tile_cols: int32 [16, 16, 64], P('row', 'col'), may hold values from 0 to 15
- counts: int32 [16, 16], P('row', 'col'), may hold values from 1 to 64, as said below
Outputs:
- final: float32 [32768, 256], P(('row', 'col'))
Inputs may be any that keep to these rules, and one draw needn't show every extreme that they name: `counts`: some grid block has all 64 slots live.
All inputs are finite; a program needn't handle non-finite values.
Results may differ from a plain program's by a relative error of at most 0.0085.
Values may be sent and summed in bfloat16 or wider, within the bound.
No kernel may reach another device: no remote copies, remote signals or barrier semaphores. Data moves between devices by JAX's collectives and lax.ppermute only.
A program may use at most 64 MiB of HBM per device.

v0:
```python
import jax
import jax.numpy as jnp
from jax import lax
from jax.sharding import PartitionSpec as P

LAYERS = 3


def propagate(panel, block_tiles, rows, cols, count, out_tiles):
    tile = block_tiles.shape[1]
    width = panel.shape[1]
    panel_tiles = panel.reshape(-1, tile, width)
    empty = jnp.zeros((out_tiles, tile, width), jnp.float32)
    slots = block_tiles.shape[0]
    chosen = panel_tiles[cols]
    prod = jnp.einsum("kab,kbd->kad", block_tiles, chosen, preferred_element_type=jnp.float32)
    live = (jnp.arange(slots, dtype=jnp.int32) < count).astype(jnp.float32)
    summed = empty.at[rows].add(prod * live[:, None, None])
    return summed.reshape(-1, width)


def per_device(embedding, tiles, tile_rows, tile_cols, counts):
    block_tiles = tiles[0, 0]
    rows = tile_rows[0, 0]
    cols = tile_cols[0, 0]
    count = counts[0, 0]
    tile = block_tiles.shape[1]
    out_tiles = lax.axis_size("col") * embedding.shape[0] // tile
    current = embedding
    total = embedding
    for layer in range(LAYERS):
        panel = lax.all_gather(current.astype(jnp.bfloat16), "row", axis=0, tiled=True)
        partial_value = propagate(panel, block_tiles, rows, cols, count, out_tiles)
        current = lax.psum_scatter(
            partial_value.astype(jnp.bfloat16), "col", scatter_dimension=0, tiled=True
        ).astype(jnp.float32)
        total = total + current
    return total / (LAYERS + 1.0)


def solution(mesh):
    return jax.shard_map(
        per_device,
        mesh=mesh,
        in_specs=(
            P(("row", "col"), None),
            P("row", "col", None, None, None),
            P("row", "col", None),
            P("row", "col", None),
            P("row", "col"),
        ),
        out_specs=P(("row", "col"), None),
        check_vma=False,
    )
```

profile of v0, /device:TPU:1, one launch (start us, length us, event | category | flops | bytes accessed | tf_op | source)
XLA Modules:
  0.0 583.2 jit_solution(5312433774719929802)
XLA Ops:
  6.5 0.0 copy-start
  6.5 0.0 all-gather.4.cloned.1.call-start
  6.5 1.7 convert_element_type.41
  8.2 0.0 all-gather.4.cloned.1.call-update
  8.3 0.0 reduce-scatter.4.cloned.1.call-start
  9.0 0.7 fusion.4
  9.6 0.7 fusion.3
  10.3 61.5 %all-gather.4.cloned.1.call-done = bf16[2048,256]{1,0:T(8,128)(2,1)} async-done(((bf16[128,256]{1,0:T(8,128)(2,1)}), bf16[2048,256]{1,0:T(8,128)(2,1)}) %all-gather.4.cloned.1.call-update) | async-done | bytes 1048592 | tf_op jit(solution)/shard_map/all_gather | solution.py:32
  71.8 4.0 gather_fusion
  75.8 0.0 copy-done
  75.8 7.2 %multiply_bitcast_fusion.2 = f32[64,128,256]{1,2,0:T(8,128)} fusion(f32[64]{0:T(128)S(1)} %compare_convert_fusion, bf16[64,128,256]{2,1,0:T(8,128)(2,1)} %gather_fusion, bf16[1,1,64,128,128]{4,3,2,1,0:T(8,128)(2,1)S(1)} %copy-done), kind=kOutput, calls=%fused_computation.8 | convolution fusion | flops 538968064 | bytes 14680320 | tf_op jit(solution)/shard_map/kab,kbd->kad/dot_general | solution.py:16
  83.0 9.0 %copy.10 = f32[64,128,256]{2,1,0:T(8,128)} copy(f32[64,128,256]{1,2,0:T(8,128)} %multiply_bitcast_fusion.2) | data formatting | bytes 16777216 | tf_op jit(solution)/shard_map/mul | solution.py:18
  92.0 1.6 broadcast.45.clone.1
  93.6 18.9 %scatter_fusion = f32[16,128,256]{2,1,0:T(8,128)} fusion(f32[16,128,256]{2,1,0:T(8,128)} %broadcast.45.clone.1, s32[64]{0:T(128)S(1)} %fusion.3, f32[64,128,256]{2,1,0:T(8,128)} %copy.10), kind=kCustom, calls=%fused_computation.3 | custom fusion | flops 2097152 | bytes 25166080 | tf_op jit(solution)/shard_map/scatter-add | solution.py:18
  112.4 2.7 convert_element_type.43
  115.1 0.0 reduce-scatter.4.cloned.1.call-update
  115.1 0.0 all-gather.6.cloned.1.call-start
  115.2 83.2 %reduce-scatter.4.cloned.1.call-done = bf16[128,256]{1,0:T(8,128)(2,1)} async-done(((bf16[2048,256]{1,0:T(8,128)(2,1)}), bf16[128,256]{1,0:T(8,128)(2,1)}) %reduce-scatter.4.cloned.1.call-update) | async-done | bytes 65552 | tf_op jit(solution)/shard_map/reduce_scatter | solution.py:34
  198.4 0.0 all-gather.6.cloned.1.call-update
  198.4 0.0 reduce-scatter.6.cloned.1.call-start
  198.4 61.7 %all-gather.6.cloned.1.call-done = bf16[2048,256]{1,0:T(8,128)(2,1)} async-done(((bf16[128,256]{1,0:T(8,128)(2,1)}), bf16[2048,256]{1,0:T(8,128)(2,1)}) %all-gather.6.cloned.1.call-update) | async-done | bytes 1048592 | tf_op jit(solution)/shard_map/all_gather | solution.py:32
  260.1 4.0 gather_fusion.1
  264.1 7.2 %multiply_bitcast_fusion.1 = f32[64,128,256]{1,2,0:T(8,128)} fusion(f32[64]{0:T(128)S(1)} %compare_convert_fusion, bf16[64,128,256]{2,1,0:T(8,128)(2,1)} %gather_fusion.1, bf16[1,1,64,128,128]{4,3,2,1,0:T(8,128)(2,1)S(1)} %copy-done), kind=kOutput, calls=%fused_computation.7 | convolution fusion | flops 538968064 | bytes 14680320 | tf_op jit(solution)/shard_map/kab,kbd->kad/dot_general | solution.py:16
  271.3 9.0 %copy.12 = f32[64,128,256]{2,1,0:T(8,128)} copy(f32[64,128,256]{1,2,0:T(8,128)} %multiply_bitcast_fusion.1) | data formatting | bytes 16777216 | tf_op jit(solution)/shard_map/mul | solution.py:18
  280.3 1.6 broadcast.45.clone
  281.9 18.9 %scatter_fusion.1 = f32[16,128,256]{2,1,0:T(8,128)} fusion(f32[16,128,256]{2,1,0:T(8,128)} %broadcast.45.clone, s32[64]{0:T(128)S(1)} %fusion.3, f32[64,128,256]{2,1,0:T(8,128)} %copy.12), kind=kCustom, calls=%fused_computation.4 | custom fusion | flops 2097152 | bytes 25166080 | tf_op jit(solution)/shard_map/scatter-add | solution.py:18
  300.8 2.7 convert_element_type.46
  303.4 0.0 reduce-scatter.6.cloned.1.call-update
  303.5 0.0 all-gather.8.cloned.1.call-start
  303.5 83.2 %reduce-scatter.6.cloned.1.call-done = bf16[128,256]{1,0:T(8,128)(2,1)} async-done(((bf16[2048,256]{1,0:T(8,128)(2,1)}), bf16[128,256]{1,0:T(8,128)(2,1)}) %reduce-scatter.6.cloned.1.call-update) | async-done | bytes 65552 | tf_op jit(solution)/shard_map/reduce_scatter | solution.py:34
  386.7 0.0 all-gather.8.cloned.1.call-update
  386.8 0.2 reduce-scatter.8.cloned.1.call-start
  387.0 61.2 %all-gather.8.cloned.1.call-done = bf16[2048,256]{1,0:T(8,128)(2,1)} async-done(((bf16[128,256]{1,0:T(8,128)(2,1)}), bf16[2048,256]{1,0:T(8,128)(2,1)}) %all-gather.8.cloned.1.call-update) | async-done | bytes 1048592 | tf_op jit(solution)/shard_map/all_gather | solution.py:32
  448.2 4.0 gather_fusion.2
  452.2 7.2 %multiply_bitcast_fusion = f32[64,128,256]{1,2,0:T(8,128)} fusion(f32[64]{0:T(128)S(1)} %compare_convert_fusion, bf16[64,128,256]{2,1,0:T(8,128)(2,1)} %gather_fusion.2, bf16[1,1,64,128,128]{4,3,2,1,0:T(8,128)(2,1)S(1)} %copy-done), kind=kOutput, calls=%fused_computation.6 | convolution fusion | flops 538968064 | bytes 14680320 | tf_op jit(solution)/shard_map/kab,kbd->kad/dot_general | solution.py:16
  459.4 9.0 %copy.14 = f32[64,128,256]{2,1,0:T(8,128)} copy(f32[64,128,256]{1,2,0:T(8,128)} %multiply_bitcast_fusion) | data formatting | bytes 16777216 | tf_op jit(solution)/shard_map/mul | solution.py:18
  468.4 1.6 broadcast.45
  469.9 18.9 %scatter_fusion.2 = f32[16,128,256]{2,1,0:T(8,128)} fusion(f32[16,128,256]{2,1,0:T(8,128)} %broadcast.45, s32[64]{0:T(128)S(1)} %fusion.3, f32[64,128,256]{2,1,0:T(8,128)} %copy.14), kind=kCustom, calls=%fused_computation.5 | custom fusion | flops 2097152 | bytes 25166080 | tf_op jit(solution)/shard_map/scatter-add | solution.py:18
  488.8 0.0 copy-start.1
  488.8 0.0 copy-start.2
  488.8 0.0 copy-start.3
  488.8 2.7 convert_element_type.49
  491.6 0.0 reduce-scatter.8.cloned.1.call-update
  491.6 83.3 %reduce-scatter.8.cloned.1.call-done = bf16[128,256]{1,0:T(8,128)(2,1)} async-done(((bf16[2048,256]{1,0:T(8,128)(2,1)}), bf16[128,256]{1,0:T(8,128)(2,1)}) %reduce-scatter.8.cloned.1.call-update) | async-done | bytes 65552 | tf_op jit(solution)/shard_map/reduce_scatter | solution.py:34
  574.8 0.0 copy-done.1
  574.8 0.0 copy-done.2
  574.8 0.0 copy-done.3
  574.8 1.5 add_multiply_fusion
  (2 shorter events, 0.0 us)
Async XLA Ops:
  6.5 69.3 %copy-start = (bf16[1,1,64,128,128]{4,3,2,1,0:T(8,128)(2,1)S(1)}, bf16[1,1,64,128,128]{4,3,2,1,0:T(8,128)(2,1)}, u32[]{:S(2)}) copy-start(bf16[1,1,64,128,128]{4,3,2,1,0:T(8,128)(2,1)} %param.6) | copy-start | bytes 6291460
  6.5 65.3 %all-gather.4.cloned.1.call-start = ((), (), s32[]{:S(2)}) async-start(), calls=%async_computation.3 | async-start | bytes 1114112 | tf_op jit(solution)/shard_map/all_gather | solution.py:32
  8.3 190.1 %reduce-scatter.4.cloned.1.call-start = ((), (), s32[]{:S(2)}) async-start(), calls=%async_computation.4 | async-start | bytes 1114112 | tf_op jit(solution)/shard_map/reduce_scatter | solution.py:34
  115.1 145.0 %all-gather.6.cloned.1.call-start = ((), (), s32[]{:S(2)}) async-start(), calls=%async_computation.5 | async-start | bytes 1114112 | tf_op jit(solution)/shard_map/all_gather | solution.py:32
  198.4 188.3 %reduce-scatter.6.cloned.1.call-start = ((), (), s32[]{:S(2)}) async-start(), calls=%async_computation.6 | async-start | bytes 1114112 | tf_op jit(solution)/shard_map/reduce_scatter | solution.py:34
  303.5 144.7 %all-gather.8.cloned.1.call-start = ((), (), s32[]{:S(2)}) async-start(), calls=%async_computation.7 | async-start | bytes 1114112 | tf_op jit(solution)/shard_map/all_gather | solution.py:32
  386.8 188.1 %reduce-scatter.8.cloned.1.call-start = ((), (), s32[]{:S(2)}) async-start(), calls=%async_computation.8 | async-start | bytes 1114112 | tf_op jit(solution)/shard_map/reduce_scatter | solution.py:34
  488.8 86.0 %copy-start.1 = (f32[128,256]{1,0:T(8,128)S(1)}, f32[128,256]{1,0:T(8,128)}, u32[]{:S(2)}) copy-start(f32[128,256]{1,0:T(8,128)} %param.5) | copy-start | bytes 393220
  488.8 86.0 %copy-start.2 = (bf16[128,256]{1,0:T(8,128)(2,1)S(1)}, bf16[128,256]{1,0:T(8,128)(2,1)}, u32[]{:S(2)}) copy-start(bf16[128,256]{1,0:T(8,128)(2,1)} %reduce-scatter.4.cloned.1.call-done) | copy-start | bytes 196612
  488.8 86.0 %copy-start.3 = (bf16[128,256]{1,0:T(8,128)(2,1)S(1)}, bf16[128,256]{1,0:T(8,128)(2,1)}, u32[]{:S(2)}) copy-start(bf16[128,256]{1,0:T(8,128)(2,1)} %reduce-scatter.6.cloned.1.call-done) | copy-start | bytes 196612
Sparse Core Ops, SparseCore 0:
  9.1 62.6 all-gather.3
  115.3 83.0 reduce-scatter.3
  200.3 59.7 all-gather.5
  303.6 83.0 reduce-scatter.5
  388.4 59.8 all-gather.7
  491.7 83.0 reduce-scatter.7
where the time goes:
time: 585 us; the launch traced here: 583 us
  waiting for transfers between devices  434 us (74%)
  other arithmetic  69.3 us (12%)
  local copies, waits for them, and re-layouts  43.6 us (7%)
  matrix products  21.5 us (4%)
  between operations  14.1 us (2%)
    reduce_scatter x3, waiting for transfers between devices, per_device(): lax.psum_scatter(partial_value.astype(jnp.bfloat16), 'col', scatter_dimen...  250 us
    all_gather x3, waiting for transfers between devices, per_device(): lax.all_gather(current.astype(jnp.bfloat16), 'row', axis=0, tiled=True)  184 us
    scatter-add x3, other arithmetic, propagate(): summed = empty.at[rows].add(prod * live[:, None, None])  56.6 us
    mul x3, local copies, waits for them, and re-layouts, propagate(): summed = empty.at[rows].add(prod * live[:, None, None])  27 us
    dot_general x3, matrix products, propagate(): jnp.einsum('kab,kbd->kad', block_tiles, chosen, preferred_element_type=jn...  21.5 us
    gather x3, local copies, waits for them, and re-layouts, propagate(): chosen = panel_tiles[cols]  11.9 us
  transfers between devices with their start and end apart: 6, of which 6 were waited for; matrix products, arithmetic and copies ran while one was open for 0% of the time, Pallas kernels for 0%

commit v1 on v0

v1 whole, which is shorter than its diff:
```python
import jax
import jax.numpy as jnp
from jax import lax
from jax.experimental import pallas as pl
from jax.experimental.pallas import tpu as pltpu
from jax.sharding import PartitionSpec as P

LAYERS = 3
MIB = 1024 * 1024


def build_kernel(n_row, n_col, own_at_ref, sib_at_ref, meta_ref, own_ref, sib_ref, dense_ref, acc_ref):
    tile = own_ref.shape[1]
    slots = own_ref.shape[0]
    half = n_col // 2
    ring = n_row // 2
    my_row, my_col = meta_ref[0], meta_ref[1]
    core = my_col & 1
    acc_ref[...] = jnp.zeros_like(acc_ref)

    def add_tiles(at_ref, tiles_ref, sibling):
        def add_tile(k, carry):
            row, col = at_ref[k], at_ref[slots + k]
            row_at = ((row ^ my_col) & 1) * half + (row >> 1)
            ahead = ((col >> 1) + ring - (my_row >> 1)) & (ring - 1)
            away = jnp.where(core == 1, ahead, (ring - ahead) & (ring - 1))
            piece = jnp.maximum(2 * away - 1 + sibling, 0)
            col_at = ((col ^ my_row) & 1) * ring + piece
            if sibling:
                keep = (away > 0) & (away < ring // 2)
            else:
                keep = away <= ring // 2

            @pl.when(keep)
            def _():
                at = (
                    pl.ds(pl.multiple_of(row_at * tile, tile), tile),
                    pl.ds(pl.multiple_of(col_at * tile, tile), tile),
                )
                acc_ref[at] += tiles_ref[k].astype(jnp.float32)

            return carry

        lax.fori_loop(0, at_ref[2 * slots], add_tile, 0)

    add_tiles(own_at_ref, own_ref, 0)
    add_tiles(sib_at_ref, sib_ref, 1)

    def emit(r, carry):
        at = pl.ds(pl.multiple_of(r * tile, tile), tile)
        dense_ref[at, :] = acc_ref[at, :].astype(jnp.bfloat16)
        return carry

    lax.fori_loop(0, dense_ref.shape[0] // tile, emit, 0)


def build_dense(own_at, sib_at, meta, own_tiles, sib_tiles, n_row, n_col):
    tile = own_tiles.shape[1]
    shape = (n_col * tile, n_row * tile)
    smem = pl.BlockSpec(memory_space=pltpu.SMEM)
    vmem = pl.BlockSpec(memory_space=pltpu.VMEM)

    def kernel(*refs):
        build_kernel(n_row, n_col, *refs)

    return pl.pallas_call(
        kernel,
        out_shape=jax.ShapeDtypeStruct(shape, jnp.bfloat16),
        in_specs=[smem, smem, smem, vmem, vmem],
        out_specs=vmem,
        scratch_shapes=[pltpu.VMEM(shape, jnp.float32)],
        compiler_params=pltpu.CompilerParams(vmem_limit_bytes=36 * MIB),
        cost_estimate=pl.CostEstimate(flops=shape[0] * shape[1], bytes_accessed=6 * shape[0] * shape[1], transcendentals=0),
        name="build_dense",
    )(own_at, sib_at, meta, own_tiles, sib_tiles)


def dot_rows(dense_ref, panel_ref, first, n_rows, step, store):
    depth = panel_ref.shape[0]
    lanes = dense_ref.shape[1] - depth if first[1] else 0

    def rows(i, carry):
        at = pl.multiple_of(i * step, step)
        store(at, jnp.dot(
            dense_ref[pl.ds(first[0] + at, step), lanes:lanes + depth],
            panel_ref[...],
            preferred_element_type=jnp.float32,
        ))
        return carry

    lax.fori_loop(0, n_rows // step, rows, 0)


def load_panel(panel_ref, refs):
    at = 0
    for ref in refs:
        rows = ref.shape[0]
        panel_ref[at:at + rows, :] = ref[...]
        at += rows


def head_multiply(dense, pieces):
    n_rows = dense.shape[0]
    depth = sum(piece.shape[0] for piece in pieces)
    width = pieces[0].shape[1]
    vmem = pl.BlockSpec(memory_space=pltpu.VMEM)

    def kernel(dense_ref, *refs):
        out_ref, panel_ref = refs[-2:]
        load_panel(panel_ref, refs[:-2])

        def store(at, value):
            out_ref[pl.ds(at, 512), :] = value

        dot_rows(dense_ref, panel_ref, (0, False), n_rows, 512, store)

    return pl.pallas_call(
        kernel,
        out_shape=jax.ShapeDtypeStruct((n_rows, width), jnp.float32),
        in_specs=[vmem] * (1 + len(pieces)),
        out_specs=vmem,
        scratch_shapes=[pltpu.VMEM((depth, width), jnp.bfloat16)],
        compiler_params=pltpu.CompilerParams(vmem_limit_bytes=24 * MIB),
        cost_estimate=pl.CostEstimate(
            flops=2 * n_rows * depth * width, bytes_accessed=2 * n_rows * depth, transcendentals=0
        ),
        name="head_multiply",
    )(dense, *pieces)


def tail_multiply(dense, head, pieces, half_index, dtype):
    n_rows = dense.shape[0] // 2
    depth = sum(piece.shape[0] for piece in pieces)
    width = pieces[0].shape[1]
    first = half_index * n_rows
    vmem = pl.BlockSpec(memory_space=pltpu.VMEM)

    def kernel(dense_ref, head_ref, *refs):
        out_ref, panel_ref = refs[-2:]
        load_panel(panel_ref, refs[:-2])

        def store(at, value):
            out_ref[pl.ds(at, 512), :] = (value + head_ref[pl.ds(first + at, 512), :]).astype(dtype)

        dot_rows(dense_ref, panel_ref, (first, True), n_rows, 512, store)

    return pl.pallas_call(
        kernel,
        out_shape=jax.ShapeDtypeStruct((n_rows, width), dtype),
        in_specs=[vmem] * (2 + len(pieces)),
        out_specs=vmem,
        scratch_shapes=[pltpu.VMEM((depth, width), jnp.bfloat16)],
        compiler_params=pltpu.CompilerParams(vmem_limit_bytes=24 * MIB),
        cost_estimate=pl.CostEstimate(
            flops=2 * n_rows * depth * width, bytes_accessed=2 * n_rows * depth, transcendentals=0
        ),
        name="tail_multiply",
    )(dense, head, *pieces)


def gather_pieces(own, n_row, n_col, build=None):
    ring = n_row // 2
    rows = own.shape[0]
    flip_x = [(i, i ^ 1) for i in range(n_row)]
    flip_core = [(j, j ^ 1) for j in range(n_col)]

    def onward(piece, by):
        pairs = []
        for i in range(n_row):
            for j in range(n_col):
                step = -by if j & 1 else by
                to = ((i >> 1) + step) % ring * 2 + (i & 1)
                pairs.append((i * n_col + j, to * n_col + j))
        return lax.ppermute(piece, ("row", "col"), pairs)

    sibling = lax.ppermute(own, "col", flip_core)
    both = jnp.concatenate([own, sibling])
    one = onward(both, 1)
    two = onward(both, 2)
    dense = None
    if build is not None:
        two, dense = lax.optimization_barrier((two, build(sibling)))
    near = jnp.concatenate([own, one, two])
    flip_near = lax.ppermute(near, "row", flip_x)
    three = onward(two, 1)
    four = onward(two[:rows], 2)
    far = jnp.concatenate([three, four])
    flip_far = lax.ppermute(far, "row", flip_x)
    return [near, far, flip_near], [flip_far], dense


def per_device(embedding, tiles, tile_rows, tile_cols, counts):
    n_row = lax.axis_size("row")
    n_col = lax.axis_size("col")
    per_dev, width = embedding.shape
    flip_core = [(j, j ^ 1) for j in range(n_col)]
    groups = [list(range(core, n_col, 2)) for core in range(2)]

    meta = jnp.stack([lax.axis_index("row"), lax.axis_index("col")]).astype(jnp.int32)
    own_at = jnp.concatenate([tile_rows[0, 0], tile_cols[0, 0], counts[0]])
    sib_at = lax.ppermute(own_at, "col", flip_core)

    def build(ready):
        own_tiles, ready = lax.optimization_barrier((tiles[0, 0], ready))
        sib_tiles = lax.ppermute(own_tiles, "col", flip_core)
        return build_dense(own_at, sib_at, meta, tiles[0, 0], sib_tiles, n_row, n_col)

    early, late, dense = gather_pieces(embedding.astype(jnp.bfloat16), n_row, n_col, build)
    total = embedding
    for layer in range(LAYERS):
        head = head_multiply(dense, early)
        theirs = tail_multiply(dense, head, late, 1, jnp.bfloat16)
        arrived = lax.ppermute(theirs, "col", flip_core)
        mine = tail_multiply(dense, head, late, 0, jnp.float32)
        pair = (mine + arrived.astype(jnp.float32)).astype(jnp.bfloat16)
        parts = lax.all_to_all(
            pair.reshape(n_col // 2, per_dev, width), "col", split_axis=0, concat_axis=0, axis_index_groups=groups
        )
        current = jnp.sum(parts.astype(jnp.float32), axis=0)
        total = total + current
        if layer + 1 < LAYERS:
            early, late, _ = gather_pieces(current.astype(jnp.bfloat16), n_row, n_col)
    return total / (LAYERS + 1.0)


def solution(mesh):
    return jax.shard_map(
        per_device,
        mesh=mesh,
        in_specs=(
            P(("row", "col"), None),
            P("row", "col", None, None, None),
            P("row", "col", None),
            P("row", "col", None),
            P("row", "col"),
        ),
        out_specs=P(("row", "col"), None),
        check_vma=False,
    )
```

time: 585 us -> 137 us (0.23)
  waiting for transfers between devices: 434 us -> 36.9 us
  other arithmetic: 69.3 us -> 3.09 us
  local copies, waits for them, and re-layouts: 43.6 us -> 1.66 us
  blocking collectives: 0 us -> 40.6 us
  starting transfers between devices: 0.38 us -> 36.7 us
  matrix products: 21.5 us -> 0 us
  Pallas kernels: 0 us -> 16.6 us
  between operations: 14.1 us -> 0.91 us
    reduce_scatter x3 -> x0, waiting for transfers between devices: 250 us -> none  [per_device(): lax.psum_scatter(partial_value.astype(jnp.bfloat16), 'col', scatter_dimen...]
    all_gather x3 -> x0, waiting for transfers between devices: 184 us -> none  [per_device(): lax.all_gather(current.astype(jnp.bfloat16), 'row', axis=0, tiled=True)]
    scatter-add x3 -> x0, other arithmetic: 56.6 us -> none  [propagate(): summed = empty.at[rows].add(prod * live[:, None, None])]
    all_to_all x0 -> x3, blocking collectives: none -> 40.6 us  [per_device(): lax.all_to_all(pair.reshape(n_col // 2, per_dev, width), 'col', split_axi...]
    ppermute x0 -> x26, waiting for transfers between devices: none -> 36.9 us  [the longest x12 20.8 us: onward(): return lax.ppermute(piece, ('row', 'col'), pairs)]
    ppermute x0 -> x26, starting transfers between devices: none -> 36.7 us  [the longest x12 13.2 us: onward(): return lax.ppermute(piece, ('row', 'col'), pairs)]
    mul x3 -> x0, local copies, waits for them, and re-layouts: 27 us -> none  [propagate(): summed = empty.at[rows].add(prod * live[:, None, None])]
    dot_general x3 -> x0, matrix products: 21.5 us -> none  [propagate(): jnp.einsum('kab,kbd->kad', block_tiles, chosen, preferred_element_type=jn...]
  transfers between devices with their start and end apart: 6 -> 26, of which waited for: 6 -> 22; matrix products, arithmetic and copies ran while one was open for 0% -> 1% of each run, Pallas kernels for 0% -> 11%
where the time goes in v1:
time: 137 us
  blocking collectives  40.6 us (30%)
  waiting for transfers between devices  36.9 us (27%)
  starting transfers between devices  36.7 us (27%)
  Pallas kernels  16.6 us (12%)
  other arithmetic  3.09 us (2%)
  local copies, waits for them, and re-layouts  1.66 us (1%)
    all_to_all x3, blocking collectives, per_device(): lax.all_to_all(pair.reshape(n_col // 2, per_dev, width), 'col', split_axi...  40.6 us
    ppermute x12, waiting for transfers between devices, onward(): return lax.ppermute(piece, ('row', 'col'), pairs)  20.8 us
    ppermute x12, starting transfers between devices, onward(): return lax.ppermute(piece, ('row', 'col'), pairs)  13.2 us
    ppermute x3, starting transfers between devices, per_device(): arrived = lax.ppermute(theirs, 'col', flip_core)  9.31 us
    ppermute x3, starting transfers between devices, gather_pieces(): sibling = lax.ppermute(own, 'col', flip_core)  8.42 us
    pallas_call x3, Pallas kernels, head_multiply(): pl.pallas_call(kernel, out_shape=jax.ShapeDtypeStruct((n_rows, width), jn...  7.92 us
    pallas_call x1, Pallas kernels, build_dense(): pl.pallas_call(kernel, out_shape=jax.ShapeDtypeStruct(shape, jnp.bfloat16...  5.15 us
    ppermute x3, waiting for transfers between devices, gather_pieces(): flip_near = lax.ppermute(near, 'row', flip_x)  5.09 us
  transfers between devices with their start and end apart: 26, of which 22 were waited for; matrix products, arithmetic and copies ran while one was open for 1% of the time, Pallas kernels for 11%

profile of v1, /device:TPU:1, one launch (start us, length us, event | category | flops | bytes accessed | tf_op | source)
XLA Modules:
  0.0 136.5 jit_solution(2454555797422847954)
XLA Ops:
  0.0 0.9 convert_element_type.36
  0.9 3.3 %collective-permute-start = (bf16[128,256]{1,0:T(8,128)(2,1)S(1)}, bf16[128,256]{1,0:T(8,128)(2,1)S(1)}, u32[]{:S(2)}, u32[]{:S(2)}) collective-permute-start(bf16[128,256]{1,0:T(8,128)(2,1)S(1)} %convert_element_type.36), channel_id=1, source_target_pairs={{0,1},{1,0},{2,3},{3,2},{4,5},{5,4},{6,7},{7,6},{8,9},{9,8},{10,11... | collective-permute-start | bytes 196616 | tf_op jit(solution)/shard_map/ppermute | solution.py:176
  4.2 0.9 collective-permute-done
  6.2 3.9 %collective-permute-start.4 = (bf16[256,256]{1,0:T(8,128)(2,1)S(1)}, bf16[256,256]{1,0:T(8,128)(2,1)S(1)}, u32[]{:S(2)}, u32[]{:S(2)}) collective-permute-start(bf16[256,256]{1,0:T(8,128)(2,1)S(1)} %pad_maximum_fusion.3), channel_id=1, source_target_pairs={{0,32},{1,225},{2,34},{3,227},{4,36},{5,229},{6,38},{7,231},{8,40}... | collective-permute-start | bytes 393224 | tf_op jit(solution)/shard_map/ppermute | solution.py:174
  10.1 1.2 collective-permute-start.1
  11.3 0.7 pad_add_fusion.refs_0_
  12.1 1.0 collective-permute-done.2.refs_1_
  13.2 1.6 %copy-done = bf16[1,1,64,128,128]{4,3,2,1,0:T(8,128)(2,1)S(1)} copy-done((bf16[1,1,64,128,128]{4,3,2,1,0:T(8,128)(2,1)S(1)}, bf16[1,1,64,128,128]{4,3,2,1,0:T(8,128)(2,1)}, u32[]{:S(2)}) %copy-start) | copy-done | bytes 2097176
  14.7 5.1 %build_dense.1.dense_ref = bf16[2048,2048]{1,0:T(8,128)(2,1)S(1)} custom-call(s32[129]{0:T(256)S(1)} %pad_add_fusion.refs_0_, s32[129]{0:T(256)S(1)} %collective-permute-done.2.refs_1_, s32[2]{0:T(128)S(1)} %pad_add_fusion.1.refs_2_, bf16[64,128,128]{2,1,0:T(8,128)(2,1)S(1)} %bitcast.11, bf16[64,128,128]{2,1,0:T(8,128)(2,1)S(1)} %collective-permute-done.3.refs_4_), custom_call_target="tpu_custom_call" | custom-call | flops 4194304 | bytes 25165824 | tf_op jit(solution)/shard_map/build_dense/pallas_call | solution.py:66
  20.0 2.3 %collective-permute-start.7 = (bf16[640,256]{1,0:T(8,128)(2,1)S(1)}, bf16[640,256]{1,0:T(8,128)(2,1)S(1)}, u32[]{:S(2)}, u32[]{:S(2)}) collective-permute-start(bf16[640,256]{1,0:T(8,128)(2,1)S(1)} %pad_maximum_fusion.refs_0_), channel_id=1, source_target_pairs={{0,16},{16,0},{32,48},{48,32},{64,80},{80,64},{96,112},{112,96},{1... | collective-permute-start | bytes 983048 | tf_op jit(solution)/shard_map/ppermute | solution.py:184
  22.3 1.8 %collective-permute-done.5 = bf16[256,256]{1,0:T(8,128)(2,1)S(1)} collective-permute-done((bf16[256,256]{1,0:T(8,128)(2,1)S(1)}, bf16[256,256]{1,0:T(8,128)(2,1)S(1)}, u32[]{:S(2)}, u32[]{:S(2)}) %collective-permute-start.5) | collective-permute-done | bytes 131104 | tf_op jit(solution)/shard_map/ppermute | solution.py:174
  24.1 2.2 %collective-permute-done.6 = bf16[128,256]{1,0:T(8,128)(2,1)S(1)} collective-permute-done((bf16[128,256]{1,0:T(8,128)(2,1)S(1)}, bf16[128,256]{1,0:T(8,128)(2,1)S(1)}, u32[]{:S(2)}, u32[]{:S(2)}) %collective-permute-start.6) | collective-permute-done | bytes 65568 | tf_op jit(solution)/shard_map/ppermute | solution.py:174
  26.4 0.8 collective-permute-start.8
  27.1 3.3 %collective-permute-done.7.refs_2_ = bf16[640,256]{1,0:T(8,128)(2,1)S(1)} collective-permute-done((bf16[640,256]{1,0:T(8,128)(2,1)S(1)}, bf16[640,256]{1,0:T(8,128)(2,1)S(1)}, u32[]{:S(2)}, u32[]{:S(2)}) %collective-permute-start.7) | collective-permute-done | bytes 327712 | tf_op jit(solution)/shard_map/ppermute | solution.py:184
  30.4 2.6 %head_multiply.3.head_ref = f32[2048,256]{1,0:T(8,128)S(1)} custom-call(bf16[2048,2048]{1,0:T(8,128)(2,1)S(1)} %build_dense.1.dense_ref, bf16[640,256]{1,0:T(8,128)(2,1)S(1)} %pad_maximum_fusion.refs_0_, bf16[384,256]{1,0:T(8,128)(2,1)S(1)} %constant_dynamic-update-slice_fusion.refs_1_, bf16[640,256]{1,0:T(8,128)(2,1)S(1)} %collective-permute-done.7.refs_2_), custom_call_target="tpu_custom_call" | custom-call | flops 1744830464 | bytes 6815744 | tf_op jit(solution)/shard_map/head_multiply/pallas_call | solution.py:117
  34.3 1.5 %collective-permute-start.9 = (bf16[1024,256]{1,0:T(8,128)(2,1)S(1)}, bf16[1024,256]{1,0:T(8,128)(2,1)S(1)}, u32[]{:S(2)}, u32[]{:S(2)}) collective-permute-start(bf16[1024,256]{1,0:T(8,128)(2,1)S(1)} %tail_multiply.7), channel_id=1, source_target_pairs={{0,1},{1,0},{2,3},{3,2},{4,5},{5,4},{6,7},{7,6},{8,9},{9,8},{10,11... | collective-permute-start | bytes 1572872 | tf_op jit(solution)/shard_map/ppermute | solution.py:213
  36.5 0.9 collective-permute-done.9
  37.5 15.0 %all_to_all.15 = bf16[8,128,256]{2,1,0:T(8,128)(2,1)S(1)} all-to-all(bf16[8,128,256]{2,1,0:T(8,128)(2,1)S(1)} %bitcast.12), channel_id=1, replica_groups={{0,2,4,6,8,10,12,14},{1,3,5,7,9,11,13,15},{16,18,20,22,24,26,28,30},{17..., dimensions={0} | all-to-all | bytes 1048576 | tf_op jit(solution)/shard_map/all_to_all | solution.py:216
  52.7 2.6 %collective-permute-start.10 = (bf16[128,256]{1,0:T(8,128)(2,1)S(1)}, bf16[128,256]{1,0:T(8,128)(2,1)S(1)}, u32[]{:S(2)}, u32[]{:S(2)}) collective-permute-start(bf16[128,256]{1,0:T(8,128)(2,1)S(1)} %convert_element_type.40), channel_id=1, source_target_pairs={{0,1},{1,0},{2,3},{3,2},{4,5},{5,4},{6,7},{7,6},{8,9},{9,8},{10,11... | collective-permute-start | bytes 196616 | tf_op jit(solution)/shard_map/ppermute | solution.py:176
  55.2 0.9 collective-permute-done.10
  56.1 1.2 collective-permute-start.12
  57.3 1.4 %collective-permute-start.11 = (bf16[256,256]{1,0:T(8,128)(2,1)S(1)}, bf16[256,256]{1,0:T(8,128)(2,1)S(1)}, u32[]{:S(2)}, u32[]{:S(2)}) collective-permute-start(bf16[256,256]{1,0:T(8,128)(2,1)S(1)} %pad_maximum_fusion.4), channel_id=1, source_target_pairs={{0,32},{1,225},{2,34},{3,227},{4,36},{5,229},{6,38},{7,231},{8,40}... | collective-permute-start | bytes 393224 | tf_op jit(solution)/shard_map/ppermute | solution.py:174
  58.7 3.9 %collective-permute-done.12 = bf16[256,256]{1,0:T(8,128)(2,1)S(1)} collective-permute-done((bf16[256,256]{1,0:T(8,128)(2,1)S(1)}, bf16[256,256]{1,0:T(8,128)(2,1)S(1)}, u32[]{:S(2)}, u32[]{:S(2)}) %collective-permute-start.12) | collective-permute-done | bytes 131104 | tf_op jit(solution)/shard_map/ppermute | solution.py:174
  62.6 1.3 collective-permute-start.13
  64.3 1.5 %collective-permute-start.14 = (bf16[128,256]{1,0:T(8,128)(2,1)S(1)}, bf16[128,256]{1,0:T(8,128)(2,1)S(1)}, u32[]{:S(2)}, u32[]{:S(2)}) collective-permute-start(bf16[128,256]{1,0:T(8,128)(2,1)S(1)} %slice.12), channel_id=1, source_target_pairs={{0,64},{1,193},{2,66},{3,195},{4,68},{5,197},{6,70},{7,199},{8,72}... | collective-permute-start | bytes 196616 | tf_op jit(solution)/shard_map/ppermute | solution.py:174
  66.4 2.9 %collective-permute-done.14 = bf16[128,256]{1,0:T(8,128)(2,1)S(1)} collective-permute-done((bf16[128,256]{1,0:T(8,128)(2,1)S(1)}, bf16[128,256]{1,0:T(8,128)(2,1)S(1)}, u32[]{:S(2)}, u32[]{:S(2)}) %collective-permute-start.14) | collective-permute-done | bytes 65568 | tf_op jit(solution)/shard_map/ppermute | solution.py:174
  69.4 1.1 collective-permute-start.16
  70.4 0.7 collective-permute-done.15.refs_2_
  71.1 2.6 %head_multiply.4.head_ref = f32[2048,256]{1,0:T(8,128)S(1)} custom-call(bf16[2048,2048]{1,0:T(8,128)(2,1)S(1)} %build_dense.1.dense_ref, bf16[640,256]{1,0:T(8,128)(2,1)S(1)} %pad_maximum_fusion.1.refs_0_, bf16[384,256]{1,0:T(8,128)(2,1)S(1)} %constant_dynamic-update-slice_fusion.2.refs_1_, bf16[640,256]{1,0:T(8,128)(2,1)S(1)} %collective-permute-done.15.refs_2_), custom_call_target="tpu_custom_call" | custom-call | flops 1744830464 | bytes 6815744 | tf_op jit(solution)/shard_map/head_multiply/pallas_call | solution.py:117
  73.8 2.0 %collective-permute-done.16.refs_0_ = bf16[384,256]{1,0:T(8,128)(2,1)S(1)} collective-permute-done((bf16[384,256]{1,0:T(8,128)(2,1)S(1)}, bf16[384,256]{1,0:T(8,128)(2,1)S(1)}, u32[]{:S(2)}, u32[]{:S(2)}) %collective-permute-start.16) | collective-permute-done | bytes 196640 | tf_op jit(solution)/shard_map/ppermute | solution.py:188
  76.4 3.8 %collective-permute-start.17 = (bf16[1024,256]{1,0:T(8,128)(2,1)S(1)}, bf16[1024,256]{1,0:T(8,128)(2,1)S(1)}, u32[]{:S(2)}, u32[]{:S(2)}) collective-permute-start(bf16[1024,256]{1,0:T(8,128)(2,1)S(1)} %tail_multiply.9), channel_id=1, source_target_pairs={{0,1},{1,0},{2,3},{3,2},{4,5},{5,4},{6,7},{7,6},{8,9},{9,8},{10,11... | collective-permute-start | bytes 1572872 | tf_op jit(solution)/shard_map/ppermute | solution.py:213
  80.8 0.9 collective-permute-done.17
  81.9 12.5 %all_to_all.16 = bf16[8,128,256]{2,1,0:T(8,128)(2,1)S(1)} all-to-all(bf16[8,128,256]{2,1,0:T(8,128)(2,1)S(1)} %bitcast.13), channel_id=1, replica_groups={{0,2,4,6,8,10,12,14},{1,3,5,7,9,11,13,15},{16,18,20,22,24,26,28,30},{17..., dimensions={0} | all-to-all | bytes 1048576 | tf_op jit(solution)/shard_map/all_to_all | solution.py:216
  94.5 2.6 %collective-permute-start.18 = (bf16[128,256]{1,0:T(8,128)(2,1)S(1)}, bf16[128,256]{1,0:T(8,128)(2,1)S(1)}, u32[]{:S(2)}, u32[]{:S(2)}) collective-permute-start(bf16[128,256]{1,0:T(8,128)(2,1)S(1)} %convert_element_type.44), channel_id=1, source_target_pairs={{0,1},{1,0},{2,3},{3,2},{4,5},{5,4},{6,7},{7,6},{8,9},{9,8},{10,11... | collective-permute-start | bytes 196616 | tf_op jit(solution)/shard_map/ppermute | solution.py:176
  97.1 0.9 collective-permute-done.18
  98.4 1.2 collective-permute-start.19
  99.6 4.5 %collective-permute-done.20 = bf16[256,256]{1,0:T(8,128)(2,1)S(1)} collective-permute-done((bf16[256,256]{1,0:T(8,128)(2,1)S(1)}, bf16[256,256]{1,0:T(8,128)(2,1)S(1)}, u32[]{:S(2)}, u32[]{:S(2)}) %collective-permute-start.20) | collective-permute-done | bytes 131104 | tf_op jit(solution)/shard_map/ppermute | solution.py:174
  104.9 1.1 collective-permute-start.23
  106.0 0.9 collective-permute-start.22
  106.9 1.0 collective-permute-done.21
  107.9 3.1 %collective-permute-done.22 = bf16[128,256]{1,0:T(8,128)(2,1)S(1)} collective-permute-done((bf16[128,256]{1,0:T(8,128)(2,1)S(1)}, bf16[128,256]{1,0:T(8,128)(2,1)S(1)}, u32[]{:S(2)}, u32[]{:S(2)}) %collective-permute-start.22) | collective-permute-done | bytes 65568 | tf_op jit(solution)/shard_map/ppermute | solution.py:174
  111.0 1.1 collective-permute-done.23.refs_2_
  112.1 2.6 %head_multiply.5.head_ref = f32[2048,256]{1,0:T(8,128)S(1)} custom-call(bf16[2048,2048]{1,0:T(8,128)(2,1)S(1)} %build_dense.1.dense_ref, bf16[640,256]{1,0:T(8,128)(2,1)S(1)} %pad_maximum_fusion.2.refs_0_, bf16[384,256]{1,0:T(8,128)(2,1)S(1)} %constant_dynamic-update-slice_fusion.4.refs_1_, bf16[640,256]{1,0:T(8,128)(2,1)S(1)} %collective-permute-done.23.refs_2_), custom_call_target="tpu_custom_call" | custom-call | flops 1744830464 | bytes 6815744 | tf_op jit(solution)/shard_map/head_multiply/pallas_call | solution.py:117
  114.7 1.8 %collective-permute-done.24.refs_0_ = bf16[384,256]{1,0:T(8,128)(2,1)S(1)} collective-permute-done((bf16[384,256]{1,0:T(8,128)(2,1)S(1)}, bf16[384,256]{1,0:T(8,128)(2,1)S(1)}, u32[]{:S(2)}, u32[]{:S(2)}) %collective-permute-start.24) | collective-permute-done | bytes 196640 | tf_op jit(solution)/shard_map/ppermute | solution.py:188
  117.1 3.9 %collective-permute-start.25 = (bf16[1024,256]{1,0:T(8,128)(2,1)S(1)}, bf16[1024,256]{1,0:T(8,128)(2,1)S(1)}, u32[]{:S(2)}, u32[]{:S(2)}) collective-permute-start(bf16[1024,256]{1,0:T(8,128)(2,1)S(1)} %tail_multiply.11), channel_id=1, source_target_pairs={{0,1},{1,0},{2,3},{3,2},{4,5},{5,4},{6,7},{7,6},{8,9},{9,8},{10,11... | collective-permute-start | bytes 1572872 | tf_op jit(solution)/shard_map/ppermute | solution.py:213
  121.7 0.9 collective-permute-done.25
  122.7 13.0 %all_to_all.17 = bf16[8,128,256]{2,1,0:T(8,128)(2,1)S(1)} all-to-all(bf16[8,128,256]{2,1,0:T(8,128)(2,1)S(1)} %bitcast.14), channel_id=1, replica_groups={{0,2,4,6,8,10,12,14},{1,3,5,7,9,11,13,15},{16,18,20,22,24,26,28,30},{17..., dimensions={0} | all-to-all | bytes 1048576 | tf_op jit(solution)/shard_map/all_to_all | solution.py:216
  135.8 0.7 add_multiply_fusion
  (48 shorter events, 7.6 us)
Async XLA Ops:
  0.9 4.2 %collective-permute-start = (bf16[128,256]{1,0:T(8,128)(2,1)S(1)}, bf16[128,256]{1,0:T(8,128)(2,1)S(1)}, u32[]{:S(2)}, u32[]{:S(2)}) collective-permute-start(bf16[128,256]{1,0:T(8,128)(2,1)S(1)} %convert_element_type.36), channel_id=1, source_target_pairs={{0,1},{1,0},{2,3},{3,2},{4,5},{5,4},{6,7},{7,6},{8,9},{9,8},{10,11... | collective-permute-start | bytes 196616 | tf_op jit(solution)/shard_map/ppermute | solution.py:176
  5.1 8.0 %collective-permute-start.3 = (bf16[64,128,128]{2,1,0:T(8,128)(2,1)}, bf16[64,128,128]{2,1,0:T(8,128)(2,1)S(1)}, u32[]{:S(2)}, u32[]{:S(2)}) collective-permute-start(bf16[64,128,128]{2,1,0:T(8,128)(2,1)} %bitcast.10), channel_id=1, source_target_pairs={{0,1},{1,0},{2,3},{3,2},{4,5},{5,4},{6,7},{7,6},{8,9},{9,8},{10,11... | collective-permute-start | bytes 6291464 | tf_op jit(solution)/shard_map/ppermute | solution.py:205
  6.2 13.8 %collective-permute-start.4 = (bf16[256,256]{1,0:T(8,128)(2,1)S(1)}, bf16[256,256]{1,0:T(8,128)(2,1)S(1)}, u32[]{:S(2)}, u32[]{:S(2)}) collective-permute-start(bf16[256,256]{1,0:T(8,128)(2,1)S(1)} %pad_maximum_fusion.3), channel_id=1, source_target_pairs={{0,32},{1,225},{2,34},{3,227},{4,36},{5,229},{6,38},{7,231},{8,40}... | collective-permute-start | bytes 393224 | tf_op jit(solution)/shard_map/ppermute | solution.py:174
  10.1 9.8 %collective-permute-start.1 = (bf16[256,256]{1,0:T(8,128)(2,1)S(1)}, bf16[256,256]{1,0:T(8,128)(2,1)S(1)}, u32[]{:S(2)}, u32[]{:S(2)}) collective-permute-start(bf16[256,256]{1,0:T(8,128)(2,1)S(1)} %pad_maximum_fusion.3), channel_id=1, source_target_pairs={{0,64},{1,193},{2,66},{3,195},{4,68},{5,197},{6,70},{7,199},{8,72}... | collective-permute-start | bytes 393224 | tf_op jit(solution)/shard_map/ppermute | solution.py:174
  12.0 1.1 collective-permute-start.2
  13.2 1.6 %copy-start = (bf16[1,1,64,128,128]{4,3,2,1,0:T(8,128)(2,1)S(1)}, bf16[1,1,64,128,128]{4,3,2,1,0:T(8,128)(2,1)}, u32[]{:S(2)}) copy-start(bf16[1,1,64,128,128]{4,3,2,1,0:T(8,128)(2,1)} %param.6) | copy-start | bytes 6291460
  19.9 4.2 %collective-permute-start.5 = (bf16[256,256]{1,0:T(8,128)(2,1)S(1)}, bf16[256,256]{1,0:T(8,128)(2,1)S(1)}, u32[]{:S(2)}, u32[]{:S(2)}) collective-permute-start(bf16[256,256]{1,0:T(8,128)(2,1)S(1)} %collective-permute-done.1), channel_id=1, source_target_pairs={{0,32},{1,225},{2,34},{3,227},{4,36},{5,229},{6,38},{7,231},{8,40}... | collective-permute-start | bytes 393224 | tf_op jit(solution)/shard_map/ppermute | solution.py:174
  20.0 10.4 %collective-permute-start.7 = (bf16[640,256]{1,0:T(8,128)(2,1)S(1)}, bf16[640,256]{1,0:T(8,128)(2,1)S(1)}, u32[]{:S(2)}, u32[]{:S(2)}) collective-permute-start(bf16[640,256]{1,0:T(8,128)(2,1)S(1)} %pad_maximum_fusion.refs_0_), channel_id=1, source_target_pairs={{0,16},{16,0},{32,48},{48,32},{64,80},{80,64},{96,112},{112,96},{1... | collective-permute-start | bytes 983048 | tf_op jit(solution)/shard_map/ppermute | solution.py:184
  22.3 4.0 %collective-permute-start.6 = (bf16[128,256]{1,0:T(8,128)(2,1)S(1)}, bf16[128,256]{1,0:T(8,128)(2,1)S(1)}, u32[]{:S(2)}, u32[]{:S(2)}) collective-permute-start(bf16[128,256]{1,0:T(8,128)(2,1)S(1)} %slice.9), channel_id=1, source_target_pairs={{0,64},{1,193},{2,66},{3,195},{4,68},{5,197},{6,70},{7,199},{8,72}... | collective-permute-start | bytes 196616 | tf_op jit(solution)/shard_map/ppermute | solution.py:174
  26.4 7.4 %collective-permute-start.8 = (bf16[384,256]{1,0:T(8,128)(2,1)S(1)}, bf16[384,256]{1,0:T(8,128)(2,1)S(1)}, u32[]{:S(2)}, u32[]{:S(2)}) collective-permute-start(bf16[384,256]{1,0:T(8,128)(2,1)S(1)} %constant_dynamic-update-slice_fusion.refs_1_), channel_id=1, source_target_pairs={{0,16},{16,0},{32,48},{48,32},{64,80},{80,64},{96,112},{112,96},{1... | collective-permute-start | bytes 589832 | tf_op jit(solution)/shard_map/ppermute | solution.py:188
  34.3 3.1 %collective-permute-start.9 = (bf16[1024,256]{1,0:T(8,128)(2,1)S(1)}, bf16[1024,256]{1,0:T(8,128)(2,1)S(1)}, u32[]{:S(2)}, u32[]{:S(2)}) collective-permute-start(bf16[1024,256]{1,0:T(8,128)(2,1)S(1)} %tail_multiply.7), channel_id=1, source_target_pairs={{0,1},{1,0},{2,3},{3,2},{4,5},{5,4},{6,7},{7,6},{8,9},{9,8},{10,11... | collective-permute-start | bytes 1572872 | tf_op jit(solution)/shard_map/ppermute | solution.py:213
  52.7 3.5 %collective-permute-start.10 = (bf16[128,256]{1,0:T(8,128)(2,1)S(1)}, bf16[128,256]{1,0:T(8,128)(2,1)S(1)}, u32[]{:S(2)}, u32[]{:S(2)}) collective-permute-start(bf16[128,256]{1,0:T(8,128)(2,1)S(1)} %convert_element_type.40), channel_id=1, source_target_pairs={{0,1},{1,0},{2,3},{3,2},{4,5},{5,4},{6,7},{7,6},{8,9},{9,8},{10,11... | collective-permute-start | bytes 196616 | tf_op jit(solution)/shard_map/ppermute | solution.py:176
  56.1 6.5 %collective-permute-start.12 = (bf16[256,256]{1,0:T(8,128)(2,1)S(1)}, bf16[256,256]{1,0:T(8,128)(2,1)S(1)}, u32[]{:S(2)}, u32[]{:S(2)}) collective-permute-start(bf16[256,256]{1,0:T(8,128)(2,1)S(1)} %pad_maximum_fusion.4), channel_id=1, source_target_pairs={{0,64},{1,193},{2,66},{3,195},{4,68},{5,197},{6,70},{7,199},{8,72}... | collective-permute-start | bytes 393224 | tf_op jit(solution)/shard_map/ppermute | solution.py:174
  57.3 6.6 %collective-permute-start.11 = (bf16[256,256]{1,0:T(8,128)(2,1)S(1)}, bf16[256,256]{1,0:T(8,128)(2,1)S(1)}, u32[]{:S(2)}, u32[]{:S(2)}) collective-permute-start(bf16[256,256]{1,0:T(8,128)(2,1)S(1)} %pad_maximum_fusion.4), channel_id=1, source_target_pairs={{0,32},{1,225},{2,34},{3,227},{4,36},{5,229},{6,38},{7,231},{8,40}... | collective-permute-start | bytes 393224 | tf_op jit(solution)/shard_map/ppermute | solution.py:174
  62.6 3.8 %collective-permute-start.13 = (bf16[256,256]{1,0:T(8,128)(2,1)S(1)}, bf16[256,256]{1,0:T(8,128)(2,1)S(1)}, u32[]{:S(2)}, u32[]{:S(2)}) collective-permute-start(bf16[256,256]{1,0:T(8,128)(2,1)S(1)} %collective-permute-done.12), channel_id=1, source_target_pairs={{0,32},{1,225},{2,34},{3,227},{4,36},{5,229},{6,38},{7,231},{8,40}... | collective-permute-start | bytes 393224 | tf_op jit(solution)/shard_map/ppermute | solution.py:174
  64.0 7.1 %collective-permute-start.15 = (bf16[640,256]{1,0:T(8,128)(2,1)S(1)}, bf16[640,256]{1,0:T(8,128)(2,1)S(1)}, u32[]{:S(2)}, u32[]{:S(2)}) collective-permute-start(bf16[640,256]{1,0:T(8,128)(2,1)S(1)} %pad_maximum_fusion.1.refs_0_), channel_id=1, source_target_pairs={{0,16},{16,0},{32,48},{48,32},{64,80},{80,64},{96,112},{112,96},{1... | collective-permute-start | bytes 983048 | tf_op jit(solution)/shard_map/ppermute | solution.py:184
  64.3 5.1 %collective-permute-start.14 = (bf16[128,256]{1,0:T(8,128)(2,1)S(1)}, bf16[128,256]{1,0:T(8,128)(2,1)S(1)}, u32[]{:S(2)}, u32[]{:S(2)}) collective-permute-start(bf16[128,256]{1,0:T(8,128)(2,1)S(1)} %slice.12), channel_id=1, source_target_pairs={{0,64},{1,193},{2,66},{3,195},{4,68},{5,197},{6,70},{7,199},{8,72}... | collective-permute-start | bytes 196616 | tf_op jit(solution)/shard_map/ppermute | solution.py:174
  69.4 6.4 %collective-permute-start.16 = (bf16[384,256]{1,0:T(8,128)(2,1)S(1)}, bf16[384,256]{1,0:T(8,128)(2,1)S(1)}, u32[]{:S(2)}, u32[]{:S(2)}) collective-permute-start(bf16[384,256]{1,0:T(8,128)(2,1)S(1)} %constant_dynamic-update-slice_fusion.2.refs_1_), channel_id=1, source_target_pairs={{0,16},{16,0},{32,48},{48,32},{64,80},{80,64},{96,112},{112,96},{1... | collective-permute-start | bytes 589832 | tf_op jit(solution)/shard_map/ppermute | solution.py:188
  76.4 5.4 %collective-permute-start.17 = (bf16[1024,256]{1,0:T(8,128)(2,1)S(1)}, bf16[1024,256]{1,0:T(8,128)(2,1)S(1)}, u32[]{:S(2)}, u32[]{:S(2)}) collective-permute-start(bf16[1024,256]{1,0:T(8,128)(2,1)S(1)} %tail_multiply.9), channel_id=1, source_target_pairs={{0,1},{1,0},{2,3},{3,2},{4,5},{5,4},{6,7},{7,6},{8,9},{9,8},{10,11... | collective-permute-start | bytes 1572872 | tf_op jit(solution)/shard_map/ppermute | solution.py:213
  94.5 3.5 %collective-permute-start.18 = (bf16[128,256]{1,0:T(8,128)(2,1)S(1)}, bf16[128,256]{1,0:T(8,128)(2,1)S(1)}, u32[]{:S(2)}, u32[]{:S(2)}) collective-permute-start(bf16[128,256]{1,0:T(8,128)(2,1)S(1)} %convert_element_type.44), channel_id=1, source_target_pairs={{0,1},{1,0},{2,3},{3,2},{4,5},{5,4},{6,7},{7,6},{8,9},{9,8},{10,11... | collective-permute-start | bytes 196616 | tf_op jit(solution)/shard_map/ppermute | solution.py:176
  98.0 6.1 %collective-permute-start.20 = (bf16[256,256]{1,0:T(8,128)(2,1)S(1)}, bf16[256,256]{1,0:T(8,128)(2,1)S(1)}, u32[]{:S(2)}, u32[]{:S(2)}) collective-permute-start(bf16[256,256]{1,0:T(8,128)(2,1)S(1)} %pad_maximum_fusion.5), channel_id=1, source_target_pairs={{0,64},{1,193},{2,66},{3,195},{4,68},{5,197},{6,70},{7,199},{8,72}... | collective-permute-start | bytes 393224 | tf_op jit(solution)/shard_map/ppermute | solution.py:174
  98.4 6.5 %collective-permute-start.19 = (bf16[256,256]{1,0:T(8,128)(2,1)S(1)}, bf16[256,256]{1,0:T(8,128)(2,1)S(1)}, u32[]{:S(2)}, u32[]{:S(2)}) collective-permute-start(bf16[256,256]{1,0:T(8,128)(2,1)S(1)} %pad_maximum_fusion.5), channel_id=1, source_target_pairs={{0,32},{1,225},{2,34},{3,227},{4,36},{5,229},{6,38},{7,231},{8,40}... | collective-permute-start | bytes 393224 | tf_op jit(solution)/shard_map/ppermute | solution.py:174
  104.1 3.8 %collective-permute-start.21 = (bf16[256,256]{1,0:T(8,128)(2,1)S(1)}, bf16[256,256]{1,0:T(8,128)(2,1)S(1)}, u32[]{:S(2)}, u32[]{:S(2)}) collective-permute-start(bf16[256,256]{1,0:T(8,128)(2,1)S(1)} %collective-permute-done.20), channel_id=1, source_target_pairs={{0,32},{1,225},{2,34},{3,227},{4,36},{5,229},{6,38},{7,231},{8,40}... | collective-permute-start | bytes 393224 | tf_op jit(solution)/shard_map/ppermute | solution.py:174
  104.9 7.2 %collective-permute-start.23 = (bf16[640,256]{1,0:T(8,128)(2,1)S(1)}, bf16[640,256]{1,0:T(8,128)(2,1)S(1)}, u32[]{:S(2)}, u32[]{:S(2)}) collective-permute-start(bf16[640,256]{1,0:T(8,128)(2,1)S(1)} %pad_maximum_fusion.2.refs_0_), channel_id=1, source_target_pairs={{0,16},{16,0},{32,48},{48,32},{64,80},{80,64},{96,112},{112,96},{1... | collective-permute-start | bytes 983048 | tf_op jit(solution)/shard_map/ppermute | solution.py:184
  106.0 5.0 %collective-permute-start.22 = (bf16[128,256]{1,0:T(8,128)(2,1)S(1)}, bf16[128,256]{1,0:T(8,128)(2,1)S(1)}, u32[]{:S(2)}, u32[]{:S(2)}) collective-permute-start(bf16[128,256]{1,0:T(8,128)(2,1)S(1)} %slice.13), channel_id=1, source_target_pairs={{0,64},{1,193},{2,66},{3,195},{4,68},{5,197},{6,70},{7,199},{8,72}... | collective-permute-start | bytes 196616 | tf_op jit(solution)/shard_map/ppermute | solution.py:174
  111.0 5.5 %collective-permute-start.24 = (bf16[384,256]{1,0:T(8,128)(2,1)S(1)}, bf16[384,256]{1,0:T(8,128)(2,1)S(1)}, u32[]{:S(2)}, u32[]{:S(2)}) collective-permute-start(bf16[384,256]{1,0:T(8,128)(2,1)S(1)} %constant_dynamic-update-slice_fusion.4.refs_1_), channel_id=1, source_target_pairs={{0,16},{16,0},{32,48},{48,32},{64,80},{80,64},{96,112},{112,96},{1... | collective-permute-start | bytes 589832 | tf_op jit(solution)/shard_map/ppermute | solution.py:188
  117.1 5.5 %collective-permute-start.25 = (bf16[1024,256]{1,0:T(8,128)(2,1)S(1)}, bf16[1024,256]{1,0:T(8,128)(2,1)S(1)}, u32[]{:S(2)}, u32[]{:S(2)}) collective-permute-start(bf16[1024,256]{1,0:T(8,128)(2,1)S(1)} %tail_multiply.11), channel_id=1, source_target_pairs={{0,1},{1,0},{2,3},{3,2},{4,5},{5,4},{6,7},{7,6},{8,9},{9,8},{10,11... | collective-permute-start | bytes 1572872 | tf_op jit(solution)/shard_map/ppermute | solution.py:213
  121.7 14.1 %copy-start.1 = (f32[128,256]{1,0:T(8,128)S(1)}, f32[128,256]{1,0:T(8,128)}, u32[]{:S(2)}) copy-start(f32[128,256]{1,0:T(8,128)} %param.5) | copy-start | bytes 393220

commit v2 on v1

--- a/solution.py
+++ b/solution.py
@@ -25,7 +25,10 @@
             ahead = ((col >> 1) + ring - (my_row >> 1)) & (ring - 1)
             away = jnp.where(core == 1, ahead, (ring - ahead) & (ring - 1))
             piece = jnp.maximum(2 * away - 1 + sibling, 0)
-            col_at = ((col ^ my_row) & 1) * ring + piece
+            late = 2 * ring - ring // 2
+            near_at = jnp.where(piece < ring - 1, piece, late)
+            far_at = jnp.where(piece < ring - 3, piece + ring - 1, piece + ring)
+            col_at = jnp.where(((col ^ my_row) & 1) == 1, far_at, near_at)
             if sibling:
                 keep = (away > 0) & (away < ring // 2)
             else:
@@ -164,29 +167,38 @@
     flip_x = [(i, i ^ 1) for i in range(n_row)]
     flip_core = [(j, j ^ 1) for j in range(n_col)]
 
-    def onward(piece, by):
+    def onward(piece, by, name):
         pairs = []
         for i in range(n_row):
             for j in range(n_col):
                 step = -by if j & 1 else by
                 to = ((i >> 1) + step) % ring * 2 + (i & 1)
                 pairs.append((i * n_col + j, to * n_col + j))
-        return lax.ppermute(piece, ("row", "col"), pairs)
-
-    sibling = lax.ppermute(own, "col", flip_core)
+        with jax.named_scope(name):
+            return lax.ppermute(piece, ("row", "col"), pairs)
+
+    def over(piece, name):
+        with jax.named_scope(name):
+            return lax.ppermute(piece, "row", flip_x)
+
+    def swap(piece):
+        with jax.named_scope("core_swap"):
+            return lax.ppermute(piece, "col", flip_core)
+
+    sibling = swap(own)
     both = jnp.concatenate([own, sibling])
-    one = onward(both, 1)
-    two = onward(both, 2)
-    dense = None
+    one = onward(both, 1, "z_one")
+    two = onward(both, 2, "z_two")
+    three = onward(both, 3, "z_three")
+    over_one = over(jnp.concatenate([own, one]), "x_one")
+    over_two = over(two, "x_two")
+    four = onward(three[:rows], 1, "z_four")
+    over_three = over(three, "x_three")
+    last, dense = four, None
     if build is not None:
-        two, dense = lax.optimization_barrier((two, build(sibling)))
-    near = jnp.concatenate([own, one, two])
-    flip_near = lax.ppermute(near, "row", flip_x)
-    three = onward(two, 1)
-    four = onward(two[:rows], 2)
-    far = jnp.concatenate([three, four])
-    flip_far = lax.ppermute(far, "row", flip_x)
-    return [near, far, flip_near], [flip_far], dense
+        last, dense = lax.optimization_barrier((four, build(sibling)))
+    over_four = over(last, "x_four")
+    return [own, one, two, three, over_one, over_two], [four, over_three, over_four], dense
 
 
 def per_device(embedding, tiles, tile_rows, tile_cols, counts):
@@ -198,11 +210,13 @@
 
     meta = jnp.stack([lax.axis_index("row"), lax.axis_index("col")]).astype(jnp.int32)
     own_at = jnp.concatenate([tile_rows[0, 0], tile_cols[0, 0], counts[0]])
-    sib_at = lax.ppermute(own_at, "col", flip_core)
+    with jax.named_scope("place_swap"):
+        sib_at = lax.ppermute(own_at, "col", flip_core)
 
     def build(ready):
         own_tiles, ready = lax.optimization_barrier((tiles[0, 0], ready))
-        sib_tiles = lax.ppermute(own_tiles, "col", flip_core)
+        with jax.named_scope("tile_swap"):
+            sib_tiles = lax.ppermute(own_tiles, "col", flip_core)
         return build_dense(own_at, sib_at, meta, tiles[0, 0], sib_tiles, n_row, n_col)
 
     early, late, dense = gather_pieces(embedding.astype(jnp.bfloat16), n_row, n_col, build)
@@ -210,7 +224,8 @@
     for layer in range(LAYERS):
         head = head_multiply(dense, early)
         theirs = tail_multiply(dense, head, late, 1, jnp.bfloat16)
-        arrived = lax.ppermute(theirs, "col", flip_core)
+        with jax.named_scope("partial_swap"):
+            arrived = lax.ppermute(theirs, "col", flip_core)
         mine = tail_multiply(dense, head, late, 0, jnp.float32)
         pair = (mine + arrived.astype(jnp.float32)).astype(jnp.bfloat16)
         parts = lax.all_to_all(

time: 137 us -> 141 us (1.029)
  starting transfers between devices: 36.7 us -> 52.4 us
  waiting for transfers between devices: 36.9 us -> 26.2 us
  Pallas kernels: 16.6 us -> 13.7 us
  blocking collectives: 40.6 us -> 42.4 us
    ppermute x12, starting transfers between devices: 13.2 us -> 20.4 us  [onward(): return lax.ppermute(piece, ('row', 'col'), pairs)]
    ppermute x9 -> x15, waiting for transfers between devices: 12.2 us -> 5.09 us  [the longest x3 2.71 us: swap(): return lax.ppermute(piece, 'col', flip_core)]
    ppermute x9 -> x15, starting transfers between devices: 13.9 us -> 20.6 us  [the longest x12 12.3 us: over(): return lax.ppermute(piece, 'row', flip_x)]
    ppermute x12, waiting for transfers between devices: 20.8 us -> 18.3 us  [onward(): return lax.ppermute(piece, ('row', 'col'), pairs)]
    pallas_call x1, Pallas kernels: 5.15 us -> 2.92 us  [build_dense(): pl.pallas_call(kernel, out_shape=jax.ShapeDtypeStruct(shape, jnp.bfloat16...]
    ppermute x1, starting transfers between devices: 0.02 us -> 2.09 us  [per_device(): sib_at = lax.ppermute(own_at, 'col', flip_core)]
    all_to_all x3, blocking collectives: 40.6 us -> 42.4 us  [per_device(): lax.all_to_all(pair.reshape(n_col // 2, per_dev, width), 'col', split_axi...]
  transfers between devices with their start and end apart: 26 -> 32, of which waited for: 22 -> 13; matrix products, arithmetic and copies ran while one was open for 1% -> 1% of each run, Pallas kernels for 11% -> 8%
where the time goes in v2:
time: 141 us; the launch traced here: 140 us
  starting transfers between devices  52.4 us (37%)
  blocking collectives  42.4 us (30%)
  waiting for transfers between devices  26.2 us (19%)
  Pallas kernels  13.7 us (10%)
  other arithmetic  3.08 us (2%)
  local copies, waits for them, and re-layouts  1.61 us (1%)
    all_to_all x3, blocking collectives, per_device(): lax.all_to_all(pair.reshape(n_col // 2, per_dev, width), 'col', split_axi...  42.4 us
    ppermute x12, starting transfers between devices, onward(): return lax.ppermute(piece, ('row', 'col'), pairs)  20.4 us
    ppermute x12, waiting for transfers between devices, onward(): return lax.ppermute(piece, ('row', 'col'), pairs)  18.3 us
    ppermute x12, starting transfers between devices, over(): return lax.ppermute(piece, 'row', flip_x)  12.3 us
    ppermute x3, starting transfers between devices, per_device(): arrived = lax.ppermute(theirs, 'col', flip_core)  8.96 us
    ppermute x3, starting transfers between devices, swap(): return lax.ppermute(piece, 'col', flip_core)  8.3 us
    pallas_call x3, Pallas kernels, head_multiply(): pl.pallas_call(kernel, out_shape=jax.ShapeDtypeStruct((n_rows, width), jn...  7.08 us
    pallas_call x6, Pallas kernels, tail_multiply(): pl.pallas_call(kernel, out_shape=jax.ShapeDtypeStruct((n_rows, width), dt...  3.67 us
  transfers between devices with their start and end apart: 32, of which 13 were waited for; matrix products, arithmetic and copies ran while one was open for 1% of the time, Pallas kernels for 8%

profile of v2, /device:TPU:1, one launch (start us, length us, event | category | flops | bytes accessed | tf_op | source)
XLA Modules:
  0.0 140.2 jit_solution(12448781649358724060)
XLA Ops:
  0.0 0.9 convert_element_type.36.refs_0_
  0.9 3.3 %collective-permute-start = (bf16[128,256]{1,0:T(8,128)(2,1)S(1)}, bf16[128,256]{1,0:T(8,128)(2,1)S(1)}, u32[]{:S(2)}, u32[]{:S(2)}) collective-permute-start(bf16[128,256]{1,0:T(8,128)(2,1)S(1)} %convert_element_type.36.refs_0_), channel_id=1, source_target_pairs={{0,1},{1,0},{2,3},{3,2},{4,5},{5,4},{6,7},{7,6},{8,9},{9,8},{10,11... | collective-permute-start | bytes 196616 | tf_op jit(solution)/shard_map/core_swap/ppermute | solution.py:186
  4.2 0.9 collective-permute-done
  5.5 3.9 %collective-permute-start.5 = (bf16[256,256]{1,0:T(8,128)(2,1)S(1)}, bf16[256,256]{1,0:T(8,128)(2,1)S(1)}, u32[]{:S(2)}, u32[]{:S(2)}) collective-permute-start(bf16[256,256]{1,0:T(8,128)(2,1)S(1)} %pad_maximum_fusion.3), channel_id=1, source_target_pairs={{0,32},{1,225},{2,34},{3,227},{4,36},{5,229},{6,38},{7,231},{8,40}... | collective-permute-start | bytes 393224 | tf_op jit(solution)/shard_map/z_one/ppermute | solution.py:178
  9.4 1.2 collective-permute-start.6
  11.8 1.3 collective-permute-start.7
  13.1 1.4 collective-permute-done.6.refs_2_
  14.5 1.2 collective-permute-start.8
  15.7 0.7 pad_add_fusion.refs_0_
  16.4 2.1 %collective-permute-start.3 = (s32[129]{0:T(256)S(1)}, s32[129]{0:T(256)S(1)}, u32[]{:S(2)}, u32[]{:S(2)}) collective-permute-start(s32[129]{0:T(256)S(1)} %pad_add_fusion.refs_0_), channel_id=1, source_target_pairs={{0,1},{1,0},{2,3},{3,2},{4,5},{5,4},{6,7},{7,6},{8,9},{9,8},{10,11... | collective-permute-start | bytes 1556 | tf_op jit(solution)/shard_map/place_swap/ppermute | solution.py:214
  18.5 3.2 %collective-permute-start.2 = (bf16[128,256]{1,0:T(8,128)(2,1)S(1)}, bf16[128,256]{1,0:T(8,128)(2,1)S(1)}, u32[]{:S(2)}, u32[]{:S(2)}) collective-permute-start(bf16[128,256]{1,0:T(8,128)(2,1)S(1)} %slice.12), channel_id=1, source_target_pairs={{0,32},{1,225},{2,34},{3,227},{4,36},{5,229},{6,38},{7,231},{8,40}... | collective-permute-start | bytes 196616 | tf_op jit(solution)/shard_map/z_four/ppermute | solution.py:178
  21.8 1.2 collective-permute-start.9
  23.0 1.6 %copy-done = bf16[1,1,64,128,128]{4,3,2,1,0:T(8,128)(2,1)S(1)} copy-done((bf16[1,1,64,128,128]{4,3,2,1,0:T(8,128)(2,1)S(1)}, bf16[1,1,64,128,128]{4,3,2,1,0:T(8,128)(2,1)}, u32[]{:S(2)}) %copy-start) | copy-done | bytes 2097176
  24.6 2.9 %build_dense.1.dense_ref = bf16[2048,2048]{1,0:T(8,128)(2,1)S(1)} custom-call(s32[129]{0:T(256)S(1)} %pad_add_fusion.refs_0_, s32[129]{0:T(256)S(1)} %collective-permute-done.3.refs_1_, s32[2]{0:T(128)S(1)} %pad_add_fusion.1.refs_2_, bf16[64,128,128]{2,1,0:T(8,128)(2,1)S(1)} %bitcast.11, bf16[64,128,128]{2,1,0:T(8,128)(2,1)S(1)} %collective-permute-done.4.refs_4_), custom_call_target="tpu_custom_call" | custom-call | flops 4194304 | bytes 25165824 | tf_op jit(solution)/shard_map/build_dense/pallas_call | solution.py:69
  27.6 1.6 %collective-permute-start.10 = (bf16[128,256]{1,0:T(8,128)(2,1)S(1)}, bf16[128,256]{1,0:T(8,128)(2,1)S(1)}, u32[]{:S(2)}, u32[]{:S(2)}) collective-permute-start(bf16[128,256]{1,0:T(8,128)(2,1)S(1)} %collective-permute-done.2.refs_0_), channel_id=1, source_target_pairs={{0,16},{16,0},{32,48},{48,32},{64,80},{80,64},{96,112},{112,96},{1... | collective-permute-start | bytes 196616 | tf_op jit(solution)/shard_map/x_four/ppermute | solution.py:182
  29.2 2.4 %head_multiply.3.head_ref = f32[2048,256]{1,0:T(8,128)S(1)} custom-call(bf16[2048,2048]{1,0:T(8,128)(2,1)S(1)} %build_dense.1.dense_ref, bf16[128,256]{1,0:T(8,128)(2,1)S(1)} %convert_element_type.36.refs_0_, bf16[256,256]{1,0:T(8,128)(2,1)S(1)} %collective-permute-done.5.refs_1_, bf16[256,256]{1,0:T(8,128)(2,1)S(1)} %collective-permute-done.6.refs_2_, ...), custom_call_target="tpu_custom_call" | custom-call | flops 1610612736 | bytes 6291456 | tf_op jit(solution)/shard_map/head_multiply/pallas_call | solution.py:120
  32.2 2.2 %collective-permute-start.11 = (bf16[1024,256]{1,0:T(8,128)(2,1)S(1)}, bf16[1024,256]{1,0:T(8,128)(2,1)S(1)}, u32[]{:S(2)}, u32[]{:S(2)}) collective-permute-start(bf16[1024,256]{1,0:T(8,128)(2,1)S(1)} %tail_multiply.7), channel_id=1, source_target_pairs={{0,1},{1,0},{2,3},{3,2},{4,5},{5,4},{6,7},{7,6},{8,9},{9,8},{10,11... | collective-permute-start | bytes 1572872 | tf_op jit(solution)/shard_map/partial_swap/ppermute | solution.py:228
  35.0 0.9 collective-permute-done.11
  36.1 16.8 %all_to_all.15 = bf16[8,128,256]{2,1,0:T(8,128)(2,1)S(1)} all-to-all(bf16[8,128,256]{2,1,0:T(8,128)(2,1)S(1)} %bitcast.12), channel_id=1, replica_groups={{0,2,4,6,8,10,12,14},{1,3,5,7,9,11,13,15},{16,18,20,22,24,26,28,30},{17..., dimensions={0} | all-to-all | bytes 1048576 | tf_op jit(solution)/shard_map/all_to_all | solution.py:231
  52.9 2.6 %collective-permute-start.12 = (bf16[128,256]{1,0:T(8,128)(2,1)S(1)}, bf16[128,256]{1,0:T(8,128)(2,1)S(1)}, u32[]{:S(2)}, u32[]{:S(2)}) collective-permute-start(bf16[128,256]{1,0:T(8,128)(2,1)S(1)} %convert_element_type.40.refs_0_), channel_id=1, source_target_pairs={{0,1},{1,0},{2,3},{3,2},{4,5},{5,4},{6,7},{7,6},{8,9},{9,8},{10,11... | collective-permute-start | bytes 196616 | tf_op jit(solution)/shard_map/core_swap/ppermute | solution.py:186
  55.5 0.9 collective-permute-done.12
  56.7 3.8 %collective-permute-start.15 = (bf16[256,256]{1,0:T(8,128)(2,1)S(1)}, bf16[256,256]{1,0:T(8,128)(2,1)S(1)}, u32[]{:S(2)}, u32[]{:S(2)}) collective-permute-start(bf16[256,256]{1,0:T(8,128)(2,1)S(1)} %pad_maximum_fusion.4), channel_id=1, source_target_pairs={{0,96},{1,161},{2,98},{3,163},{4,100},{5,165},{6,102},{7,167},{8,1... | collective-permute-start | bytes 393224 | tf_op jit(solution)/shard_map/z_three/ppermute | solution.py:178
  60.5 1.5 %collective-permute-start.14 = (bf16[256,256]{1,0:T(8,128)(2,1)S(1)}, bf16[256,256]{1,0:T(8,128)(2,1)S(1)}, u32[]{:S(2)}, u32[]{:S(2)}) collective-permute-start(bf16[256,256]{1,0:T(8,128)(2,1)S(1)} %pad_maximum_fusion.4), channel_id=1, source_target_pairs={{0,64},{1,193},{2,66},{3,195},{4,68},{5,197},{6,70},{7,199},{8,72}... | collective-permute-start | bytes 393224 | tf_op jit(solution)/shard_map/z_two/ppermute | solution.py:178
  62.2 8.0 %collective-permute-done.14.refs_2_ = bf16[256,256]{1,0:T(8,128)(2,1)S(1)} collective-permute-done((bf16[256,256]{1,0:T(8,128)(2,1)S(1)}, bf16[256,256]{1,0:T(8,128)(2,1)S(1)}, u32[]{:S(2)}, u32[]{:S(2)}) %collective-permute-start.14) | collective-permute-done | bytes 131104 | tf_op jit(solution)/shard_map/z_two/ppermute | solution.py:178
  70.4 1.4 %collective-permute-start.19 = (bf16[256,256]{1,0:T(8,128)(2,1)S(1)}, bf16[256,256]{1,0:T(8,128)(2,1)S(1)}, u32[]{:S(2)}, u32[]{:S(2)}) collective-permute-start(bf16[256,256]{1,0:T(8,128)(2,1)S(1)} %collective-permute-done.15.refs_3_), channel_id=1, source_target_pairs={{0,16},{16,0},{32,48},{48,32},{64,80},{80,64},{96,112},{112,96},{1... | collective-permute-start | bytes 393224 | tf_op jit(solution)/shard_map/x_three/ppermute | solution.py:182
  71.8 1.6 %collective-permute-done.18.refs_0_ = bf16[128,256]{1,0:T(8,128)(2,1)S(1)} collective-permute-done((bf16[128,256]{1,0:T(8,128)(2,1)S(1)}, bf16[128,256]{1,0:T(8,128)(2,1)S(1)}, u32[]{:S(2)}, u32[]{:S(2)}) %collective-permute-start.18) | collective-permute-done | bytes 65568 | tf_op jit(solution)/shard_map/z_four/ppermute | solution.py:178
  73.4 1.8 %collective-permute-start.20 = (bf16[128,256]{1,0:T(8,128)(2,1)S(1)}, bf16[128,256]{1,0:T(8,128)(2,1)S(1)}, u32[]{:S(2)}, u32[]{:S(2)}) collective-permute-start(bf16[128,256]{1,0:T(8,128)(2,1)S(1)} %collective-permute-done.18.refs_0_), channel_id=1, source_target_pairs={{0,16},{16,0},{32,48},{48,32},{64,80},{80,64},{96,112},{112,96},{1... | collective-permute-start | bytes 196616 | tf_op jit(solution)/shard_map/x_four/ppermute | solution.py:182
  75.1 2.4 %head_multiply.4.head_ref = f32[2048,256]{1,0:T(8,128)S(1)} custom-call(bf16[2048,2048]{1,0:T(8,128)(2,1)S(1)} %build_dense.1.dense_ref, bf16[128,256]{1,0:T(8,128)(2,1)S(1)} %convert_element_type.40.refs_0_, bf16[256,256]{1,0:T(8,128)(2,1)S(1)} %collective-permute-done.13.refs_1_, bf16[256,256]{1,0:T(8,128)(2,1)S(1)} %collective-permute-done.14.refs_2_, ...), custom_call_target="tpu_custom_call" | custom-call | flops 1610612736 | bytes 6291456 | tf_op jit(solution)/shard_map/head_multiply/pallas_call | solution.py:120
  77.5 1.2 collective-permute-done.20.refs_2_
  79.3 2.3 %collective-permute-start.21 = (bf16[1024,256]{1,0:T(8,128)(2,1)S(1)}, bf16[1024,256]{1,0:T(8,128)(2,1)S(1)}, u32[]{:S(2)}, u32[]{:S(2)}) collective-permute-start(bf16[1024,256]{1,0:T(8,128)(2,1)S(1)} %tail_multiply.9), channel_id=1, source_target_pairs={{0,1},{1,0},{2,3},{3,2},{4,5},{5,4},{6,7},{7,6},{8,9},{9,8},{10,11... | collective-permute-start | bytes 1572872 | tf_op jit(solution)/shard_map/partial_swap/ppermute | solution.py:228
  82.2 0.9 collective-permute-done.21
  83.2 12.6 %all_to_all.16 = bf16[8,128,256]{2,1,0:T(8,128)(2,1)S(1)} all-to-all(bf16[8,128,256]{2,1,0:T(8,128)(2,1)S(1)} %bitcast.13), channel_id=1, replica_groups={{0,2,4,6,8,10,12,14},{1,3,5,7,9,11,13,15},{16,18,20,22,24,26,28,30},{17..., dimensions={0} | all-to-all | bytes 1048576 | tf_op jit(solution)/shard_map/all_to_all | solution.py:231
  95.9 2.4 %collective-permute-start.22 = (bf16[128,256]{1,0:T(8,128)(2,1)S(1)}, bf16[128,256]{1,0:T(8,128)(2,1)S(1)}, u32[]{:S(2)}, u32[]{:S(2)}) collective-permute-start(bf16[128,256]{1,0:T(8,128)(2,1)S(1)} %convert_element_type.44.refs_0_), channel_id=1, source_target_pairs={{0,1},{1,0},{2,3},{3,2},{4,5},{5,4},{6,7},{7,6},{8,9},{9,8},{10,11... | collective-permute-start | bytes 196616 | tf_op jit(solution)/shard_map/core_swap/ppermute | solution.py:186
  98.3 0.9 collective-permute-done.22
  99.2 1.4 collective-permute-start.23
  100.6 2.2 %collective-permute-start.25 = (bf16[256,256]{1,0:T(8,128)(2,1)S(1)}, bf16[256,256]{1,0:T(8,128)(2,1)S(1)}, u32[]{:S(2)}, u32[]{:S(2)}) collective-permute-start(bf16[256,256]{1,0:T(8,128)(2,1)S(1)} %pad_maximum_fusion.5), channel_id=1, source_target_pairs={{0,96},{1,161},{2,98},{3,163},{4,100},{5,165},{6,102},{7,167},{8,1... | collective-permute-start | bytes 393224 | tf_op jit(solution)/shard_map/z_three/ppermute | solution.py:178
  102.8 1.2 collective-permute-start.24
  104.0 0.8 collective-permute-start.26
  104.8 5.7 %collective-permute-done.24.refs_2_ = bf16[256,256]{1,0:T(8,128)(2,1)S(1)} collective-permute-done((bf16[256,256]{1,0:T(8,128)(2,1)S(1)}, bf16[256,256]{1,0:T(8,128)(2,1)S(1)}, u32[]{:S(2)}, u32[]{:S(2)}) %collective-permute-start.24) | collective-permute-done | bytes 131104 | tf_op jit(solution)/shard_map/z_two/ppermute | solution.py:178
  110.6 2.0 %collective-permute-start.27 = (bf16[256,256]{1,0:T(8,128)(2,1)S(1)}, bf16[256,256]{1,0:T(8,128)(2,1)S(1)}, u32[]{:S(2)}, u32[]{:S(2)}) collective-permute-start(bf16[256,256]{1,0:T(8,128)(2,1)S(1)} %collective-permute-done.24.refs_2_), channel_id=1, source_target_pairs={{0,16},{16,0},{32,48},{48,32},{64,80},{80,64},{96,112},{112,96},{1... | collective-permute-start | bytes 393224 | tf_op jit(solution)/shard_map/x_two/ppermute | solution.py:182
  112.6 1.0 collective-permute-start.28
  113.6 0.8 collective-permute-start.29
  114.5 1.6 %collective-permute-done.28.refs_0_ = bf16[128,256]{1,0:T(8,128)(2,1)S(1)} collective-permute-done((bf16[128,256]{1,0:T(8,128)(2,1)S(1)}, bf16[128,256]{1,0:T(8,128)(2,1)S(1)}, u32[]{:S(2)}, u32[]{:S(2)}) %collective-permute-start.28) | collective-permute-done | bytes 65568 | tf_op jit(solution)/shard_map/z_four/ppermute | solution.py:178
  116.1 2.4 %head_multiply.5.head_ref = f32[2048,256]{1,0:T(8,128)S(1)} custom-call(bf16[2048,2048]{1,0:T(8,128)(2,1)S(1)} %build_dense.1.dense_ref, bf16[128,256]{1,0:T(8,128)(2,1)S(1)} %convert_element_type.44.refs_0_, bf16[256,256]{1,0:T(8,128)(2,1)S(1)} %collective-permute-done.23.refs_1_, bf16[256,256]{1,0:T(8,128)(2,1)S(1)} %collective-permute-done.24.refs_2_, ...), custom_call_target="tpu_custom_call" | custom-call | flops 1610612736 | bytes 6291456 | tf_op jit(solution)/shard_map/head_multiply/pallas_call | solution.py:120
  118.5 1.2 collective-permute-done.30.refs_2_
  120.3 4.4 %collective-permute-start.31 = (bf16[1024,256]{1,0:T(8,128)(2,1)S(1)}, bf16[1024,256]{1,0:T(8,128)(2,1)S(1)}, u32[]{:S(2)}, u32[]{:S(2)}) collective-permute-start(bf16[1024,256]{1,0:T(8,128)(2,1)S(1)} %tail_multiply.11), channel_id=1, source_target_pairs={{0,1},{1,0},{2,3},{3,2},{4,5},{5,4},{6,7},{7,6},{8,9},{9,8},{10,11... | collective-permute-start | bytes 1572872 | tf_op jit(solution)/shard_map/partial_swap/ppermute | solution.py:228
  125.3 0.9 collective-permute-done.31
  126.4 13.1 %all_to_all.17 = bf16[8,128,256]{2,1,0:T(8,128)(2,1)S(1)} all-to-all(bf16[8,128,256]{2,1,0:T(8,128)(2,1)S(1)} %bitcast.14), channel_id=1, replica_groups={{0,2,4,6,8,10,12,14},{1,3,5,7,9,11,13,15},{16,18,20,22,24,26,28,30},{17..., dimensions={0} | all-to-all | bytes 1048576 | tf_op jit(solution)/shard_map/all_to_all | solution.py:231
  (54 shorter events, 6.7 us)
Async XLA Ops:
  0.9 4.2 %collective-permute-start = (bf16[128,256]{1,0:T(8,128)(2,1)S(1)}, bf16[128,256]{1,0:T(8,128)(2,1)S(1)}, u32[]{:S(2)}, u32[]{:S(2)}) collective-permute-start(bf16[128,256]{1,0:T(8,128)(2,1)S(1)} %convert_element_type.36.refs_0_), channel_id=1, source_target_pairs={{0,1},{1,0},{2,3},{3,2},{4,5},{5,4},{6,7},{7,6},{8,9},{9,8},{10,11... | collective-permute-start | bytes 196616 | tf_op jit(solution)/shard_map/core_swap/ppermute | solution.py:186
  5.1 17.9 %collective-permute-start.4 = (bf16[64,128,128]{2,1,0:T(8,128)(2,1)}, bf16[64,128,128]{2,1,0:T(8,128)(2,1)S(1)}, u32[]{:S(2)}, u32[]{:S(2)}) collective-permute-start(bf16[64,128,128]{2,1,0:T(8,128)(2,1)} %bitcast.10), channel_id=1, source_target_pairs={{0,1},{1,0},{2,3},{3,2},{4,5},{5,4},{6,7},{7,6},{8,9},{9,8},{10,11... | collective-permute-start | bytes 6291464 | tf_op jit(solution)/shard_map/tile_swap/ppermute | solution.py:219
  5.5 6.3 %collective-permute-start.5 = (bf16[256,256]{1,0:T(8,128)(2,1)S(1)}, bf16[256,256]{1,0:T(8,128)(2,1)S(1)}, u32[]{:S(2)}, u32[]{:S(2)}) collective-permute-start(bf16[256,256]{1,0:T(8,128)(2,1)S(1)} %pad_maximum_fusion.3), channel_id=1, source_target_pairs={{0,32},{1,225},{2,34},{3,227},{4,36},{5,229},{6,38},{7,231},{8,40}... | collective-permute-start | bytes 393224 | tf_op jit(solution)/shard_map/z_one/ppermute | solution.py:178
  9.4 5.1 %collective-permute-start.6 = (bf16[256,256]{1,0:T(8,128)(2,1)S(1)}, bf16[256,256]{1,0:T(8,128)(2,1)S(1)}, u32[]{:S(2)}, u32[]{:S(2)}) collective-permute-start(bf16[256,256]{1,0:T(8,128)(2,1)S(1)} %pad_maximum_fusion.3), channel_id=1, source_target_pairs={{0,64},{1,193},{2,66},{3,195},{4,68},{5,197},{6,70},{7,199},{8,72}... | collective-permute-start | bytes 393224 | tf_op jit(solution)/shard_map/z_two/ppermute | solution.py:178
  11.2 7.3 %collective-permute-start.1 = (bf16[256,256]{1,0:T(8,128)(2,1)S(1)}, bf16[256,256]{1,0:T(8,128)(2,1)S(1)}, u32[]{:S(2)}, u32[]{:S(2)}) collective-permute-start(bf16[256,256]{1,0:T(8,128)(2,1)S(1)} %pad_maximum_fusion.3), channel_id=1, source_target_pairs={{0,96},{1,161},{2,98},{3,163},{4,100},{5,165},{6,102},{7,167},{8,1... | collective-permute-start | bytes 393224 | tf_op jit(solution)/shard_map/z_three/ppermute | solution.py:178
  11.8 17.4 %collective-permute-start.7 = (bf16[384,256]{1,0:T(8,128)(2,1)S(1)}, bf16[384,256]{1,0:T(8,128)(2,1)S(1)}, u32[]{:S(2)}, u32[]{:S(2)}) collective-permute-start(bf16[384,256]{1,0:T(8,128)(2,1)S(1)} %pad_maximum_fusion), channel_id=1, source_target_pairs={{0,16},{16,0},{32,48},{48,32},{64,80},{80,64},{96,112},{112,96},{1... | collective-permute-start | bytes 589832 | tf_op jit(solution)/shard_map/x_one/ppermute | solution.py:182
  14.5 14.7 %collective-permute-start.8 = (bf16[256,256]{1,0:T(8,128)(2,1)S(1)}, bf16[256,256]{1,0:T(8,128)(2,1)S(1)}, u32[]{:S(2)}, u32[]{:S(2)}) collective-permute-start(bf16[256,256]{1,0:T(8,128)(2,1)S(1)} %collective-permute-done.6.refs_2_), channel_id=1, source_target_pairs={{0,16},{16,0},{32,48},{48,32},{64,80},{80,64},{96,112},{112,96},{1... | collective-permute-start | bytes 393224 | tf_op jit(solution)/shard_map/x_two/ppermute | solution.py:182
  16.4 5.3 %collective-permute-start.3 = (s32[129]{0:T(256)S(1)}, s32[129]{0:T(256)S(1)}, u32[]{:S(2)}, u32[]{:S(2)}) collective-permute-start(s32[129]{0:T(256)S(1)} %pad_add_fusion.refs_0_), channel_id=1, source_target_pairs={{0,1},{1,0},{2,3},{3,2},{4,5},{5,4},{6,7},{7,6},{8,9},{9,8},{10,11... | collective-permute-start | bytes 1556 | tf_op jit(solution)/shard_map/place_swap/ppermute | solution.py:214
  18.5 9.0 %collective-permute-start.2 = (bf16[128,256]{1,0:T(8,128)(2,1)S(1)}, bf16[128,256]{1,0:T(8,128)(2,1)S(1)}, u32[]{:S(2)}, u32[]{:S(2)}) collective-permute-start(bf16[128,256]{1,0:T(8,128)(2,1)S(1)} %slice.12), channel_id=1, source_target_pairs={{0,32},{1,225},{2,34},{3,227},{4,36},{5,229},{6,38},{7,231},{8,40}... | collective-permute-start | bytes 196616 | tf_op jit(solution)/shard_map/z_four/ppermute | solution.py:178
  21.8 9.8 %collective-permute-start.9 = (bf16[256,256]{1,0:T(8,128)(2,1)S(1)}, bf16[256,256]{1,0:T(8,128)(2,1)S(1)}, u32[]{:S(2)}, u32[]{:S(2)}) collective-permute-start(bf16[256,256]{1,0:T(8,128)(2,1)S(1)} %collective-permute-done.1.refs_3_), channel_id=1, source_target_pairs={{0,16},{16,0},{32,48},{48,32},{64,80},{80,64},{96,112},{112,96},{1... | collective-permute-start | bytes 393224 | tf_op jit(solution)/shard_map/x_three/ppermute | solution.py:182
  23.0 1.6 %copy-start = (bf16[1,1,64,128,128]{4,3,2,1,0:T(8,128)(2,1)S(1)}, bf16[1,1,64,128,128]{4,3,2,1,0:T(8,128)(2,1)}, u32[]{:S(2)}) copy-start(bf16[1,1,64,128,128]{4,3,2,1,0:T(8,128)(2,1)} %param.6) | copy-start | bytes 6291460
  27.6 4.0 %collective-permute-start.10 = (bf16[128,256]{1,0:T(8,128)(2,1)S(1)}, bf16[128,256]{1,0:T(8,128)(2,1)S(1)}, u32[]{:S(2)}, u32[]{:S(2)}) collective-permute-start(bf16[128,256]{1,0:T(8,128)(2,1)S(1)} %collective-permute-done.2.refs_0_), channel_id=1, source_target_pairs={{0,16},{16,0},{32,48},{48,32},{64,80},{80,64},{96,112},{112,96},{1... | collective-permute-start | bytes 196616 | tf_op jit(solution)/shard_map/x_four/ppermute | solution.py:182
  32.2 3.8 %collective-permute-start.11 = (bf16[1024,256]{1,0:T(8,128)(2,1)S(1)}, bf16[1024,256]{1,0:T(8,128)(2,1)S(1)}, u32[]{:S(2)}, u32[]{:S(2)}) collective-permute-start(bf16[1024,256]{1,0:T(8,128)(2,1)S(1)} %tail_multiply.7), channel_id=1, source_target_pairs={{0,1},{1,0},{2,3},{3,2},{4,5},{5,4},{6,7},{7,6},{8,9},{9,8},{10,11... | collective-permute-start | bytes 1572872 | tf_op jit(solution)/shard_map/partial_swap/ppermute | solution.py:228
  52.9 3.5 %collective-permute-start.12 = (bf16[128,256]{1,0:T(8,128)(2,1)S(1)}, bf16[128,256]{1,0:T(8,128)(2,1)S(1)}, u32[]{:S(2)}, u32[]{:S(2)}) collective-permute-start(bf16[128,256]{1,0:T(8,128)(2,1)S(1)} %convert_element_type.40.refs_0_), channel_id=1, source_target_pairs={{0,1},{1,0},{2,3},{3,2},{4,5},{5,4},{6,7},{7,6},{8,9},{9,8},{10,11... | collective-permute-start | bytes 196616 | tf_op jit(solution)/shard_map/core_swap/ppermute | solution.py:186
  56.4 5.6 %collective-permute-start.13 = (bf16[256,256]{1,0:T(8,128)(2,1)S(1)}, bf16[256,256]{1,0:T(8,128)(2,1)S(1)}, u32[]{:S(2)}, u32[]{:S(2)}) collective-permute-start(bf16[256,256]{1,0:T(8,128)(2,1)S(1)} %pad_maximum_fusion.4), channel_id=1, source_target_pairs={{0,32},{1,225},{2,34},{3,227},{4,36},{5,229},{6,38},{7,231},{8,40}... | collective-permute-start | bytes 393224 | tf_op jit(solution)/shard_map/z_one/ppermute | solution.py:178
  56.7 13.4 %collective-permute-start.15 = (bf16[256,256]{1,0:T(8,128)(2,1)S(1)}, bf16[256,256]{1,0:T(8,128)(2,1)S(1)}, u32[]{:S(2)}, u32[]{:S(2)}) collective-permute-start(bf16[256,256]{1,0:T(8,128)(2,1)S(1)} %pad_maximum_fusion.4), channel_id=1, source_target_pairs={{0,96},{1,161},{2,98},{3,163},{4,100},{5,165},{6,102},{7,167},{8,1... | collective-permute-start | bytes 393224 | tf_op jit(solution)/shard_map/z_three/ppermute | solution.py:178
  60.5 9.6 %collective-permute-start.14 = (bf16[256,256]{1,0:T(8,128)(2,1)S(1)}, bf16[256,256]{1,0:T(8,128)(2,1)S(1)}, u32[]{:S(2)}, u32[]{:S(2)}) collective-permute-start(bf16[256,256]{1,0:T(8,128)(2,1)S(1)} %pad_maximum_fusion.4), channel_id=1, source_target_pairs={{0,64},{1,193},{2,66},{3,195},{4,68},{5,197},{6,70},{7,199},{8,72}... | collective-permute-start | bytes 393224 | tf_op jit(solution)/shard_map/z_two/ppermute | solution.py:178
  62.1 13.1 %collective-permute-start.16 = (bf16[384,256]{1,0:T(8,128)(2,1)S(1)}, bf16[384,256]{1,0:T(8,128)(2,1)S(1)}, u32[]{:S(2)}, u32[]{:S(2)}) collective-permute-start(bf16[384,256]{1,0:T(8,128)(2,1)S(1)} %pad_maximum_fusion.1), channel_id=1, source_target_pairs={{0,16},{16,0},{32,48},{48,32},{64,80},{80,64},{96,112},{112,96},{1... | collective-permute-start | bytes 589832 | tf_op jit(solution)/shard_map/x_one/ppermute | solution.py:182
  70.2 5.0 %collective-permute-start.17 = (bf16[256,256]{1,0:T(8,128)(2,1)S(1)}, bf16[256,256]{1,0:T(8,128)(2,1)S(1)}, u32[]{:S(2)}, u32[]{:S(2)}) collective-permute-start(bf16[256,256]{1,0:T(8,128)(2,1)S(1)} %collective-permute-done.14.refs_2_), channel_id=1, source_target_pairs={{0,16},{16,0},{32,48},{48,32},{64,80},{80,64},{96,112},{112,96},{1... | collective-permute-start | bytes 393224 | tf_op jit(solution)/shard_map/x_two/ppermute | solution.py:182
  70.2 3.2 %collective-permute-start.18 = (bf16[128,256]{1,0:T(8,128)(2,1)S(1)}, bf16[128,256]{1,0:T(8,128)(2,1)S(1)}, u32[]{:S(2)}, u32[]{:S(2)}) collective-permute-start(bf16[128,256]{1,0:T(8,128)(2,1)S(1)} %slice.13), channel_id=1, source_target_pairs={{0,32},{1,225},{2,34},{3,227},{4,36},{5,229},{6,38},{7,231},{8,40}... | collective-permute-start | bytes 196616 | tf_op jit(solution)/shard_map/z_four/ppermute | solution.py:178
  70.4 8.3 %collective-permute-start.19 = (bf16[256,256]{1,0:T(8,128)(2,1)S(1)}, bf16[256,256]{1,0:T(8,128)(2,1)S(1)}, u32[]{:S(2)}, u32[]{:S(2)}) collective-permute-start(bf16[256,256]{1,0:T(8,128)(2,1)S(1)} %collective-permute-done.15.refs_3_), channel_id=1, source_target_pairs={{0,16},{16,0},{32,48},{48,32},{64,80},{80,64},{96,112},{112,96},{1... | collective-permute-start | bytes 393224 | tf_op jit(solution)/shard_map/x_three/ppermute | solution.py:182
  73.4 5.3 %collective-permute-start.20 = (bf16[128,256]{1,0:T(8,128)(2,1)S(1)}, bf16[128,256]{1,0:T(8,128)(2,1)S(1)}, u32[]{:S(2)}, u32[]{:S(2)}) collective-permute-start(bf16[128,256]{1,0:T(8,128)(2,1)S(1)} %collective-permute-done.18.refs_0_), channel_id=1, source_target_pairs={{0,16},{16,0},{32,48},{48,32},{64,80},{80,64},{96,112},{112,96},{1... | collective-permute-start | bytes 196616 | tf_op jit(solution)/shard_map/x_four/ppermute | solution.py:182
  79.3 3.8 %collective-permute-start.21 = (bf16[1024,256]{1,0:T(8,128)(2,1)S(1)}, bf16[1024,256]{1,0:T(8,128)(2,1)S(1)}, u32[]{:S(2)}, u32[]{:S(2)}) collective-permute-start(bf16[1024,256]{1,0:T(8,128)(2,1)S(1)} %tail_multiply.9), channel_id=1, source_target_pairs={{0,1},{1,0},{2,3},{3,2},{4,5},{5,4},{6,7},{7,6},{8,9},{9,8},{10,11... | collective-permute-start | bytes 1572872 | tf_op jit(solution)/shard_map/partial_swap/ppermute | solution.py:228
  95.9 3.3 %collective-permute-start.22 = (bf16[128,256]{1,0:T(8,128)(2,1)S(1)}, bf16[128,256]{1,0:T(8,128)(2,1)S(1)}, u32[]{:S(2)}, u32[]{:S(2)}) collective-permute-start(bf16[128,256]{1,0:T(8,128)(2,1)S(1)} %convert_element_type.44.refs_0_), channel_id=1, source_target_pairs={{0,1},{1,0},{2,3},{3,2},{4,5},{5,4},{6,7},{7,6},{8,9},{9,8},{10,11... | collective-permute-start | bytes 196616 | tf_op jit(solution)/shard_map/core_swap/ppermute | solution.py:186
  99.2 4.7 %collective-permute-start.23 = (bf16[256,256]{1,0:T(8,128)(2,1)S(1)}, bf16[256,256]{1,0:T(8,128)(2,1)S(1)}, u32[]{:S(2)}, u32[]{:S(2)}) collective-permute-start(bf16[256,256]{1,0:T(8,128)(2,1)S(1)} %pad_maximum_fusion.5), channel_id=1, source_target_pairs={{0,32},{1,225},{2,34},{3,227},{4,36},{5,229},{6,38},{7,231},{8,40}... | collective-permute-start | bytes 393224 | tf_op jit(solution)/shard_map/z_one/ppermute | solution.py:178
  100.6 12.0 %collective-permute-start.25 = (bf16[256,256]{1,0:T(8,128)(2,1)S(1)}, bf16[256,256]{1,0:T(8,128)(2,1)S(1)}, u32[]{:S(2)}, u32[]{:S(2)}) collective-permute-start(bf16[256,256]{1,0:T(8,128)(2,1)S(1)} %pad_maximum_fusion.5), channel_id=1, source_target_pairs={{0,96},{1,161},{2,98},{3,163},{4,100},{5,165},{6,102},{7,167},{8,1... | collective-permute-start | bytes 393224 | tf_op jit(solution)/shard_map/z_three/ppermute | solution.py:178
  102.8 7.8 %collective-permute-start.24 = (bf16[256,256]{1,0:T(8,128)(2,1)S(1)}, bf16[256,256]{1,0:T(8,128)(2,1)S(1)}, u32[]{:S(2)}, u32[]{:S(2)}) collective-permute-start(bf16[256,256]{1,0:T(8,128)(2,1)S(1)} %pad_maximum_fusion.5), channel_id=1, source_target_pairs={{0,64},{1,193},{2,66},{3,195},{4,68},{5,197},{6,70},{7,199},{8,72}... | collective-permute-start | bytes 393224 | tf_op jit(solution)/shard_map/z_two/ppermute | solution.py:178
  104.0 12.1 %collective-permute-start.26 = (bf16[384,256]{1,0:T(8,128)(2,1)S(1)}, bf16[384,256]{1,0:T(8,128)(2,1)S(1)}, u32[]{:S(2)}, u32[]{:S(2)}) collective-permute-start(bf16[384,256]{1,0:T(8,128)(2,1)S(1)} %pad_maximum_fusion.2), channel_id=1, source_target_pairs={{0,16},{16,0},{32,48},{48,32},{64,80},{80,64},{96,112},{112,96},{1... | collective-permute-start | bytes 589832 | tf_op jit(solution)/shard_map/x_one/ppermute | solution.py:182
  110.6 5.5 %collective-permute-start.27 = (bf16[256,256]{1,0:T(8,128)(2,1)S(1)}, bf16[256,256]{1,0:T(8,128)(2,1)S(1)}, u32[]{:S(2)}, u32[]{:S(2)}) collective-permute-start(bf16[256,256]{1,0:T(8,128)(2,1)S(1)} %collective-permute-done.24.refs_2_), channel_id=1, source_target_pairs={{0,16},{16,0},{32,48},{48,32},{64,80},{80,64},{96,112},{112,96},{1... | collective-permute-start | bytes 393224 | tf_op jit(solution)/shard_map/x_two/ppermute | solution.py:182
  112.6 3.5 %collective-permute-start.28 = (bf16[128,256]{1,0:T(8,128)(2,1)S(1)}, bf16[128,256]{1,0:T(8,128)(2,1)S(1)}, u32[]{:S(2)}, u32[]{:S(2)}) collective-permute-start(bf16[128,256]{1,0:T(8,128)(2,1)S(1)} %slice.14), channel_id=1, source_target_pairs={{0,32},{1,225},{2,34},{3,227},{4,36},{5,229},{6,38},{7,231},{8,40}... | collective-permute-start | bytes 196616 | tf_op jit(solution)/shard_map/z_four/ppermute | solution.py:178
  113.6 6.0 %collective-permute-start.29 = (bf16[256,256]{1,0:T(8,128)(2,1)S(1)}, bf16[256,256]{1,0:T(8,128)(2,1)S(1)}, u32[]{:S(2)}, u32[]{:S(2)}) collective-permute-start(bf16[256,256]{1,0:T(8,128)(2,1)S(1)} %collective-permute-done.25.refs_3_), channel_id=1, source_target_pairs={{0,16},{16,0},{32,48},{48,32},{64,80},{80,64},{96,112},{112,96},{1... | collective-permute-start | bytes 393224 | tf_op jit(solution)/shard_map/x_three/ppermute | solution.py:182
  116.1 3.6 %collective-permute-start.30 = (bf16[128,256]{1,0:T(8,128)(2,1)S(1)}, bf16[128,256]{1,0:T(8,128)(2,1)S(1)}, u32[]{:S(2)}, u32[]{:S(2)}) collective-permute-start(bf16[128,256]{1,0:T(8,128)(2,1)S(1)} %collective-permute-done.28.refs_0_), channel_id=1, source_target_pairs={{0,16},{16,0},{32,48},{48,32},{64,80},{80,64},{96,112},{112,96},{1... | collective-permute-start | bytes 196616 | tf_op jit(solution)/shard_map/x_four/ppermute | solution.py:182
  120.3 6.0 %collective-permute-start.31 = (bf16[1024,256]{1,0:T(8,128)(2,1)S(1)}, bf16[1024,256]{1,0:T(8,128)(2,1)S(1)}, u32[]{:S(2)}, u32[]{:S(2)}) collective-permute-start(bf16[1024,256]{1,0:T(8,128)(2,1)S(1)} %tail_multiply.11), channel_id=1, source_target_pairs={{0,1},{1,0},{2,3},{3,2},{4,5},{5,4},{6,7},{7,6},{8,9},{9,8},{10,11... | collective-permute-start | bytes 1572872 | tf_op jit(solution)/shard_map/partial_swap/ppermute | solution.py:228
  125.3 14.2 %copy-start.1 = (f32[128,256]{1,0:T(8,128)S(1)}, f32[128,256]{1,0:T(8,128)}, u32[]{:S(2)}) copy-start(f32[128,256]{1,0:T(8,128)} %param.5) | copy-start | bytes 393220

commit v3 on v2

--- a/solution.py
+++ b/solution.py
@@ -187,18 +187,22 @@
 
     sibling = swap(own)
     both = jnp.concatenate([own, sibling])
+    over_own = over(own, "x_own")
     one = onward(both, 1, "z_one")
     two = onward(both, 2, "z_two")
     three = onward(both, 3, "z_three")
-    over_one = over(jnp.concatenate([own, one]), "x_one")
+    one, over_own = lax.optimization_barrier((one, over_own))
+    over_one = over(one, "x_one")
+    two, one = lax.optimization_barrier((two, one))
     over_two = over(two, "x_two")
-    four = onward(three[:rows], 1, "z_four")
+    four = onward(two[:rows], 2, "z_four")
+    three, two = lax.optimization_barrier((three, two))
     over_three = over(three, "x_three")
     last, dense = four, None
     if build is not None:
         last, dense = lax.optimization_barrier((four, build(sibling)))
     over_four = over(last, "x_four")
-    return [own, one, two, three, over_one, over_two], [four, over_three, over_four], dense
+    return [own, one, two, three, over_own, over_one, over_two], [four, over_three, over_four], dense
 
 
 def per_device(embedding, tiles, tile_rows, tile_cols, counts):

time: 141 us -> 140 us (level)
  waiting for transfers between devices: 26.2 us -> 21.9 us
  blocking collectives: 42.4 us -> 44.7 us
  starting transfers between devices: 52.4 us -> 54.2 us
    ppermute x12, waiting for transfers between devices: 18.3 us -> 11.6 us  [onward(): return lax.ppermute(piece, ('row', 'col'), pairs)]
    ppermute x3, starting transfers between devices: 8.96 us -> 13.1 us  [per_device(): arrived = lax.ppermute(theirs, 'col', flip_core)]
    ppermute x12, starting transfers between devices: 20.4 us -> 17.3 us  [onward(): return lax.ppermute(piece, ('row', 'col'), pairs)]
    ppermute x12 -> x15, waiting for transfers between devices: 2.38 us -> 4.83 us  [over(): return lax.ppermute(piece, 'row', flip_x)]
    all_to_all x3, blocking collectives: 42.4 us -> 44.7 us  [per_device(): lax.all_to_all(pair.reshape(n_col // 2, per_dev, width), 'col', split_axi...]
    ppermute x12 -> x15, starting transfers between devices: 12.3 us -> 13 us  [over(): return lax.ppermute(piece, 'row', flip_x)]
  transfers between devices with their start and end apart: 32 -> 35, of which waited for: 13 -> 18; matrix products, arithmetic and copies ran while one was open for 1% -> 1% of each run, Pallas kernels for 8% -> 9%
where the time goes in v3:
time: 140 us
  starting transfers between devices  54.2 us (39%)
  blocking collectives  44.7 us (32%)
  waiting for transfers between devices  21.9 us (16%)
  Pallas kernels  14.2 us (10%)
  other arithmetic  3.04 us (2%)
  local copies, waits for them, and re-layouts  1.61 us (1%)
    all_to_all x3, blocking collectives, per_device(): lax.all_to_all(pair.reshape(n_col // 2, per_dev, width), 'col', split_axi...  44.7 us
    ppermute x12, starting transfers between devices, onward(): return lax.ppermute(piece, ('row', 'col'), pairs)  17.3 us
    ppermute x3, starting transfers between devices, per_device(): arrived = lax.ppermute(theirs, 'col', flip_core)  13.1 us
    ppermute x15, starting transfers between devices, over(): return lax.ppermute(piece, 'row', flip_x)  13 us
    ppermute x12, waiting for transfers between devices, onward(): return lax.ppermute(piece, ('row', 'col'), pairs)  11.6 us
    ppermute x3, starting transfers between devices, swap(): return lax.ppermute(piece, 'col', flip_core)  8.31 us
    pallas_call x3, Pallas kernels, head_multiply(): pl.pallas_call(kernel, out_shape=jax.ShapeDtypeStruct((n_rows, width), jn...  7.08 us
    ppermute x15, waiting for transfers between devices, over(): return lax.ppermute(piece, 'row', flip_x)  4.83 us
  transfers between devices with their start and end apart: 35, of which 18 were waited for; matrix products, arithmetic and copies ran while one was open for 1% of the time, Pallas kernels for 9%

profile of v3, /device:TPU:1, one launch (start us, length us, event | category | flops | bytes accessed | tf_op | source)
XLA Modules:
  0.0 140.5 jit_solution(852356749257150926)
XLA Ops:
  0.0 0.9 convert_element_type.36.refs_0_
  0.9 3.3 %collective-permute-start = (bf16[128,256]{1,0:T(8,128)(2,1)S(1)}, bf16[128,256]{1,0:T(8,128)(2,1)S(1)}, u32[]{:S(2)}, u32[]{:S(2)}) collective-permute-start(bf16[128,256]{1,0:T(8,128)(2,1)S(1)} %convert_element_type.36.refs_0_), channel_id=1, source_target_pairs={{0,1},{1,0},{2,3},{3,2},{4,5},{5,4},{6,7},{7,6},{8,9},{9,8},{10,11... | collective-permute-start | bytes 196616 | tf_op jit(solution)/shard_map/core_swap/ppermute | solution.py:186
  4.2 0.9 collective-permute-done
  5.5 3.9 %collective-permute-start.2 = (bf16[256,256]{1,0:T(8,128)(2,1)S(1)}, bf16[256,256]{1,0:T(8,128)(2,1)S(1)}, u32[]{:S(2)}, u32[]{:S(2)}) collective-permute-start(bf16[256,256]{1,0:T(8,128)(2,1)S(1)} %pad_maximum_fusion), channel_id=1, source_target_pairs={{0,32},{1,225},{2,34},{3,227},{4,36},{5,229},{6,38},{7,231},{8,40}... | collective-permute-start | bytes 393224 | tf_op jit(solution)/shard_map/z_one/ppermute | solution.py:178
  9.4 1.2 collective-permute-start.1
  10.6 1.2 collective-permute-start.3
  12.9 1.1 collective-permute-done.3.refs_4_
  14.0 1.2 collective-permute-start.8
  15.7 0.7 pad_add_fusion.refs_0_
  16.4 2.1 %collective-permute-start.5 = (s32[129]{0:T(256)S(1)}, s32[129]{0:T(256)S(1)}, u32[]{:S(2)}, u32[]{:S(2)}) collective-permute-start(s32[129]{0:T(256)S(1)} %pad_add_fusion.refs_0_), channel_id=1, source_target_pairs={{0,1},{1,0},{2,3},{3,2},{4,5},{5,4},{6,7},{7,6},{8,9},{9,8},{10,11... | collective-permute-start | bytes 1556 | tf_op jit(solution)/shard_map/place_swap/ppermute | solution.py:218
  18.5 4.1 %collective-permute-start.4 = (bf16[128,256]{1,0:T(8,128)(2,1)S(1)}, bf16[128,256]{1,0:T(8,128)(2,1)S(1)}, u32[]{:S(2)}, u32[]{:S(2)}) collective-permute-start(bf16[128,256]{1,0:T(8,128)(2,1)S(1)} %slice.9), channel_id=1, source_target_pairs={{0,64},{1,193},{2,66},{3,195},{4,68},{5,197},{6,70},{7,199},{8,72}... | collective-permute-start | bytes 196616 | tf_op jit(solution)/shard_map/z_four/ppermute | solution.py:178
  22.7 1.2 collective-permute-start.10
  23.9 1.6 %copy-done = bf16[1,1,64,128,128]{4,3,2,1,0:T(8,128)(2,1)S(1)} copy-done((bf16[1,1,64,128,128]{4,3,2,1,0:T(8,128)(2,1)S(1)}, bf16[1,1,64,128,128]{4,3,2,1,0:T(8,128)(2,1)}, u32[]{:S(2)}) %copy-start) | copy-done | bytes 2097176
  25.5 3.4 %build_dense.1.dense_ref = bf16[2048,2048]{1,0:T(8,128)(2,1)S(1)} custom-call(s32[129]{0:T(256)S(1)} %pad_add_fusion.refs_0_, s32[129]{0:T(256)S(1)} %collective-permute-done.5.refs_1_, s32[2]{0:T(128)S(1)} %pad_add_fusion.1.refs_2_, bf16[64,128,128]{2,1,0:T(8,128)(2,1)S(1)} %bitcast.11, bf16[64,128,128]{2,1,0:T(8,128)(2,1)S(1)} %collective-permute-done.6.refs_4_), custom_call_target="tpu_custom_call" | custom-call | flops 4194304 | bytes 25165824 | tf_op jit(solution)/shard_map/build_dense/pallas_call | solution.py:69
  28.9 0.7 collective-permute-start.11
  29.6 2.4 %head_multiply.3.head_ref = f32[2048,256]{1,0:T(8,128)S(1)} custom-call(bf16[2048,2048]{1,0:T(8,128)(2,1)S(1)} %build_dense.1.dense_ref, bf16[128,256]{1,0:T(8,128)(2,1)S(1)} %convert_element_type.36.refs_0_, bf16[256,256]{1,0:T(8,128)(2,1)S(1)} %collective-permute-done.2.refs_1_, bf16[256,256]{1,0:T(8,128)(2,1)S(1)} %collective-permute-done.1.refs_2_, ...), custom_call_target="tpu_custom_call" | custom-call | flops 1610612736 | bytes 6291456 | tf_op jit(solution)/shard_map/head_multiply/pallas_call | solution.py:120
  32.8 2.8 %collective-permute-start.12 = (bf16[1024,256]{1,0:T(8,128)(2,1)S(1)}, bf16[1024,256]{1,0:T(8,128)(2,1)S(1)}, u32[]{:S(2)}, u32[]{:S(2)}) collective-permute-start(bf16[1024,256]{1,0:T(8,128)(2,1)S(1)} %tail_multiply.7), channel_id=1, source_target_pairs={{0,1},{1,0},{2,3},{3,2},{4,5},{5,4},{6,7},{7,6},{8,9},{9,8},{10,11... | collective-permute-start | bytes 1572872 | tf_op jit(solution)/shard_map/partial_swap/ppermute | solution.py:232
  36.2 0.9 collective-permute-done.12
  37.3 18.5 %all_to_all.15 = bf16[8,128,256]{2,1,0:T(8,128)(2,1)S(1)} all-to-all(bf16[8,128,256]{2,1,0:T(8,128)(2,1)S(1)} %bitcast.12), channel_id=1, replica_groups={{0,2,4,6,8,10,12,14},{1,3,5,7,9,11,13,15},{16,18,20,22,24,26,28,30},{17..., dimensions={0} | all-to-all | bytes 1048576 | tf_op jit(solution)/shard_map/all_to_all | solution.py:235
  55.9 2.6 %collective-permute-start.13 = (bf16[128,256]{1,0:T(8,128)(2,1)S(1)}, bf16[128,256]{1,0:T(8,128)(2,1)S(1)}, u32[]{:S(2)}, u32[]{:S(2)}) collective-permute-start(bf16[128,256]{1,0:T(8,128)(2,1)S(1)} %convert_element_type.40.refs_0_), channel_id=1, source_target_pairs={{0,1},{1,0},{2,3},{3,2},{4,5},{5,4},{6,7},{7,6},{8,9},{9,8},{10,11... | collective-permute-start | bytes 196616 | tf_op jit(solution)/shard_map/core_swap/ppermute | solution.py:186
  58.5 0.9 collective-permute-done.13
  59.8 3.4 %collective-permute-start.17 = (bf16[256,256]{1,0:T(8,128)(2,1)S(1)}, bf16[256,256]{1,0:T(8,128)(2,1)S(1)}, u32[]{:S(2)}, u32[]{:S(2)}) collective-permute-start(bf16[256,256]{1,0:T(8,128)(2,1)S(1)} %pad_maximum_fusion.1), channel_id=1, source_target_pairs={{0,96},{1,161},{2,98},{3,163},{4,100},{5,165},{6,102},{7,167},{8,1... | collective-permute-start | bytes 393224 | tf_op jit(solution)/shard_map/z_three/ppermute | solution.py:178
  63.2 1.4 collective-permute-done.15.refs_1_
  65.0 1.0 collective-permute-start.19
  66.1 0.9 collective-permute-start.20
  67.0 3.5 %collective-permute-done.17.refs_3_ = bf16[256,256]{1,0:T(8,128)(2,1)S(1)} collective-permute-done((bf16[256,256]{1,0:T(8,128)(2,1)S(1)}, bf16[256,256]{1,0:T(8,128)(2,1)S(1)}, u32[]{:S(2)}, u32[]{:S(2)}) %collective-permute-start.17) | collective-permute-done | bytes 131104 | tf_op jit(solution)/shard_map/z_three/ppermute | solution.py:178
  71.1 0.9 collective-permute-start.22
  72.0 2.4 %head_multiply.4.head_ref = f32[2048,256]{1,0:T(8,128)S(1)} custom-call(bf16[2048,2048]{1,0:T(8,128)(2,1)S(1)} %build_dense.1.dense_ref, bf16[128,256]{1,0:T(8,128)(2,1)S(1)} %convert_element_type.40.refs_0_, bf16[256,256]{1,0:T(8,128)(2,1)S(1)} %collective-permute-done.15.refs_1_, bf16[256,256]{1,0:T(8,128)(2,1)S(1)} %collective-permute-done.14.refs_2_, ...), custom_call_target="tpu_custom_call" | custom-call | flops 1610612736 | bytes 6291456 | tf_op jit(solution)/shard_map/head_multiply/pallas_call | solution.py:120
  74.3 2.7 %collective-permute-done.22.refs_2_ = bf16[128,256]{1,0:T(8,128)(2,1)S(1)} collective-permute-done((bf16[128,256]{1,0:T(8,128)(2,1)S(1)}, bf16[128,256]{1,0:T(8,128)(2,1)S(1)}, u32[]{:S(2)}, u32[]{:S(2)}) %collective-permute-start.22) | collective-permute-done | bytes 65568 | tf_op jit(solution)/shard_map/x_four/ppermute | solution.py:182
  77.6 4.4 %collective-permute-start.23 = (bf16[1024,256]{1,0:T(8,128)(2,1)S(1)}, bf16[1024,256]{1,0:T(8,128)(2,1)S(1)}, u32[]{:S(2)}, u32[]{:S(2)}) collective-permute-start(bf16[1024,256]{1,0:T(8,128)(2,1)S(1)} %tail_multiply.9), channel_id=1, source_target_pairs={{0,1},{1,0},{2,3},{3,2},{4,5},{5,4},{6,7},{7,6},{8,9},{9,8},{10,11... | collective-permute-start | bytes 1572872 | tf_op jit(solution)/shard_map/partial_swap/ppermute | solution.py:232
  82.7 0.9 collective-permute-done.23
  83.7 12.5 %all_to_all.16 = bf16[8,128,256]{2,1,0:T(8,128)(2,1)S(1)} all-to-all(bf16[8,128,256]{2,1,0:T(8,128)(2,1)S(1)} %bitcast.13), channel_id=1, replica_groups={{0,2,4,6,8,10,12,14},{1,3,5,7,9,11,13,15},{16,18,20,22,24,26,28,30},{17..., dimensions={0} | all-to-all | bytes 1048576 | tf_op jit(solution)/shard_map/all_to_all | solution.py:235
  96.4 2.4 %collective-permute-start.24 = (bf16[128,256]{1,0:T(8,128)(2,1)S(1)}, bf16[128,256]{1,0:T(8,128)(2,1)S(1)}, u32[]{:S(2)}, u32[]{:S(2)}) collective-permute-start(bf16[128,256]{1,0:T(8,128)(2,1)S(1)} %convert_element_type.44.refs_0_), channel_id=1, source_target_pairs={{0,1},{1,0},{2,3},{3,2},{4,5},{5,4},{6,7},{7,6},{8,9},{9,8},{10,11... | collective-permute-start | bytes 196616 | tf_op jit(solution)/shard_map/core_swap/ppermute | solution.py:186
  98.8 0.9 collective-permute-done.24
  99.8 1.0 collective-permute-start.25
  100.8 0.7 collective-permute-start.27
  101.4 1.9 %collective-permute-start.28 = (bf16[256,256]{1,0:T(8,128)(2,1)S(1)}, bf16[256,256]{1,0:T(8,128)(2,1)S(1)}, u32[]{:S(2)}, u32[]{:S(2)}) collective-permute-start(bf16[256,256]{1,0:T(8,128)(2,1)S(1)} %pad_maximum_fusion.2), channel_id=1, source_target_pairs={{0,96},{1,161},{2,98},{3,163},{4,100},{5,165},{6,102},{7,167},{8,1... | collective-permute-start | bytes 393224 | tf_op jit(solution)/shard_map/z_three/ppermute | solution.py:178
  103.9 2.4 %collective-permute-start.29 = (bf16[256,256]{1,0:T(8,128)(2,1)S(1)}, bf16[256,256]{1,0:T(8,128)(2,1)S(1)}, u32[]{:S(2)}, u32[]{:S(2)}) collective-permute-start(bf16[256,256]{1,0:T(8,128)(2,1)S(1)} %collective-permute-done.26.refs_1_), channel_id=1, source_target_pairs={{0,16},{16,0},{32,48},{48,32},{64,80},{80,64},{96,112},{112,96},{1... | collective-permute-start | bytes 393224 | tf_op jit(solution)/shard_map/x_one/ppermute | solution.py:182
  106.3 3.4 %collective-permute-done.25.refs_2_ = bf16[256,256]{1,0:T(8,128)(2,1)S(1)} collective-permute-done((bf16[256,256]{1,0:T(8,128)(2,1)S(1)}, bf16[256,256]{1,0:T(8,128)(2,1)S(1)}, u32[]{:S(2)}, u32[]{:S(2)}) %collective-permute-start.25) | collective-permute-done | bytes 131104 | tf_op jit(solution)/shard_map/z_two/ppermute | solution.py:178
  109.8 1.4 collective-permute-done.28.refs_3_
  111.2 1.7 %collective-permute-start.32 = (bf16[256,256]{1,0:T(8,128)(2,1)S(1)}, bf16[256,256]{1,0:T(8,128)(2,1)S(1)}, u32[]{:S(2)}, u32[]{:S(2)}) collective-permute-start(bf16[256,256]{1,0:T(8,128)(2,1)S(1)} %collective-permute-done.28.refs_3_), channel_id=1, source_target_pairs={{0,16},{16,0},{32,48},{48,32},{64,80},{80,64},{96,112},{112,96},{1... | collective-permute-start | bytes 393224 | tf_op jit(solution)/shard_map/x_three/ppermute | solution.py:182
  112.9 1.0 collective-permute-done.31.refs_0_
  114.0 1.3 collective-permute-start.33
  115.3 2.4 %head_multiply.5.head_ref = f32[2048,256]{1,0:T(8,128)S(1)} custom-call(bf16[2048,2048]{1,0:T(8,128)(2,1)S(1)} %build_dense.1.dense_ref, bf16[128,256]{1,0:T(8,128)(2,1)S(1)} %convert_element_type.44.refs_0_, bf16[256,256]{1,0:T(8,128)(2,1)S(1)} %collective-permute-done.26.refs_1_, bf16[256,256]{1,0:T(8,128)(2,1)S(1)} %collective-permute-done.25.refs_2_, ...), custom_call_target="tpu_custom_call" | custom-call | flops 1610612736 | bytes 6291456 | tf_op jit(solution)/shard_map/head_multiply/pallas_call | solution.py:120
  118.6 5.8 %collective-permute-start.34 = (bf16[1024,256]{1,0:T(8,128)(2,1)S(1)}, bf16[1024,256]{1,0:T(8,128)(2,1)S(1)}, u32[]{:S(2)}, u32[]{:S(2)}) collective-permute-start(bf16[1024,256]{1,0:T(8,128)(2,1)S(1)} %tail_multiply.11), channel_id=1, source_target_pairs={{0,1},{1,0},{2,3},{3,2},{4,5},{5,4},{6,7},{7,6},{8,9},{9,8},{10,11... | collective-permute-start | bytes 1572872 | tf_op jit(solution)/shard_map/partial_swap/ppermute | solution.py:232
  125.1 0.9 collective-permute-done.34
  126.1 13.6 %all_to_all.17 = bf16[8,128,256]{2,1,0:T(8,128)(2,1)S(1)} all-to-all(bf16[8,128,256]{2,1,0:T(8,128)(2,1)S(1)} %bitcast.14), channel_id=1, replica_groups={{0,2,4,6,8,10,12,14},{1,3,5,7,9,11,13,15},{16,18,20,22,24,26,28,30},{17..., dimensions={0} | all-to-all | bytes 1048576 | tf_op jit(solution)/shard_map/all_to_all | solution.py:235
  139.8 0.7 add_multiply_fusion
  (57 shorter events, 8.4 us)
Async XLA Ops:
  0.9 4.2 %collective-permute-start = (bf16[128,256]{1,0:T(8,128)(2,1)S(1)}, bf16[128,256]{1,0:T(8,128)(2,1)S(1)}, u32[]{:S(2)}, u32[]{:S(2)}) collective-permute-start(bf16[128,256]{1,0:T(8,128)(2,1)S(1)} %convert_element_type.36.refs_0_), channel_id=1, source_target_pairs={{0,1},{1,0},{2,3},{3,2},{4,5},{5,4},{6,7},{7,6},{8,9},{9,8},{10,11... | collective-permute-start | bytes 196616 | tf_op jit(solution)/shard_map/core_swap/ppermute | solution.py:186
  5.1 18.8 %collective-permute-start.6 = (bf16[64,128,128]{2,1,0:T(8,128)(2,1)}, bf16[64,128,128]{2,1,0:T(8,128)(2,1)S(1)}, u32[]{:S(2)}, u32[]{:S(2)}) collective-permute-start(bf16[64,128,128]{2,1,0:T(8,128)(2,1)} %bitcast.10), channel_id=1, source_target_pairs={{0,1},{1,0},{2,3},{3,2},{4,5},{5,4},{6,7},{7,6},{8,9},{9,8},{10,11... | collective-permute-start | bytes 6291464 | tf_op jit(solution)/shard_map/tile_swap/ppermute | solution.py:223
  5.5 8.5 %collective-permute-start.2 = (bf16[256,256]{1,0:T(8,128)(2,1)S(1)}, bf16[256,256]{1,0:T(8,128)(2,1)S(1)}, u32[]{:S(2)}, u32[]{:S(2)}) collective-permute-start(bf16[256,256]{1,0:T(8,128)(2,1)S(1)} %pad_maximum_fusion), channel_id=1, source_target_pairs={{0,32},{1,225},{2,34},{3,227},{4,36},{5,229},{6,38},{7,231},{8,40}... | collective-permute-start | bytes 393224 | tf_op jit(solution)/shard_map/z_one/ppermute | solution.py:178
  9.4 5.8 %collective-permute-start.1 = (bf16[256,256]{1,0:T(8,128)(2,1)S(1)}, bf16[256,256]{1,0:T(8,128)(2,1)S(1)}, u32[]{:S(2)}, u32[]{:S(2)}) collective-permute-start(bf16[256,256]{1,0:T(8,128)(2,1)S(1)} %pad_maximum_fusion), channel_id=1, source_target_pairs={{0,64},{1,193},{2,66},{3,195},{4,68},{5,197},{6,70},{7,199},{8,72}... | collective-permute-start | bytes 393224 | tf_op jit(solution)/shard_map/z_two/ppermute | solution.py:178
  10.6 3.4 %collective-permute-start.3 = (bf16[128,256]{1,0:T(8,128)(2,1)S(1)}, bf16[128,256]{1,0:T(8,128)(2,1)S(1)}, u32[]{:S(2)}, u32[]{:S(2)}) collective-permute-start(bf16[128,256]{1,0:T(8,128)(2,1)S(1)} %convert_element_type.36.refs_0_), channel_id=1, source_target_pairs={{0,16},{16,0},{32,48},{48,32},{64,80},{80,64},{96,112},{112,96},{1... | collective-permute-start | bytes 196616 | tf_op jit(solution)/shard_map/x_own/ppermute | solution.py:182
  11.8 6.7 %collective-permute-start.7 = (bf16[256,256]{1,0:T(8,128)(2,1)S(1)}, bf16[256,256]{1,0:T(8,128)(2,1)S(1)}, u32[]{:S(2)}, u32[]{:S(2)}) collective-permute-start(bf16[256,256]{1,0:T(8,128)(2,1)S(1)} %pad_maximum_fusion), channel_id=1, source_target_pairs={{0,96},{1,161},{2,98},{3,163},{4,100},{5,165},{6,102},{7,167},{8,1... | collective-permute-start | bytes 393224 | tf_op jit(solution)/shard_map/z_three/ppermute | solution.py:178
  14.0 15.6 %collective-permute-start.8 = (bf16[256,256]{1,0:T(8,128)(2,1)S(1)}, bf16[256,256]{1,0:T(8,128)(2,1)S(1)}, u32[]{:S(2)}, u32[]{:S(2)}) collective-permute-start(bf16[256,256]{1,0:T(8,128)(2,1)S(1)} %collective-permute-done.2.refs_1_), channel_id=1, source_target_pairs={{0,16},{16,0},{32,48},{48,32},{64,80},{80,64},{96,112},{112,96},{1... | collective-permute-start | bytes 393224 | tf_op jit(solution)/shard_map/x_one/ppermute | solution.py:182
  15.2 14.4 %collective-permute-start.9 = (bf16[256,256]{1,0:T(8,128)(2,1)S(1)}, bf16[256,256]{1,0:T(8,128)(2,1)S(1)}, u32[]{:S(2)}, u32[]{:S(2)}) collective-permute-start(bf16[256,256]{1,0:T(8,128)(2,1)S(1)} %collective-permute-done.1.refs_2_), channel_id=1, source_target_pairs={{0,16},{16,0},{32,48},{48,32},{64,80},{80,64},{96,112},{112,96},{1... | collective-permute-start | bytes 393224 | tf_op jit(solution)/shard_map/x_two/ppermute | solution.py:182
  16.4 6.3 %collective-permute-start.5 = (s32[129]{0:T(256)S(1)}, s32[129]{0:T(256)S(1)}, u32[]{:S(2)}, u32[]{:S(2)}) collective-permute-start(s32[129]{0:T(256)S(1)} %pad_add_fusion.refs_0_), channel_id=1, source_target_pairs={{0,1},{1,0},{2,3},{3,2},{4,5},{5,4},{6,7},{7,6},{8,9},{9,8},{10,11... | collective-permute-start | bytes 1556 | tf_op jit(solution)/shard_map/place_swap/ppermute | solution.py:218
  18.5 10.4 %collective-permute-start.4 = (bf16[128,256]{1,0:T(8,128)(2,1)S(1)}, bf16[128,256]{1,0:T(8,128)(2,1)S(1)}, u32[]{:S(2)}, u32[]{:S(2)}) collective-permute-start(bf16[128,256]{1,0:T(8,128)(2,1)S(1)} %slice.9), channel_id=1, source_target_pairs={{0,64},{1,193},{2,66},{3,195},{4,68},{5,197},{6,70},{7,199},{8,72}... | collective-permute-start | bytes 196616 | tf_op jit(solution)/shard_map/z_four/ppermute | solution.py:178
  22.7 9.3 %collective-permute-start.10 = (bf16[256,256]{1,0:T(8,128)(2,1)S(1)}, bf16[256,256]{1,0:T(8,128)(2,1)S(1)}, u32[]{:S(2)}, u32[]{:S(2)}) collective-permute-start(bf16[256,256]{1,0:T(8,128)(2,1)S(1)} %collective-permute-done.7.refs_3_), channel_id=1, source_target_pairs={{0,16},{16,0},{32,48},{48,32},{64,80},{80,64},{96,112},{112,96},{1... | collective-permute-start | bytes 393224 | tf_op jit(solution)/shard_map/x_three/ppermute | solution.py:182
  23.9 1.6 %copy-start = (bf16[1,1,64,128,128]{4,3,2,1,0:T(8,128)(2,1)S(1)}, bf16[1,1,64,128,128]{4,3,2,1,0:T(8,128)(2,1)}, u32[]{:S(2)}) copy-start(bf16[1,1,64,128,128]{4,3,2,1,0:T(8,128)(2,1)} %param.6) | copy-start | bytes 6291460
  28.9 3.2 %collective-permute-start.11 = (bf16[128,256]{1,0:T(8,128)(2,1)S(1)}, bf16[128,256]{1,0:T(8,128)(2,1)S(1)}, u32[]{:S(2)}, u32[]{:S(2)}) collective-permute-start(bf16[128,256]{1,0:T(8,128)(2,1)S(1)} %collective-permute-done.4.refs_0_), channel_id=1, source_target_pairs={{0,16},{16,0},{32,48},{48,32},{64,80},{80,64},{96,112},{112,96},{1... | collective-permute-start | bytes 196616 | tf_op jit(solution)/shard_map/x_four/ppermute | solution.py:182
  32.8 4.4 %collective-permute-start.12 = (bf16[1024,256]{1,0:T(8,128)(2,1)S(1)}, bf16[1024,256]{1,0:T(8,128)(2,1)S(1)}, u32[]{:S(2)}, u32[]{:S(2)}) collective-permute-start(bf16[1024,256]{1,0:T(8,128)(2,1)S(1)} %tail_multiply.7), channel_id=1, source_target_pairs={{0,1},{1,0},{2,3},{3,2},{4,5},{5,4},{6,7},{7,6},{8,9},{9,8},{10,11... | collective-permute-start | bytes 1572872 | tf_op jit(solution)/shard_map/partial_swap/ppermute | solution.py:232
  55.9 3.5 %collective-permute-start.13 = (bf16[128,256]{1,0:T(8,128)(2,1)S(1)}, bf16[128,256]{1,0:T(8,128)(2,1)S(1)}, u32[]{:S(2)}, u32[]{:S(2)}) collective-permute-start(bf16[128,256]{1,0:T(8,128)(2,1)S(1)} %convert_element_type.40.refs_0_), channel_id=1, source_target_pairs={{0,1},{1,0},{2,3},{3,2},{4,5},{5,4},{6,7},{7,6},{8,9},{9,8},{10,11... | collective-permute-start | bytes 196616 | tf_op jit(solution)/shard_map/core_swap/ppermute | solution.py:186
  59.4 5.2 %collective-permute-start.15 = (bf16[256,256]{1,0:T(8,128)(2,1)S(1)}, bf16[256,256]{1,0:T(8,128)(2,1)S(1)}, u32[]{:S(2)}, u32[]{:S(2)}) collective-permute-start(bf16[256,256]{1,0:T(8,128)(2,1)S(1)} %pad_maximum_fusion.1), channel_id=1, source_target_pairs={{0,32},{1,225},{2,34},{3,227},{4,36},{5,229},{6,38},{7,231},{8,40}... | collective-permute-start | bytes 393224 | tf_op jit(solution)/shard_map/z_one/ppermute | solution.py:178
  59.5 5.6 %collective-permute-start.14 = (bf16[256,256]{1,0:T(8,128)(2,1)S(1)}, bf16[256,256]{1,0:T(8,128)(2,1)S(1)}, u32[]{:S(2)}, u32[]{:S(2)}) collective-permute-start(bf16[256,256]{1,0:T(8,128)(2,1)S(1)} %pad_maximum_fusion.1), channel_id=1, source_target_pairs={{0,64},{1,193},{2,66},{3,195},{4,68},{5,197},{6,70},{7,199},{8,72}... | collective-permute-start | bytes 393224 | tf_op jit(solution)/shard_map/z_two/ppermute | solution.py:178
  59.7 3.5 %collective-permute-start.16 = (bf16[128,256]{1,0:T(8,128)(2,1)S(1)}, bf16[128,256]{1,0:T(8,128)(2,1)S(1)}, u32[]{:S(2)}, u32[]{:S(2)}) collective-permute-start(bf16[128,256]{1,0:T(8,128)(2,1)S(1)} %convert_element_type.40.refs_0_), channel_id=1, source_target_pairs={{0,16},{16,0},{32,48},{48,32},{64,80},{80,64},{96,112},{112,96},{1... | collective-permute-start | bytes 196616 | tf_op jit(solution)/shard_map/x_own/ppermute | solution.py:182
  59.8 10.7 %collective-permute-start.17 = (bf16[256,256]{1,0:T(8,128)(2,1)S(1)}, bf16[256,256]{1,0:T(8,128)(2,1)S(1)}, u32[]{:S(2)}, u32[]{:S(2)}) collective-permute-start(bf16[256,256]{1,0:T(8,128)(2,1)S(1)} %pad_maximum_fusion.1), channel_id=1, source_target_pairs={{0,96},{1,161},{2,98},{3,163},{4,100},{5,165},{6,102},{7,167},{8,1... | collective-permute-start | bytes 393224 | tf_op jit(solution)/shard_map/z_three/ppermute | solution.py:178
  64.6 7.4 %collective-permute-start.18 = (bf16[256,256]{1,0:T(8,128)(2,1)S(1)}, bf16[256,256]{1,0:T(8,128)(2,1)S(1)}, u32[]{:S(2)}, u32[]{:S(2)}) collective-permute-start(bf16[256,256]{1,0:T(8,128)(2,1)S(1)} %collective-permute-done.15.refs_1_), channel_id=1, source_target_pairs={{0,16},{16,0},{32,48},{48,32},{64,80},{80,64},{96,112},{112,96},{1... | collective-permute-start | bytes 393224 | tf_op jit(solution)/shard_map/x_one/ppermute | solution.py:182
  65.0 6.9 %collective-permute-start.19 = (bf16[256,256]{1,0:T(8,128)(2,1)S(1)}, bf16[256,256]{1,0:T(8,128)(2,1)S(1)}, u32[]{:S(2)}, u32[]{:S(2)}) collective-permute-start(bf16[256,256]{1,0:T(8,128)(2,1)S(1)} %collective-permute-done.14.refs_2_), channel_id=1, source_target_pairs={{0,16},{16,0},{32,48},{48,32},{64,80},{80,64},{96,112},{112,96},{1... | collective-permute-start | bytes 393224 | tf_op jit(solution)/shard_map/x_two/ppermute | solution.py:182
  66.1 5.0 %collective-permute-start.20 = (bf16[128,256]{1,0:T(8,128)(2,1)S(1)}, bf16[128,256]{1,0:T(8,128)(2,1)S(1)}, u32[]{:S(2)}, u32[]{:S(2)}) collective-permute-start(bf16[128,256]{1,0:T(8,128)(2,1)S(1)} %slice.10), channel_id=1, source_target_pairs={{0,64},{1,193},{2,66},{3,195},{4,68},{5,197},{6,70},{7,199},{8,72}... | collective-permute-start | bytes 196616 | tf_op jit(solution)/shard_map/z_four/ppermute | solution.py:178
  70.5 6.5 %collective-permute-start.21 = (bf16[256,256]{1,0:T(8,128)(2,1)S(1)}, bf16[256,256]{1,0:T(8,128)(2,1)S(1)}, u32[]{:S(2)}, u32[]{:S(2)}) collective-permute-start(bf16[256,256]{1,0:T(8,128)(2,1)S(1)} %collective-permute-done.17.refs_3_), channel_id=1, source_target_pairs={{0,16},{16,0},{32,48},{48,32},{64,80},{80,64},{96,112},{112,96},{1... | collective-permute-start | bytes 393224 | tf_op jit(solution)/shard_map/x_three/ppermute | solution.py:182
  71.1 5.9 %collective-permute-start.22 = (bf16[128,256]{1,0:T(8,128)(2,1)S(1)}, bf16[128,256]{1,0:T(8,128)(2,1)S(1)}, u32[]{:S(2)}, u32[]{:S(2)}) collective-permute-start(bf16[128,256]{1,0:T(8,128)(2,1)S(1)} %collective-permute-done.20.refs_0_), channel_id=1, source_target_pairs={{0,16},{16,0},{32,48},{48,32},{64,80},{80,64},{96,112},{112,96},{1... | collective-permute-start | bytes 196616 | tf_op jit(solution)/shard_map/x_four/ppermute | solution.py:182
  77.6 6.0 %collective-permute-start.23 = (bf16[1024,256]{1,0:T(8,128)(2,1)S(1)}, bf16[1024,256]{1,0:T(8,128)(2,1)S(1)}, u32[]{:S(2)}, u32[]{:S(2)}) collective-permute-start(bf16[1024,256]{1,0:T(8,128)(2,1)S(1)} %tail_multiply.9), channel_id=1, source_target_pairs={{0,1},{1,0},{2,3},{3,2},{4,5},{5,4},{6,7},{7,6},{8,9},{9,8},{10,11... | collective-permute-start | bytes 1572872 | tf_op jit(solution)/shard_map/partial_swap/ppermute | solution.py:232
  96.4 3.3 %collective-permute-start.24 = (bf16[128,256]{1,0:T(8,128)(2,1)S(1)}, bf16[128,256]{1,0:T(8,128)(2,1)S(1)}, u32[]{:S(2)}, u32[]{:S(2)}) collective-permute-start(bf16[128,256]{1,0:T(8,128)(2,1)S(1)} %convert_element_type.44.refs_0_), channel_id=1, source_target_pairs={{0,1},{1,0},{2,3},{3,2},{4,5},{5,4},{6,7},{7,6},{8,9},{9,8},{10,11... | collective-permute-start | bytes 196616 | tf_op jit(solution)/shard_map/core_swap/ppermute | solution.py:186
  99.7 4.2 %collective-permute-start.26 = (bf16[256,256]{1,0:T(8,128)(2,1)S(1)}, bf16[256,256]{1,0:T(8,128)(2,1)S(1)}, u32[]{:S(2)}, u32[]{:S(2)}) collective-permute-start(bf16[256,256]{1,0:T(8,128)(2,1)S(1)} %pad_maximum_fusion.2), channel_id=1, source_target_pairs={{0,32},{1,225},{2,34},{3,227},{4,36},{5,229},{6,38},{7,231},{8,40}... | collective-permute-start | bytes 393224 | tf_op jit(solution)/shard_map/z_one/ppermute | solution.py:178
  99.8 9.9 %collective-permute-start.25 = (bf16[256,256]{1,0:T(8,128)(2,1)S(1)}, bf16[256,256]{1,0:T(8,128)(2,1)S(1)}, u32[]{:S(2)}, u32[]{:S(2)}) collective-permute-start(bf16[256,256]{1,0:T(8,128)(2,1)S(1)} %pad_maximum_fusion.2), channel_id=1, source_target_pairs={{0,64},{1,193},{2,66},{3,195},{4,68},{5,197},{6,70},{7,199},{8,72}... | collective-permute-start | bytes 393224 | tf_op jit(solution)/shard_map/z_two/ppermute | solution.py:178
  100.8 3.1 %collective-permute-start.27 = (bf16[128,256]{1,0:T(8,128)(2,1)S(1)}, bf16[128,256]{1,0:T(8,128)(2,1)S(1)}, u32[]{:S(2)}, u32[]{:S(2)}) collective-permute-start(bf16[128,256]{1,0:T(8,128)(2,1)S(1)} %convert_element_type.44.refs_0_), channel_id=1, source_target_pairs={{0,16},{16,0},{32,48},{48,32},{64,80},{80,64},{96,112},{112,96},{1... | collective-permute-start | bytes 196616 | tf_op jit(solution)/shard_map/x_own/ppermute | solution.py:182
  101.4 9.8 %collective-permute-start.28 = (bf16[256,256]{1,0:T(8,128)(2,1)S(1)}, bf16[256,256]{1,0:T(8,128)(2,1)S(1)}, u32[]{:S(2)}, u32[]{:S(2)}) collective-permute-start(bf16[256,256]{1,0:T(8,128)(2,1)S(1)} %pad_maximum_fusion.2), channel_id=1, source_target_pairs={{0,96},{1,161},{2,98},{3,163},{4,100},{5,165},{6,102},{7,167},{8,1... | collective-permute-start | bytes 393224 | tf_op jit(solution)/shard_map/z_three/ppermute | solution.py:178
  103.9 11.4 %collective-permute-start.29 = (bf16[256,256]{1,0:T(8,128)(2,1)S(1)}, bf16[256,256]{1,0:T(8,128)(2,1)S(1)}, u32[]{:S(2)}, u32[]{:S(2)}) collective-permute-start(bf16[256,256]{1,0:T(8,128)(2,1)S(1)} %collective-permute-done.26.refs_1_), channel_id=1, source_target_pairs={{0,16},{16,0},{32,48},{48,32},{64,80},{80,64},{96,112},{112,96},{1... | collective-permute-start | bytes 393224 | tf_op jit(solution)/shard_map/x_one/ppermute | solution.py:182
  109.7 5.6 %collective-permute-start.30 = (bf16[256,256]{1,0:T(8,128)(2,1)S(1)}, bf16[256,256]{1,0:T(8,128)(2,1)S(1)}, u32[]{:S(2)}, u32[]{:S(2)}) collective-permute-start(bf16[256,256]{1,0:T(8,128)(2,1)S(1)} %collective-permute-done.25.refs_2_), channel_id=1, source_target_pairs={{0,16},{16,0},{32,48},{48,32},{64,80},{80,64},{96,112},{112,96},{1... | collective-permute-start | bytes 393224 | tf_op jit(solution)/shard_map/x_two/ppermute | solution.py:182
  109.7 4.2 %collective-permute-start.31 = (bf16[128,256]{1,0:T(8,128)(2,1)S(1)}, bf16[128,256]{1,0:T(8,128)(2,1)S(1)}, u32[]{:S(2)}, u32[]{:S(2)}) collective-permute-start(bf16[128,256]{1,0:T(8,128)(2,1)S(1)} %slice.11), channel_id=1, source_target_pairs={{0,64},{1,193},{2,66},{3,195},{4,68},{5,197},{6,70},{7,199},{8,72}... | collective-permute-start | bytes 196616 | tf_op jit(solution)/shard_map/z_four/ppermute | solution.py:178
  111.2 6.8 %collective-permute-start.32 = (bf16[256,256]{1,0:T(8,128)(2,1)S(1)}, bf16[256,256]{1,0:T(8,128)(2,1)S(1)}, u32[]{:S(2)}, u32[]{:S(2)}) collective-permute-start(bf16[256,256]{1,0:T(8,128)(2,1)S(1)} %collective-permute-done.28.refs_3_), channel_id=1, source_target_pairs={{0,16},{16,0},{32,48},{48,32},{64,80},{80,64},{96,112},{112,96},{1... | collective-permute-start | bytes 393224 | tf_op jit(solution)/shard_map/x_three/ppermute | solution.py:182
  114.0 4.0 %collective-permute-start.33 = (bf16[128,256]{1,0:T(8,128)(2,1)S(1)}, bf16[128,256]{1,0:T(8,128)(2,1)S(1)}, u32[]{:S(2)}, u32[]{:S(2)}) collective-permute-start(bf16[128,256]{1,0:T(8,128)(2,1)S(1)} %collective-permute-done.31.refs_0_), channel_id=1, source_target_pairs={{0,16},{16,0},{32,48},{48,32},{64,80},{80,64},{96,112},{112,96},{1... | collective-permute-start | bytes 196616 | tf_op jit(solution)/shard_map/x_four/ppermute | solution.py:182
  118.6 7.4 %collective-permute-start.34 = (bf16[1024,256]{1,0:T(8,128)(2,1)S(1)}, bf16[1024,256]{1,0:T(8,128)(2,1)S(1)}, u32[]{:S(2)}, u32[]{:S(2)}) collective-permute-start(bf16[1024,256]{1,0:T(8,128)(2,1)S(1)} %tail_multiply.11), channel_id=1, source_target_pairs={{0,1},{1,0},{2,3},{3,2},{4,5},{5,4},{6,7},{7,6},{8,9},{9,8},{10,11... | collective-permute-start | bytes 1572872 | tf_op jit(solution)/shard_map/partial_swap/ppermute | solution.py:232
  125.1 14.7 %copy-start.1 = (f32[128,256]{1,0:T(8,128)S(1)}, f32[128,256]{1,0:T(8,128)}, u32[]{:S(2)}) copy-start(f32[128,256]{1,0:T(8,128)} %param.5) | copy-start | bytes 393220

commit v4 on v3

--- a/solution.py
+++ b/solution.py
@@ -191,6 +191,16 @@
     one = onward(both, 1, "z_one")
     two = onward(both, 2, "z_two")
     three = onward(both, 3, "z_three")
+    if build is None:
+        four = onward(own, 4, "z_four")
+        one, over_own = lax.optimization_barrier((one, over_own))
+        over_one = over(one, "x_one")
+        two, one = lax.optimization_barrier((two, one))
+        over_two = over(two, "x_two")
+        three, two = lax.optimization_barrier((three, two))
+        far = jnp.concatenate([three, four])
+        over_far = over(far, "x_far")
+        return [own, one, two, three, over_own, over_one, over_two], [four, over_far], None
     one, over_own = lax.optimization_barrier((one, over_own))
     over_one = over(one, "x_one")
     two, one = lax.optimization_barrier((two, one))
@@ -198,9 +208,7 @@
     four = onward(two[:rows], 2, "z_four")
     three, two = lax.optimization_barrier((three, two))
     over_three = over(three, "x_three")
-    last, dense = four, None
-    if build is not None:
-        last, dense = lax.optimization_barrier((four, build(sibling)))
+    last, dense = lax.optimization_barrier((four, build(sibling)))
     over_four = over(last, "x_four")
     return [own, one, two, three, over_own, over_one, over_two], [four, over_three, over_four], dense
 
@@ -221,7 +229,9 @@
         own_tiles, ready = lax.optimization_barrier((tiles[0, 0], ready))
         with jax.named_scope("tile_swap"):
             sib_tiles = lax.ppermute(own_tiles, "col", flip_core)
-        return build_dense(own_at, sib_at, meta, tiles[0, 0], sib_tiles, n_row, n_col)
+        with jax.named_scope("tile_stay"):
+            own_tiles = lax.ppermute(own_tiles, "col", [(j, j) for j in range(n_col)])
+        return build_dense(own_at, sib_at, meta, own_tiles, sib_tiles, n_row, n_col)
 
     early, late, dense = gather_pieces(embedding.astype(jnp.bfloat16), n_row, n_col, build)
     total = embedding

time: 140 us -> 142 us (1.014); the launches traced: 140 us -> 141 us
  starting transfers between devices: 54.2 us -> 60 us
  blocking collectives: 44.7 us -> 41.5 us
  waiting for transfers between devices: 21.9 us -> 19.9 us
  local copies, waits for them, and re-layouts: 1.61 us -> 0.01 us
    ppermute x12, starting transfers between devices: 17.3 us -> 33.4 us  [onward(): return lax.ppermute(piece, ('row', 'col'), pairs)]
    ppermute x15 -> x13, starting transfers between devices: 13 us -> 7.13 us  [over(): return lax.ppermute(piece, 'row', flip_x)]
    ppermute x3, starting transfers between devices: 13.1 us -> 8.12 us  [per_device(): arrived = lax.ppermute(theirs, 'col', flip_core)]
    all_to_all x3, blocking collectives: 44.7 us -> 41.5 us  [per_device(): lax.all_to_all(pair.reshape(n_col // 2, per_dev, width), 'col', split_axi...]
    ppermute x12, waiting for transfers between devices: 11.6 us -> 9 us  [onward(): return lax.ppermute(piece, ('row', 'col'), pairs)]
    ppermute x0 -> x1, starting transfers between devices: none -> 1.59 us  [build(): own_tiles = lax.ppermute(own_tiles, 'col', [(j, j) for j in range(n_col)])]
    unnamed x4 -> x2, local copies, waits for them, and re-layouts: 1.6 us -> 0.01 us
    ppermute x15 -> x13, waiting for transfers between devices: 4.83 us -> 4.99 us  [over(): return lax.ppermute(piece, 'row', flip_x)]
  transfers between devices with their start and end apart: 35 -> 34, of which waited for: 18 -> 16; matrix products, arithmetic and copies ran while one was open for 1% -> 1% of each run, Pallas kernels for 9% -> 10%
where the time goes in v4:
time: 142 us; the launch traced here: 141 us
  starting transfers between devices  60 us (42%)
  blocking collectives  41.5 us (29%)
  waiting for transfers between devices  19.9 us (14%)
  Pallas kernels  15.6 us (11%)
  other arithmetic  3.05 us (2%)
    all_to_all x3, blocking collectives, per_device(): lax.all_to_all(pair.reshape(n_col // 2, per_dev, width), 'col', split_axi...  41.5 us
    ppermute x12, starting transfers between devices, onward(): return lax.ppermute(piece, ('row', 'col'), pairs)  33.4 us
    ppermute x12, waiting for transfers between devices, onward(): return lax.ppermute(piece, ('row', 'col'), pairs)  9 us
    ppermute x3, starting transfers between devices, swap(): return lax.ppermute(piece, 'col', flip_core)  8.42 us
    ppermute x3, starting transfers between devices, per_device(): arrived = lax.ppermute(theirs, 'col', flip_core)  8.12 us
    ppermute x13, starting transfers between devices, over(): return lax.ppermute(piece, 'row', flip_x)  7.13 us
    pallas_call x3, Pallas kernels, head_multiply(): pl.pallas_call(kernel, out_shape=jax.ShapeDtypeStruct((n_rows, width), jn...  7.07 us
    ppermute x13, waiting for transfers between devices, over(): return lax.ppermute(piece, 'row', flip_x)  4.99 us
  transfers between devices with their start and end apart: 34, of which 16 were waited for; matrix products, arithmetic and copies ran while one was open for 1% of the time, Pallas kernels for 10%

profile of v4, /device:TPU:1, one launch (start us, length us, event | category | flops | bytes accessed | tf_op | source)
XLA Modules:
  0.0 140.8 jit_solution(7502697707056240494)
XLA Ops:
  0.0 0.9 convert_element_type.36.refs_0_
  0.9 3.3 %collective-permute-start = (bf16[128,256]{1,0:T(8,128)(2,1)S(1)}, bf16[128,256]{1,0:T(8,128)(2,1)S(1)}, u32[]{:S(2)}, u32[]{:S(2)}) collective-permute-start(bf16[128,256]{1,0:T(8,128)(2,1)S(1)} %convert_element_type.36.refs_0_), channel_id=1, source_target_pairs={{0,1},{1,0},{2,3},{3,2},{4,5},{5,4},{6,7},{7,6},{8,9},{9,8},{10,11... | collective-permute-start | bytes 196616 | tf_op jit(solution)/shard_map/core_swap/ppermute | solution.py:186
  4.2 0.9 collective-permute-done
  5.1 1.6 %collective-permute-start.6 = (bf16[64,128,128]{2,1,0:T(8,128)(2,1)}, bf16[64,128,128]{2,1,0:T(8,128)(2,1)S(1)}, u32[]{:S(2)}, u32[]{:S(2)}) collective-permute-start(bf16[64,128,128]{2,1,0:T(8,128)(2,1)} %bitcast.15), channel_id=1, source_target_pairs={{0,0},{1,1},{2,2},{3,3},{4,4},{5,5},{6,6},{7,7},{8,8},{9,9},{10,10... | collective-permute-start | bytes 6291464 | tf_op jit(solution)/shard_map/tile_stay/ppermute | solution.py:233
  7.1 5.1 %collective-permute-start.2 = (bf16[256,256]{1,0:T(8,128)(2,1)S(1)}, bf16[256,256]{1,0:T(8,128)(2,1)S(1)}, u32[]{:S(2)}, u32[]{:S(2)}) collective-permute-start(bf16[256,256]{1,0:T(8,128)(2,1)S(1)} %pad_maximum_fusion.2), channel_id=1, source_target_pairs={{0,32},{1,225},{2,34},{3,227},{4,36},{5,229},{6,38},{7,231},{8,40}... | collective-permute-start | bytes 393224 | tf_op jit(solution)/shard_map/z_one/ppermute | solution.py:178
  12.2 1.2 collective-permute-start.1
  13.4 2.0 %collective-permute-start.8 = (bf16[256,256]{1,0:T(8,128)(2,1)S(1)}, bf16[256,256]{1,0:T(8,128)(2,1)S(1)}, u32[]{:S(2)}, u32[]{:S(2)}) collective-permute-start(bf16[256,256]{1,0:T(8,128)(2,1)S(1)} %pad_maximum_fusion.2), channel_id=1, source_target_pairs={{0,96},{1,161},{2,98},{3,163},{4,100},{5,165},{6,102},{7,167},{8,1... | collective-permute-start | bytes 393224 | tf_op jit(solution)/shard_map/z_three/ppermute | solution.py:178
  16.0 0.8 pad_add_fusion.refs_0_
  16.8 1.0 collective-permute-start.5
  18.6 0.7 collective-permute-start.9
  19.2 6.2 %collective-permute-start.4 = (bf16[128,256]{1,0:T(8,128)(2,1)S(1)}, bf16[128,256]{1,0:T(8,128)(2,1)S(1)}, u32[]{:S(2)}, u32[]{:S(2)}) collective-permute-start(bf16[128,256]{1,0:T(8,128)(2,1)S(1)} %slice.3), channel_id=1, source_target_pairs={{0,64},{1,193},{2,66},{3,195},{4,68},{5,197},{6,70},{7,199},{8,72}... | collective-permute-start | bytes 196616 | tf_op jit(solution)/shard_map/z_four/ppermute | solution.py:178
  25.8 4.8 %build_dense.1.dense_ref = bf16[2048,2048]{1,0:T(8,128)(2,1)S(1)} custom-call(s32[129]{0:T(256)S(1)} %pad_add_fusion.refs_0_, s32[129]{0:T(256)S(1)} %collective-permute-done.5.refs_1_, s32[2]{0:T(128)S(1)} %pad_add_fusion.1.refs_2_, bf16[64,128,128]{2,1,0:T(8,128)(2,1)S(1)} %collective-permute-done.6.refs_3_, ...), custom_call_target="tpu_custom_call" | custom-call | flops 4194304 | bytes 25165824 | tf_op jit(solution)/shard_map/build_dense/pallas_call | solution.py:69
  31.1 2.4 %head_multiply.3.head_ref = f32[2048,256]{1,0:T(8,128)S(1)} custom-call(bf16[2048,2048]{1,0:T(8,128)(2,1)S(1)} %build_dense.1.dense_ref, bf16[128,256]{1,0:T(8,128)(2,1)S(1)} %convert_element_type.36.refs_0_, bf16[256,256]{1,0:T(8,128)(2,1)S(1)} %collective-permute-done.2.refs_1_, bf16[256,256]{1,0:T(8,128)(2,1)S(1)} %collective-permute-done.1.refs_2_, ...), custom_call_target="tpu_custom_call" | custom-call | flops 1610612736 | bytes 6291456 | tf_op jit(solution)/shard_map/head_multiply/pallas_call | solution.py:120
  33.8 0.6 tail_multiply.7
  34.4 2.1 %collective-permute-start.13 = (bf16[1024,256]{1,0:T(8,128)(2,1)S(1)}, bf16[1024,256]{1,0:T(8,128)(2,1)S(1)}, u32[]{:S(2)}, u32[]{:S(2)}) collective-permute-start(bf16[1024,256]{1,0:T(8,128)(2,1)S(1)} %tail_multiply.7), channel_id=1, source_target_pairs={{0,1},{1,0},{2,3},{3,2},{4,5},{5,4},{6,7},{7,6},{8,9},{9,8},{10,11... | collective-permute-start | bytes 1572872 | tf_op jit(solution)/shard_map/partial_swap/ppermute | solution.py:242
  37.2 0.9 collective-permute-done.13
  38.2 16.3 %all_to_all.15 = bf16[8,128,256]{2,1,0:T(8,128)(2,1)S(1)} all-to-all(bf16[8,128,256]{2,1,0:T(8,128)(2,1)S(1)} %bitcast.10), channel_id=1, replica_groups={{0,2,4,6,8,10,12,14},{1,3,5,7,9,11,13,15},{16,18,20,22,24,26,28,30},{17..., dimensions={0} | all-to-all | bytes 1048576 | tf_op jit(solution)/shard_map/all_to_all | solution.py:245
  54.6 2.6 %collective-permute-start.14 = (bf16[128,256]{1,0:T(8,128)(2,1)S(1)}, bf16[128,256]{1,0:T(8,128)(2,1)S(1)}, u32[]{:S(2)}, u32[]{:S(2)}) collective-permute-start(bf16[128,256]{1,0:T(8,128)(2,1)S(1)} %convert_element_type.40.refs_0_), channel_id=1, source_target_pairs={{0,1},{1,0},{2,3},{3,2},{4,5},{5,4},{6,7},{7,6},{8,9},{9,8},{10,11... | collective-permute-start | bytes 196616 | tf_op jit(solution)/shard_map/core_swap/ppermute | solution.py:186
  57.2 0.9 collective-permute-done.14
  58.1 2.6 %collective-permute-start.16 = (bf16[256,256]{1,0:T(8,128)(2,1)S(1)}, bf16[256,256]{1,0:T(8,128)(2,1)S(1)}, u32[]{:S(2)}, u32[]{:S(2)}) collective-permute-start(bf16[256,256]{1,0:T(8,128)(2,1)S(1)} %pad_maximum_fusion.3), channel_id=1, source_target_pairs={{0,32},{1,225},{2,34},{3,227},{4,36},{5,229},{6,38},{7,231},{8,40}... | collective-permute-start | bytes 393224 | tf_op jit(solution)/shard_map/z_one/ppermute | solution.py:178
  60.7 1.3 collective-permute-start.15
  62.1 2.6 %collective-permute-start.18 = (bf16[256,256]{1,0:T(8,128)(2,1)S(1)}, bf16[256,256]{1,0:T(8,128)(2,1)S(1)}, u32[]{:S(2)}, u32[]{:S(2)}) collective-permute-start(bf16[256,256]{1,0:T(8,128)(2,1)S(1)} %pad_maximum_fusion.3), channel_id=1, source_target_pairs={{0,96},{1,161},{2,98},{3,163},{4,100},{5,165},{6,102},{7,167},{8,1... | collective-permute-start | bytes 393224 | tf_op jit(solution)/shard_map/z_three/ppermute | solution.py:178
  64.7 2.8 %collective-permute-start.21 = (bf16[128,256]{1,0:T(8,128)(2,1)S(1)}, bf16[128,256]{1,0:T(8,128)(2,1)S(1)}, u32[]{:S(2)}, u32[]{:S(2)}) collective-permute-start(bf16[128,256]{1,0:T(8,128)(2,1)S(1)} %convert_element_type.40.refs_0_), channel_id=1, source_target_pairs={{0,128},{1,129},{2,130},{3,131},{4,132},{5,133},{6,134},{7,135},{8... | collective-permute-start | bytes 196616 | tf_op jit(solution)/shard_map/z_four/ppermute | solution.py:178
  67.8 1.1 collective-permute-start.19
  69.3 2.8 %collective-permute-done.21.refs_0_ = bf16[128,256]{1,0:T(8,128)(2,1)S(1)} collective-permute-done((bf16[128,256]{1,0:T(8,128)(2,1)S(1)}, bf16[128,256]{1,0:T(8,128)(2,1)S(1)}, u32[]{:S(2)}, u32[]{:S(2)}) %collective-permute-start.21) | collective-permute-done | bytes 65568 | tf_op jit(solution)/shard_map/z_four/ppermute | solution.py:178
  72.1 1.3 collective-permute-start.22
  73.4 0.8 collective-permute-done.20.refs_6_
  74.2 2.4 %head_multiply.4.head_ref = f32[2048,256]{1,0:T(8,128)S(1)} custom-call(bf16[2048,2048]{1,0:T(8,128)(2,1)S(1)} %build_dense.1.dense_ref, bf16[128,256]{1,0:T(8,128)(2,1)S(1)} %convert_element_type.40.refs_0_, bf16[256,256]{1,0:T(8,128)(2,1)S(1)} %collective-permute-done.16.refs_1_, bf16[256,256]{1,0:T(8,128)(2,1)S(1)} %collective-permute-done.15.refs_2_, ...), custom_call_target="tpu_custom_call" | custom-call | flops 1610612736 | bytes 6291456 | tf_op jit(solution)/shard_map/head_multiply/pallas_call | solution.py:120
  76.6 1.4 collective-permute-done.22.refs_1_
  78.6 3.2 %collective-permute-start.23 = (bf16[1024,256]{1,0:T(8,128)(2,1)S(1)}, bf16[1024,256]{1,0:T(8,128)(2,1)S(1)}, u32[]{:S(2)}, u32[]{:S(2)}) collective-permute-start(bf16[1024,256]{1,0:T(8,128)(2,1)S(1)} %tail_multiply.9), channel_id=1, source_target_pairs={{0,1},{1,0},{2,3},{3,2},{4,5},{5,4},{6,7},{7,6},{8,9},{9,8},{10,11... | collective-permute-start | bytes 1572872 | tf_op jit(solution)/shard_map/partial_swap/ppermute | solution.py:242
  82.4 0.9 collective-permute-done.23
  83.4 12.6 %all_to_all.16 = bf16[8,128,256]{2,1,0:T(8,128)(2,1)S(1)} all-to-all(bf16[8,128,256]{2,1,0:T(8,128)(2,1)S(1)} %bitcast.11), channel_id=1, replica_groups={{0,2,4,6,8,10,12,14},{1,3,5,7,9,11,13,15},{16,18,20,22,24,26,28,30},{17..., dimensions={0} | all-to-all | bytes 1048576 | tf_op jit(solution)/shard_map/all_to_all | solution.py:245
  96.1 2.6 %collective-permute-start.24 = (bf16[128,256]{1,0:T(8,128)(2,1)S(1)}, bf16[128,256]{1,0:T(8,128)(2,1)S(1)}, u32[]{:S(2)}, u32[]{:S(2)}) collective-permute-start(bf16[128,256]{1,0:T(8,128)(2,1)S(1)} %convert_element_type.44.refs_0_), channel_id=1, source_target_pairs={{0,1},{1,0},{2,3},{3,2},{4,5},{5,4},{6,7},{7,6},{8,9},{9,8},{10,11... | collective-permute-start | bytes 196616 | tf_op jit(solution)/shard_map/core_swap/ppermute | solution.py:186
  98.7 0.9 collective-permute-done.24
  99.6 3.0 %collective-permute-start.26 = (bf16[256,256]{1,0:T(8,128)(2,1)S(1)}, bf16[256,256]{1,0:T(8,128)(2,1)S(1)}, u32[]{:S(2)}, u32[]{:S(2)}) collective-permute-start(bf16[256,256]{1,0:T(8,128)(2,1)S(1)} %pad_maximum_fusion.4), channel_id=1, source_target_pairs={{0,32},{1,225},{2,34},{3,227},{4,36},{5,229},{6,38},{7,231},{8,40}... | collective-permute-start | bytes 393224 | tf_op jit(solution)/shard_map/z_one/ppermute | solution.py:178
  102.6 1.0 collective-permute-start.25
  103.6 2.9 %collective-permute-start.28 = (bf16[256,256]{1,0:T(8,128)(2,1)S(1)}, bf16[256,256]{1,0:T(8,128)(2,1)S(1)}, u32[]{:S(2)}, u32[]{:S(2)}) collective-permute-start(bf16[256,256]{1,0:T(8,128)(2,1)S(1)} %pad_maximum_fusion.4), channel_id=1, source_target_pairs={{0,96},{1,161},{2,98},{3,163},{4,100},{5,165},{6,102},{7,167},{8,1... | collective-permute-start | bytes 393224 | tf_op jit(solution)/shard_map/z_three/ppermute | solution.py:178
  106.5 2.7 %collective-permute-start.31 = (bf16[128,256]{1,0:T(8,128)(2,1)S(1)}, bf16[128,256]{1,0:T(8,128)(2,1)S(1)}, u32[]{:S(2)}, u32[]{:S(2)}) collective-permute-start(bf16[128,256]{1,0:T(8,128)(2,1)S(1)} %convert_element_type.44.refs_0_), channel_id=1, source_target_pairs={{0,128},{1,129},{2,130},{3,131},{4,132},{5,133},{6,134},{7,135},{8... | collective-permute-start | bytes 196616 | tf_op jit(solution)/shard_map/z_four/ppermute | solution.py:178
  109.2 0.7 collective-permute-done.27.refs_4_
  109.9 0.7 collective-permute-start.29
  111.4 5.8 %collective-permute-done.31.refs_0_ = bf16[128,256]{1,0:T(8,128)(2,1)S(1)} collective-permute-done((bf16[128,256]{1,0:T(8,128)(2,1)S(1)}, bf16[128,256]{1,0:T(8,128)(2,1)S(1)}, u32[]{:S(2)}, u32[]{:S(2)}) %collective-permute-start.31) | collective-permute-done | bytes 65568 | tf_op jit(solution)/shard_map/z_four/ppermute | solution.py:178
  117.2 1.5 %collective-permute-start.32 = (bf16[384,256]{1,0:T(8,128)(2,1)S(1)}, bf16[384,256]{1,0:T(8,128)(2,1)S(1)}, u32[]{:S(2)}, u32[]{:S(2)}) collective-permute-start(bf16[384,256]{1,0:T(8,128)(2,1)S(1)} %pad_maximum_fusion.1), channel_id=1, source_target_pairs={{0,16},{16,0},{32,48},{48,32},{64,80},{80,64},{96,112},{112,96},{1... | collective-permute-start | bytes 589832 | tf_op jit(solution)/shard_map/x_far/ppermute | solution.py:182
  118.7 2.4 %head_multiply.5.head_ref = f32[2048,256]{1,0:T(8,128)S(1)} custom-call(bf16[2048,2048]{1,0:T(8,128)(2,1)S(1)} %build_dense.1.dense_ref, bf16[128,256]{1,0:T(8,128)(2,1)S(1)} %convert_element_type.44.refs_0_, bf16[256,256]{1,0:T(8,128)(2,1)S(1)} %collective-permute-done.26.refs_1_, bf16[256,256]{1,0:T(8,128)(2,1)S(1)} %collective-permute-done.25.refs_2_, ...), custom_call_target="tpu_custom_call" | custom-call | flops 1610612736 | bytes 6291456 | tf_op jit(solution)/shard_map/head_multiply/pallas_call | solution.py:120
  121.1 1.4 collective-permute-done.32.refs_1_
  123.1 2.8 %collective-permute-start.33 = (bf16[1024,256]{1,0:T(8,128)(2,1)S(1)}, bf16[1024,256]{1,0:T(8,128)(2,1)S(1)}, u32[]{:S(2)}, u32[]{:S(2)}) collective-permute-start(bf16[1024,256]{1,0:T(8,128)(2,1)S(1)} %tail_multiply.11), channel_id=1, source_target_pairs={{0,1},{1,0},{2,3},{3,2},{4,5},{5,4},{6,7},{7,6},{8,9},{9,8},{10,11... | collective-permute-start | bytes 1572872 | tf_op jit(solution)/shard_map/partial_swap/ppermute | solution.py:242
  126.5 0.9 collective-permute-done.33
  127.5 12.6 %all_to_all.17 = bf16[8,128,256]{2,1,0:T(8,128)(2,1)S(1)} all-to-all(bf16[8,128,256]{2,1,0:T(8,128)(2,1)S(1)} %bitcast.12), channel_id=1, replica_groups={{0,2,4,6,8,10,12,14},{1,3,5,7,9,11,13,15},{16,18,20,22,24,26,28,30},{17..., dimensions={0} | all-to-all | bytes 1048576 | tf_op jit(solution)/shard_map/all_to_all | solution.py:245
  140.2 0.7 add_multiply_fusion
  (53 shorter events, 7.5 us)
Async XLA Ops:
  0.9 4.2 %collective-permute-start = (bf16[128,256]{1,0:T(8,128)(2,1)S(1)}, bf16[128,256]{1,0:T(8,128)(2,1)S(1)}, u32[]{:S(2)}, u32[]{:S(2)}) collective-permute-start(bf16[128,256]{1,0:T(8,128)(2,1)S(1)} %convert_element_type.36.refs_0_), channel_id=1, source_target_pairs={{0,1},{1,0},{2,3},{3,2},{4,5},{5,4},{6,7},{7,6},{8,9},{9,8},{10,11... | collective-permute-start | bytes 196616 | tf_op jit(solution)/shard_map/core_swap/ppermute | solution.py:186
  5.1 20.3 %collective-permute-start.6 = (bf16[64,128,128]{2,1,0:T(8,128)(2,1)}, bf16[64,128,128]{2,1,0:T(8,128)(2,1)S(1)}, u32[]{:S(2)}, u32[]{:S(2)}) collective-permute-start(bf16[64,128,128]{2,1,0:T(8,128)(2,1)} %bitcast.15), channel_id=1, source_target_pairs={{0,0},{1,1},{2,2},{3,3},{4,4},{5,5},{6,6},{7,7},{8,8},{9,9},{10,10... | collective-permute-start | bytes 6291464 | tf_op jit(solution)/shard_map/tile_stay/ppermute | solution.py:233
  6.7 19.0 %collective-permute-start.7 = (bf16[64,128,128]{2,1,0:T(8,128)(2,1)}, bf16[64,128,128]{2,1,0:T(8,128)(2,1)}, u32[]{:S(2)}, u32[]{:S(2)}) collective-permute-start(bf16[64,128,128]{2,1,0:T(8,128)(2,1)} %bitcast.16), channel_id=1, source_target_pairs={{0,1},{1,0},{2,3},{3,2},{4,5},{5,4},{6,7},{7,6},{8,9},{9,8},{10,11... | collective-permute-start | bytes 6291464 | tf_op jit(solution)/shard_map/tile_swap/ppermute | solution.py:231
  7.1 6.3 %collective-permute-start.3 = (bf16[128,256]{1,0:T(8,128)(2,1)S(1)}, bf16[128,256]{1,0:T(8,128)(2,1)S(1)}, u32[]{:S(2)}, u32[]{:S(2)}) collective-permute-start(bf16[128,256]{1,0:T(8,128)(2,1)S(1)} %convert_element_type.36.refs_0_), channel_id=1, source_target_pairs={{0,16},{16,0},{32,48},{48,32},{64,80},{80,64},{96,112},{112,96},{1... | collective-permute-start | bytes 196616 | tf_op jit(solution)/shard_map/x_own/ppermute | solution.py:182
  7.1 9.7 %collective-permute-start.2 = (bf16[256,256]{1,0:T(8,128)(2,1)S(1)}, bf16[256,256]{1,0:T(8,128)(2,1)S(1)}, u32[]{:S(2)}, u32[]{:S(2)}) collective-permute-start(bf16[256,256]{1,0:T(8,128)(2,1)S(1)} %pad_maximum_fusion.2), channel_id=1, source_target_pairs={{0,32},{1,225},{2,34},{3,227},{4,36},{5,229},{6,38},{7,231},{8,40}... | collective-permute-start | bytes 393224 | tf_op jit(solution)/shard_map/z_one/ppermute | solution.py:178
  12.2 5.5 %collective-permute-start.1 = (bf16[256,256]{1,0:T(8,128)(2,1)S(1)}, bf16[256,256]{1,0:T(8,128)(2,1)S(1)}, u32[]{:S(2)}, u32[]{:S(2)}) collective-permute-start(bf16[256,256]{1,0:T(8,128)(2,1)S(1)} %pad_maximum_fusion.2), channel_id=1, source_target_pairs={{0,64},{1,193},{2,66},{3,195},{4,68},{5,197},{6,70},{7,199},{8,72}... | collective-permute-start | bytes 393224 | tf_op jit(solution)/shard_map/z_two/ppermute | solution.py:178
  13.4 5.8 %collective-permute-start.8 = (bf16[256,256]{1,0:T(8,128)(2,1)S(1)}, bf16[256,256]{1,0:T(8,128)(2,1)S(1)}, u32[]{:S(2)}, u32[]{:S(2)}) collective-permute-start(bf16[256,256]{1,0:T(8,128)(2,1)S(1)} %pad_maximum_fusion.2), channel_id=1, source_target_pairs={{0,96},{1,161},{2,98},{3,163},{4,100},{5,165},{6,102},{7,167},{8,1... | collective-permute-start | bytes 393224 | tf_op jit(solution)/shard_map/z_three/ppermute | solution.py:178
  16.8 1.8 %collective-permute-start.5 = (s32[129]{0:T(256)S(1)}, s32[129]{0:T(256)S(1)}, u32[]{:S(2)}, u32[]{:S(2)}) collective-permute-start(s32[129]{0:T(256)S(1)} %pad_add_fusion.refs_0_), channel_id=1, source_target_pairs={{0,1},{1,0},{2,3},{3,2},{4,5},{5,4},{6,7},{7,6},{8,9},{9,8},{10,11... | collective-permute-start | bytes 1556 | tf_op jit(solution)/shard_map/place_swap/ppermute | solution.py:226
  17.7 13.3 %collective-permute-start.10 = (bf16[256,256]{1,0:T(8,128)(2,1)S(1)}, bf16[256,256]{1,0:T(8,128)(2,1)S(1)}, u32[]{:S(2)}, u32[]{:S(2)}) collective-permute-start(bf16[256,256]{1,0:T(8,128)(2,1)S(1)} %collective-permute-done.1.refs_2_), channel_id=1, source_target_pairs={{0,16},{16,0},{32,48},{48,32},{64,80},{80,64},{96,112},{112,96},{1... | collective-permute-start | bytes 393224 | tf_op jit(solution)/shard_map/x_two/ppermute | solution.py:182
  18.6 12.5 %collective-permute-start.9 = (bf16[256,256]{1,0:T(8,128)(2,1)S(1)}, bf16[256,256]{1,0:T(8,128)(2,1)S(1)}, u32[]{:S(2)}, u32[]{:S(2)}) collective-permute-start(bf16[256,256]{1,0:T(8,128)(2,1)S(1)} %collective-permute-done.2.refs_1_), channel_id=1, source_target_pairs={{0,16},{16,0},{32,48},{48,32},{64,80},{80,64},{96,112},{112,96},{1... | collective-permute-start | bytes 393224 | tf_op jit(solution)/shard_map/x_one/ppermute | solution.py:182
  19.2 11.3 %collective-permute-start.4 = (bf16[128,256]{1,0:T(8,128)(2,1)S(1)}, bf16[128,256]{1,0:T(8,128)(2,1)S(1)}, u32[]{:S(2)}, u32[]{:S(2)}) collective-permute-start(bf16[128,256]{1,0:T(8,128)(2,1)S(1)} %slice.3), channel_id=1, source_target_pairs={{0,64},{1,193},{2,66},{3,195},{4,68},{5,197},{6,70},{7,199},{8,72}... | collective-permute-start | bytes 196616 | tf_op jit(solution)/shard_map/z_four/ppermute | solution.py:178
  25.5 8.0 %collective-permute-start.11 = (bf16[256,256]{1,0:T(8,128)(2,1)S(1)}, bf16[256,256]{1,0:T(8,128)(2,1)S(1)}, u32[]{:S(2)}, u32[]{:S(2)}) collective-permute-start(bf16[256,256]{1,0:T(8,128)(2,1)S(1)} %collective-permute-done.8.refs_3_), channel_id=1, source_target_pairs={{0,16},{16,0},{32,48},{48,32},{64,80},{80,64},{96,112},{112,96},{1... | collective-permute-start | bytes 393224 | tf_op jit(solution)/shard_map/x_three/ppermute | solution.py:182
  30.6 3.2 %collective-permute-start.12 = (bf16[128,256]{1,0:T(8,128)(2,1)S(1)}, bf16[128,256]{1,0:T(8,128)(2,1)S(1)}, u32[]{:S(2)}, u32[]{:S(2)}) collective-permute-start(bf16[128,256]{1,0:T(8,128)(2,1)S(1)} %collective-permute-done.4.refs_0_), channel_id=1, source_target_pairs={{0,16},{16,0},{32,48},{48,32},{64,80},{80,64},{96,112},{112,96},{1... | collective-permute-start | bytes 196616 | tf_op jit(solution)/shard_map/x_four/ppermute | solution.py:182
  34.4 3.7 %collective-permute-start.13 = (bf16[1024,256]{1,0:T(8,128)(2,1)S(1)}, bf16[1024,256]{1,0:T(8,128)(2,1)S(1)}, u32[]{:S(2)}, u32[]{:S(2)}) collective-permute-start(bf16[1024,256]{1,0:T(8,128)(2,1)S(1)} %tail_multiply.7), channel_id=1, source_target_pairs={{0,1},{1,0},{2,3},{3,2},{4,5},{5,4},{6,7},{7,6},{8,9},{9,8},{10,11... | collective-permute-start | bytes 1572872 | tf_op jit(solution)/shard_map/partial_swap/ppermute | solution.py:242
  54.6 3.5 %collective-permute-start.14 = (bf16[128,256]{1,0:T(8,128)(2,1)S(1)}, bf16[128,256]{1,0:T(8,128)(2,1)S(1)}, u32[]{:S(2)}, u32[]{:S(2)}) collective-permute-start(bf16[128,256]{1,0:T(8,128)(2,1)S(1)} %convert_element_type.40.refs_0_), channel_id=1, source_target_pairs={{0,1},{1,0},{2,3},{3,2},{4,5},{5,4},{6,7},{7,6},{8,9},{9,8},{10,11... | collective-permute-start | bytes 196616 | tf_op jit(solution)/shard_map/core_swap/ppermute | solution.py:186
  58.1 9.7 %collective-permute-start.16 = (bf16[256,256]{1,0:T(8,128)(2,1)S(1)}, bf16[256,256]{1,0:T(8,128)(2,1)S(1)}, u32[]{:S(2)}, u32[]{:S(2)}) collective-permute-start(bf16[256,256]{1,0:T(8,128)(2,1)S(1)} %pad_maximum_fusion.3), channel_id=1, source_target_pairs={{0,32},{1,225},{2,34},{3,227},{4,36},{5,229},{6,38},{7,231},{8,40}... | collective-permute-start | bytes 393224 | tf_op jit(solution)/shard_map/z_one/ppermute | solution.py:178
  60.7 8.2 %collective-permute-start.15 = (bf16[256,256]{1,0:T(8,128)(2,1)S(1)}, bf16[256,256]{1,0:T(8,128)(2,1)S(1)}, u32[]{:S(2)}, u32[]{:S(2)}) collective-permute-start(bf16[256,256]{1,0:T(8,128)(2,1)S(1)} %pad_maximum_fusion.3), channel_id=1, source_target_pairs={{0,64},{1,193},{2,66},{3,195},{4,68},{5,197},{6,70},{7,199},{8,72}... | collective-permute-start | bytes 393224 | tf_op jit(solution)/shard_map/z_two/ppermute | solution.py:178
  62.1 7.2 %collective-permute-start.18 = (bf16[256,256]{1,0:T(8,128)(2,1)S(1)}, bf16[256,256]{1,0:T(8,128)(2,1)S(1)}, u32[]{:S(2)}, u32[]{:S(2)}) collective-permute-start(bf16[256,256]{1,0:T(8,128)(2,1)S(1)} %pad_maximum_fusion.3), channel_id=1, source_target_pairs={{0,96},{1,161},{2,98},{3,163},{4,100},{5,165},{6,102},{7,167},{8,1... | collective-permute-start | bytes 393224 | tf_op jit(solution)/shard_map/z_three/ppermute | solution.py:178
  64.7 3.1 %collective-permute-start.17 = (bf16[128,256]{1,0:T(8,128)(2,1)S(1)}, bf16[128,256]{1,0:T(8,128)(2,1)S(1)}, u32[]{:S(2)}, u32[]{:S(2)}) collective-permute-start(bf16[128,256]{1,0:T(8,128)(2,1)S(1)} %convert_element_type.40.refs_0_), channel_id=1, source_target_pairs={{0,16},{16,0},{32,48},{48,32},{64,80},{80,64},{96,112},{112,96},{1... | collective-permute-start | bytes 196616 | tf_op jit(solution)/shard_map/x_own/ppermute | solution.py:182
  64.7 7.4 %collective-permute-start.21 = (bf16[128,256]{1,0:T(8,128)(2,1)S(1)}, bf16[128,256]{1,0:T(8,128)(2,1)S(1)}, u32[]{:S(2)}, u32[]{:S(2)}) collective-permute-start(bf16[128,256]{1,0:T(8,128)(2,1)S(1)} %convert_element_type.40.refs_0_), channel_id=1, source_target_pairs={{0,128},{1,129},{2,130},{3,131},{4,132},{5,133},{6,134},{7,135},{8... | collective-permute-start | bytes 196616 | tf_op jit(solution)/shard_map/z_four/ppermute | solution.py:178
  67.8 6.4 %collective-permute-start.19 = (bf16[256,256]{1,0:T(8,128)(2,1)S(1)}, bf16[256,256]{1,0:T(8,128)(2,1)S(1)}, u32[]{:S(2)}, u32[]{:S(2)}) collective-permute-start(bf16[256,256]{1,0:T(8,128)(2,1)S(1)} %collective-permute-done.16.refs_1_), channel_id=1, source_target_pairs={{0,16},{16,0},{32,48},{48,32},{64,80},{80,64},{96,112},{112,96},{1... | collective-permute-start | bytes 393224 | tf_op jit(solution)/shard_map/x_one/ppermute | solution.py:182
  68.9 5.3 %collective-permute-start.20 = (bf16[256,256]{1,0:T(8,128)(2,1)S(1)}, bf16[256,256]{1,0:T(8,128)(2,1)S(1)}, u32[]{:S(2)}, u32[]{:S(2)}) collective-permute-start(bf16[256,256]{1,0:T(8,128)(2,1)S(1)} %collective-permute-done.15.refs_2_), channel_id=1, source_target_pairs={{0,16},{16,0},{32,48},{48,32},{64,80},{80,64},{96,112},{112,96},{1... | collective-permute-start | bytes 393224 | tf_op jit(solution)/shard_map/x_two/ppermute | solution.py:182
  72.1 5.9 %collective-permute-start.22 = (bf16[384,256]{1,0:T(8,128)(2,1)S(1)}, bf16[384,256]{1,0:T(8,128)(2,1)S(1)}, u32[]{:S(2)}, u32[]{:S(2)}) collective-permute-start(bf16[384,256]{1,0:T(8,128)(2,1)S(1)} %pad_maximum_fusion), channel_id=1, source_target_pairs={{0,16},{16,0},{32,48},{48,32},{64,80},{80,64},{96,112},{112,96},{1... | collective-permute-start | bytes 589832 | tf_op jit(solution)/shard_map/x_far/ppermute | solution.py:182
  78.6 4.7 %collective-permute-start.23 = (bf16[1024,256]{1,0:T(8,128)(2,1)S(1)}, bf16[1024,256]{1,0:T(8,128)(2,1)S(1)}, u32[]{:S(2)}, u32[]{:S(2)}) collective-permute-start(bf16[1024,256]{1,0:T(8,128)(2,1)S(1)} %tail_multiply.9), channel_id=1, source_target_pairs={{0,1},{1,0},{2,3},{3,2},{4,5},{5,4},{6,7},{7,6},{8,9},{9,8},{10,11... | collective-permute-start | bytes 1572872 | tf_op jit(solution)/shard_map/partial_swap/ppermute | solution.py:242
  96.1 3.5 %collective-permute-start.24 = (bf16[128,256]{1,0:T(8,128)(2,1)S(1)}, bf16[128,256]{1,0:T(8,128)(2,1)S(1)}, u32[]{:S(2)}, u32[]{:S(2)}) collective-permute-start(bf16[128,256]{1,0:T(8,128)(2,1)S(1)} %convert_element_type.44.refs_0_), channel_id=1, source_target_pairs={{0,1},{1,0},{2,3},{3,2},{4,5},{5,4},{6,7},{7,6},{8,9},{9,8},{10,11... | collective-permute-start | bytes 196616 | tf_op jit(solution)/shard_map/core_swap/ppermute | solution.py:186
  99.6 10.3 %collective-permute-start.26 = (bf16[256,256]{1,0:T(8,128)(2,1)S(1)}, bf16[256,256]{1,0:T(8,128)(2,1)S(1)}, u32[]{:S(2)}, u32[]{:S(2)}) collective-permute-start(bf16[256,256]{1,0:T(8,128)(2,1)S(1)} %pad_maximum_fusion.4), channel_id=1, source_target_pairs={{0,32},{1,225},{2,34},{3,227},{4,36},{5,229},{6,38},{7,231},{8,40}... | collective-permute-start | bytes 393224 | tf_op jit(solution)/shard_map/z_one/ppermute | solution.py:178
  102.6 8.5 %collective-permute-start.25 = (bf16[256,256]{1,0:T(8,128)(2,1)S(1)}, bf16[256,256]{1,0:T(8,128)(2,1)S(1)}, u32[]{:S(2)}, u32[]{:S(2)}) collective-permute-start(bf16[256,256]{1,0:T(8,128)(2,1)S(1)} %pad_maximum_fusion.4), channel_id=1, source_target_pairs={{0,64},{1,193},{2,66},{3,195},{4,68},{5,197},{6,70},{7,199},{8,72}... | collective-permute-start | bytes 393224 | tf_op jit(solution)/shard_map/z_two/ppermute | solution.py:178
  103.6 7.8 %collective-permute-start.28 = (bf16[256,256]{1,0:T(8,128)(2,1)S(1)}, bf16[256,256]{1,0:T(8,128)(2,1)S(1)}, u32[]{:S(2)}, u32[]{:S(2)}) collective-permute-start(bf16[256,256]{1,0:T(8,128)(2,1)S(1)} %pad_maximum_fusion.4), channel_id=1, source_target_pairs={{0,96},{1,161},{2,98},{3,163},{4,100},{5,165},{6,102},{7,167},{8,1... | collective-permute-start | bytes 393224 | tf_op jit(solution)/shard_map/z_three/ppermute | solution.py:178
  106.5 3.4 %collective-permute-start.27 = (bf16[128,256]{1,0:T(8,128)(2,1)S(1)}, bf16[128,256]{1,0:T(8,128)(2,1)S(1)}, u32[]{:S(2)}, u32[]{:S(2)}) collective-permute-start(bf16[128,256]{1,0:T(8,128)(2,1)S(1)} %convert_element_type.44.refs_0_), channel_id=1, source_target_pairs={{0,16},{16,0},{32,48},{48,32},{64,80},{80,64},{96,112},{112,96},{1... | collective-permute-start | bytes 196616 | tf_op jit(solution)/shard_map/x_own/ppermute | solution.py:182
  106.5 10.6 %collective-permute-start.31 = (bf16[128,256]{1,0:T(8,128)(2,1)S(1)}, bf16[128,256]{1,0:T(8,128)(2,1)S(1)}, u32[]{:S(2)}, u32[]{:S(2)}) collective-permute-start(bf16[128,256]{1,0:T(8,128)(2,1)S(1)} %convert_element_type.44.refs_0_), channel_id=1, source_target_pairs={{0,128},{1,129},{2,130},{3,131},{4,132},{5,133},{6,134},{7,135},{8... | collective-permute-start | bytes 196616 | tf_op jit(solution)/shard_map/z_four/ppermute | solution.py:178
  109.9 8.8 %collective-permute-start.29 = (bf16[256,256]{1,0:T(8,128)(2,1)S(1)}, bf16[256,256]{1,0:T(8,128)(2,1)S(1)}, u32[]{:S(2)}, u32[]{:S(2)}) collective-permute-start(bf16[256,256]{1,0:T(8,128)(2,1)S(1)} %collective-permute-done.26.refs_1_), channel_id=1, source_target_pairs={{0,16},{16,0},{32,48},{48,32},{64,80},{80,64},{96,112},{112,96},{1... | collective-permute-start | bytes 393224 | tf_op jit(solution)/shard_map/x_one/ppermute | solution.py:182
  111.1 7.6 %collective-permute-start.30 = (bf16[256,256]{1,0:T(8,128)(2,1)S(1)}, bf16[256,256]{1,0:T(8,128)(2,1)S(1)}, u32[]{:S(2)}, u32[]{:S(2)}) collective-permute-start(bf16[256,256]{1,0:T(8,128)(2,1)S(1)} %collective-permute-done.25.refs_2_), channel_id=1, source_target_pairs={{0,16},{16,0},{32,48},{48,32},{64,80},{80,64},{96,112},{112,96},{1... | collective-permute-start | bytes 393224 | tf_op jit(solution)/shard_map/x_two/ppermute | solution.py:182
  117.2 5.3 %collective-permute-start.32 = (bf16[384,256]{1,0:T(8,128)(2,1)S(1)}, bf16[384,256]{1,0:T(8,128)(2,1)S(1)}, u32[]{:S(2)}, u32[]{:S(2)}) collective-permute-start(bf16[384,256]{1,0:T(8,128)(2,1)S(1)} %pad_maximum_fusion.1), channel_id=1, source_target_pairs={{0,16},{16,0},{32,48},{48,32},{64,80},{80,64},{96,112},{112,96},{1... | collective-permute-start | bytes 589832 | tf_op jit(solution)/shard_map/x_far/ppermute | solution.py:182
  123.1 4.3 %collective-permute-start.33 = (bf16[1024,256]{1,0:T(8,128)(2,1)S(1)}, bf16[1024,256]{1,0:T(8,128)(2,1)S(1)}, u32[]{:S(2)}, u32[]{:S(2)}) collective-permute-start(bf16[1024,256]{1,0:T(8,128)(2,1)S(1)} %tail_multiply.11), channel_id=1, source_target_pairs={{0,1},{1,0},{2,3},{3,2},{4,5},{5,4},{6,7},{7,6},{8,9},{9,8},{10,11... | collective-permute-start | bytes 1572872 | tf_op jit(solution)/shard_map/partial_swap/ppermute | solution.py:242
  126.5 13.7 %copy-start = (f32[128,256]{1,0:T(8,128)S(1)}, f32[128,256]{1,0:T(8,128)}, u32[]{:S(2)}) copy-start(f32[128,256]{1,0:T(8,128)} %param.5) | copy-start | bytes 393220

commit v5 on v1

--- a/solution.py
+++ b/solution.py
@@ -173,6 +173,9 @@
                 pairs.append((i * n_col + j, to * n_col + j))
         return lax.ppermute(piece, ("row", "col"), pairs)
 
+    def over(piece):
+        return lax.ppermute(piece, "row", flip_x)
+
     sibling = lax.ppermute(own, "col", flip_core)
     both = jnp.concatenate([own, sibling])
     one = onward(both, 1)
@@ -180,13 +183,14 @@
     dense = None
     if build is not None:
         two, dense = lax.optimization_barrier((two, build(sibling)))
-    near = jnp.concatenate([own, one, two])
-    flip_near = lax.ppermute(near, "row", flip_x)
+        over_near = [over(jnp.concatenate([own, one, two]))]
+    else:
+        two, over_own = lax.optimization_barrier((two, over(own)))
+        over_near = [over_own, over(jnp.concatenate([one, two]))]
     three = onward(two, 1)
     four = onward(two[:rows], 2)
     far = jnp.concatenate([three, four])
-    flip_far = lax.ppermute(far, "row", flip_x)
-    return [near, far, flip_near], [flip_far], dense
+    return [own, one, two, far] + over_near, [over(far)], dense
 
 
 def per_device(embedding, tiles, tile_rows, tile_cols, counts):

time: 137 us -> 137 us (level)
  waiting for transfers between devices: 36.9 us -> 32.4 us
  starting transfers between devices: 36.7 us -> 40.2 us
  blocking collectives: 40.6 us -> 43 us
  Pallas kernels: 16.6 us -> 14.9 us
    ppermute x12, waiting for transfers between devices: 20.8 us -> 14.7 us  [onward(): return lax.ppermute(piece, ('row', 'col'), pairs)]
    all_to_all x3, blocking collectives: 40.6 us -> 43 us  [per_device(): lax.all_to_all(pair.reshape(n_col // 2, per_dev, width), 'col', split_axi...]
    ppermute x6 -> x8, starting transfers between devices: 5.45 us -> 7.76 us  [over(): return lax.ppermute(piece, 'row', flip_x)]
    pallas_call x1, Pallas kernels: 5.15 us -> 3.37 us  [build_dense(): pl.pallas_call(kernel, out_shape=jax.ShapeDtypeStruct(shape, jnp.bfloat16...]
    ppermute x6 -> x8, waiting for transfers between devices: 9.53 us -> 11.2 us  [over(): return lax.ppermute(piece, 'row', flip_x)]
  transfers between devices with their start and end apart: 26 -> 28, of which waited for: 22 -> 21; matrix products, arithmetic and copies ran while one was open for 1% -> 1% of each run, Pallas kernels for 11% -> 10%
where the time goes in v5:
time: 137 us; the launch traced here: 136 us
  blocking collectives  43 us (31%)
  starting transfers between devices  40.2 us (29%)
  waiting for transfers between devices  32.4 us (24%)
  Pallas kernels  14.9 us (11%)
  other arithmetic  3.09 us (2%)
  local copies, waits for them, and re-layouts  1.66 us (1%)
    all_to_all x3, blocking collectives, per_device(): lax.all_to_all(pair.reshape(n_col // 2, per_dev, width), 'col', split_axi...  43 us
    ppermute x12, waiting for transfers between devices, onward(): return lax.ppermute(piece, ('row', 'col'), pairs)  14.7 us
    ppermute x12, starting transfers between devices, onward(): return lax.ppermute(piece, ('row', 'col'), pairs)  13.8 us
    ppermute x8, waiting for transfers between devices, over(): return lax.ppermute(piece, 'row', flip_x)  11.2 us
    ppermute x3, starting transfers between devices, per_device(): arrived = lax.ppermute(theirs, 'col', flip_core)  9.94 us
    ppermute x3, starting transfers between devices, gather_pieces(): sibling = lax.ppermute(own, 'col', flip_core)  8.42 us
    pallas_call x3, Pallas kernels, head_multiply(): pl.pallas_call(kernel, out_shape=jax.ShapeDtypeStruct((n_rows, width), jn...  7.92 us
    ppermute x8, starting transfers between devices, over(): return lax.ppermute(piece, 'row', flip_x)  7.76 us
  transfers between devices with their start and end apart: 28, of which 21 were waited for; matrix products, arithmetic and copies ran while one was open for 1% of the time, Pallas kernels for 10%

profile of v5, /device:TPU:1, one launch (start us, length us, event | category | flops | bytes accessed | tf_op | source)
XLA Modules:
  0.0 136.2 jit_solution(13471609859242803188)
XLA Ops:
  0.0 0.9 convert_element_type.36.refs_0_
  0.9 3.3 %collective-permute-start = (bf16[128,256]{1,0:T(8,128)(2,1)S(1)}, bf16[128,256]{1,0:T(8,128)(2,1)S(1)}, u32[]{:S(2)}, u32[]{:S(2)}) collective-permute-start(bf16[128,256]{1,0:T(8,128)(2,1)S(1)} %convert_element_type.36.refs_0_), channel_id=1, source_target_pairs={{0,1},{1,0},{2,3},{3,2},{4,5},{5,4},{6,7},{7,6},{8,9},{9,8},{10,11... | collective-permute-start | bytes 196616 | tf_op jit(solution)/shard_map/ppermute | solution.py:179
  4.2 0.9 collective-permute-done
  6.2 3.9 %collective-permute-start.4 = (bf16[256,256]{1,0:T(8,128)(2,1)S(1)}, bf16[256,256]{1,0:T(8,128)(2,1)S(1)}, u32[]{:S(2)}, u32[]{:S(2)}) collective-permute-start(bf16[256,256]{1,0:T(8,128)(2,1)S(1)} %pad_maximum_fusion.3), channel_id=1, source_target_pairs={{0,32},{1,225},{2,34},{3,227},{4,36},{5,229},{6,38},{7,231},{8,40}... | collective-permute-start | bytes 393224 | tf_op jit(solution)/shard_map/ppermute | solution.py:174
  10.1 1.2 collective-permute-start.1
  11.3 0.7 pad_add_fusion.refs_0_
  12.1 1.0 collective-permute-done.2.refs_1_
  13.2 1.6 %copy-done = bf16[1,1,64,128,128]{4,3,2,1,0:T(8,128)(2,1)S(1)} copy-done((bf16[1,1,64,128,128]{4,3,2,1,0:T(8,128)(2,1)S(1)}, bf16[1,1,64,128,128]{4,3,2,1,0:T(8,128)(2,1)}, u32[]{:S(2)}) %copy-start) | copy-done | bytes 2097176
  14.7 3.4 %build_dense.1.dense_ref = bf16[2048,2048]{1,0:T(8,128)(2,1)S(1)} custom-call(s32[129]{0:T(256)S(1)} %pad_add_fusion.refs_0_, s32[129]{0:T(256)S(1)} %collective-permute-done.2.refs_1_, s32[2]{0:T(128)S(1)} %pad_add_fusion.1.refs_2_, bf16[64,128,128]{2,1,0:T(8,128)(2,1)S(1)} %bitcast.11, bf16[64,128,128]{2,1,0:T(8,128)(2,1)S(1)} %collective-permute-done.3.refs_4_), custom_call_target="tpu_custom_call" | custom-call | flops 4194304 | bytes 25165824 | tf_op jit(solution)/shard_map/build_dense/pallas_call | solution.py:66
  18.9 2.2 %collective-permute-start.7 = (bf16[640,256]{1,0:T(8,128)(2,1)S(1)}, bf16[640,256]{1,0:T(8,128)(2,1)S(1)}, u32[]{:S(2)}, u32[]{:S(2)}) collective-permute-start(bf16[640,256]{1,0:T(8,128)(2,1)S(1)} %pad_maximum_fusion), channel_id=1, source_target_pairs={{0,16},{16,0},{32,48},{48,32},{64,80},{80,64},{96,112},{112,96},{1... | collective-permute-start | bytes 983048 | tf_op jit(solution)/shard_map/ppermute | solution.py:177
  21.1 0.9 collective-permute-done.5
  22.0 3.0 %collective-permute-done.6 = bf16[128,256]{1,0:T(8,128)(2,1)S(1)} collective-permute-done((bf16[128,256]{1,0:T(8,128)(2,1)S(1)}, bf16[128,256]{1,0:T(8,128)(2,1)S(1)}, u32[]{:S(2)}, u32[]{:S(2)}) %collective-permute-start.6) | collective-permute-done | bytes 65568 | tf_op jit(solution)/shard_map/ppermute | solution.py:174
  25.0 0.7 collective-permute-start.8
  25.7 2.1 %collective-permute-done.7.refs_4_ = bf16[640,256]{1,0:T(8,128)(2,1)S(1)} collective-permute-done((bf16[640,256]{1,0:T(8,128)(2,1)S(1)}, bf16[640,256]{1,0:T(8,128)(2,1)S(1)}, u32[]{:S(2)}, u32[]{:S(2)}) %collective-permute-start.7) | collective-permute-done | bytes 327712 | tf_op jit(solution)/shard_map/ppermute | solution.py:177
  27.8 2.6 %head_multiply.3.head_ref = f32[2048,256]{1,0:T(8,128)S(1)} custom-call(bf16[2048,2048]{1,0:T(8,128)(2,1)S(1)} %build_dense.1.dense_ref, bf16[128,256]{1,0:T(8,128)(2,1)S(1)} %convert_element_type.36.refs_0_, bf16[256,256]{1,0:T(8,128)(2,1)S(1)} %collective-permute-done.4.refs_1_, bf16[256,256]{1,0:T(8,128)(2,1)S(1)} %collective-permute-done.1.refs_2_, ...), custom_call_target="tpu_custom_call" | custom-call | flops 1744830464 | bytes 6815744 | tf_op jit(solution)/shard_map/head_multiply/pallas_call | solution.py:117
  30.5 0.8 collective-permute-done.8.refs_0_
  31.9 3.2 %collective-permute-start.9 = (bf16[1024,256]{1,0:T(8,128)(2,1)S(1)}, bf16[1024,256]{1,0:T(8,128)(2,1)S(1)}, u32[]{:S(2)}, u32[]{:S(2)}) collective-permute-start(bf16[1024,256]{1,0:T(8,128)(2,1)S(1)} %tail_multiply.7), channel_id=1, source_target_pairs={{0,1},{1,0},{2,3},{3,2},{4,5},{5,4},{6,7},{7,6},{8,9},{9,8},{10,11... | collective-permute-start | bytes 1572872 | tf_op jit(solution)/shard_map/ppermute | solution.py:217
  35.7 0.9 collective-permute-done.9
  36.8 16.6 %all_to_all.15 = bf16[8,128,256]{2,1,0:T(8,128)(2,1)S(1)} all-to-all(bf16[8,128,256]{2,1,0:T(8,128)(2,1)S(1)} %bitcast.12), channel_id=1, replica_groups={{0,2,4,6,8,10,12,14},{1,3,5,7,9,11,13,15},{16,18,20,22,24,26,28,30},{17..., dimensions={0} | all-to-all | bytes 1048576 | tf_op jit(solution)/shard_map/all_to_all | solution.py:220
  53.4 2.6 %collective-permute-start.10 = (bf16[128,256]{1,0:T(8,128)(2,1)S(1)}, bf16[128,256]{1,0:T(8,128)(2,1)S(1)}, u32[]{:S(2)}, u32[]{:S(2)}) collective-permute-start(bf16[128,256]{1,0:T(8,128)(2,1)S(1)} %convert_element_type.40.refs_0_), channel_id=1, source_target_pairs={{0,1},{1,0},{2,3},{3,2},{4,5},{5,4},{6,7},{7,6},{8,9},{9,8},{10,11... | collective-permute-start | bytes 196616 | tf_op jit(solution)/shard_map/ppermute | solution.py:179
  56.0 0.9 collective-permute-done.10
  56.9 1.2 collective-permute-start.12
  59.0 2.5 %collective-permute-done.13.refs_4_ = bf16[128,256]{1,0:T(8,128)(2,1)S(1)} collective-permute-done((bf16[128,256]{1,0:T(8,128)(2,1)S(1)}, bf16[128,256]{1,0:T(8,128)(2,1)S(1)}, u32[]{:S(2)}, u32[]{:S(2)}) %collective-permute-start.13) | collective-permute-done | bytes 65568 | tf_op jit(solution)/shard_map/ppermute | solution.py:177
  61.5 1.4 collective-permute-done.12.refs_2_
  62.9 2.9 %collective-permute-start.14 = (bf16[256,256]{1,0:T(8,128)(2,1)S(1)}, bf16[256,256]{1,0:T(8,128)(2,1)S(1)}, u32[]{:S(2)}, u32[]{:S(2)}) collective-permute-start(bf16[256,256]{1,0:T(8,128)(2,1)S(1)} %collective-permute-done.12.refs_2_), channel_id=1, source_target_pairs={{0,32},{1,225},{2,34},{3,227},{4,36},{5,229},{6,38},{7,231},{8,40}... | collective-permute-start | bytes 393224 | tf_op jit(solution)/shard_map/ppermute | solution.py:174
  66.0 1.7 %collective-permute-done.14 = bf16[256,256]{1,0:T(8,128)(2,1)S(1)} collective-permute-done((bf16[256,256]{1,0:T(8,128)(2,1)S(1)}, bf16[256,256]{1,0:T(8,128)(2,1)S(1)}, u32[]{:S(2)}, u32[]{:S(2)}) %collective-permute-start.14) | collective-permute-done | bytes 131104 | tf_op jit(solution)/shard_map/ppermute | solution.py:174
  67.7 2.6 %collective-permute-done.15 = bf16[128,256]{1,0:T(8,128)(2,1)S(1)} collective-permute-done((bf16[128,256]{1,0:T(8,128)(2,1)S(1)}, bf16[128,256]{1,0:T(8,128)(2,1)S(1)}, u32[]{:S(2)}, u32[]{:S(2)}) %collective-permute-start.15) | collective-permute-done | bytes 65568 | tf_op jit(solution)/shard_map/ppermute | solution.py:174
  70.3 1.1 collective-permute-start.17
  71.3 2.3 %collective-permute-done.16.refs_5_ = bf16[512,256]{1,0:T(8,128)(2,1)S(1)} collective-permute-done((bf16[512,256]{1,0:T(8,128)(2,1)S(1)}, bf16[512,256]{1,0:T(8,128)(2,1)S(1)}, u32[]{:S(2)}, u32[]{:S(2)}) %collective-permute-start.16) | collective-permute-done | bytes 262176 | tf_op jit(solution)/shard_map/ppermute | solution.py:177
  73.6 2.6 %head_multiply.4.head_ref = f32[2048,256]{1,0:T(8,128)S(1)} custom-call(bf16[2048,2048]{1,0:T(8,128)(2,1)S(1)} %build_dense.1.dense_ref, bf16[128,256]{1,0:T(8,128)(2,1)S(1)} %convert_element_type.40.refs_0_, bf16[256,256]{1,0:T(8,128)(2,1)S(1)} %collective-permute-done.11.refs_1_, bf16[256,256]{1,0:T(8,128)(2,1)S(1)} %collective-permute-done.12.refs_2_, ...), custom_call_target="tpu_custom_call" | custom-call | flops 1744830464 | bytes 6815744 | tf_op jit(solution)/shard_map/head_multiply/pallas_call | solution.py:117
  76.9 2.8 %collective-permute-start.18 = (bf16[1024,256]{1,0:T(8,128)(2,1)S(1)}, bf16[1024,256]{1,0:T(8,128)(2,1)S(1)}, u32[]{:S(2)}, u32[]{:S(2)}) collective-permute-start(bf16[1024,256]{1,0:T(8,128)(2,1)S(1)} %tail_multiply.9), channel_id=1, source_target_pairs={{0,1},{1,0},{2,3},{3,2},{4,5},{5,4},{6,7},{7,6},{8,9},{9,8},{10,11... | collective-permute-start | bytes 1572872 | tf_op jit(solution)/shard_map/ppermute | solution.py:217
  80.3 0.9 collective-permute-done.18
  81.4 13.5 %all_to_all.16 = bf16[8,128,256]{2,1,0:T(8,128)(2,1)S(1)} all-to-all(bf16[8,128,256]{2,1,0:T(8,128)(2,1)S(1)} %bitcast.13), channel_id=1, replica_groups={{0,2,4,6,8,10,12,14},{1,3,5,7,9,11,13,15},{16,18,20,22,24,26,28,30},{17..., dimensions={0} | all-to-all | bytes 1048576 | tf_op jit(solution)/shard_map/all_to_all | solution.py:220
  95.0 2.6 %collective-permute-start.19 = (bf16[128,256]{1,0:T(8,128)(2,1)S(1)}, bf16[128,256]{1,0:T(8,128)(2,1)S(1)}, u32[]{:S(2)}, u32[]{:S(2)}) collective-permute-start(bf16[128,256]{1,0:T(8,128)(2,1)S(1)} %convert_element_type.44.refs_0_), channel_id=1, source_target_pairs={{0,1},{1,0},{2,3},{3,2},{4,5},{5,4},{6,7},{7,6},{8,9},{9,8},{10,11... | collective-permute-start | bytes 196616 | tf_op jit(solution)/shard_map/ppermute | solution.py:179
  97.6 0.9 collective-permute-done.19
  99.9 2.5 %collective-permute-done.22.refs_4_ = bf16[128,256]{1,0:T(8,128)(2,1)S(1)} collective-permute-done((bf16[128,256]{1,0:T(8,128)(2,1)S(1)}, bf16[128,256]{1,0:T(8,128)(2,1)S(1)}, u32[]{:S(2)}, u32[]{:S(2)}) %collective-permute-start.22) | collective-permute-done | bytes 65568 | tf_op jit(solution)/shard_map/ppermute | solution.py:177
  102.4 1.1 collective-permute-done.21.refs_2_
  103.6 2.5 %collective-permute-start.23 = (bf16[256,256]{1,0:T(8,128)(2,1)S(1)}, bf16[256,256]{1,0:T(8,128)(2,1)S(1)}, u32[]{:S(2)}, u32[]{:S(2)}) collective-permute-start(bf16[256,256]{1,0:T(8,128)(2,1)S(1)} %collective-permute-done.21.refs_2_), channel_id=1, source_target_pairs={{0,32},{1,225},{2,34},{3,227},{4,36},{5,229},{6,38},{7,231},{8,40}... | collective-permute-start | bytes 393224 | tf_op jit(solution)/shard_map/ppermute | solution.py:174
  106.2 0.8 collective-permute-start.25
  107.0 1.1 collective-permute-done.23
  108.1 2.9 %collective-permute-done.24 = bf16[128,256]{1,0:T(8,128)(2,1)S(1)} collective-permute-done((bf16[128,256]{1,0:T(8,128)(2,1)S(1)}, bf16[128,256]{1,0:T(8,128)(2,1)S(1)}, u32[]{:S(2)}, u32[]{:S(2)}) %collective-permute-start.24) | collective-permute-done | bytes 65568 | tf_op jit(solution)/shard_map/ppermute | solution.py:174
  111.0 1.6 %collective-permute-start.26 = (bf16[384,256]{1,0:T(8,128)(2,1)S(1)}, bf16[384,256]{1,0:T(8,128)(2,1)S(1)}, u32[]{:S(2)}, u32[]{:S(2)}) collective-permute-start(bf16[384,256]{1,0:T(8,128)(2,1)S(1)} %constant_dynamic-update-slice_fusion.4.refs_3_), channel_id=1, source_target_pairs={{0,16},{16,0},{32,48},{48,32},{64,80},{80,64},{96,112},{112,96},{1... | collective-permute-start | bytes 589832 | tf_op jit(solution)/shard_map/ppermute | solution.py:177
  112.7 2.6 %head_multiply.5.head_ref = f32[2048,256]{1,0:T(8,128)S(1)} custom-call(bf16[2048,2048]{1,0:T(8,128)(2,1)S(1)} %build_dense.1.dense_ref, bf16[128,256]{1,0:T(8,128)(2,1)S(1)} %convert_element_type.44.refs_0_, bf16[256,256]{1,0:T(8,128)(2,1)S(1)} %collective-permute-done.20.refs_1_, bf16[256,256]{1,0:T(8,128)(2,1)S(1)} %collective-permute-done.21.refs_2_, ...), custom_call_target="tpu_custom_call" | custom-call | flops 1744830464 | bytes 6815744 | tf_op jit(solution)/shard_map/head_multiply/pallas_call | solution.py:117
  115.3 1.1 collective-permute-done.26.refs_0_
  117.0 3.9 %collective-permute-start.27 = (bf16[1024,256]{1,0:T(8,128)(2,1)S(1)}, bf16[1024,256]{1,0:T(8,128)(2,1)S(1)}, u32[]{:S(2)}, u32[]{:S(2)}) collective-permute-start(bf16[1024,256]{1,0:T(8,128)(2,1)S(1)} %tail_multiply.11), channel_id=1, source_target_pairs={{0,1},{1,0},{2,3},{3,2},{4,5},{5,4},{6,7},{7,6},{8,9},{9,8},{10,11... | collective-permute-start | bytes 1572872 | tf_op jit(solution)/shard_map/ppermute | solution.py:217
  121.5 0.9 collective-permute-done.27
  122.5 12.9 %all_to_all.17 = bf16[8,128,256]{2,1,0:T(8,128)(2,1)S(1)} all-to-all(bf16[8,128,256]{2,1,0:T(8,128)(2,1)S(1)} %bitcast.14), channel_id=1, replica_groups={{0,2,4,6,8,10,12,14},{1,3,5,7,9,11,13,15},{16,18,20,22,24,26,28,30},{17..., dimensions={0} | all-to-all | bytes 1048576 | tf_op jit(solution)/shard_map/all_to_all | solution.py:220
  135.5 0.7 add_multiply_fusion
  (52 shorter events, 8.2 us)
Async XLA Ops:
  0.9 4.2 %collective-permute-start = (bf16[128,256]{1,0:T(8,128)(2,1)S(1)}, bf16[128,256]{1,0:T(8,128)(2,1)S(1)}, u32[]{:S(2)}, u32[]{:S(2)}) collective-permute-start(bf16[128,256]{1,0:T(8,128)(2,1)S(1)} %convert_element_type.36.refs_0_), channel_id=1, source_target_pairs={{0,1},{1,0},{2,3},{3,2},{4,5},{5,4},{6,7},{7,6},{8,9},{9,8},{10,11... | collective-permute-start | bytes 196616 | tf_op jit(solution)/shard_map/ppermute | solution.py:179
  5.1 8.0 %collective-permute-start.3 = (bf16[64,128,128]{2,1,0:T(8,128)(2,1)}, bf16[64,128,128]{2,1,0:T(8,128)(2,1)S(1)}, u32[]{:S(2)}, u32[]{:S(2)}) collective-permute-start(bf16[64,128,128]{2,1,0:T(8,128)(2,1)} %bitcast.10), channel_id=1, source_target_pairs={{0,1},{1,0},{2,3},{3,2},{4,5},{5,4},{6,7},{7,6},{8,9},{9,8},{10,11... | collective-permute-start | bytes 6291464 | tf_op jit(solution)/shard_map/ppermute | solution.py:209
  6.2 12.7 %collective-permute-start.4 = (bf16[256,256]{1,0:T(8,128)(2,1)S(1)}, bf16[256,256]{1,0:T(8,128)(2,1)S(1)}, u32[]{:S(2)}, u32[]{:S(2)}) collective-permute-start(bf16[256,256]{1,0:T(8,128)(2,1)S(1)} %pad_maximum_fusion.3), channel_id=1, source_target_pairs={{0,32},{1,225},{2,34},{3,227},{4,36},{5,229},{6,38},{7,231},{8,40}... | collective-permute-start | bytes 393224 | tf_op jit(solution)/shard_map/ppermute | solution.py:174
  10.1 8.1 %collective-permute-start.1 = (bf16[256,256]{1,0:T(8,128)(2,1)S(1)}, bf16[256,256]{1,0:T(8,128)(2,1)S(1)}, u32[]{:S(2)}, u32[]{:S(2)}) collective-permute-start(bf16[256,256]{1,0:T(8,128)(2,1)S(1)} %pad_maximum_fusion.3), channel_id=1, source_target_pairs={{0,64},{1,193},{2,66},{3,195},{4,68},{5,197},{6,70},{7,199},{8,72}... | collective-permute-start | bytes 393224 | tf_op jit(solution)/shard_map/ppermute | solution.py:174
  12.0 1.1 collective-permute-start.2
  13.2 1.6 %copy-start = (bf16[1,1,64,128,128]{4,3,2,1,0:T(8,128)(2,1)S(1)}, bf16[1,1,64,128,128]{4,3,2,1,0:T(8,128)(2,1)}, u32[]{:S(2)}) copy-start(bf16[1,1,64,128,128]{4,3,2,1,0:T(8,128)(2,1)} %param.6) | copy-start | bytes 6291460
  18.1 3.9 %collective-permute-start.5 = (bf16[256,256]{1,0:T(8,128)(2,1)S(1)}, bf16[256,256]{1,0:T(8,128)(2,1)S(1)}, u32[]{:S(2)}, u32[]{:S(2)}) collective-permute-start(bf16[256,256]{1,0:T(8,128)(2,1)S(1)} %collective-permute-done.1.refs_2_), channel_id=1, source_target_pairs={{0,32},{1,225},{2,34},{3,227},{4,36},{5,229},{6,38},{7,231},{8,40}... | collective-permute-start | bytes 393224 | tf_op jit(solution)/shard_map/ppermute | solution.py:174
  18.9 9.0 %collective-permute-start.7 = (bf16[640,256]{1,0:T(8,128)(2,1)S(1)}, bf16[640,256]{1,0:T(8,128)(2,1)S(1)}, u32[]{:S(2)}, u32[]{:S(2)}) collective-permute-start(bf16[640,256]{1,0:T(8,128)(2,1)S(1)} %pad_maximum_fusion), channel_id=1, source_target_pairs={{0,16},{16,0},{32,48},{48,32},{64,80},{80,64},{96,112},{112,96},{1... | collective-permute-start | bytes 983048 | tf_op jit(solution)/shard_map/ppermute | solution.py:177
  21.0 4.0 %collective-permute-start.6 = (bf16[128,256]{1,0:T(8,128)(2,1)S(1)}, bf16[128,256]{1,0:T(8,128)(2,1)S(1)}, u32[]{:S(2)}, u32[]{:S(2)}) collective-permute-start(bf16[128,256]{1,0:T(8,128)(2,1)S(1)} %slice.9), channel_id=1, source_target_pairs={{0,64},{1,193},{2,66},{3,195},{4,68},{5,197},{6,70},{7,199},{8,72}... | collective-permute-start | bytes 196616 | tf_op jit(solution)/shard_map/ppermute | solution.py:174
  25.0 6.2 %collective-permute-start.8 = (bf16[384,256]{1,0:T(8,128)(2,1)S(1)}, bf16[384,256]{1,0:T(8,128)(2,1)S(1)}, u32[]{:S(2)}, u32[]{:S(2)}) collective-permute-start(bf16[384,256]{1,0:T(8,128)(2,1)S(1)} %constant_dynamic-update-slice_fusion.refs_3_), channel_id=1, source_target_pairs={{0,16},{16,0},{32,48},{48,32},{64,80},{80,64},{96,112},{112,96},{1... | collective-permute-start | bytes 589832 | tf_op jit(solution)/shard_map/ppermute | solution.py:177
  31.9 4.8 %collective-permute-start.9 = (bf16[1024,256]{1,0:T(8,128)(2,1)S(1)}, bf16[1024,256]{1,0:T(8,128)(2,1)S(1)}, u32[]{:S(2)}, u32[]{:S(2)}) collective-permute-start(bf16[1024,256]{1,0:T(8,128)(2,1)S(1)} %tail_multiply.7), channel_id=1, source_target_pairs={{0,1},{1,0},{2,3},{3,2},{4,5},{5,4},{6,7},{7,6},{8,9},{9,8},{10,11... | collective-permute-start | bytes 1572872 | tf_op jit(solution)/shard_map/ppermute | solution.py:217
  53.4 3.5 %collective-permute-start.10 = (bf16[128,256]{1,0:T(8,128)(2,1)S(1)}, bf16[128,256]{1,0:T(8,128)(2,1)S(1)}, u32[]{:S(2)}, u32[]{:S(2)}) collective-permute-start(bf16[128,256]{1,0:T(8,128)(2,1)S(1)} %convert_element_type.40.refs_0_), channel_id=1, source_target_pairs={{0,1},{1,0},{2,3},{3,2},{4,5},{5,4},{6,7},{7,6},{8,9},{9,8},{10,11... | collective-permute-start | bytes 196616 | tf_op jit(solution)/shard_map/ppermute | solution.py:179
  56.9 6.0 %collective-permute-start.12 = (bf16[256,256]{1,0:T(8,128)(2,1)S(1)}, bf16[256,256]{1,0:T(8,128)(2,1)S(1)}, u32[]{:S(2)}, u32[]{:S(2)}) collective-permute-start(bf16[256,256]{1,0:T(8,128)(2,1)S(1)} %pad_maximum_fusion.4), channel_id=1, source_target_pairs={{0,64},{1,193},{2,66},{3,195},{4,68},{5,197},{6,70},{7,199},{8,72}... | collective-permute-start | bytes 393224 | tf_op jit(solution)/shard_map/ppermute | solution.py:174
  58.0 7.7 %collective-permute-start.11 = (bf16[256,256]{1,0:T(8,128)(2,1)S(1)}, bf16[256,256]{1,0:T(8,128)(2,1)S(1)}, u32[]{:S(2)}, u32[]{:S(2)}) collective-permute-start(bf16[256,256]{1,0:T(8,128)(2,1)S(1)} %pad_maximum_fusion.4), channel_id=1, source_target_pairs={{0,32},{1,225},{2,34},{3,227},{4,36},{5,229},{6,38},{7,231},{8,40}... | collective-permute-start | bytes 393224 | tf_op jit(solution)/shard_map/ppermute | solution.py:174
  58.4 3.1 %collective-permute-start.13 = (bf16[128,256]{1,0:T(8,128)(2,1)S(1)}, bf16[128,256]{1,0:T(8,128)(2,1)S(1)}, u32[]{:S(2)}, u32[]{:S(2)}) collective-permute-start(bf16[128,256]{1,0:T(8,128)(2,1)S(1)} %convert_element_type.40.refs_0_), channel_id=1, source_target_pairs={{0,16},{16,0},{32,48},{48,32},{64,80},{80,64},{96,112},{112,96},{1... | collective-permute-start | bytes 196616 | tf_op jit(solution)/shard_map/ppermute | solution.py:177
  62.9 4.8 %collective-permute-start.14 = (bf16[256,256]{1,0:T(8,128)(2,1)S(1)}, bf16[256,256]{1,0:T(8,128)(2,1)S(1)}, u32[]{:S(2)}, u32[]{:S(2)}) collective-permute-start(bf16[256,256]{1,0:T(8,128)(2,1)S(1)} %collective-permute-done.12.refs_2_), channel_id=1, source_target_pairs={{0,32},{1,225},{2,34},{3,227},{4,36},{5,229},{6,38},{7,231},{8,40}... | collective-permute-start | bytes 393224 | tf_op jit(solution)/shard_map/ppermute | solution.py:174
  65.8 7.9 %collective-permute-start.16 = (bf16[512,256]{1,0:T(8,128)(2,1)S(1)}, bf16[512,256]{1,0:T(8,128)(2,1)S(1)}, u32[]{:S(2)}, u32[]{:S(2)}) collective-permute-start(bf16[512,256]{1,0:T(8,128)(2,1)S(1)} %pad_maximum_fusion.1), channel_id=1, source_target_pairs={{0,16},{16,0},{32,48},{48,32},{64,80},{80,64},{96,112},{112,96},{1... | collective-permute-start | bytes 786440 | tf_op jit(solution)/shard_map/ppermute | solution.py:177
  65.9 4.4 %collective-permute-start.15 = (bf16[128,256]{1,0:T(8,128)(2,1)S(1)}, bf16[128,256]{1,0:T(8,128)(2,1)S(1)}, u32[]{:S(2)}, u32[]{:S(2)}) collective-permute-start(bf16[128,256]{1,0:T(8,128)(2,1)S(1)} %slice.10), channel_id=1, source_target_pairs={{0,64},{1,193},{2,66},{3,195},{4,68},{5,197},{6,70},{7,199},{8,72}... | collective-permute-start | bytes 196616 | tf_op jit(solution)/shard_map/ppermute | solution.py:174
  70.3 6.0 %collective-permute-start.17 = (bf16[384,256]{1,0:T(8,128)(2,1)S(1)}, bf16[384,256]{1,0:T(8,128)(2,1)S(1)}, u32[]{:S(2)}, u32[]{:S(2)}) collective-permute-start(bf16[384,256]{1,0:T(8,128)(2,1)S(1)} %constant_dynamic-update-slice_fusion.2.refs_3_), channel_id=1, source_target_pairs={{0,16},{16,0},{32,48},{48,32},{64,80},{80,64},{96,112},{112,96},{1... | collective-permute-start | bytes 589832 | tf_op jit(solution)/shard_map/ppermute | solution.py:177
  76.9 4.4 %collective-permute-start.18 = (bf16[1024,256]{1,0:T(8,128)(2,1)S(1)}, bf16[1024,256]{1,0:T(8,128)(2,1)S(1)}, u32[]{:S(2)}, u32[]{:S(2)}) collective-permute-start(bf16[1024,256]{1,0:T(8,128)(2,1)S(1)} %tail_multiply.9), channel_id=1, source_target_pairs={{0,1},{1,0},{2,3},{3,2},{4,5},{5,4},{6,7},{7,6},{8,9},{9,8},{10,11... | collective-permute-start | bytes 1572872 | tf_op jit(solution)/shard_map/ppermute | solution.py:217
  95.0 3.5 %collective-permute-start.19 = (bf16[128,256]{1,0:T(8,128)(2,1)S(1)}, bf16[128,256]{1,0:T(8,128)(2,1)S(1)}, u32[]{:S(2)}, u32[]{:S(2)}) collective-permute-start(bf16[128,256]{1,0:T(8,128)(2,1)S(1)} %convert_element_type.44.refs_0_), channel_id=1, source_target_pairs={{0,1},{1,0},{2,3},{3,2},{4,5},{5,4},{6,7},{7,6},{8,9},{9,8},{10,11... | collective-permute-start | bytes 196616 | tf_op jit(solution)/shard_map/ppermute | solution.py:179
  98.5 5.1 %collective-permute-start.21 = (bf16[256,256]{1,0:T(8,128)(2,1)S(1)}, bf16[256,256]{1,0:T(8,128)(2,1)S(1)}, u32[]{:S(2)}, u32[]{:S(2)}) collective-permute-start(bf16[256,256]{1,0:T(8,128)(2,1)S(1)} %pad_maximum_fusion.5), channel_id=1, source_target_pairs={{0,64},{1,193},{2,66},{3,195},{4,68},{5,197},{6,70},{7,199},{8,72}... | collective-permute-start | bytes 393224 | tf_op jit(solution)/shard_map/ppermute | solution.py:174
  98.8 7.3 %collective-permute-start.20 = (bf16[256,256]{1,0:T(8,128)(2,1)S(1)}, bf16[256,256]{1,0:T(8,128)(2,1)S(1)}, u32[]{:S(2)}, u32[]{:S(2)}) collective-permute-start(bf16[256,256]{1,0:T(8,128)(2,1)S(1)} %pad_maximum_fusion.5), channel_id=1, source_target_pairs={{0,32},{1,225},{2,34},{3,227},{4,36},{5,229},{6,38},{7,231},{8,40}... | collective-permute-start | bytes 393224 | tf_op jit(solution)/shard_map/ppermute | solution.py:174
  99.3 3.1 %collective-permute-start.22 = (bf16[128,256]{1,0:T(8,128)(2,1)S(1)}, bf16[128,256]{1,0:T(8,128)(2,1)S(1)}, u32[]{:S(2)}, u32[]{:S(2)}) collective-permute-start(bf16[128,256]{1,0:T(8,128)(2,1)S(1)} %convert_element_type.44.refs_0_), channel_id=1, source_target_pairs={{0,16},{16,0},{32,48},{48,32},{64,80},{80,64},{96,112},{112,96},{1... | collective-permute-start | bytes 196616 | tf_op jit(solution)/shard_map/ppermute | solution.py:177
  103.6 4.5 %collective-permute-start.23 = (bf16[256,256]{1,0:T(8,128)(2,1)S(1)}, bf16[256,256]{1,0:T(8,128)(2,1)S(1)}, u32[]{:S(2)}, u32[]{:S(2)}) collective-permute-start(bf16[256,256]{1,0:T(8,128)(2,1)S(1)} %collective-permute-done.21.refs_2_), channel_id=1, source_target_pairs={{0,32},{1,225},{2,34},{3,227},{4,36},{5,229},{6,38},{7,231},{8,40}... | collective-permute-start | bytes 393224 | tf_op jit(solution)/shard_map/ppermute | solution.py:174
  106.2 6.5 %collective-permute-start.25 = (bf16[512,256]{1,0:T(8,128)(2,1)S(1)}, bf16[512,256]{1,0:T(8,128)(2,1)S(1)}, u32[]{:S(2)}, u32[]{:S(2)}) collective-permute-start(bf16[512,256]{1,0:T(8,128)(2,1)S(1)} %pad_maximum_fusion.2), channel_id=1, source_target_pairs={{0,16},{16,0},{32,48},{48,32},{64,80},{80,64},{96,112},{112,96},{1... | collective-permute-start | bytes 786440 | tf_op jit(solution)/shard_map/ppermute | solution.py:177
  107.0 4.0 %collective-permute-start.24 = (bf16[128,256]{1,0:T(8,128)(2,1)S(1)}, bf16[128,256]{1,0:T(8,128)(2,1)S(1)}, u32[]{:S(2)}, u32[]{:S(2)}) collective-permute-start(bf16[128,256]{1,0:T(8,128)(2,1)S(1)} %slice.11), channel_id=1, source_target_pairs={{0,64},{1,193},{2,66},{3,195},{4,68},{5,197},{6,70},{7,199},{8,72}... | collective-permute-start | bytes 196616 | tf_op jit(solution)/shard_map/ppermute | solution.py:174
  111.0 5.4 %collective-permute-start.26 = (bf16[384,256]{1,0:T(8,128)(2,1)S(1)}, bf16[384,256]{1,0:T(8,128)(2,1)S(1)}, u32[]{:S(2)}, u32[]{:S(2)}) collective-permute-start(bf16[384,256]{1,0:T(8,128)(2,1)S(1)} %constant_dynamic-update-slice_fusion.4.refs_3_), channel_id=1, source_target_pairs={{0,16},{16,0},{32,48},{48,32},{64,80},{80,64},{96,112},{112,96},{1... | collective-permute-start | bytes 589832 | tf_op jit(solution)/shard_map/ppermute | solution.py:177
  117.0 5.4 %collective-permute-start.27 = (bf16[1024,256]{1,0:T(8,128)(2,1)S(1)}, bf16[1024,256]{1,0:T(8,128)(2,1)S(1)}, u32[]{:S(2)}, u32[]{:S(2)}) collective-permute-start(bf16[1024,256]{1,0:T(8,128)(2,1)S(1)} %tail_multiply.11), channel_id=1, source_target_pairs={{0,1},{1,0},{2,3},{3,2},{4,5},{5,4},{6,7},{7,6},{8,9},{9,8},{10,11... | collective-permute-start | bytes 1572872 | tf_op jit(solution)/shard_map/ppermute | solution.py:217
  121.5 14.0 %copy-start.1 = (f32[128,256]{1,0:T(8,128)S(1)}, f32[128,256]{1,0:T(8,128)}, u32[]{:S(2)}) copy-start(f32[128,256]{1,0:T(8,128)} %param.5) | copy-start | bytes 393220

commit v6 on v2

--- a/solution.py
+++ b/solution.py
@@ -189,16 +189,22 @@
     both = jnp.concatenate([own, sibling])
     one = onward(both, 1, "z_one")
     two = onward(both, 2, "z_two")
-    three = onward(both, 3, "z_three")
-    over_one = over(jnp.concatenate([own, one]), "x_one")
-    over_two = over(two, "x_two")
-    four = onward(three[:rows], 1, "z_four")
-    over_three = over(three, "x_three")
-    last, dense = four, None
     if build is not None:
+        three = onward(both, 3, "z_three")
+        over_one = over(jnp.concatenate([own, one]), "x_one")
+        over_two = over(two, "x_two")
+        four = onward(three[:rows], 1, "z_four")
+        over_three = over(three, "x_three")
         last, dense = lax.optimization_barrier((four, build(sibling)))
-    over_four = over(last, "x_four")
-    return [own, one, two, three, over_one, over_two], [four, over_three, over_four], dense
+        over_four = over(last, "x_four")
+        return [own, one, two, three, over_one, over_two], [four, over_three, over_four], dense
+    two, over_own = lax.optimization_barrier((two, over(own, "x_own")))
+    over_near = over(jnp.concatenate([one, two]), "x_near")
+    three = onward(two, 1, "z_three")
+    four = onward(two[:rows], 2, "z_four")
+    far = jnp.concatenate([three, four])
+    over_far = over(far, "x_far")
+    return [own, one, two, three, over_own, over_near], [four, over_far], None
 
 
 def per_device(embedding, tiles, tile_rows, tile_cols, counts):

time: 141 us -> 137 us (0.972)
  starting transfers between devices: 52.4 us -> 48.6 us
    ppermute x12 -> x10, waiting for transfers between devices: 2.38 us -> 10 us  [over(): return lax.ppermute(piece, 'row', flip_x)]
    ppermute x12, waiting for transfers between devices: 18.3 us -> 10.7 us  [onward(): return lax.ppermute(piece, ('row', 'col'), pairs)]
    ppermute x12 -> x10, starting transfers between devices: 12.3 us -> 7.43 us  [over(): return lax.ppermute(piece, 'row', flip_x)]
    ppermute x3, starting transfers between devices: 8.96 us -> 12.5 us  [per_device(): arrived = lax.ppermute(theirs, 'col', flip_core)]
    ppermute x12, starting transfers between devices: 20.4 us -> 18 us  [onward(): return lax.ppermute(piece, ('row', 'col'), pairs)]
  transfers between devices with their start and end apart: 32 -> 30, of which waited for: 13 -> 17; matrix products, arithmetic and copies ran while one was open for 1% -> 1% of each run, Pallas kernels for 8% -> 9%
where the time goes in v6:
time: 137 us
  starting transfers between devices  48.6 us (35%)
  blocking collectives  41.8 us (31%)
  waiting for transfers between devices  26.2 us (19%)
  Pallas kernels  14.8 us (11%)
  other arithmetic  3.12 us (2%)
  local copies, waits for them, and re-layouts  1.61 us (1%)
    all_to_all x3, blocking collectives, per_device(): lax.all_to_all(pair.reshape(n_col // 2, per_dev, width), 'col', split_axi...  41.8 us
    ppermute x12, starting transfers between devices, onward(): return lax.ppermute(piece, ('row', 'col'), pairs)  18 us
    ppermute x3, starting transfers between devices, per_device(): arrived = lax.ppermute(theirs, 'col', flip_core)  12.5 us
    ppermute x12, waiting for transfers between devices, onward(): return lax.ppermute(piece, ('row', 'col'), pairs)  10.7 us
    ppermute x10, waiting for transfers between devices, over(): return lax.ppermute(piece, 'row', flip_x)  10 us
    ppermute x3, starting transfers between devices, swap(): return lax.ppermute(piece, 'col', flip_core)  8.15 us
    ppermute x10, starting transfers between devices, over(): return lax.ppermute(piece, 'row', flip_x)  7.43 us
    pallas_call x3, Pallas kernels, head_multiply(): pl.pallas_call(kernel, out_shape=jax.ShapeDtypeStruct((n_rows, width), jn...  7.08 us
  transfers between devices with their start and end apart: 30, of which 17 were waited for; matrix products, arithmetic and copies ran while one was open for 1% of the time, Pallas kernels for 9%

profile of v6, /device:TPU:1, one launch (start us, length us, event | category | flops | bytes accessed | tf_op | source)
XLA Modules:
  0.0 136.9 jit_solution(12927497144986342488)
XLA Ops:
  0.0 0.9 convert_element_type.36.refs_0_
  0.9 3.3 %collective-permute-start = (bf16[128,256]{1,0:T(8,128)(2,1)S(1)}, bf16[128,256]{1,0:T(8,128)(2,1)S(1)}, u32[]{:S(2)}, u32[]{:S(2)}) collective-permute-start(bf16[128,256]{1,0:T(8,128)(2,1)S(1)} %convert_element_type.36.refs_0_), channel_id=1, source_target_pairs={{0,1},{1,0},{2,3},{3,2},{4,5},{5,4},{6,7},{7,6},{8,9},{9,8},{10,11... | collective-permute-start | bytes 196616 | tf_op jit(solution)/shard_map/core_swap/ppermute | solution.py:186
  4.2 0.9 collective-permute-done
  5.5 3.9 %collective-permute-start.5 = (bf16[256,256]{1,0:T(8,128)(2,1)S(1)}, bf16[256,256]{1,0:T(8,128)(2,1)S(1)}, u32[]{:S(2)}, u32[]{:S(2)}) collective-permute-start(bf16[256,256]{1,0:T(8,128)(2,1)S(1)} %pad_maximum_fusion.5), channel_id=1, source_target_pairs={{0,32},{1,225},{2,34},{3,227},{4,36},{5,229},{6,38},{7,231},{8,40}... | collective-permute-start | bytes 393224 | tf_op jit(solution)/shard_map/z_one/ppermute | solution.py:178
  9.4 1.2 collective-permute-start.6
  11.8 1.3 collective-permute-start.7
  13.1 1.4 %collective-permute-done.6.refs_2_ = bf16[256,256]{1,0:T(8,128)(2,1)S(1)} collective-permute-done((bf16[256,256]{1,0:T(8,128)(2,1)S(1)}, bf16[256,256]{1,0:T(8,128)(2,1)S(1)}, u32[]{:S(2)}, u32[]{:S(2)}) %collective-permute-start.6) | collective-permute-done | bytes 131104 | tf_op jit(solution)/shard_map/z_two/ppermute | solution.py:178
  14.5 1.2 collective-permute-start.8
  15.7 0.7 pad_add_fusion.refs_0_
  16.4 2.1 %collective-permute-start.3 = (s32[129]{0:T(256)S(1)}, s32[129]{0:T(256)S(1)}, u32[]{:S(2)}, u32[]{:S(2)}) collective-permute-start(s32[129]{0:T(256)S(1)} %pad_add_fusion.refs_0_), channel_id=1, source_target_pairs={{0,1},{1,0},{2,3},{3,2},{4,5},{5,4},{6,7},{7,6},{8,9},{9,8},{10,11... | collective-permute-start | bytes 1556 | tf_op jit(solution)/shard_map/place_swap/ppermute | solution.py:220
  18.5 3.2 %collective-permute-start.2 = (bf16[128,256]{1,0:T(8,128)(2,1)S(1)}, bf16[128,256]{1,0:T(8,128)(2,1)S(1)}, u32[]{:S(2)}, u32[]{:S(2)}) collective-permute-start(bf16[128,256]{1,0:T(8,128)(2,1)S(1)} %slice.12), channel_id=1, source_target_pairs={{0,32},{1,225},{2,34},{3,227},{4,36},{5,229},{6,38},{7,231},{8,40}... | collective-permute-start | bytes 196616 | tf_op jit(solution)/shard_map/z_four/ppermute | solution.py:178
  21.8 1.2 collective-permute-start.9
  23.0 1.6 %copy-done = bf16[1,1,64,128,128]{4,3,2,1,0:T(8,128)(2,1)S(1)} copy-done((bf16[1,1,64,128,128]{4,3,2,1,0:T(8,128)(2,1)S(1)}, bf16[1,1,64,128,128]{4,3,2,1,0:T(8,128)(2,1)}, u32[]{:S(2)}) %copy-start) | copy-done | bytes 2097176
  24.6 4.0 %build_dense.1.dense_ref = bf16[2048,2048]{1,0:T(8,128)(2,1)S(1)} custom-call(s32[129]{0:T(256)S(1)} %pad_add_fusion.refs_0_, s32[129]{0:T(256)S(1)} %collective-permute-done.3.refs_1_, s32[2]{0:T(128)S(1)} %pad_add_fusion.1.refs_2_, bf16[64,128,128]{2,1,0:T(8,128)(2,1)S(1)} %bitcast.11, bf16[64,128,128]{2,1,0:T(8,128)(2,1)S(1)} %collective-permute-done.4.refs_4_), custom_call_target="tpu_custom_call" | custom-call | flops 4194304 | bytes 25165824 | tf_op jit(solution)/shard_map/build_dense/pallas_call | solution.py:69
  28.8 2.4 %head_multiply.3.head_ref = f32[2048,256]{1,0:T(8,128)S(1)} custom-call(bf16[2048,2048]{1,0:T(8,128)(2,1)S(1)} %build_dense.1.dense_ref, bf16[128,256]{1,0:T(8,128)(2,1)S(1)} %convert_element_type.36.refs_0_, bf16[256,256]{1,0:T(8,128)(2,1)S(1)} %collective-permute-done.5.refs_1_, bf16[256,256]{1,0:T(8,128)(2,1)S(1)} %collective-permute-done.6.refs_2_, ...), custom_call_target="tpu_custom_call" | custom-call | flops 1610612736 | bytes 6291456 | tf_op jit(solution)/shard_map/head_multiply/pallas_call | solution.py:120
  31.2 0.7 collective-permute-done.10.refs_2_
  32.5 3.0 %collective-permute-start.11 = (bf16[1024,256]{1,0:T(8,128)(2,1)S(1)}, bf16[1024,256]{1,0:T(8,128)(2,1)S(1)}, u32[]{:S(2)}, u32[]{:S(2)}) collective-permute-start(bf16[1024,256]{1,0:T(8,128)(2,1)S(1)} %tail_multiply.7), channel_id=1, source_target_pairs={{0,1},{1,0},{2,3},{3,2},{4,5},{5,4},{6,7},{7,6},{8,9},{9,8},{10,11... | collective-permute-start | bytes 1572872 | tf_op jit(solution)/shard_map/partial_swap/ppermute | solution.py:234
  36.1 0.9 collective-permute-done.11
  37.2 16.1 %all_to_all.15 = bf16[8,128,256]{2,1,0:T(8,128)(2,1)S(1)} all-to-all(bf16[8,128,256]{2,1,0:T(8,128)(2,1)S(1)} %bitcast.12), channel_id=1, replica_groups={{0,2,4,6,8,10,12,14},{1,3,5,7,9,11,13,15},{16,18,20,22,24,26,28,30},{17..., dimensions={0} | all-to-all | bytes 1048576 | tf_op jit(solution)/shard_map/all_to_all | solution.py:237
  53.3 2.6 %collective-permute-start.12 = (bf16[128,256]{1,0:T(8,128)(2,1)S(1)}, bf16[128,256]{1,0:T(8,128)(2,1)S(1)}, u32[]{:S(2)}, u32[]{:S(2)}) collective-permute-start(bf16[128,256]{1,0:T(8,128)(2,1)S(1)} %convert_element_type.40.refs_0_), channel_id=1, source_target_pairs={{0,1},{1,0},{2,3},{3,2},{4,5},{5,4},{6,7},{7,6},{8,9},{9,8},{10,11... | collective-permute-start | bytes 196616 | tf_op jit(solution)/shard_map/core_swap/ppermute | solution.py:186
  55.9 0.9 collective-permute-done.12
  57.2 1.3 collective-permute-start.13
  58.8 2.9 %collective-permute-done.15.refs_4_ = bf16[128,256]{1,0:T(8,128)(2,1)S(1)} collective-permute-done((bf16[128,256]{1,0:T(8,128)(2,1)S(1)}, bf16[128,256]{1,0:T(8,128)(2,1)S(1)}, u32[]{:S(2)}, u32[]{:S(2)}) %collective-permute-start.15) | collective-permute-done | bytes 65568 | tf_op jit(solution)/shard_map/x_own/ppermute | solution.py:182
  61.6 1.1 collective-permute-done.14.refs_2_
  62.8 2.2 %collective-permute-start.16 = (bf16[256,256]{1,0:T(8,128)(2,1)S(1)}, bf16[256,256]{1,0:T(8,128)(2,1)S(1)}, u32[]{:S(2)}, u32[]{:S(2)}) collective-permute-start(bf16[256,256]{1,0:T(8,128)(2,1)S(1)} %collective-permute-done.14.refs_2_), channel_id=1, source_target_pairs={{0,32},{1,225},{2,34},{3,227},{4,36},{5,229},{6,38},{7,231},{8,40}... | collective-permute-start | bytes 393224 | tf_op jit(solution)/shard_map/z_three/ppermute | solution.py:178
  65.1 1.0 collective-permute-start.18
  66.2 4.0 %collective-permute-done.18.refs_0_ = bf16[128,256]{1,0:T(8,128)(2,1)S(1)} collective-permute-done((bf16[128,256]{1,0:T(8,128)(2,1)S(1)}, bf16[128,256]{1,0:T(8,128)(2,1)S(1)}, u32[]{:S(2)}, u32[]{:S(2)}) %collective-permute-start.18) | collective-permute-done | bytes 65568 | tf_op jit(solution)/shard_map/z_four/ppermute | solution.py:178
  70.2 0.9 collective-permute-start.19
  71.1 2.4 %head_multiply.4.head_ref = f32[2048,256]{1,0:T(8,128)S(1)} custom-call(bf16[2048,2048]{1,0:T(8,128)(2,1)S(1)} %build_dense.1.dense_ref, bf16[128,256]{1,0:T(8,128)(2,1)S(1)} %convert_element_type.40.refs_0_, bf16[256,256]{1,0:T(8,128)(2,1)S(1)} %collective-permute-done.13.refs_1_, bf16[256,256]{1,0:T(8,128)(2,1)S(1)} %collective-permute-done.14.refs_2_, ...), custom_call_target="tpu_custom_call" | custom-call | flops 1610612736 | bytes 6291456 | tf_op jit(solution)/shard_map/head_multiply/pallas_call | solution.py:120
  73.5 1.8 %collective-permute-done.19.refs_1_ = bf16[384,256]{1,0:T(8,128)(2,1)S(1)} collective-permute-done((bf16[384,256]{1,0:T(8,128)(2,1)S(1)}, bf16[384,256]{1,0:T(8,128)(2,1)S(1)}, u32[]{:S(2)}, u32[]{:S(2)}) %collective-permute-start.19) | collective-permute-done | bytes 196640 | tf_op jit(solution)/shard_map/x_far/ppermute | solution.py:182
  75.9 5.0 %collective-permute-start.20 = (bf16[1024,256]{1,0:T(8,128)(2,1)S(1)}, bf16[1024,256]{1,0:T(8,128)(2,1)S(1)}, u32[]{:S(2)}, u32[]{:S(2)}) collective-permute-start(bf16[1024,256]{1,0:T(8,128)(2,1)S(1)} %tail_multiply.9), channel_id=1, source_target_pairs={{0,1},{1,0},{2,3},{3,2},{4,5},{5,4},{6,7},{7,6},{8,9},{9,8},{10,11... | collective-permute-start | bytes 1572872 | tf_op jit(solution)/shard_map/partial_swap/ppermute | solution.py:234
  81.5 0.9 collective-permute-done.20
  82.6 12.7 %all_to_all.16 = bf16[8,128,256]{2,1,0:T(8,128)(2,1)S(1)} all-to-all(bf16[8,128,256]{2,1,0:T(8,128)(2,1)S(1)} %bitcast.13), channel_id=1, replica_groups={{0,2,4,6,8,10,12,14},{1,3,5,7,9,11,13,15},{16,18,20,22,24,26,28,30},{17..., dimensions={0} | all-to-all | bytes 1048576 | tf_op jit(solution)/shard_map/all_to_all | solution.py:237
  95.3 2.3 %collective-permute-start.21 = (bf16[128,256]{1,0:T(8,128)(2,1)S(1)}, bf16[128,256]{1,0:T(8,128)(2,1)S(1)}, u32[]{:S(2)}, u32[]{:S(2)}) collective-permute-start(bf16[128,256]{1,0:T(8,128)(2,1)S(1)} %convert_element_type.44.refs_0_), channel_id=1, source_target_pairs={{0,1},{1,0},{2,3},{3,2},{4,5},{5,4},{6,7},{7,6},{8,9},{9,8},{10,11... | collective-permute-start | bytes 196616 | tf_op jit(solution)/shard_map/core_swap/ppermute | solution.py:186
  97.6 0.9 collective-permute-done.21
  98.6 2.0 %collective-permute-start.22 = (bf16[256,256]{1,0:T(8,128)(2,1)S(1)}, bf16[256,256]{1,0:T(8,128)(2,1)S(1)}, u32[]{:S(2)}, u32[]{:S(2)}) collective-permute-start(bf16[256,256]{1,0:T(8,128)(2,1)S(1)} %pad_maximum_fusion.7), channel_id=1, source_target_pairs={{0,32},{1,225},{2,34},{3,227},{4,36},{5,229},{6,38},{7,231},{8,40}... | collective-permute-start | bytes 393224 | tf_op jit(solution)/shard_map/z_one/ppermute | solution.py:178
  100.6 1.0 collective-permute-start.24
  101.6 2.6 %collective-permute-done.24.refs_4_ = bf16[128,256]{1,0:T(8,128)(2,1)S(1)} collective-permute-done((bf16[128,256]{1,0:T(8,128)(2,1)S(1)}, bf16[128,256]{1,0:T(8,128)(2,1)S(1)}, u32[]{:S(2)}, u32[]{:S(2)}) %collective-permute-start.24) | collective-permute-done | bytes 65568 | tf_op jit(solution)/shard_map/x_own/ppermute | solution.py:182
  104.9 0.6 collective-permute-done.22.refs_1_
  105.6 1.2 collective-permute-start.26
  106.8 1.6 %collective-permute-start.27 = (bf16[128,256]{1,0:T(8,128)(2,1)S(1)}, bf16[128,256]{1,0:T(8,128)(2,1)S(1)}, u32[]{:S(2)}, u32[]{:S(2)}) collective-permute-start(bf16[128,256]{1,0:T(8,128)(2,1)S(1)} %slice.11), channel_id=1, source_target_pairs={{0,64},{1,193},{2,66},{3,195},{4,68},{5,197},{6,70},{7,199},{8,72}... | collective-permute-start | bytes 196616 | tf_op jit(solution)/shard_map/z_four/ppermute | solution.py:178
  108.4 3.4 %collective-permute-done.27.refs_0_ = bf16[128,256]{1,0:T(8,128)(2,1)S(1)} collective-permute-done((bf16[128,256]{1,0:T(8,128)(2,1)S(1)}, bf16[128,256]{1,0:T(8,128)(2,1)S(1)}, u32[]{:S(2)}, u32[]{:S(2)}) %collective-permute-start.27) | collective-permute-done | bytes 65568 | tf_op jit(solution)/shard_map/z_four/ppermute | solution.py:178
  112.0 2.4 %head_multiply.5.head_ref = f32[2048,256]{1,0:T(8,128)S(1)} custom-call(bf16[2048,2048]{1,0:T(8,128)(2,1)S(1)} %build_dense.1.dense_ref, bf16[128,256]{1,0:T(8,128)(2,1)S(1)} %convert_element_type.44.refs_0_, bf16[256,256]{1,0:T(8,128)(2,1)S(1)} %collective-permute-done.22.refs_1_, bf16[256,256]{1,0:T(8,128)(2,1)S(1)} %collective-permute-done.23.refs_2_, ...), custom_call_target="tpu_custom_call" | custom-call | flops 1610612736 | bytes 6291456 | tf_op jit(solution)/shard_map/head_multiply/pallas_call | solution.py:120
  114.3 2.1 %collective-permute-done.28.refs_1_ = bf16[384,256]{1,0:T(8,128)(2,1)S(1)} collective-permute-done((bf16[384,256]{1,0:T(8,128)(2,1)S(1)}, bf16[384,256]{1,0:T(8,128)(2,1)S(1)}, u32[]{:S(2)}, u32[]{:S(2)}) %collective-permute-start.28) | collective-permute-done | bytes 196640 | tf_op jit(solution)/shard_map/x_far/ppermute | solution.py:182
  117.0 4.5 %collective-permute-start.29 = (bf16[1024,256]{1,0:T(8,128)(2,1)S(1)}, bf16[1024,256]{1,0:T(8,128)(2,1)S(1)}, u32[]{:S(2)}, u32[]{:S(2)}) collective-permute-start(bf16[1024,256]{1,0:T(8,128)(2,1)S(1)} %tail_multiply.11), channel_id=1, source_target_pairs={{0,1},{1,0},{2,3},{3,2},{4,5},{5,4},{6,7},{7,6},{8,9},{9,8},{10,11... | collective-permute-start | bytes 1572872 | tf_op jit(solution)/shard_map/partial_swap/ppermute | solution.py:234
  122.1 0.9 collective-permute-done.29
  123.1 13.0 %all_to_all.17 = bf16[8,128,256]{2,1,0:T(8,128)(2,1)S(1)} all-to-all(bf16[8,128,256]{2,1,0:T(8,128)(2,1)S(1)} %bitcast.14), channel_id=1, replica_groups={{0,2,4,6,8,10,12,14},{1,3,5,7,9,11,13,15},{16,18,20,22,24,26,28,30},{17..., dimensions={0} | all-to-all | bytes 1048576 | tf_op jit(solution)/shard_map/all_to_all | solution.py:237
  136.2 0.7 add_multiply_fusion
  (52 shorter events, 7.1 us)
Async XLA Ops:
  0.9 4.2 %collective-permute-start = (bf16[128,256]{1,0:T(8,128)(2,1)S(1)}, bf16[128,256]{1,0:T(8,128)(2,1)S(1)}, u32[]{:S(2)}, u32[]{:S(2)}) collective-permute-start(bf16[128,256]{1,0:T(8,128)(2,1)S(1)} %convert_element_type.36.refs_0_), channel_id=1, source_target_pairs={{0,1},{1,0},{2,3},{3,2},{4,5},{5,4},{6,7},{7,6},{8,9},{9,8},{10,11... | collective-permute-start | bytes 196616 | tf_op jit(solution)/shard_map/core_swap/ppermute | solution.py:186
  5.1 17.9 %collective-permute-start.4 = (bf16[64,128,128]{2,1,0:T(8,128)(2,1)}, bf16[64,128,128]{2,1,0:T(8,128)(2,1)S(1)}, u32[]{:S(2)}, u32[]{:S(2)}) collective-permute-start(bf16[64,128,128]{2,1,0:T(8,128)(2,1)} %bitcast.10), channel_id=1, source_target_pairs={{0,1},{1,0},{2,3},{3,2},{4,5},{5,4},{6,7},{7,6},{8,9},{9,8},{10,11... | collective-permute-start | bytes 6291464 | tf_op jit(solution)/shard_map/tile_swap/ppermute | solution.py:225
  5.5 6.3 %collective-permute-start.5 = (bf16[256,256]{1,0:T(8,128)(2,1)S(1)}, bf16[256,256]{1,0:T(8,128)(2,1)S(1)}, u32[]{:S(2)}, u32[]{:S(2)}) collective-permute-start(bf16[256,256]{1,0:T(8,128)(2,1)S(1)} %pad_maximum_fusion.5), channel_id=1, source_target_pairs={{0,32},{1,225},{2,34},{3,227},{4,36},{5,229},{6,38},{7,231},{8,40}... | collective-permute-start | bytes 393224 | tf_op jit(solution)/shard_map/z_one/ppermute | solution.py:178
  9.4 5.1 %collective-permute-start.6 = (bf16[256,256]{1,0:T(8,128)(2,1)S(1)}, bf16[256,256]{1,0:T(8,128)(2,1)S(1)}, u32[]{:S(2)}, u32[]{:S(2)}) collective-permute-start(bf16[256,256]{1,0:T(8,128)(2,1)S(1)} %pad_maximum_fusion.5), channel_id=1, source_target_pairs={{0,64},{1,193},{2,66},{3,195},{4,68},{5,197},{6,70},{7,199},{8,72}... | collective-permute-start | bytes 393224 | tf_op jit(solution)/shard_map/z_two/ppermute | solution.py:178
  11.2 7.3 %collective-permute-start.1 = (bf16[256,256]{1,0:T(8,128)(2,1)S(1)}, bf16[256,256]{1,0:T(8,128)(2,1)S(1)}, u32[]{:S(2)}, u32[]{:S(2)}) collective-permute-start(bf16[256,256]{1,0:T(8,128)(2,1)S(1)} %pad_maximum_fusion.5), channel_id=1, source_target_pairs={{0,96},{1,161},{2,98},{3,163},{4,100},{5,165},{6,102},{7,167},{8,1... | collective-permute-start | bytes 393224 | tf_op jit(solution)/shard_map/z_three/ppermute | solution.py:178
  11.8 17.0 %collective-permute-start.7 = (bf16[384,256]{1,0:T(8,128)(2,1)S(1)}, bf16[384,256]{1,0:T(8,128)(2,1)S(1)}, u32[]{:S(2)}, u32[]{:S(2)}) collective-permute-start(bf16[384,256]{1,0:T(8,128)(2,1)S(1)} %pad_maximum_fusion.2), channel_id=1, source_target_pairs={{0,16},{16,0},{32,48},{48,32},{64,80},{80,64},{96,112},{112,96},{1... | collective-permute-start | bytes 589832 | tf_op jit(solution)/shard_map/x_one/ppermute | solution.py:182
  14.5 14.3 %collective-permute-start.8 = (bf16[256,256]{1,0:T(8,128)(2,1)S(1)}, bf16[256,256]{1,0:T(8,128)(2,1)S(1)}, u32[]{:S(2)}, u32[]{:S(2)}) collective-permute-start(bf16[256,256]{1,0:T(8,128)(2,1)S(1)} %collective-permute-done.6.refs_2_), channel_id=1, source_target_pairs={{0,16},{16,0},{32,48},{48,32},{64,80},{80,64},{96,112},{112,96},{1... | collective-permute-start | bytes 393224 | tf_op jit(solution)/shard_map/x_two/ppermute | solution.py:182
  16.4 5.3 %collective-permute-start.3 = (s32[129]{0:T(256)S(1)}, s32[129]{0:T(256)S(1)}, u32[]{:S(2)}, u32[]{:S(2)}) collective-permute-start(s32[129]{0:T(256)S(1)} %pad_add_fusion.refs_0_), channel_id=1, source_target_pairs={{0,1},{1,0},{2,3},{3,2},{4,5},{5,4},{6,7},{7,6},{8,9},{9,8},{10,11... | collective-permute-start | bytes 1556 | tf_op jit(solution)/shard_map/place_swap/ppermute | solution.py:220
  18.5 10.1 %collective-permute-start.2 = (bf16[128,256]{1,0:T(8,128)(2,1)S(1)}, bf16[128,256]{1,0:T(8,128)(2,1)S(1)}, u32[]{:S(2)}, u32[]{:S(2)}) collective-permute-start(bf16[128,256]{1,0:T(8,128)(2,1)S(1)} %slice.12), channel_id=1, source_target_pairs={{0,32},{1,225},{2,34},{3,227},{4,36},{5,229},{6,38},{7,231},{8,40}... | collective-permute-start | bytes 196616 | tf_op jit(solution)/shard_map/z_four/ppermute | solution.py:178
  21.8 9.4 %collective-permute-start.9 = (bf16[256,256]{1,0:T(8,128)(2,1)S(1)}, bf16[256,256]{1,0:T(8,128)(2,1)S(1)}, u32[]{:S(2)}, u32[]{:S(2)}) collective-permute-start(bf16[256,256]{1,0:T(8,128)(2,1)S(1)} %collective-permute-done.1.refs_3_), channel_id=1, source_target_pairs={{0,16},{16,0},{32,48},{48,32},{64,80},{80,64},{96,112},{112,96},{1... | collective-permute-start | bytes 393224 | tf_op jit(solution)/shard_map/x_three/ppermute | solution.py:182
  23.0 1.6 %copy-start = (bf16[1,1,64,128,128]{4,3,2,1,0:T(8,128)(2,1)S(1)}, bf16[1,1,64,128,128]{4,3,2,1,0:T(8,128)(2,1)}, u32[]{:S(2)}) copy-start(bf16[1,1,64,128,128]{4,3,2,1,0:T(8,128)(2,1)} %param.6) | copy-start | bytes 6291460
  28.7 3.2 %collective-permute-start.10 = (bf16[128,256]{1,0:T(8,128)(2,1)S(1)}, bf16[128,256]{1,0:T(8,128)(2,1)S(1)}, u32[]{:S(2)}, u32[]{:S(2)}) collective-permute-start(bf16[128,256]{1,0:T(8,128)(2,1)S(1)} %collective-permute-done.2.refs_0_), channel_id=1, source_target_pairs={{0,16},{16,0},{32,48},{48,32},{64,80},{80,64},{96,112},{112,96},{1... | collective-permute-start | bytes 196616 | tf_op jit(solution)/shard_map/x_four/ppermute | solution.py:182
  32.5 4.5 %collective-permute-start.11 = (bf16[1024,256]{1,0:T(8,128)(2,1)S(1)}, bf16[1024,256]{1,0:T(8,128)(2,1)S(1)}, u32[]{:S(2)}, u32[]{:S(2)}) collective-permute-start(bf16[1024,256]{1,0:T(8,128)(2,1)S(1)} %tail_multiply.7), channel_id=1, source_target_pairs={{0,1},{1,0},{2,3},{3,2},{4,5},{5,4},{6,7},{7,6},{8,9},{9,8},{10,11... | collective-permute-start | bytes 1572872 | tf_op jit(solution)/shard_map/partial_swap/ppermute | solution.py:234
  53.3 3.5 %collective-permute-start.12 = (bf16[128,256]{1,0:T(8,128)(2,1)S(1)}, bf16[128,256]{1,0:T(8,128)(2,1)S(1)}, u32[]{:S(2)}, u32[]{:S(2)}) collective-permute-start(bf16[128,256]{1,0:T(8,128)(2,1)S(1)} %convert_element_type.40.refs_0_), channel_id=1, source_target_pairs={{0,1},{1,0},{2,3},{3,2},{4,5},{5,4},{6,7},{7,6},{8,9},{9,8},{10,11... | collective-permute-start | bytes 196616 | tf_op jit(solution)/shard_map/core_swap/ppermute | solution.py:186
  56.8 6.0 %collective-permute-start.14 = (bf16[256,256]{1,0:T(8,128)(2,1)S(1)}, bf16[256,256]{1,0:T(8,128)(2,1)S(1)}, u32[]{:S(2)}, u32[]{:S(2)}) collective-permute-start(bf16[256,256]{1,0:T(8,128)(2,1)S(1)} %pad_maximum_fusion.6), channel_id=1, source_target_pairs={{0,64},{1,193},{2,66},{3,195},{4,68},{5,197},{6,70},{7,199},{8,72}... | collective-permute-start | bytes 393224 | tf_op jit(solution)/shard_map/z_two/ppermute | solution.py:178
  57.2 7.8 %collective-permute-start.13 = (bf16[256,256]{1,0:T(8,128)(2,1)S(1)}, bf16[256,256]{1,0:T(8,128)(2,1)S(1)}, u32[]{:S(2)}, u32[]{:S(2)}) collective-permute-start(bf16[256,256]{1,0:T(8,128)(2,1)S(1)} %pad_maximum_fusion.6), channel_id=1, source_target_pairs={{0,32},{1,225},{2,34},{3,227},{4,36},{5,229},{6,38},{7,231},{8,40}... | collective-permute-start | bytes 393224 | tf_op jit(solution)/shard_map/z_one/ppermute | solution.py:178
  58.5 3.1 %collective-permute-start.15 = (bf16[128,256]{1,0:T(8,128)(2,1)S(1)}, bf16[128,256]{1,0:T(8,128)(2,1)S(1)}, u32[]{:S(2)}, u32[]{:S(2)}) collective-permute-start(bf16[128,256]{1,0:T(8,128)(2,1)S(1)} %convert_element_type.40.refs_0_), channel_id=1, source_target_pairs={{0,16},{16,0},{32,48},{48,32},{64,80},{80,64},{96,112},{112,96},{1... | collective-permute-start | bytes 196616 | tf_op jit(solution)/shard_map/x_own/ppermute | solution.py:182
  62.8 7.5 %collective-permute-start.16 = (bf16[256,256]{1,0:T(8,128)(2,1)S(1)}, bf16[256,256]{1,0:T(8,128)(2,1)S(1)}, u32[]{:S(2)}, u32[]{:S(2)}) collective-permute-start(bf16[256,256]{1,0:T(8,128)(2,1)S(1)} %collective-permute-done.14.refs_2_), channel_id=1, source_target_pairs={{0,32},{1,225},{2,34},{3,227},{4,36},{5,229},{6,38},{7,231},{8,40}... | collective-permute-start | bytes 393224 | tf_op jit(solution)/shard_map/z_three/ppermute | solution.py:178
  65.0 6.1 %collective-permute-start.17 = (bf16[512,256]{1,0:T(8,128)(2,1)S(1)}, bf16[512,256]{1,0:T(8,128)(2,1)S(1)}, u32[]{:S(2)}, u32[]{:S(2)}) collective-permute-start(bf16[512,256]{1,0:T(8,128)(2,1)S(1)} %pad_maximum_fusion), channel_id=1, source_target_pairs={{0,16},{16,0},{32,48},{48,32},{64,80},{80,64},{96,112},{112,96},{1... | collective-permute-start | bytes 786440 | tf_op jit(solution)/shard_map/x_near/ppermute | solution.py:182
  65.1 5.1 %collective-permute-start.18 = (bf16[128,256]{1,0:T(8,128)(2,1)S(1)}, bf16[128,256]{1,0:T(8,128)(2,1)S(1)}, u32[]{:S(2)}, u32[]{:S(2)}) collective-permute-start(bf16[128,256]{1,0:T(8,128)(2,1)S(1)} %slice.10), channel_id=1, source_target_pairs={{0,64},{1,193},{2,66},{3,195},{4,68},{5,197},{6,70},{7,199},{8,72}... | collective-permute-start | bytes 196616 | tf_op jit(solution)/shard_map/z_four/ppermute | solution.py:178
  70.2 5.0 %collective-permute-start.19 = (bf16[384,256]{1,0:T(8,128)(2,1)S(1)}, bf16[384,256]{1,0:T(8,128)(2,1)S(1)}, u32[]{:S(2)}, u32[]{:S(2)}) collective-permute-start(bf16[384,256]{1,0:T(8,128)(2,1)S(1)} %pad_maximum_fusion.3), channel_id=1, source_target_pairs={{0,16},{16,0},{32,48},{48,32},{64,80},{80,64},{96,112},{112,96},{1... | collective-permute-start | bytes 589832 | tf_op jit(solution)/shard_map/x_far/ppermute | solution.py:182
  75.9 6.6 %collective-permute-start.20 = (bf16[1024,256]{1,0:T(8,128)(2,1)S(1)}, bf16[1024,256]{1,0:T(8,128)(2,1)S(1)}, u32[]{:S(2)}, u32[]{:S(2)}) collective-permute-start(bf16[1024,256]{1,0:T(8,128)(2,1)S(1)} %tail_multiply.9), channel_id=1, source_target_pairs={{0,1},{1,0},{2,3},{3,2},{4,5},{5,4},{6,7},{7,6},{8,9},{9,8},{10,11... | collective-permute-start | bytes 1572872 | tf_op jit(solution)/shard_map/partial_swap/ppermute | solution.py:234
  95.3 3.2 %collective-permute-start.21 = (bf16[128,256]{1,0:T(8,128)(2,1)S(1)}, bf16[128,256]{1,0:T(8,128)(2,1)S(1)}, u32[]{:S(2)}, u32[]{:S(2)}) collective-permute-start(bf16[128,256]{1,0:T(8,128)(2,1)S(1)} %convert_element_type.44.refs_0_), channel_id=1, source_target_pairs={{0,1},{1,0},{2,3},{3,2},{4,5},{5,4},{6,7},{7,6},{8,9},{9,8},{10,11... | collective-permute-start | bytes 196616 | tf_op jit(solution)/shard_map/core_swap/ppermute | solution.py:186
  98.5 5.9 %collective-permute-start.23 = (bf16[256,256]{1,0:T(8,128)(2,1)S(1)}, bf16[256,256]{1,0:T(8,128)(2,1)S(1)}, u32[]{:S(2)}, u32[]{:S(2)}) collective-permute-start(bf16[256,256]{1,0:T(8,128)(2,1)S(1)} %pad_maximum_fusion.7), channel_id=1, source_target_pairs={{0,64},{1,193},{2,66},{3,195},{4,68},{5,197},{6,70},{7,199},{8,72}... | collective-permute-start | bytes 393224 | tf_op jit(solution)/shard_map/z_two/ppermute | solution.py:178
  98.6 7.0 %collective-permute-start.22 = (bf16[256,256]{1,0:T(8,128)(2,1)S(1)}, bf16[256,256]{1,0:T(8,128)(2,1)S(1)}, u32[]{:S(2)}, u32[]{:S(2)}) collective-permute-start(bf16[256,256]{1,0:T(8,128)(2,1)S(1)} %pad_maximum_fusion.7), channel_id=1, source_target_pairs={{0,32},{1,225},{2,34},{3,227},{4,36},{5,229},{6,38},{7,231},{8,40}... | collective-permute-start | bytes 393224 | tf_op jit(solution)/shard_map/z_one/ppermute | solution.py:178
  100.6 3.6 %collective-permute-start.24 = (bf16[128,256]{1,0:T(8,128)(2,1)S(1)}, bf16[128,256]{1,0:T(8,128)(2,1)S(1)}, u32[]{:S(2)}, u32[]{:S(2)}) collective-permute-start(bf16[128,256]{1,0:T(8,128)(2,1)S(1)} %convert_element_type.44.refs_0_), channel_id=1, source_target_pairs={{0,16},{16,0},{32,48},{48,32},{64,80},{80,64},{96,112},{112,96},{1... | collective-permute-start | bytes 196616 | tf_op jit(solution)/shard_map/x_own/ppermute | solution.py:182
  104.4 7.4 %collective-permute-start.25 = (bf16[256,256]{1,0:T(8,128)(2,1)S(1)}, bf16[256,256]{1,0:T(8,128)(2,1)S(1)}, u32[]{:S(2)}, u32[]{:S(2)}) collective-permute-start(bf16[256,256]{1,0:T(8,128)(2,1)S(1)} %collective-permute-done.23.refs_2_), channel_id=1, source_target_pairs={{0,32},{1,225},{2,34},{3,227},{4,36},{5,229},{6,38},{7,231},{8,40}... | collective-permute-start | bytes 393224 | tf_op jit(solution)/shard_map/z_three/ppermute | solution.py:178
  105.6 6.4 %collective-permute-start.26 = (bf16[512,256]{1,0:T(8,128)(2,1)S(1)}, bf16[512,256]{1,0:T(8,128)(2,1)S(1)}, u32[]{:S(2)}, u32[]{:S(2)}) collective-permute-start(bf16[512,256]{1,0:T(8,128)(2,1)S(1)} %pad_maximum_fusion.1), channel_id=1, source_target_pairs={{0,16},{16,0},{32,48},{48,32},{64,80},{80,64},{96,112},{112,96},{1... | collective-permute-start | bytes 786440 | tf_op jit(solution)/shard_map/x_near/ppermute | solution.py:182
  106.8 5.0 %collective-permute-start.27 = (bf16[128,256]{1,0:T(8,128)(2,1)S(1)}, bf16[128,256]{1,0:T(8,128)(2,1)S(1)}, u32[]{:S(2)}, u32[]{:S(2)}) collective-permute-start(bf16[128,256]{1,0:T(8,128)(2,1)S(1)} %slice.11), channel_id=1, source_target_pairs={{0,64},{1,193},{2,66},{3,195},{4,68},{5,197},{6,70},{7,199},{8,72}... | collective-permute-start | bytes 196616 | tf_op jit(solution)/shard_map/z_four/ppermute | solution.py:178
  111.8 4.6 %collective-permute-start.28 = (bf16[384,256]{1,0:T(8,128)(2,1)S(1)}, bf16[384,256]{1,0:T(8,128)(2,1)S(1)}, u32[]{:S(2)}, u32[]{:S(2)}) collective-permute-start(bf16[384,256]{1,0:T(8,128)(2,1)S(1)} %pad_maximum_fusion.4), channel_id=1, source_target_pairs={{0,16},{16,0},{32,48},{48,32},{64,80},{80,64},{96,112},{112,96},{1... | collective-permute-start | bytes 589832 | tf_op jit(solution)/shard_map/x_far/ppermute | solution.py:182
  117.0 6.0 %collective-permute-start.29 = (bf16[1024,256]{1,0:T(8,128)(2,1)S(1)}, bf16[1024,256]{1,0:T(8,128)(2,1)S(1)}, u32[]{:S(2)}, u32[]{:S(2)}) collective-permute-start(bf16[1024,256]{1,0:T(8,128)(2,1)S(1)} %tail_multiply.11), channel_id=1, source_target_pairs={{0,1},{1,0},{2,3},{3,2},{4,5},{5,4},{6,7},{7,6},{8,9},{9,8},{10,11... | collective-permute-start | bytes 1572872 | tf_op jit(solution)/shard_map/partial_swap/ppermute | solution.py:234
  122.1 14.1 %copy-start.1 = (f32[128,256]{1,0:T(8,128)S(1)}, f32[128,256]{1,0:T(8,128)}, u32[]{:S(2)}) copy-start(f32[128,256]{1,0:T(8,128)} %param.5) | copy-start | bytes 393220

commit v7 on v5

--- a/solution.py
+++ b/solution.py
@@ -9,17 +9,27 @@
 MIB = 1024 * 1024
 
 
-def build_kernel(n_row, n_col, own_at_ref, sib_at_ref, meta_ref, own_ref, sib_ref, dense_ref, acc_ref):
+def build_kernel(
+    n_row, n_col, own_at_ref, sib_at_ref, meta_ref, own_ref, sib_ref, dense_ref, last_ref, before_ref, cell_ref
+):
     tile = own_ref.shape[1]
     slots = own_ref.shape[0]
     half = n_col // 2
     ring = n_row // 2
     my_row, my_col = meta_ref[0], meta_ref[1]
     core = my_col & 1
-    acc_ref[...] = jnp.zeros_like(acc_ref)
+    dense_ref[...] = jnp.zeros_like(dense_ref)
+
+    def clear(cell, carry):
+        last_ref[cell] = -1
+        return carry
+
+    lax.fori_loop(0, n_row * n_col, clear, 0)
 
     def add_tiles(at_ref, tiles_ref, sibling):
-        def add_tile(k, carry):
+        count = at_ref[2 * slots]
+
+        def link(k, carry):
             row, col = at_ref[k], at_ref[slots + k]
             row_at = ((row ^ my_col) & 1) * half + (row >> 1)
             ahead = ((col >> 1) + ring - (my_row >> 1)) & (ring - 1)
@@ -30,28 +40,41 @@
                 keep = (away > 0) & (away < ring // 2)
             else:
                 keep = away <= ring // 2
+            cell = row_at * n_row + col_at
+            cell_ref[k] = jnp.where(keep, cell, -1)
 
             @pl.when(keep)
             def _():
+                before_ref[k] = last_ref[cell]
+                last_ref[cell] = k
+
+            return carry
+
+        lax.fori_loop(0, count, link, 0)
+
+        def write(k, carry):
+            cell = jnp.maximum(cell_ref[k], 0)
+
+            @pl.when((cell_ref[k] >= 0) & (last_ref[cell] == k))
+            def _():
+                def add(state):
+                    j, value = state
+                    return before_ref[j], value + tiles_ref[j].astype(jnp.float32)
+
+                start = (before_ref[k], tiles_ref[k].astype(jnp.float32))
+                _, value = lax.while_loop(lambda state: state[0] >= 0, add, start)
                 at = (
-                    pl.ds(pl.multiple_of(row_at * tile, tile), tile),
-                    pl.ds(pl.multiple_of(col_at * tile, tile), tile),
+                    pl.ds(pl.multiple_of((cell // n_row) * tile, tile), tile),
+                    pl.ds(pl.multiple_of((cell % n_row) * tile, tile), tile),
                 )
-                acc_ref[at] += tiles_ref[k].astype(jnp.float32)
+                dense_ref[at] = value.astype(jnp.bfloat16)
 
             return carry
 
-        lax.fori_loop(0, at_ref[2 * slots], add_tile, 0)
+        lax.fori_loop(0, count, write, 0)
 
     add_tiles(own_at_ref, own_ref, 0)
     add_tiles(sib_at_ref, sib_ref, 1)
-
-    def emit(r, carry):
-        at = pl.ds(pl.multiple_of(r * tile, tile), tile)
-        dense_ref[at, :] = acc_ref[at, :].astype(jnp.bfloat16)
-        return carry
-
-    lax.fori_loop(0, dense_ref.shape[0] // tile, emit, 0)
 
 
 def build_dense(own_at, sib_at, meta, own_tiles, sib_tiles, n_row, n_col):
@@ -68,7 +91,11 @@
         out_shape=jax.ShapeDtypeStruct(shape, jnp.bfloat16),
         in_specs=[smem, smem, smem, vmem, vmem],
         out_specs=vmem,
-        scratch_shapes=[pltpu.VMEM(shape, jnp.float32)],
+        scratch_shapes=[
+            pltpu.SMEM((n_row * n_col,), jnp.int32),
+            pltpu.SMEM((own_tiles.shape[0],), jnp.int32),
+            pltpu.SMEM((own_tiles.shape[0],), jnp.int32),
+        ],
         compiler_params=pltpu.CompilerParams(vmem_limit_bytes=36 * MIB),
         cost_estimate=pl.CostEstimate(flops=shape[0] * shape[1], bytes_accessed=6 * shape[0] * shape[1], transcendentals=0),
         name="build_dense",
@@ -180,17 +207,15 @@
     both = jnp.concatenate([own, sibling])
     one = onward(both, 1)
     two = onward(both, 2)
+    two, over_own = lax.optimization_barrier((two, over(own)))
     dense = None
     if build is not None:
         two, dense = lax.optimization_barrier((two, build(sibling)))
-        over_near = [over(jnp.concatenate([own, one, two]))]
-    else:
-        two, over_own = lax.optimization_barrier((two, over(own)))
-        over_near = [over_own, over(jnp.concatenate([one, two]))]
+    over_near = over(jnp.concatenate([one, two]))
     three = onward(two, 1)
     four = onward(two[:rows], 2)
     far = jnp.concatenate([three, four])
-    return [own, one, two, far] + over_near, [over(far)], dense
+    return [own, one, two, far, over_own, over_near], [over(far)], dense
 
 
 def per_device(embedding, tiles, tile_rows, tile_cols, counts):

time: 137 us -> 144 us (1.051); the launches traced: 136 us -> 145 us
  starting transfers between devices: 40.2 us -> 49.5 us
    ppermute x12, starting transfers between devices: 13.8 us -> 21 us  [onward(): return lax.ppermute(piece, ('row', 'col'), pairs)]
    ppermute x3, starting transfers between devices: 9.94 us -> 13 us  [per_device(): arrived = lax.ppermute(theirs, 'col', flip_core)]
    ppermute x8 -> x9, starting transfers between devices: 7.76 us -> 6.66 us  [over(): return lax.ppermute(piece, 'row', flip_x)]
    ppermute x8 -> x9, waiting for transfers between devices: 11.2 us -> 11.2 us  [over(): return lax.ppermute(piece, 'row', flip_x)]
  transfers between devices with their start and end apart: 28 -> 29, of which waited for: 21 -> 18; matrix products, arithmetic and copies ran while one was open for 1% -> 1% of each run, Pallas kernels for 10% -> 9%
where the time goes in v7:
time: 144 us; the launch traced here: 145 us
  starting transfers between devices  49.5 us (34%)
  blocking collectives  43.5 us (30%)
  waiting for transfers between devices  31 us (22%)
  Pallas kernels  15.1 us (10%)
  other arithmetic  3.08 us (2%)
  local copies, waits for them, and re-layouts  1.66 us (1%)
    all_to_all x3, blocking collectives, per_device(): lax.all_to_all(pair.reshape(n_col // 2, per_dev, width), 'col', split_axi...  43.5 us
    ppermute x12, starting transfers between devices, onward(): return lax.ppermute(piece, ('row', 'col'), pairs)  21 us
    ppermute x12, waiting for transfers between devices, onward(): return lax.ppermute(piece, ('row', 'col'), pairs)  14.3 us
    ppermute x3, starting transfers between devices, per_device(): arrived = lax.ppermute(theirs, 'col', flip_core)  13 us
    ppermute x9, waiting for transfers between devices, over(): return lax.ppermute(piece, 'row', flip_x)  11.2 us
    ppermute x3, starting transfers between devices, gather_pieces(): sibling = lax.ppermute(own, 'col', flip_core)  8.42 us
    pallas_call x3, Pallas kernels, head_multiply(): pl.pallas_call(kernel, out_shape=jax.ShapeDtypeStruct((n_rows, width), jn...  7.91 us
    ppermute x9, starting transfers between devices, over(): return lax.ppermute(piece, 'row', flip_x)  6.66 us
  transfers between devices with their start and end apart: 29, of which 18 were waited for; matrix products, arithmetic and copies ran while one was open for 1% of the time, Pallas kernels for 9%

profile of v7, /device:TPU:1, one launch (start us, length us, event | category | flops | bytes accessed | tf_op | source)
XLA Modules:
  0.0 144.7 jit_solution(8958623610348048496)
XLA Ops:
  0.0 0.9 convert_element_type.36.refs_0_
  0.9 3.3 %collective-permute-start = (bf16[128,256]{1,0:T(8,128)(2,1)S(1)}, bf16[128,256]{1,0:T(8,128)(2,1)S(1)}, u32[]{:S(2)}, u32[]{:S(2)}) collective-permute-start(bf16[128,256]{1,0:T(8,128)(2,1)S(1)} %convert_element_type.36.refs_0_), channel_id=1, source_target_pairs={{0,1},{1,0},{2,3},{3,2},{4,5},{5,4},{6,7},{7,6},{8,9},{9,8},{10,11... | collective-permute-start | bytes 196616 | tf_op jit(solution)/shard_map/ppermute | solution.py:206
  4.2 0.9 collective-permute-done
  6.2 5.1 %collective-permute-start.5 = (bf16[256,256]{1,0:T(8,128)(2,1)S(1)}, bf16[256,256]{1,0:T(8,128)(2,1)S(1)}, u32[]{:S(2)}, u32[]{:S(2)}) collective-permute-start(bf16[256,256]{1,0:T(8,128)(2,1)S(1)} %pad_maximum_fusion.3), channel_id=1, source_target_pairs={{0,32},{1,225},{2,34},{3,227},{4,36},{5,229},{6,38},{7,231},{8,40}... | collective-permute-start | bytes 393224 | tf_op jit(solution)/shard_map/ppermute | solution.py:201
  11.3 1.2 collective-permute-start.1
  12.5 0.7 pad_add_fusion.refs_0_
  13.3 3.0 %collective-permute-done.1.refs_2_ = bf16[256,256]{1,0:T(8,128)(2,1)S(1)} collective-permute-done((bf16[256,256]{1,0:T(8,128)(2,1)S(1)}, bf16[256,256]{1,0:T(8,128)(2,1)S(1)}, u32[]{:S(2)}, u32[]{:S(2)}) %collective-permute-start.1) | collective-permute-done | bytes 131104 | tf_op jit(solution)/shard_map/ppermute | solution.py:201
  16.4 1.6 %copy-done = bf16[1,1,64,128,128]{4,3,2,1,0:T(8,128)(2,1)S(1)} copy-done((bf16[1,1,64,128,128]{4,3,2,1,0:T(8,128)(2,1)S(1)}, bf16[1,1,64,128,128]{4,3,2,1,0:T(8,128)(2,1)}, u32[]{:S(2)}) %copy-start) | copy-done | bytes 2097176
  17.9 3.6 %build_dense.1.dense_ref = bf16[2048,2048]{1,0:T(8,128)(2,1)S(1)} custom-call(s32[129]{0:T(256)S(1)} %pad_add_fusion.refs_0_, s32[129]{0:T(256)S(1)} %collective-permute-done.3.refs_1_, s32[2]{0:T(128)S(1)} %pad_add_fusion.1.refs_2_, bf16[64,128,128]{2,1,0:T(8,128)(2,1)S(1)} %bitcast.11, bf16[64,128,128]{2,1,0:T(8,128)(2,1)S(1)} %collective-permute-done.4.refs_4_), custom_call_target="tpu_custom_call" | custom-call | flops 4194304 | bytes 25165824 | tf_op jit(solution)/shard_map/build_dense/pallas_call | solution.py:89
  21.5 3.3 %collective-permute-start.6 = (bf16[256,256]{1,0:T(8,128)(2,1)S(1)}, bf16[256,256]{1,0:T(8,128)(2,1)S(1)}, u32[]{:S(2)}, u32[]{:S(2)}) collective-permute-start(bf16[256,256]{1,0:T(8,128)(2,1)S(1)} %collective-permute-done.1.refs_2_), channel_id=1, source_target_pairs={{0,32},{1,225},{2,34},{3,227},{4,36},{5,229},{6,38},{7,231},{8,40}... | collective-permute-start | bytes 393224 | tf_op jit(solution)/shard_map/ppermute | solution.py:201
  24.8 1.8 %collective-permute-start.8 = (bf16[512,256]{1,0:T(8,128)(2,1)S(1)}, bf16[512,256]{1,0:T(8,128)(2,1)S(1)}, u32[]{:S(2)}, u32[]{:S(2)}) collective-permute-start(bf16[512,256]{1,0:T(8,128)(2,1)S(1)} %pad_maximum_fusion), channel_id=1, source_target_pairs={{0,16},{16,0},{32,48},{48,32},{64,80},{80,64},{96,112},{112,96},{1... | collective-permute-start | bytes 786440 | tf_op jit(solution)/shard_map/ppermute | solution.py:204
  27.1 3.6 %collective-permute-done.7 = bf16[128,256]{1,0:T(8,128)(2,1)S(1)} collective-permute-done((bf16[128,256]{1,0:T(8,128)(2,1)S(1)}, bf16[128,256]{1,0:T(8,128)(2,1)S(1)}, u32[]{:S(2)}, u32[]{:S(2)}) %collective-permute-start.7) | collective-permute-done | bytes 65568 | tf_op jit(solution)/shard_map/ppermute | solution.py:201
  31.0 2.4 %collective-permute-done.8.refs_5_ = bf16[512,256]{1,0:T(8,128)(2,1)S(1)} collective-permute-done((bf16[512,256]{1,0:T(8,128)(2,1)S(1)}, bf16[512,256]{1,0:T(8,128)(2,1)S(1)}, u32[]{:S(2)}, u32[]{:S(2)}) %collective-permute-start.8) | collective-permute-done | bytes 262176 | tf_op jit(solution)/shard_map/ppermute | solution.py:204
  33.4 2.6 %head_multiply.3.head_ref = f32[2048,256]{1,0:T(8,128)S(1)} custom-call(bf16[2048,2048]{1,0:T(8,128)(2,1)S(1)} %build_dense.1.dense_ref, bf16[128,256]{1,0:T(8,128)(2,1)S(1)} %convert_element_type.36.refs_0_, bf16[256,256]{1,0:T(8,128)(2,1)S(1)} %collective-permute-done.5.refs_1_, bf16[256,256]{1,0:T(8,128)(2,1)S(1)} %collective-permute-done.1.refs_2_, ...), custom_call_target="tpu_custom_call" | custom-call | flops 1744830464 | bytes 6815744 | tf_op jit(solution)/shard_map/head_multiply/pallas_call | solution.py:144
  36.1 0.6 tail_multiply.7
  36.7 2.7 %collective-permute-start.10 = (bf16[1024,256]{1,0:T(8,128)(2,1)S(1)}, bf16[1024,256]{1,0:T(8,128)(2,1)S(1)}, u32[]{:S(2)}, u32[]{:S(2)}) collective-permute-start(bf16[1024,256]{1,0:T(8,128)(2,1)S(1)} %tail_multiply.7), channel_id=1, source_target_pairs={{0,1},{1,0},{2,3},{3,2},{4,5},{5,4},{6,7},{7,6},{8,9},{9,8},{10,11... | collective-permute-start | bytes 1572872 | tf_op jit(solution)/shard_map/ppermute | solution.py:242
  40.0 0.9 collective-permute-done.10
  41.1 17.7 %all_to_all.15 = bf16[8,128,256]{2,1,0:T(8,128)(2,1)S(1)} all-to-all(bf16[8,128,256]{2,1,0:T(8,128)(2,1)S(1)} %bitcast.12), channel_id=1, replica_groups={{0,2,4,6,8,10,12,14},{1,3,5,7,9,11,13,15},{16,18,20,22,24,26,28,30},{17..., dimensions={0} | all-to-all | bytes 1048576 | tf_op jit(solution)/shard_map/all_to_all | solution.py:245
  58.9 2.6 %collective-permute-start.11 = (bf16[128,256]{1,0:T(8,128)(2,1)S(1)}, bf16[128,256]{1,0:T(8,128)(2,1)S(1)}, u32[]{:S(2)}, u32[]{:S(2)}) collective-permute-start(bf16[128,256]{1,0:T(8,128)(2,1)S(1)} %convert_element_type.40.refs_0_), channel_id=1, source_target_pairs={{0,1},{1,0},{2,3},{3,2},{4,5},{5,4},{6,7},{7,6},{8,9},{9,8},{10,11... | collective-permute-start | bytes 196616 | tf_op jit(solution)/shard_map/ppermute | solution.py:206
  61.4 0.9 collective-permute-done.11
  62.3 1.4 collective-permute-start.13
  63.7 3.6 %collective-permute-start.12 = (bf16[256,256]{1,0:T(8,128)(2,1)S(1)}, bf16[256,256]{1,0:T(8,128)(2,1)S(1)}, u32[]{:S(2)}, u32[]{:S(2)}) collective-permute-start(bf16[256,256]{1,0:T(8,128)(2,1)S(1)} %pad_maximum_fusion.4), channel_id=1, source_target_pairs={{0,32},{1,225},{2,34},{3,227},{4,36},{5,229},{6,38},{7,231},{8,40}... | collective-permute-start | bytes 393224 | tf_op jit(solution)/shard_map/ppermute | solution.py:201
  67.3 3.8 %collective-permute-done.14.refs_4_ = bf16[128,256]{1,0:T(8,128)(2,1)S(1)} collective-permute-done((bf16[128,256]{1,0:T(8,128)(2,1)S(1)}, bf16[128,256]{1,0:T(8,128)(2,1)S(1)}, u32[]{:S(2)}, u32[]{:S(2)}) %collective-permute-start.14) | collective-permute-done | bytes 65568 | tf_op jit(solution)/shard_map/ppermute | solution.py:204
  71.8 1.3 collective-permute-start.16
  73.1 1.9 %collective-permute-done.15 = bf16[256,256]{1,0:T(8,128)(2,1)S(1)} collective-permute-done((bf16[256,256]{1,0:T(8,128)(2,1)S(1)}, bf16[256,256]{1,0:T(8,128)(2,1)S(1)}, u32[]{:S(2)}, u32[]{:S(2)}) %collective-permute-start.15) | collective-permute-done | bytes 131104 | tf_op jit(solution)/shard_map/ppermute | solution.py:201
  75.0 1.1 collective-permute-done.16
  76.1 1.0 collective-permute-start.18
  77.5 2.6 %head_multiply.4.head_ref = f32[2048,256]{1,0:T(8,128)S(1)} custom-call(bf16[2048,2048]{1,0:T(8,128)(2,1)S(1)} %build_dense.1.dense_ref, bf16[128,256]{1,0:T(8,128)(2,1)S(1)} %convert_element_type.40.refs_0_, bf16[256,256]{1,0:T(8,128)(2,1)S(1)} %collective-permute-done.12.refs_1_, bf16[256,256]{1,0:T(8,128)(2,1)S(1)} %collective-permute-done.13.refs_2_, ...), custom_call_target="tpu_custom_call" | custom-call | flops 1744830464 | bytes 6815744 | tf_op jit(solution)/shard_map/head_multiply/pallas_call | solution.py:144
  80.1 1.3 collective-permute-done.18.refs_0_
  82.0 4.9 %collective-permute-start.19 = (bf16[1024,256]{1,0:T(8,128)(2,1)S(1)}, bf16[1024,256]{1,0:T(8,128)(2,1)S(1)}, u32[]{:S(2)}, u32[]{:S(2)}) collective-permute-start(bf16[1024,256]{1,0:T(8,128)(2,1)S(1)} %tail_multiply.9), channel_id=1, source_target_pairs={{0,1},{1,0},{2,3},{3,2},{4,5},{5,4},{6,7},{7,6},{8,9},{9,8},{10,11... | collective-permute-start | bytes 1572872 | tf_op jit(solution)/shard_map/ppermute | solution.py:242
  87.6 0.9 collective-permute-done.19
  88.6 12.8 %all_to_all.16 = bf16[8,128,256]{2,1,0:T(8,128)(2,1)S(1)} all-to-all(bf16[8,128,256]{2,1,0:T(8,128)(2,1)S(1)} %bitcast.13), channel_id=1, replica_groups={{0,2,4,6,8,10,12,14},{1,3,5,7,9,11,13,15},{16,18,20,22,24,26,28,30},{17..., dimensions={0} | all-to-all | bytes 1048576 | tf_op jit(solution)/shard_map/all_to_all | solution.py:245
  101.5 2.6 %collective-permute-start.20 = (bf16[128,256]{1,0:T(8,128)(2,1)S(1)}, bf16[128,256]{1,0:T(8,128)(2,1)S(1)}, u32[]{:S(2)}, u32[]{:S(2)}) collective-permute-start(bf16[128,256]{1,0:T(8,128)(2,1)S(1)} %convert_element_type.44.refs_0_), channel_id=1, source_target_pairs={{0,1},{1,0},{2,3},{3,2},{4,5},{5,4},{6,7},{7,6},{8,9},{9,8},{10,11... | collective-permute-start | bytes 196616 | tf_op jit(solution)/shard_map/ppermute | solution.py:206
  104.1 0.9 collective-permute-done.20
  105.6 1.2 collective-permute-start.21
  106.8 1.5 %collective-permute-start.23 = (bf16[128,256]{1,0:T(8,128)(2,1)S(1)}, bf16[128,256]{1,0:T(8,128)(2,1)S(1)}, u32[]{:S(2)}, u32[]{:S(2)}) collective-permute-start(bf16[128,256]{1,0:T(8,128)(2,1)S(1)} %convert_element_type.44.refs_0_), channel_id=1, source_target_pairs={{0,16},{16,0},{32,48},{48,32},{64,80},{80,64},{96,112},{112,96},{1... | collective-permute-start | bytes 196616 | tf_op jit(solution)/shard_map/ppermute | solution.py:204
  108.3 1.8 %collective-permute-done.23.refs_4_ = bf16[128,256]{1,0:T(8,128)(2,1)S(1)} collective-permute-done((bf16[128,256]{1,0:T(8,128)(2,1)S(1)}, bf16[128,256]{1,0:T(8,128)(2,1)S(1)}, u32[]{:S(2)}, u32[]{:S(2)}) %collective-permute-start.23) | collective-permute-done | bytes 65568 | tf_op jit(solution)/shard_map/ppermute | solution.py:204
  110.1 1.1 collective-permute-done.22.refs_2_
  111.2 1.8 %collective-permute-start.24 = (bf16[256,256]{1,0:T(8,128)(2,1)S(1)}, bf16[256,256]{1,0:T(8,128)(2,1)S(1)}, u32[]{:S(2)}, u32[]{:S(2)}) collective-permute-start(bf16[256,256]{1,0:T(8,128)(2,1)S(1)} %collective-permute-done.22.refs_2_), channel_id=1, source_target_pairs={{0,32},{1,225},{2,34},{3,227},{4,36},{5,229},{6,38},{7,231},{8,40}... | collective-permute-start | bytes 393224 | tf_op jit(solution)/shard_map/ppermute | solution.py:201
  113.0 1.0 collective-permute-start.26
  114.0 1.0 collective-permute-start.25
  115.1 3.7 %collective-permute-done.25 = bf16[128,256]{1,0:T(8,128)(2,1)S(1)} collective-permute-done((bf16[128,256]{1,0:T(8,128)(2,1)S(1)}, bf16[128,256]{1,0:T(8,128)(2,1)S(1)}, u32[]{:S(2)}, u32[]{:S(2)}) %collective-permute-start.25) | collective-permute-done | bytes 65568 | tf_op jit(solution)/shard_map/ppermute | solution.py:201
  119.3 2.6 %head_multiply.5.head_ref = f32[2048,256]{1,0:T(8,128)S(1)} custom-call(bf16[2048,2048]{1,0:T(8,128)(2,1)S(1)} %build_dense.1.dense_ref, bf16[128,256]{1,0:T(8,128)(2,1)S(1)} %convert_element_type.44.refs_0_, bf16[256,256]{1,0:T(8,128)(2,1)S(1)} %collective-permute-done.21.refs_1_, bf16[256,256]{1,0:T(8,128)(2,1)S(1)} %collective-permute-done.22.refs_2_, ...), custom_call_target="tpu_custom_call" | custom-call | flops 1744830464 | bytes 6815744 | tf_op jit(solution)/shard_map/head_multiply/pallas_call | solution.py:144
  121.9 1.4 collective-permute-done.27.refs_0_
  123.9 5.3 %collective-permute-start.28 = (bf16[1024,256]{1,0:T(8,128)(2,1)S(1)}, bf16[1024,256]{1,0:T(8,128)(2,1)S(1)}, u32[]{:S(2)}, u32[]{:S(2)}) collective-permute-start(bf16[1024,256]{1,0:T(8,128)(2,1)S(1)} %tail_multiply.11), channel_id=1, source_target_pairs={{0,1},{1,0},{2,3},{3,2},{4,5},{5,4},{6,7},{7,6},{8,9},{9,8},{10,11... | collective-permute-start | bytes 1572872 | tf_op jit(solution)/shard_map/ppermute | solution.py:242
  129.8 0.9 collective-permute-done.28
  130.9 13.0 %all_to_all.17 = bf16[8,128,256]{2,1,0:T(8,128)(2,1)S(1)} all-to-all(bf16[8,128,256]{2,1,0:T(8,128)(2,1)S(1)} %bitcast.14), channel_id=1, replica_groups={{0,2,4,6,8,10,12,14},{1,3,5,7,9,11,13,15},{16,18,20,22,24,26,28,30},{17..., dimensions={0} | all-to-all | bytes 1048576 | tf_op jit(solution)/shard_map/all_to_all | solution.py:245
  144.0 0.7 add_multiply_fusion
  (54 shorter events, 7.0 us)
Async XLA Ops:
  0.9 4.2 %collective-permute-start = (bf16[128,256]{1,0:T(8,128)(2,1)S(1)}, bf16[128,256]{1,0:T(8,128)(2,1)S(1)}, u32[]{:S(2)}, u32[]{:S(2)}) collective-permute-start(bf16[128,256]{1,0:T(8,128)(2,1)S(1)} %convert_element_type.36.refs_0_), channel_id=1, source_target_pairs={{0,1},{1,0},{2,3},{3,2},{4,5},{5,4},{6,7},{7,6},{8,9},{9,8},{10,11... | collective-permute-start | bytes 196616 | tf_op jit(solution)/shard_map/ppermute | solution.py:206
  5.1 11.2 %collective-permute-start.4 = (bf16[64,128,128]{2,1,0:T(8,128)(2,1)}, bf16[64,128,128]{2,1,0:T(8,128)(2,1)S(1)}, u32[]{:S(2)}, u32[]{:S(2)}) collective-permute-start(bf16[64,128,128]{2,1,0:T(8,128)(2,1)} %bitcast.10), channel_id=1, source_target_pairs={{0,1},{1,0},{2,3},{3,2},{4,5},{5,4},{6,7},{7,6},{8,9},{9,8},{10,11... | collective-permute-start | bytes 6291464 | tf_op jit(solution)/shard_map/ppermute | solution.py:234
  5.5 7.8 %collective-permute-start.2 = (bf16[128,256]{1,0:T(8,128)(2,1)S(1)}, bf16[128,256]{1,0:T(8,128)(2,1)S(1)}, u32[]{:S(2)}, u32[]{:S(2)}) collective-permute-start(bf16[128,256]{1,0:T(8,128)(2,1)S(1)} %convert_element_type.36.refs_0_), channel_id=1, source_target_pairs={{0,16},{16,0},{32,48},{48,32},{64,80},{80,64},{96,112},{112,96},{1... | collective-permute-start | bytes 196616 | tf_op jit(solution)/shard_map/ppermute | solution.py:204
  6.2 18.6 %collective-permute-start.5 = (bf16[256,256]{1,0:T(8,128)(2,1)S(1)}, bf16[256,256]{1,0:T(8,128)(2,1)S(1)}, u32[]{:S(2)}, u32[]{:S(2)}) collective-permute-start(bf16[256,256]{1,0:T(8,128)(2,1)S(1)} %pad_maximum_fusion.3), channel_id=1, source_target_pairs={{0,32},{1,225},{2,34},{3,227},{4,36},{5,229},{6,38},{7,231},{8,40}... | collective-permute-start | bytes 393224 | tf_op jit(solution)/shard_map/ppermute | solution.py:201
  11.3 5.1 %collective-permute-start.1 = (bf16[256,256]{1,0:T(8,128)(2,1)S(1)}, bf16[256,256]{1,0:T(8,128)(2,1)S(1)}, u32[]{:S(2)}, u32[]{:S(2)}) collective-permute-start(bf16[256,256]{1,0:T(8,128)(2,1)S(1)} %pad_maximum_fusion.3), channel_id=1, source_target_pairs={{0,64},{1,193},{2,66},{3,195},{4,68},{5,197},{6,70},{7,199},{8,72}... | collective-permute-start | bytes 393224 | tf_op jit(solution)/shard_map/ppermute | solution.py:201
  13.2 3.1 %collective-permute-start.3 = (s32[129]{0:T(256)S(1)}, s32[129]{0:T(256)S(1)}, u32[]{:S(2)}, u32[]{:S(2)}) collective-permute-start(s32[129]{0:T(256)S(1)} %pad_add_fusion.refs_0_), channel_id=1, source_target_pairs={{0,1},{1,0},{2,3},{3,2},{4,5},{5,4},{6,7},{7,6},{8,9},{9,8},{10,11... | collective-permute-start | bytes 1556 | tf_op jit(solution)/shard_map/ppermute | solution.py:230
  16.4 1.6 %copy-start = (bf16[1,1,64,128,128]{4,3,2,1,0:T(8,128)(2,1)S(1)}, bf16[1,1,64,128,128]{4,3,2,1,0:T(8,128)(2,1)}, u32[]{:S(2)}) copy-start(bf16[1,1,64,128,128]{4,3,2,1,0:T(8,128)(2,1)} %param.6) | copy-start | bytes 6291460
  21.5 5.5 %collective-permute-start.6 = (bf16[256,256]{1,0:T(8,128)(2,1)S(1)}, bf16[256,256]{1,0:T(8,128)(2,1)S(1)}, u32[]{:S(2)}, u32[]{:S(2)}) collective-permute-start(bf16[256,256]{1,0:T(8,128)(2,1)S(1)} %collective-permute-done.1.refs_2_), channel_id=1, source_target_pairs={{0,32},{1,225},{2,34},{3,227},{4,36},{5,229},{6,38},{7,231},{8,40}... | collective-permute-start | bytes 393224 | tf_op jit(solution)/shard_map/ppermute | solution.py:201
  24.8 8.6 %collective-permute-start.8 = (bf16[512,256]{1,0:T(8,128)(2,1)S(1)}, bf16[512,256]{1,0:T(8,128)(2,1)S(1)}, u32[]{:S(2)}, u32[]{:S(2)}) collective-permute-start(bf16[512,256]{1,0:T(8,128)(2,1)S(1)} %pad_maximum_fusion), channel_id=1, source_target_pairs={{0,16},{16,0},{32,48},{48,32},{64,80},{80,64},{96,112},{112,96},{1... | collective-permute-start | bytes 786440 | tf_op jit(solution)/shard_map/ppermute | solution.py:204
  26.6 4.1 %collective-permute-start.7 = (bf16[128,256]{1,0:T(8,128)(2,1)S(1)}, bf16[128,256]{1,0:T(8,128)(2,1)S(1)}, u32[]{:S(2)}, u32[]{:S(2)}) collective-permute-start(bf16[128,256]{1,0:T(8,128)(2,1)S(1)} %slice.9), channel_id=1, source_target_pairs={{0,64},{1,193},{2,66},{3,195},{4,68},{5,197},{6,70},{7,199},{8,72}... | collective-permute-start | bytes 196616 | tf_op jit(solution)/shard_map/ppermute | solution.py:201
  30.7 5.4 %collective-permute-start.9 = (bf16[384,256]{1,0:T(8,128)(2,1)S(1)}, bf16[384,256]{1,0:T(8,128)(2,1)S(1)}, u32[]{:S(2)}, u32[]{:S(2)}) collective-permute-start(bf16[384,256]{1,0:T(8,128)(2,1)S(1)} %constant_dynamic-update-slice_fusion.refs_3_), channel_id=1, source_target_pairs={{0,16},{16,0},{32,48},{48,32},{64,80},{80,64},{96,112},{112,96},{1... | collective-permute-start | bytes 589832 | tf_op jit(solution)/shard_map/ppermute | solution.py:204
  36.7 4.3 %collective-permute-start.10 = (bf16[1024,256]{1,0:T(8,128)(2,1)S(1)}, bf16[1024,256]{1,0:T(8,128)(2,1)S(1)}, u32[]{:S(2)}, u32[]{:S(2)}) collective-permute-start(bf16[1024,256]{1,0:T(8,128)(2,1)S(1)} %tail_multiply.7), channel_id=1, source_target_pairs={{0,1},{1,0},{2,3},{3,2},{4,5},{5,4},{6,7},{7,6},{8,9},{9,8},{10,11... | collective-permute-start | bytes 1572872 | tf_op jit(solution)/shard_map/ppermute | solution.py:242
  58.9 3.5 %collective-permute-start.11 = (bf16[128,256]{1,0:T(8,128)(2,1)S(1)}, bf16[128,256]{1,0:T(8,128)(2,1)S(1)}, u32[]{:S(2)}, u32[]{:S(2)}) collective-permute-start(bf16[128,256]{1,0:T(8,128)(2,1)S(1)} %convert_element_type.40.refs_0_), channel_id=1, source_target_pairs={{0,1},{1,0},{2,3},{3,2},{4,5},{5,4},{6,7},{7,6},{8,9},{9,8},{10,11... | collective-permute-start | bytes 196616 | tf_op jit(solution)/shard_map/ppermute | solution.py:206
  62.3 8.8 %collective-permute-start.13 = (bf16[256,256]{1,0:T(8,128)(2,1)S(1)}, bf16[256,256]{1,0:T(8,128)(2,1)S(1)}, u32[]{:S(2)}, u32[]{:S(2)}) collective-permute-start(bf16[256,256]{1,0:T(8,128)(2,1)S(1)} %pad_maximum_fusion.4), channel_id=1, source_target_pairs={{0,64},{1,193},{2,66},{3,195},{4,68},{5,197},{6,70},{7,199},{8,72}... | collective-permute-start | bytes 393224 | tf_op jit(solution)/shard_map/ppermute | solution.py:201
  63.7 7.5 %collective-permute-start.12 = (bf16[256,256]{1,0:T(8,128)(2,1)S(1)}, bf16[256,256]{1,0:T(8,128)(2,1)S(1)}, u32[]{:S(2)}, u32[]{:S(2)}) collective-permute-start(bf16[256,256]{1,0:T(8,128)(2,1)S(1)} %pad_maximum_fusion.4), channel_id=1, source_target_pairs={{0,32},{1,225},{2,34},{3,227},{4,36},{5,229},{6,38},{7,231},{8,40}... | collective-permute-start | bytes 393224 | tf_op jit(solution)/shard_map/ppermute | solution.py:201
  67.3 3.8 %collective-permute-start.14 = (bf16[128,256]{1,0:T(8,128)(2,1)S(1)}, bf16[128,256]{1,0:T(8,128)(2,1)S(1)}, u32[]{:S(2)}, u32[]{:S(2)}) collective-permute-start(bf16[128,256]{1,0:T(8,128)(2,1)S(1)} %convert_element_type.40.refs_0_), channel_id=1, source_target_pairs={{0,16},{16,0},{32,48},{48,32},{64,80},{80,64},{96,112},{112,96},{1... | collective-permute-start | bytes 196616 | tf_op jit(solution)/shard_map/ppermute | solution.py:204
  71.2 3.8 %collective-permute-start.15 = (bf16[256,256]{1,0:T(8,128)(2,1)S(1)}, bf16[256,256]{1,0:T(8,128)(2,1)S(1)}, u32[]{:S(2)}, u32[]{:S(2)}) collective-permute-start(bf16[256,256]{1,0:T(8,128)(2,1)S(1)} %collective-permute-done.13.refs_2_), channel_id=1, source_target_pairs={{0,32},{1,225},{2,34},{3,227},{4,36},{5,229},{6,38},{7,231},{8,40}... | collective-permute-start | bytes 393224 | tf_op jit(solution)/shard_map/ppermute | solution.py:201
  71.2 6.2 %collective-permute-start.17 = (bf16[512,256]{1,0:T(8,128)(2,1)S(1)}, bf16[512,256]{1,0:T(8,128)(2,1)S(1)}, u32[]{:S(2)}, u32[]{:S(2)}) collective-permute-start(bf16[512,256]{1,0:T(8,128)(2,1)S(1)} %pad_maximum_fusion.1), channel_id=1, source_target_pairs={{0,16},{16,0},{32,48},{48,32},{64,80},{80,64},{96,112},{112,96},{1... | collective-permute-start | bytes 786440 | tf_op jit(solution)/shard_map/ppermute | solution.py:204
  71.8 4.3 %collective-permute-start.16 = (bf16[128,256]{1,0:T(8,128)(2,1)S(1)}, bf16[128,256]{1,0:T(8,128)(2,1)S(1)}, u32[]{:S(2)}, u32[]{:S(2)}) collective-permute-start(bf16[128,256]{1,0:T(8,128)(2,1)S(1)} %slice.10), channel_id=1, source_target_pairs={{0,64},{1,193},{2,66},{3,195},{4,68},{5,197},{6,70},{7,199},{8,72}... | collective-permute-start | bytes 196616 | tf_op jit(solution)/shard_map/ppermute | solution.py:201
  76.1 5.4 %collective-permute-start.18 = (bf16[384,256]{1,0:T(8,128)(2,1)S(1)}, bf16[384,256]{1,0:T(8,128)(2,1)S(1)}, u32[]{:S(2)}, u32[]{:S(2)}) collective-permute-start(bf16[384,256]{1,0:T(8,128)(2,1)S(1)} %constant_dynamic-update-slice_fusion.2.refs_3_), channel_id=1, source_target_pairs={{0,16},{16,0},{32,48},{48,32},{64,80},{80,64},{96,112},{112,96},{1... | collective-permute-start | bytes 589832 | tf_op jit(solution)/shard_map/ppermute | solution.py:204
  82.0 6.5 %collective-permute-start.19 = (bf16[1024,256]{1,0:T(8,128)(2,1)S(1)}, bf16[1024,256]{1,0:T(8,128)(2,1)S(1)}, u32[]{:S(2)}, u32[]{:S(2)}) collective-permute-start(bf16[1024,256]{1,0:T(8,128)(2,1)S(1)} %tail_multiply.9), channel_id=1, source_target_pairs={{0,1},{1,0},{2,3},{3,2},{4,5},{5,4},{6,7},{7,6},{8,9},{9,8},{10,11... | collective-permute-start | bytes 1572872 | tf_op jit(solution)/shard_map/ppermute | solution.py:242
  101.5 3.5 %collective-permute-start.20 = (bf16[128,256]{1,0:T(8,128)(2,1)S(1)}, bf16[128,256]{1,0:T(8,128)(2,1)S(1)}, u32[]{:S(2)}, u32[]{:S(2)}) collective-permute-start(bf16[128,256]{1,0:T(8,128)(2,1)S(1)} %convert_element_type.44.refs_0_), channel_id=1, source_target_pairs={{0,1},{1,0},{2,3},{3,2},{4,5},{5,4},{6,7},{7,6},{8,9},{9,8},{10,11... | collective-permute-start | bytes 196616 | tf_op jit(solution)/shard_map/ppermute | solution.py:206
  105.0 6.2 %collective-permute-start.22 = (bf16[256,256]{1,0:T(8,128)(2,1)S(1)}, bf16[256,256]{1,0:T(8,128)(2,1)S(1)}, u32[]{:S(2)}, u32[]{:S(2)}) collective-permute-start(bf16[256,256]{1,0:T(8,128)(2,1)S(1)} %pad_maximum_fusion.5), channel_id=1, source_target_pairs={{0,64},{1,193},{2,66},{3,195},{4,68},{5,197},{6,70},{7,199},{8,72}... | collective-permute-start | bytes 393224 | tf_op jit(solution)/shard_map/ppermute | solution.py:201
  105.6 7.4 %collective-permute-start.21 = (bf16[256,256]{1,0:T(8,128)(2,1)S(1)}, bf16[256,256]{1,0:T(8,128)(2,1)S(1)}, u32[]{:S(2)}, u32[]{:S(2)}) collective-permute-start(bf16[256,256]{1,0:T(8,128)(2,1)S(1)} %pad_maximum_fusion.5), channel_id=1, source_target_pairs={{0,32},{1,225},{2,34},{3,227},{4,36},{5,229},{6,38},{7,231},{8,40}... | collective-permute-start | bytes 393224 | tf_op jit(solution)/shard_map/ppermute | solution.py:201
  106.8 3.3 %collective-permute-start.23 = (bf16[128,256]{1,0:T(8,128)(2,1)S(1)}, bf16[128,256]{1,0:T(8,128)(2,1)S(1)}, u32[]{:S(2)}, u32[]{:S(2)}) collective-permute-start(bf16[128,256]{1,0:T(8,128)(2,1)S(1)} %convert_element_type.44.refs_0_), channel_id=1, source_target_pairs={{0,16},{16,0},{32,48},{48,32},{64,80},{80,64},{96,112},{112,96},{1... | collective-permute-start | bytes 196616 | tf_op jit(solution)/shard_map/ppermute | solution.py:204
  111.2 3.9 %collective-permute-start.24 = (bf16[256,256]{1,0:T(8,128)(2,1)S(1)}, bf16[256,256]{1,0:T(8,128)(2,1)S(1)}, u32[]{:S(2)}, u32[]{:S(2)}) collective-permute-start(bf16[256,256]{1,0:T(8,128)(2,1)S(1)} %collective-permute-done.22.refs_2_), channel_id=1, source_target_pairs={{0,32},{1,225},{2,34},{3,227},{4,36},{5,229},{6,38},{7,231},{8,40}... | collective-permute-start | bytes 393224 | tf_op jit(solution)/shard_map/ppermute | solution.py:201
  113.0 6.3 %collective-permute-start.26 = (bf16[512,256]{1,0:T(8,128)(2,1)S(1)}, bf16[512,256]{1,0:T(8,128)(2,1)S(1)}, u32[]{:S(2)}, u32[]{:S(2)}) collective-permute-start(bf16[512,256]{1,0:T(8,128)(2,1)S(1)} %pad_maximum_fusion.2), channel_id=1, source_target_pairs={{0,16},{16,0},{32,48},{48,32},{64,80},{80,64},{96,112},{112,96},{1... | collective-permute-start | bytes 786440 | tf_op jit(solution)/shard_map/ppermute | solution.py:204
  114.0 4.7 %collective-permute-start.25 = (bf16[128,256]{1,0:T(8,128)(2,1)S(1)}, bf16[128,256]{1,0:T(8,128)(2,1)S(1)}, u32[]{:S(2)}, u32[]{:S(2)}) collective-permute-start(bf16[128,256]{1,0:T(8,128)(2,1)S(1)} %slice.11), channel_id=1, source_target_pairs={{0,64},{1,193},{2,66},{3,195},{4,68},{5,197},{6,70},{7,199},{8,72}... | collective-permute-start | bytes 196616 | tf_op jit(solution)/shard_map/ppermute | solution.py:201
  118.8 4.5 %collective-permute-start.27 = (bf16[384,256]{1,0:T(8,128)(2,1)S(1)}, bf16[384,256]{1,0:T(8,128)(2,1)S(1)}, u32[]{:S(2)}, u32[]{:S(2)}) collective-permute-start(bf16[384,256]{1,0:T(8,128)(2,1)S(1)} %constant_dynamic-update-slice_fusion.4.refs_3_), channel_id=1, source_target_pairs={{0,16},{16,0},{32,48},{48,32},{64,80},{80,64},{96,112},{112,96},{1... | collective-permute-start | bytes 589832 | tf_op jit(solution)/shard_map/ppermute | solution.py:204
  123.9 6.9 %collective-permute-start.28 = (bf16[1024,256]{1,0:T(8,128)(2,1)S(1)}, bf16[1024,256]{1,0:T(8,128)(2,1)S(1)}, u32[]{:S(2)}, u32[]{:S(2)}) collective-permute-start(bf16[1024,256]{1,0:T(8,128)(2,1)S(1)} %tail_multiply.11), channel_id=1, source_target_pairs={{0,1},{1,0},{2,3},{3,2},{4,5},{5,4},{6,7},{7,6},{8,9},{9,8},{10,11... | collective-permute-start | bytes 1572872 | tf_op jit(solution)/shard_map/ppermute | solution.py:242
  129.8 14.1 %copy-start.1 = (f32[128,256]{1,0:T(8,128)S(1)}, f32[128,256]{1,0:T(8,128)}, u32[]{:S(2)}) copy-start(f32[128,256]{1,0:T(8,128)} %param.5) | copy-start | bytes 393220

commit v8 on v1

--- a/solution.py
+++ b/solution.py
@@ -173,20 +173,35 @@
                 pairs.append((i * n_col + j, to * n_col + j))
         return lax.ppermute(piece, ("row", "col"), pairs)
 
+    def over(piece, name):
+        with jax.named_scope(name):
+            return lax.ppermute(piece, "row", flip_x)
+
     sibling = lax.ppermute(own, "col", flip_core)
     both = jnp.concatenate([own, sibling])
-    one = onward(both, 1)
-    two = onward(both, 2)
-    dense = None
+    with jax.named_scope("z_one"):
+        one = onward(both, 1)
+    with jax.named_scope("z_two"):
+        two = onward(both, 2)
     if build is not None:
-        two, dense = lax.optimization_barrier((two, build(sibling)))
-    near = jnp.concatenate([own, one, two])
-    flip_near = lax.ppermute(near, "row", flip_x)
-    three = onward(two, 1)
-    four = onward(two[:rows], 2)
+        with jax.named_scope("z_three"):
+            three = onward(both, 3)
+        over_one = over(jnp.concatenate([own, one]), "x_one")
+        over_two = over(two, "x_two")
+        with jax.named_scope("z_four"):
+            four = onward(three[:rows], 1)
+        over_three = over(three, "x_three")
+        last, dense = lax.optimization_barrier((four, build(sibling)))
+        over_four = over(last, "x_four")
+        return [own, one, two, three, four, over_one, over_two], [over_three, over_four], dense
+    one, over_own = lax.optimization_barrier((one, over(own, "x_own")))
+    over_near = over(jnp.concatenate([one, two]), "x_near")
+    with jax.named_scope("z_three"):
+        three = onward(two, 1)
+    with jax.named_scope("z_four"):
+        four = onward(two[:rows], 2)
     far = jnp.concatenate([three, four])
-    flip_far = lax.ppermute(far, "row", flip_x)
-    return [near, far, flip_near], [flip_far], dense
+    return [own, one, two, far, over_own, over_near], [over(far, "x_far")], None
 
 
 def per_device(embedding, tiles, tile_rows, tile_cols, counts):

time: 137 us -> 137 us (level)
  starting transfers between devices: 36.7 us -> 49.1 us
  waiting for transfers between devices: 36.9 us -> 24.8 us
    ppermute x6 -> x10, waiting for transfers between devices: 9.53 us -> 2.92 us  [over(): return lax.ppermute(piece, 'row', flip_x)]
    ppermute x12, starting transfers between devices: 13.2 us -> 17.7 us  [onward(): return lax.ppermute(piece, ('row', 'col'), pairs)]
    ppermute x12, waiting for transfers between devices: 20.8 us -> 16.4 us  [onward(): return lax.ppermute(piece, ('row', 'col'), pairs)]
    ppermute x3, starting transfers between devices: 9.31 us -> 12.7 us  [per_device(): arrived = lax.ppermute(theirs, 'col', flip_core)]
    ppermute x6 -> x10, starting transfers between devices: 5.45 us -> 7.78 us  [over(): return lax.ppermute(piece, 'row', flip_x)]
    ppermute x1, starting transfers between devices: 0.02 us -> 2.09 us  [per_device(): sib_at = lax.ppermute(own_at, 'col', flip_core)]
  transfers between devices with their start and end apart: 26 -> 30, of which waited for: 22 -> 18; matrix products, arithmetic and copies ran while one was open for 1% -> 1% of each run, Pallas kernels for 11% -> 10%
where the time goes in v8:
time: 137 us; the launch traced here: 136 us
  starting transfers between devices  49.1 us (36%)
  blocking collectives  41.6 us (30%)
  waiting for transfers between devices  24.8 us (18%)
  Pallas kernels  15.3 us (11%)
  other arithmetic  3.07 us (2%)
  local copies, waits for them, and re-layouts  1.64 us (1%)
    all_to_all x3, blocking collectives, per_device(): lax.all_to_all(pair.reshape(n_col // 2, per_dev, width), 'col', split_axi...  41.6 us
    ppermute x12, starting transfers between devices, onward(): return lax.ppermute(piece, ('row', 'col'), pairs)  17.7 us
    ppermute x12, waiting for transfers between devices, onward(): return lax.ppermute(piece, ('row', 'col'), pairs)  16.4 us
    ppermute x3, starting transfers between devices, per_device(): arrived = lax.ppermute(theirs, 'col', flip_core)  12.7 us
    ppermute x3, starting transfers between devices, gather_pieces(): sibling = lax.ppermute(own, 'col', flip_core)  8.42 us
    pallas_call x3, Pallas kernels, head_multiply(): pl.pallas_call(kernel, out_shape=jax.ShapeDtypeStruct((n_rows, width), jn...  7.92 us
    ppermute x10, starting transfers between devices, over(): return lax.ppermute(piece, 'row', flip_x)  7.78 us
    pallas_call x1, Pallas kernels, build_dense(): pl.pallas_call(kernel, out_shape=jax.ShapeDtypeStruct(shape, jnp.bfloat16...  3.85 us
  transfers between devices with their start and end apart: 30, of which 18 were waited for; matrix products, arithmetic and copies ran while one was open for 1% of the time, Pallas kernels for 10%

profile of v8, /device:TPU:1, one launch (start us, length us, event | category | flops | bytes accessed | tf_op | source)
XLA Modules:
  0.0 136.4 jit_solution(10170466679379929244)
XLA Ops:
  0.0 0.9 convert_element_type.36.refs_0_
  0.9 3.3 %collective-permute-start = (bf16[128,256]{1,0:T(8,128)(2,1)S(1)}, bf16[128,256]{1,0:T(8,128)(2,1)S(1)}, u32[]{:S(2)}, u32[]{:S(2)}) collective-permute-start(bf16[128,256]{1,0:T(8,128)(2,1)S(1)} %convert_element_type.36.refs_0_), channel_id=1, source_target_pairs={{0,1},{1,0},{2,3},{3,2},{4,5},{5,4},{6,7},{7,6},{8,9},{9,8},{10,11... | collective-permute-start | bytes 196616 | tf_op jit(solution)/shard_map/ppermute | solution.py:180
  4.2 0.9 collective-permute-done
  5.5 3.9 %collective-permute-start.5 = (bf16[256,256]{1,0:T(8,128)(2,1)S(1)}, bf16[256,256]{1,0:T(8,128)(2,1)S(1)}, u32[]{:S(2)}, u32[]{:S(2)}) collective-permute-start(bf16[256,256]{1,0:T(8,128)(2,1)S(1)} %pad_maximum_fusion.3), channel_id=1, source_target_pairs={{0,32},{1,225},{2,34},{3,227},{4,36},{5,229},{6,38},{7,231},{8,40}... | collective-permute-start | bytes 393224 | tf_op jit(solution)/shard_map/z_one/ppermute | solution.py:174
  9.4 1.2 collective-permute-start.6
  11.8 1.3 collective-permute-start.7
  13.1 1.4 %collective-permute-done.6.refs_2_ = bf16[256,256]{1,0:T(8,128)(2,1)S(1)} collective-permute-done((bf16[256,256]{1,0:T(8,128)(2,1)S(1)}, bf16[256,256]{1,0:T(8,128)(2,1)S(1)}, u32[]{:S(2)}, u32[]{:S(2)}) %collective-permute-start.6) | collective-permute-done | bytes 131104 | tf_op jit(solution)/shard_map/z_two/ppermute | solution.py:174
  14.5 1.2 collective-permute-start.8
  15.7 0.7 pad_add_fusion.refs_0_
  16.4 2.1 %collective-permute-start.3 = (s32[129]{0:T(256)S(1)}, s32[129]{0:T(256)S(1)}, u32[]{:S(2)}, u32[]{:S(2)}) collective-permute-start(s32[129]{0:T(256)S(1)} %pad_add_fusion.refs_0_), channel_id=1, source_target_pairs={{0,1},{1,0},{2,3},{3,2},{4,5},{5,4},{6,7},{7,6},{8,9},{9,8},{10,11... | collective-permute-start | bytes 1556 | tf_op jit(solution)/shard_map/ppermute | solution.py:216
  18.5 3.2 %collective-permute-start.2 = (bf16[128,256]{1,0:T(8,128)(2,1)S(1)}, bf16[128,256]{1,0:T(8,128)(2,1)S(1)}, u32[]{:S(2)}, u32[]{:S(2)}) collective-permute-start(bf16[128,256]{1,0:T(8,128)(2,1)S(1)} %slice.12), channel_id=1, source_target_pairs={{0,32},{1,225},{2,34},{3,227},{4,36},{5,229},{6,38},{7,231},{8,40}... | collective-permute-start | bytes 196616 | tf_op jit(solution)/shard_map/z_four/ppermute | solution.py:174
  21.8 1.2 collective-permute-start.9
  23.0 1.6 %copy-done = bf16[1,1,64,128,128]{4,3,2,1,0:T(8,128)(2,1)S(1)} copy-done((bf16[1,1,64,128,128]{4,3,2,1,0:T(8,128)(2,1)S(1)}, bf16[1,1,64,128,128]{4,3,2,1,0:T(8,128)(2,1)}, u32[]{:S(2)}) %copy-start) | copy-done | bytes 2097176
  24.6 3.8 %build_dense.1.dense_ref = bf16[2048,2048]{1,0:T(8,128)(2,1)S(1)} custom-call(s32[129]{0:T(256)S(1)} %pad_add_fusion.refs_0_, s32[129]{0:T(256)S(1)} %collective-permute-done.3.refs_1_, s32[2]{0:T(128)S(1)} %pad_add_fusion.1.refs_2_, bf16[64,128,128]{2,1,0:T(8,128)(2,1)S(1)} %bitcast.11, bf16[64,128,128]{2,1,0:T(8,128)(2,1)S(1)} %collective-permute-done.4.refs_4_), custom_call_target="tpu_custom_call" | custom-call | flops 4194304 | bytes 25165824 | tf_op jit(solution)/shard_map/build_dense/pallas_call | solution.py:66
  28.6 2.6 %head_multiply.3.head_ref = f32[2048,256]{1,0:T(8,128)S(1)} custom-call(bf16[2048,2048]{1,0:T(8,128)(2,1)S(1)} %build_dense.1.dense_ref, bf16[128,256]{1,0:T(8,128)(2,1)S(1)} %convert_element_type.36.refs_0_, bf16[256,256]{1,0:T(8,128)(2,1)S(1)} %collective-permute-done.5.refs_1_, bf16[256,256]{1,0:T(8,128)(2,1)S(1)} %collective-permute-done.6.refs_2_, ...), custom_call_target="tpu_custom_call" | custom-call | flops 1744830464 | bytes 6815744 | tf_op jit(solution)/shard_map/head_multiply/pallas_call | solution.py:117
  32.3 3.1 %collective-permute-start.11 = (bf16[1024,256]{1,0:T(8,128)(2,1)S(1)}, bf16[1024,256]{1,0:T(8,128)(2,1)S(1)}, u32[]{:S(2)}, u32[]{:S(2)}) collective-permute-start(bf16[1024,256]{1,0:T(8,128)(2,1)S(1)} %tail_multiply.7), channel_id=1, source_target_pairs={{0,1},{1,0},{2,3},{3,2},{4,5},{5,4},{6,7},{7,6},{8,9},{9,8},{10,11... | collective-permute-start | bytes 1572872 | tf_op jit(solution)/shard_map/ppermute | solution.py:228
  35.4 0.6 tail_multiply.6
  36.0 0.9 collective-permute-done.11
  37.1 15.7 %all_to_all.15 = bf16[8,128,256]{2,1,0:T(8,128)(2,1)S(1)} all-to-all(bf16[8,128,256]{2,1,0:T(8,128)(2,1)S(1)} %bitcast.12), channel_id=1, replica_groups={{0,2,4,6,8,10,12,14},{1,3,5,7,9,11,13,15},{16,18,20,22,24,26,28,30},{17..., dimensions={0} | all-to-all | bytes 1048576 | tf_op jit(solution)/shard_map/all_to_all | solution.py:231
  52.9 2.6 %collective-permute-start.12 = (bf16[128,256]{1,0:T(8,128)(2,1)S(1)}, bf16[128,256]{1,0:T(8,128)(2,1)S(1)}, u32[]{:S(2)}, u32[]{:S(2)}) collective-permute-start(bf16[128,256]{1,0:T(8,128)(2,1)S(1)} %convert_element_type.40.refs_0_), channel_id=1, source_target_pairs={{0,1},{1,0},{2,3},{3,2},{4,5},{5,4},{6,7},{7,6},{8,9},{9,8},{10,11... | collective-permute-start | bytes 196616 | tf_op jit(solution)/shard_map/ppermute | solution.py:180
  55.4 0.9 collective-permute-done.12
  56.4 2.1 %collective-permute-start.13 = (bf16[256,256]{1,0:T(8,128)(2,1)S(1)}, bf16[256,256]{1,0:T(8,128)(2,1)S(1)}, u32[]{:S(2)}, u32[]{:S(2)}) collective-permute-start(bf16[256,256]{1,0:T(8,128)(2,1)S(1)} %pad_maximum_fusion.4), channel_id=1, source_target_pairs={{0,32},{1,225},{2,34},{3,227},{4,36},{5,229},{6,38},{7,231},{8,40}... | collective-permute-start | bytes 393224 | tf_op jit(solution)/shard_map/z_one/ppermute | solution.py:174
  58.6 2.6 %collective-permute-done.15.refs_2_ = bf16[256,256]{1,0:T(8,128)(2,1)S(1)} collective-permute-done((bf16[256,256]{1,0:T(8,128)(2,1)S(1)}, bf16[256,256]{1,0:T(8,128)(2,1)S(1)}, u32[]{:S(2)}, u32[]{:S(2)}) %collective-permute-start.15) | collective-permute-done | bytes 131104 | tf_op jit(solution)/shard_map/z_two/ppermute | solution.py:174
  61.2 3.8 %collective-permute-start.16 = (bf16[256,256]{1,0:T(8,128)(2,1)S(1)}, bf16[256,256]{1,0:T(8,128)(2,1)S(1)}, u32[]{:S(2)}, u32[]{:S(2)}) collective-permute-start(bf16[256,256]{1,0:T(8,128)(2,1)S(1)} %collective-permute-done.15.refs_2_), channel_id=1, source_target_pairs={{0,32},{1,225},{2,34},{3,227},{4,36},{5,229},{6,38},{7,231},{8,40}... | collective-permute-start | bytes 393224 | tf_op jit(solution)/shard_map/z_three/ppermute | solution.py:174
  65.5 1.7 %collective-permute-done.16 = bf16[256,256]{1,0:T(8,128)(2,1)S(1)} collective-permute-done((bf16[256,256]{1,0:T(8,128)(2,1)S(1)}, bf16[256,256]{1,0:T(8,128)(2,1)S(1)}, u32[]{:S(2)}, u32[]{:S(2)}) %collective-permute-start.16) | collective-permute-done | bytes 131104 | tf_op jit(solution)/shard_map/z_three/ppermute | solution.py:174
  67.2 2.9 %collective-permute-done.17 = bf16[128,256]{1,0:T(8,128)(2,1)S(1)} collective-permute-done((bf16[128,256]{1,0:T(8,128)(2,1)S(1)}, bf16[128,256]{1,0:T(8,128)(2,1)S(1)}, u32[]{:S(2)}, u32[]{:S(2)}) %collective-permute-start.17) | collective-permute-done | bytes 65568 | tf_op jit(solution)/shard_map/z_four/ppermute | solution.py:174
  70.0 1.1 collective-permute-start.19
  71.2 2.6 %head_multiply.4.head_ref = f32[2048,256]{1,0:T(8,128)S(1)} custom-call(bf16[2048,2048]{1,0:T(8,128)(2,1)S(1)} %build_dense.1.dense_ref, bf16[128,256]{1,0:T(8,128)(2,1)S(1)} %convert_element_type.40.refs_0_, bf16[256,256]{1,0:T(8,128)(2,1)S(1)} %collective-permute-done.13.refs_1_, bf16[256,256]{1,0:T(8,128)(2,1)S(1)} %collective-permute-done.15.refs_2_, ...), custom_call_target="tpu_custom_call" | custom-call | flops 1744830464 | bytes 6815744 | tf_op jit(solution)/shard_map/head_multiply/pallas_call | solution.py:117
  73.9 1.4 %collective-permute-done.19.refs_0_ = bf16[384,256]{1,0:T(8,128)(2,1)S(1)} collective-permute-done((bf16[384,256]{1,0:T(8,128)(2,1)S(1)}, bf16[384,256]{1,0:T(8,128)(2,1)S(1)}, u32[]{:S(2)}, u32[]{:S(2)}) %collective-permute-start.19) | collective-permute-done | bytes 196640 | tf_op jit(solution)/shard_map/x_far/ppermute | solution.py:178
  75.3 0.6 tail_multiply.9
  75.9 5.2 %collective-permute-start.20 = (bf16[1024,256]{1,0:T(8,128)(2,1)S(1)}, bf16[1024,256]{1,0:T(8,128)(2,1)S(1)}, u32[]{:S(2)}, u32[]{:S(2)}) collective-permute-start(bf16[1024,256]{1,0:T(8,128)(2,1)S(1)} %tail_multiply.9), channel_id=1, source_target_pairs={{0,1},{1,0},{2,3},{3,2},{4,5},{5,4},{6,7},{7,6},{8,9},{9,8},{10,11... | collective-permute-start | bytes 1572872 | tf_op jit(solution)/shard_map/ppermute | solution.py:228
  81.7 0.9 collective-permute-done.20
  82.7 12.9 %all_to_all.16 = bf16[8,128,256]{2,1,0:T(8,128)(2,1)S(1)} all-to-all(bf16[8,128,256]{2,1,0:T(8,128)(2,1)S(1)} %bitcast.13), channel_id=1, replica_groups={{0,2,4,6,8,10,12,14},{1,3,5,7,9,11,13,15},{16,18,20,22,24,26,28,30},{17..., dimensions={0} | all-to-all | bytes 1048576 | tf_op jit(solution)/shard_map/all_to_all | solution.py:231
  95.8 2.6 %collective-permute-start.21 = (bf16[128,256]{1,0:T(8,128)(2,1)S(1)}, bf16[128,256]{1,0:T(8,128)(2,1)S(1)}, u32[]{:S(2)}, u32[]{:S(2)}) collective-permute-start(bf16[128,256]{1,0:T(8,128)(2,1)S(1)} %convert_element_type.44.refs_0_), channel_id=1, source_target_pairs={{0,1},{1,0},{2,3},{3,2},{4,5},{5,4},{6,7},{7,6},{8,9},{9,8},{10,11... | collective-permute-start | bytes 196616 | tf_op jit(solution)/shard_map/ppermute | solution.py:180
  98.3 0.9 collective-permute-done.21
  99.3 1.5 %collective-permute-start.22 = (bf16[256,256]{1,0:T(8,128)(2,1)S(1)}, bf16[256,256]{1,0:T(8,128)(2,1)S(1)}, u32[]{:S(2)}, u32[]{:S(2)}) collective-permute-start(bf16[256,256]{1,0:T(8,128)(2,1)S(1)} %pad_maximum_fusion.5), channel_id=1, source_target_pairs={{0,32},{1,225},{2,34},{3,227},{4,36},{5,229},{6,38},{7,231},{8,40}... | collective-permute-start | bytes 393224 | tf_op jit(solution)/shard_map/z_one/ppermute | solution.py:174
  100.8 3.6 %collective-permute-done.24.refs_2_ = bf16[256,256]{1,0:T(8,128)(2,1)S(1)} collective-permute-done((bf16[256,256]{1,0:T(8,128)(2,1)S(1)}, bf16[256,256]{1,0:T(8,128)(2,1)S(1)}, u32[]{:S(2)}, u32[]{:S(2)}) %collective-permute-start.24) | collective-permute-done | bytes 131104 | tf_op jit(solution)/shard_map/z_two/ppermute | solution.py:174
  104.4 0.7 collective-permute-start.25
  105.1 0.7 collective-permute-done.22.refs_1_
  105.8 1.3 collective-permute-start.27
  108.2 3.1 %collective-permute-done.26 = bf16[128,256]{1,0:T(8,128)(2,1)S(1)} collective-permute-done((bf16[128,256]{1,0:T(8,128)(2,1)S(1)}, bf16[128,256]{1,0:T(8,128)(2,1)S(1)}, u32[]{:S(2)}, u32[]{:S(2)}) %collective-permute-start.26) | collective-permute-done | bytes 65568 | tf_op jit(solution)/shard_map/z_four/ppermute | solution.py:174
  111.3 1.1 collective-permute-start.28
  112.4 2.6 %head_multiply.5.head_ref = f32[2048,256]{1,0:T(8,128)S(1)} custom-call(bf16[2048,2048]{1,0:T(8,128)(2,1)S(1)} %build_dense.1.dense_ref, bf16[128,256]{1,0:T(8,128)(2,1)S(1)} %convert_element_type.44.refs_0_, bf16[256,256]{1,0:T(8,128)(2,1)S(1)} %collective-permute-done.22.refs_1_, bf16[256,256]{1,0:T(8,128)(2,1)S(1)} %collective-permute-done.24.refs_2_, ...), custom_call_target="tpu_custom_call" | custom-call | flops 1744830464 | bytes 6815744 | tf_op jit(solution)/shard_map/head_multiply/pallas_call | solution.py:117
  115.0 1.0 collective-permute-done.28.refs_0_
  116.6 4.4 %collective-permute-start.29 = (bf16[1024,256]{1,0:T(8,128)(2,1)S(1)}, bf16[1024,256]{1,0:T(8,128)(2,1)S(1)}, u32[]{:S(2)}, u32[]{:S(2)}) collective-permute-start(bf16[1024,256]{1,0:T(8,128)(2,1)S(1)} %tail_multiply.11), channel_id=1, source_target_pairs={{0,1},{1,0},{2,3},{3,2},{4,5},{5,4},{6,7},{7,6},{8,9},{9,8},{10,11... | collective-permute-start | bytes 1572872 | tf_op jit(solution)/shard_map/ppermute | solution.py:228
  121.6 0.9 collective-permute-done.29
  122.7 12.9 %all_to_all.17 = bf16[8,128,256]{2,1,0:T(8,128)(2,1)S(1)} all-to-all(bf16[8,128,256]{2,1,0:T(8,128)(2,1)S(1)} %bitcast.14), channel_id=1, replica_groups={{0,2,4,6,8,10,12,14},{1,3,5,7,9,11,13,15},{16,18,20,22,24,26,28,30},{17..., dimensions={0} | all-to-all | bytes 1048576 | tf_op jit(solution)/shard_map/all_to_all | solution.py:231
  135.7 0.7 add_multiply_fusion
  (54 shorter events, 6.4 us)
Async XLA Ops:
  0.9 4.2 %collective-permute-start = (bf16[128,256]{1,0:T(8,128)(2,1)S(1)}, bf16[128,256]{1,0:T(8,128)(2,1)S(1)}, u32[]{:S(2)}, u32[]{:S(2)}) collective-permute-start(bf16[128,256]{1,0:T(8,128)(2,1)S(1)} %convert_element_type.36.refs_0_), channel_id=1, source_target_pairs={{0,1},{1,0},{2,3},{3,2},{4,5},{5,4},{6,7},{7,6},{8,9},{9,8},{10,11... | collective-permute-start | bytes 196616 | tf_op jit(solution)/shard_map/ppermute | solution.py:180
  5.1 17.9 %collective-permute-start.4 = (bf16[64,128,128]{2,1,0:T(8,128)(2,1)}, bf16[64,128,128]{2,1,0:T(8,128)(2,1)S(1)}, u32[]{:S(2)}, u32[]{:S(2)}) collective-permute-start(bf16[64,128,128]{2,1,0:T(8,128)(2,1)} %bitcast.10), channel_id=1, source_target_pairs={{0,1},{1,0},{2,3},{3,2},{4,5},{5,4},{6,7},{7,6},{8,9},{9,8},{10,11... | collective-permute-start | bytes 6291464 | tf_op jit(solution)/shard_map/ppermute | solution.py:220
  5.5 6.3 %collective-permute-start.5 = (bf16[256,256]{1,0:T(8,128)(2,1)S(1)}, bf16[256,256]{1,0:T(8,128)(2,1)S(1)}, u32[]{:S(2)}, u32[]{:S(2)}) collective-permute-start(bf16[256,256]{1,0:T(8,128)(2,1)S(1)} %pad_maximum_fusion.3), channel_id=1, source_target_pairs={{0,32},{1,225},{2,34},{3,227},{4,36},{5,229},{6,38},{7,231},{8,40}... | collective-permute-start | bytes 393224 | tf_op jit(solution)/shard_map/z_one/ppermute | solution.py:174
  9.4 5.1 %collective-permute-start.6 = (bf16[256,256]{1,0:T(8,128)(2,1)S(1)}, bf16[256,256]{1,0:T(8,128)(2,1)S(1)}, u32[]{:S(2)}, u32[]{:S(2)}) collective-permute-start(bf16[256,256]{1,0:T(8,128)(2,1)S(1)} %pad_maximum_fusion.3), channel_id=1, source_target_pairs={{0,64},{1,193},{2,66},{3,195},{4,68},{5,197},{6,70},{7,199},{8,72}... | collective-permute-start | bytes 393224 | tf_op jit(solution)/shard_map/z_two/ppermute | solution.py:174
  11.2 7.3 %collective-permute-start.1 = (bf16[256,256]{1,0:T(8,128)(2,1)S(1)}, bf16[256,256]{1,0:T(8,128)(2,1)S(1)}, u32[]{:S(2)}, u32[]{:S(2)}) collective-permute-start(bf16[256,256]{1,0:T(8,128)(2,1)S(1)} %pad_maximum_fusion.3), channel_id=1, source_target_pairs={{0,96},{1,161},{2,98},{3,163},{4,100},{5,165},{6,102},{7,167},{8,1... | collective-permute-start | bytes 393224 | tf_op jit(solution)/shard_map/z_three/ppermute | solution.py:174
  11.8 16.8 %collective-permute-start.7 = (bf16[384,256]{1,0:T(8,128)(2,1)S(1)}, bf16[384,256]{1,0:T(8,128)(2,1)S(1)}, u32[]{:S(2)}, u32[]{:S(2)}) collective-permute-start(bf16[384,256]{1,0:T(8,128)(2,1)S(1)} %pad_maximum_fusion.2), channel_id=1, source_target_pairs={{0,16},{16,0},{32,48},{48,32},{64,80},{80,64},{96,112},{112,96},{1... | collective-permute-start | bytes 589832 | tf_op jit(solution)/shard_map/x_one/ppermute | solution.py:178
  14.5 14.1 %collective-permute-start.8 = (bf16[256,256]{1,0:T(8,128)(2,1)S(1)}, bf16[256,256]{1,0:T(8,128)(2,1)S(1)}, u32[]{:S(2)}, u32[]{:S(2)}) collective-permute-start(bf16[256,256]{1,0:T(8,128)(2,1)S(1)} %collective-permute-done.6.refs_2_), channel_id=1, source_target_pairs={{0,16},{16,0},{32,48},{48,32},{64,80},{80,64},{96,112},{112,96},{1... | collective-permute-start | bytes 393224 | tf_op jit(solution)/shard_map/x_two/ppermute | solution.py:178
  16.4 5.3 %collective-permute-start.3 = (s32[129]{0:T(256)S(1)}, s32[129]{0:T(256)S(1)}, u32[]{:S(2)}, u32[]{:S(2)}) collective-permute-start(s32[129]{0:T(256)S(1)} %pad_add_fusion.refs_0_), channel_id=1, source_target_pairs={{0,1},{1,0},{2,3},{3,2},{4,5},{5,4},{6,7},{7,6},{8,9},{9,8},{10,11... | collective-permute-start | bytes 1556 | tf_op jit(solution)/shard_map/ppermute | solution.py:216
  18.5 9.9 %collective-permute-start.2 = (bf16[128,256]{1,0:T(8,128)(2,1)S(1)}, bf16[128,256]{1,0:T(8,128)(2,1)S(1)}, u32[]{:S(2)}, u32[]{:S(2)}) collective-permute-start(bf16[128,256]{1,0:T(8,128)(2,1)S(1)} %slice.12), channel_id=1, source_target_pairs={{0,32},{1,225},{2,34},{3,227},{4,36},{5,229},{6,38},{7,231},{8,40}... | collective-permute-start | bytes 196616 | tf_op jit(solution)/shard_map/z_four/ppermute | solution.py:174
  21.8 9.5 %collective-permute-start.9 = (bf16[256,256]{1,0:T(8,128)(2,1)S(1)}, bf16[256,256]{1,0:T(8,128)(2,1)S(1)}, u32[]{:S(2)}, u32[]{:S(2)}) collective-permute-start(bf16[256,256]{1,0:T(8,128)(2,1)S(1)} %collective-permute-done.1.refs_3_), channel_id=1, source_target_pairs={{0,16},{16,0},{32,48},{48,32},{64,80},{80,64},{96,112},{112,96},{1... | collective-permute-start | bytes 393224 | tf_op jit(solution)/shard_map/x_three/ppermute | solution.py:178
  23.0 1.6 %copy-start = (bf16[1,1,64,128,128]{4,3,2,1,0:T(8,128)(2,1)S(1)}, bf16[1,1,64,128,128]{4,3,2,1,0:T(8,128)(2,1)}, u32[]{:S(2)}) copy-start(bf16[1,1,64,128,128]{4,3,2,1,0:T(8,128)(2,1)} %param.6) | copy-start | bytes 6291460
  28.5 3.2 %collective-permute-start.10 = (bf16[128,256]{1,0:T(8,128)(2,1)S(1)}, bf16[128,256]{1,0:T(8,128)(2,1)S(1)}, u32[]{:S(2)}, u32[]{:S(2)}) collective-permute-start(bf16[128,256]{1,0:T(8,128)(2,1)S(1)} %collective-permute-done.2.refs_4_), channel_id=1, source_target_pairs={{0,16},{16,0},{32,48},{48,32},{64,80},{80,64},{96,112},{112,96},{1... | collective-permute-start | bytes 196616 | tf_op jit(solution)/shard_map/x_four/ppermute | solution.py:178
  32.3 4.7 %collective-permute-start.11 = (bf16[1024,256]{1,0:T(8,128)(2,1)S(1)}, bf16[1024,256]{1,0:T(8,128)(2,1)S(1)}, u32[]{:S(2)}, u32[]{:S(2)}) collective-permute-start(bf16[1024,256]{1,0:T(8,128)(2,1)S(1)} %tail_multiply.7), channel_id=1, source_target_pairs={{0,1},{1,0},{2,3},{3,2},{4,5},{5,4},{6,7},{7,6},{8,9},{9,8},{10,11... | collective-permute-start | bytes 1572872 | tf_op jit(solution)/shard_map/ppermute | solution.py:228
  52.9 3.5 %collective-permute-start.12 = (bf16[128,256]{1,0:T(8,128)(2,1)S(1)}, bf16[128,256]{1,0:T(8,128)(2,1)S(1)}, u32[]{:S(2)}, u32[]{:S(2)}) collective-permute-start(bf16[128,256]{1,0:T(8,128)(2,1)S(1)} %convert_element_type.40.refs_0_), channel_id=1, source_target_pairs={{0,1},{1,0},{2,3},{3,2},{4,5},{5,4},{6,7},{7,6},{8,9},{9,8},{10,11... | collective-permute-start | bytes 196616 | tf_op jit(solution)/shard_map/ppermute | solution.py:180
  56.3 4.9 %collective-permute-start.15 = (bf16[256,256]{1,0:T(8,128)(2,1)S(1)}, bf16[256,256]{1,0:T(8,128)(2,1)S(1)}, u32[]{:S(2)}, u32[]{:S(2)}) collective-permute-start(bf16[256,256]{1,0:T(8,128)(2,1)S(1)} %pad_maximum_fusion.4), channel_id=1, source_target_pairs={{0,64},{1,193},{2,66},{3,195},{4,68},{5,197},{6,70},{7,199},{8,72}... | collective-permute-start | bytes 393224 | tf_op jit(solution)/shard_map/z_two/ppermute | solution.py:174
  56.4 8.6 %collective-permute-start.13 = (bf16[256,256]{1,0:T(8,128)(2,1)S(1)}, bf16[256,256]{1,0:T(8,128)(2,1)S(1)}, u32[]{:S(2)}, u32[]{:S(2)}) collective-permute-start(bf16[256,256]{1,0:T(8,128)(2,1)S(1)} %pad_maximum_fusion.4), channel_id=1, source_target_pairs={{0,32},{1,225},{2,34},{3,227},{4,36},{5,229},{6,38},{7,231},{8,40}... | collective-permute-start | bytes 393224 | tf_op jit(solution)/shard_map/z_one/ppermute | solution.py:174
  58.6 6.4 %collective-permute-start.14 = (bf16[128,256]{1,0:T(8,128)(2,1)S(1)}, bf16[128,256]{1,0:T(8,128)(2,1)S(1)}, u32[]{:S(2)}, u32[]{:S(2)}) collective-permute-start(bf16[128,256]{1,0:T(8,128)(2,1)S(1)} %convert_element_type.40.refs_0_), channel_id=1, source_target_pairs={{0,16},{16,0},{32,48},{48,32},{64,80},{80,64},{96,112},{112,96},{1... | collective-permute-start | bytes 196616 | tf_op jit(solution)/shard_map/x_own/ppermute | solution.py:178
  61.2 5.9 %collective-permute-start.16 = (bf16[256,256]{1,0:T(8,128)(2,1)S(1)}, bf16[256,256]{1,0:T(8,128)(2,1)S(1)}, u32[]{:S(2)}, u32[]{:S(2)}) collective-permute-start(bf16[256,256]{1,0:T(8,128)(2,1)S(1)} %collective-permute-done.15.refs_2_), channel_id=1, source_target_pairs={{0,32},{1,225},{2,34},{3,227},{4,36},{5,229},{6,38},{7,231},{8,40}... | collective-permute-start | bytes 393224 | tf_op jit(solution)/shard_map/z_three/ppermute | solution.py:174
  65.0 6.2 %collective-permute-start.18 = (bf16[512,256]{1,0:T(8,128)(2,1)S(1)}, bf16[512,256]{1,0:T(8,128)(2,1)S(1)}, u32[]{:S(2)}, u32[]{:S(2)}) collective-permute-start(bf16[512,256]{1,0:T(8,128)(2,1)S(1)} %pad_maximum_fusion), channel_id=1, source_target_pairs={{0,16},{16,0},{32,48},{48,32},{64,80},{80,64},{96,112},{112,96},{1... | collective-permute-start | bytes 786440 | tf_op jit(solution)/shard_map/x_near/ppermute | solution.py:178
  65.5 4.6 %collective-permute-start.17 = (bf16[128,256]{1,0:T(8,128)(2,1)S(1)}, bf16[128,256]{1,0:T(8,128)(2,1)S(1)}, u32[]{:S(2)}, u32[]{:S(2)}) collective-permute-start(bf16[128,256]{1,0:T(8,128)(2,1)S(1)} %slice.13), channel_id=1, source_target_pairs={{0,64},{1,193},{2,66},{3,195},{4,68},{5,197},{6,70},{7,199},{8,72}... | collective-permute-start | bytes 196616 | tf_op jit(solution)/shard_map/z_four/ppermute | solution.py:174
  70.0 5.2 %collective-permute-start.19 = (bf16[384,256]{1,0:T(8,128)(2,1)S(1)}, bf16[384,256]{1,0:T(8,128)(2,1)S(1)}, u32[]{:S(2)}, u32[]{:S(2)}) collective-permute-start(bf16[384,256]{1,0:T(8,128)(2,1)S(1)} %constant_dynamic-update-slice_fusion.refs_3_), channel_id=1, source_target_pairs={{0,16},{16,0},{32,48},{48,32},{64,80},{80,64},{96,112},{112,96},{1... | collective-permute-start | bytes 589832 | tf_op jit(solution)/shard_map/x_far/ppermute | solution.py:178
  75.9 6.7 %collective-permute-start.20 = (bf16[1024,256]{1,0:T(8,128)(2,1)S(1)}, bf16[1024,256]{1,0:T(8,128)(2,1)S(1)}, u32[]{:S(2)}, u32[]{:S(2)}) collective-permute-start(bf16[1024,256]{1,0:T(8,128)(2,1)S(1)} %tail_multiply.9), channel_id=1, source_target_pairs={{0,1},{1,0},{2,3},{3,2},{4,5},{5,4},{6,7},{7,6},{8,9},{9,8},{10,11... | collective-permute-start | bytes 1572872 | tf_op jit(solution)/shard_map/ppermute | solution.py:228
  95.8 3.5 %collective-permute-start.21 = (bf16[128,256]{1,0:T(8,128)(2,1)S(1)}, bf16[128,256]{1,0:T(8,128)(2,1)S(1)}, u32[]{:S(2)}, u32[]{:S(2)}) collective-permute-start(bf16[128,256]{1,0:T(8,128)(2,1)S(1)} %convert_element_type.44.refs_0_), channel_id=1, source_target_pairs={{0,1},{1,0},{2,3},{3,2},{4,5},{5,4},{6,7},{7,6},{8,9},{9,8},{10,11... | collective-permute-start | bytes 196616 | tf_op jit(solution)/shard_map/ppermute | solution.py:180
  99.2 5.1 %collective-permute-start.24 = (bf16[256,256]{1,0:T(8,128)(2,1)S(1)}, bf16[256,256]{1,0:T(8,128)(2,1)S(1)}, u32[]{:S(2)}, u32[]{:S(2)}) collective-permute-start(bf16[256,256]{1,0:T(8,128)(2,1)S(1)} %pad_maximum_fusion.5), channel_id=1, source_target_pairs={{0,64},{1,193},{2,66},{3,195},{4,68},{5,197},{6,70},{7,199},{8,72}... | collective-permute-start | bytes 393224 | tf_op jit(solution)/shard_map/z_two/ppermute | solution.py:174
  99.3 6.4 %collective-permute-start.22 = (bf16[256,256]{1,0:T(8,128)(2,1)S(1)}, bf16[256,256]{1,0:T(8,128)(2,1)S(1)}, u32[]{:S(2)}, u32[]{:S(2)}) collective-permute-start(bf16[256,256]{1,0:T(8,128)(2,1)S(1)} %pad_maximum_fusion.5), channel_id=1, source_target_pairs={{0,32},{1,225},{2,34},{3,227},{4,36},{5,229},{6,38},{7,231},{8,40}... | collective-permute-start | bytes 393224 | tf_op jit(solution)/shard_map/z_one/ppermute | solution.py:174
  100.8 4.3 %collective-permute-start.23 = (bf16[128,256]{1,0:T(8,128)(2,1)S(1)}, bf16[128,256]{1,0:T(8,128)(2,1)S(1)}, u32[]{:S(2)}, u32[]{:S(2)}) collective-permute-start(bf16[128,256]{1,0:T(8,128)(2,1)S(1)} %convert_element_type.44.refs_0_), channel_id=1, source_target_pairs={{0,16},{16,0},{32,48},{48,32},{64,80},{80,64},{96,112},{112,96},{1... | collective-permute-start | bytes 196616 | tf_op jit(solution)/shard_map/x_own/ppermute | solution.py:178
  104.4 3.8 %collective-permute-start.25 = (bf16[256,256]{1,0:T(8,128)(2,1)S(1)}, bf16[256,256]{1,0:T(8,128)(2,1)S(1)}, u32[]{:S(2)}, u32[]{:S(2)}) collective-permute-start(bf16[256,256]{1,0:T(8,128)(2,1)S(1)} %collective-permute-done.24.refs_2_), channel_id=1, source_target_pairs={{0,32},{1,225},{2,34},{3,227},{4,36},{5,229},{6,38},{7,231},{8,40}... | collective-permute-start | bytes 393224 | tf_op jit(solution)/shard_map/z_three/ppermute | solution.py:174
  105.8 6.6 %collective-permute-start.27 = (bf16[512,256]{1,0:T(8,128)(2,1)S(1)}, bf16[512,256]{1,0:T(8,128)(2,1)S(1)}, u32[]{:S(2)}, u32[]{:S(2)}) collective-permute-start(bf16[512,256]{1,0:T(8,128)(2,1)S(1)} %pad_maximum_fusion.1), channel_id=1, source_target_pairs={{0,16},{16,0},{32,48},{48,32},{64,80},{80,64},{96,112},{112,96},{1... | collective-permute-start | bytes 786440 | tf_op jit(solution)/shard_map/x_near/ppermute | solution.py:178
  107.1 4.2 %collective-permute-start.26 = (bf16[128,256]{1,0:T(8,128)(2,1)S(1)}, bf16[128,256]{1,0:T(8,128)(2,1)S(1)}, u32[]{:S(2)}, u32[]{:S(2)}) collective-permute-start(bf16[128,256]{1,0:T(8,128)(2,1)S(1)} %slice.14), channel_id=1, source_target_pairs={{0,64},{1,193},{2,66},{3,195},{4,68},{5,197},{6,70},{7,199},{8,72}... | collective-permute-start | bytes 196616 | tf_op jit(solution)/shard_map/z_four/ppermute | solution.py:174
  111.3 4.7 %collective-permute-start.28 = (bf16[384,256]{1,0:T(8,128)(2,1)S(1)}, bf16[384,256]{1,0:T(8,128)(2,1)S(1)}, u32[]{:S(2)}, u32[]{:S(2)}) collective-permute-start(bf16[384,256]{1,0:T(8,128)(2,1)S(1)} %constant_dynamic-update-slice_fusion.2.refs_3_), channel_id=1, source_target_pairs={{0,16},{16,0},{32,48},{48,32},{64,80},{80,64},{96,112},{112,96},{1... | collective-permute-start | bytes 589832 | tf_op jit(solution)/shard_map/x_far/ppermute | solution.py:178
  116.6 6.0 %collective-permute-start.29 = (bf16[1024,256]{1,0:T(8,128)(2,1)S(1)}, bf16[1024,256]{1,0:T(8,128)(2,1)S(1)}, u32[]{:S(2)}, u32[]{:S(2)}) collective-permute-start(bf16[1024,256]{1,0:T(8,128)(2,1)S(1)} %tail_multiply.11), channel_id=1, source_target_pairs={{0,1},{1,0},{2,3},{3,2},{4,5},{5,4},{6,7},{7,6},{8,9},{9,8},{10,11... | collective-permute-start | bytes 1572872 | tf_op jit(solution)/shard_map/ppermute | solution.py:228
  121.6 14.0 %copy-start.1 = (f32[128,256]{1,0:T(8,128)S(1)}, f32[128,256]{1,0:T(8,128)}, u32[]{:S(2)}) copy-start(f32[128,256]{1,0:T(8,128)} %param.5) | copy-start | bytes 393220

commit v9 on v8

--- a/solution.py
+++ b/solution.py
@@ -194,7 +194,7 @@
         last, dense = lax.optimization_barrier((four, build(sibling)))
         over_four = over(last, "x_four")
         return [own, one, two, three, four, over_one, over_two], [over_three, over_four], dense
-    one, over_own = lax.optimization_barrier((one, over(own, "x_own")))
+    two, over_own = lax.optimization_barrier((two, over(own, "x_own")))
     over_near = over(jnp.concatenate([one, two]), "x_near")
     with jax.named_scope("z_three"):
         three = onward(two, 1)

time: 137 us -> 137 us (level)
  starting transfers between devices: 49.1 us -> 51.3 us
  waiting for transfers between devices: 24.8 us -> 22.8 us
    ppermute x12, waiting for transfers between devices: 16.4 us -> 8.23 us  [onward(): return lax.ppermute(piece, ('row', 'col'), pairs)]
    ppermute x10, waiting for transfers between devices: 2.92 us -> 9.1 us  [over(): return lax.ppermute(piece, 'row', flip_x)]
    ppermute x12, starting transfers between devices: 17.7 us -> 19.1 us  [onward(): return lax.ppermute(piece, ('row', 'col'), pairs)]
  transfers between devices with their start and end apart: 30 -> 30, of which waited for: 18 -> 17; matrix products, arithmetic and copies ran while one was open for 1% -> 1% of each run, Pallas kernels for 10% -> 9%
where the time goes in v9:
time: 137 us; the launch traced here: 136 us
  starting transfers between devices  51.3 us (37%)
  blocking collectives  42.1 us (31%)
  waiting for transfers between devices  22.8 us (17%)
  Pallas kernels  14.6 us (11%)
  other arithmetic  3.07 us (2%)
  local copies, waits for them, and re-layouts  1.64 us (1%)
    all_to_all x3, blocking collectives, per_device(): lax.all_to_all(pair.reshape(n_col // 2, per_dev, width), 'col', split_axi...  42.1 us
    ppermute x12, starting transfers between devices, onward(): return lax.ppermute(piece, ('row', 'col'), pairs)  19.1 us
    ppermute x3, starting transfers between devices, per_device(): arrived = lax.ppermute(theirs, 'col', flip_core)  13.5 us
    ppermute x10, waiting for transfers between devices, over(): return lax.ppermute(piece, 'row', flip_x)  9.1 us
    ppermute x3, starting transfers between devices, gather_pieces(): sibling = lax.ppermute(own, 'col', flip_core)  8.3 us
    ppermute x12, waiting for transfers between devices, onward(): return lax.ppermute(piece, ('row', 'col'), pairs)  8.23 us
    ppermute x10, starting transfers between devices, over(): return lax.ppermute(piece, 'row', flip_x)  7.99 us
    pallas_call x3, Pallas kernels, head_multiply(): pl.pallas_call(kernel, out_shape=jax.ShapeDtypeStruct((n_rows, width), jn...  7.92 us
  transfers between devices with their start and end apart: 30, of which 17 were waited for; matrix products, arithmetic and copies ran while one was open for 1% of the time, Pallas kernels for 9%

profile of v9, /device:TPU:1, one launch (start us, length us, event | category | flops | bytes accessed | tf_op | source)
XLA Modules:
  0.0 136.5 jit_solution(6659703883156702069)
XLA Ops:
  0.0 0.9 convert_element_type.36.refs_0_
  0.9 3.3 %collective-permute-start = (bf16[128,256]{1,0:T(8,128)(2,1)S(1)}, bf16[128,256]{1,0:T(8,128)(2,1)S(1)}, u32[]{:S(2)}, u32[]{:S(2)}) collective-permute-start(bf16[128,256]{1,0:T(8,128)(2,1)S(1)} %convert_element_type.36.refs_0_), channel_id=1, source_target_pairs={{0,1},{1,0},{2,3},{3,2},{4,5},{5,4},{6,7},{7,6},{8,9},{9,8},{10,11... | collective-permute-start | bytes 196616 | tf_op jit(solution)/shard_map/ppermute | solution.py:180
  4.2 0.9 collective-permute-done
  5.5 3.9 %collective-permute-start.5 = (bf16[256,256]{1,0:T(8,128)(2,1)S(1)}, bf16[256,256]{1,0:T(8,128)(2,1)S(1)}, u32[]{:S(2)}, u32[]{:S(2)}) collective-permute-start(bf16[256,256]{1,0:T(8,128)(2,1)S(1)} %pad_maximum_fusion.3), channel_id=1, source_target_pairs={{0,32},{1,225},{2,34},{3,227},{4,36},{5,229},{6,38},{7,231},{8,40}... | collective-permute-start | bytes 393224 | tf_op jit(solution)/shard_map/z_one/ppermute | solution.py:174
  9.4 1.2 collective-permute-start.6
  11.8 1.3 collective-permute-start.7
  13.1 1.4 %collective-permute-done.6.refs_2_ = bf16[256,256]{1,0:T(8,128)(2,1)S(1)} collective-permute-done((bf16[256,256]{1,0:T(8,128)(2,1)S(1)}, bf16[256,256]{1,0:T(8,128)(2,1)S(1)}, u32[]{:S(2)}, u32[]{:S(2)}) %collective-permute-start.6) | collective-permute-done | bytes 131104 | tf_op jit(solution)/shard_map/z_two/ppermute | solution.py:174
  14.5 1.2 collective-permute-start.8
  15.7 0.7 pad_add_fusion.refs_0_
  16.4 2.1 %collective-permute-start.3 = (s32[129]{0:T(256)S(1)}, s32[129]{0:T(256)S(1)}, u32[]{:S(2)}, u32[]{:S(2)}) collective-permute-start(s32[129]{0:T(256)S(1)} %pad_add_fusion.refs_0_), channel_id=1, source_target_pairs={{0,1},{1,0},{2,3},{3,2},{4,5},{5,4},{6,7},{7,6},{8,9},{9,8},{10,11... | collective-permute-start | bytes 1556 | tf_op jit(solution)/shard_map/ppermute | solution.py:216
  18.5 3.2 %collective-permute-start.2 = (bf16[128,256]{1,0:T(8,128)(2,1)S(1)}, bf16[128,256]{1,0:T(8,128)(2,1)S(1)}, u32[]{:S(2)}, u32[]{:S(2)}) collective-permute-start(bf16[128,256]{1,0:T(8,128)(2,1)S(1)} %slice.12), channel_id=1, source_target_pairs={{0,32},{1,225},{2,34},{3,227},{4,36},{5,229},{6,38},{7,231},{8,40}... | collective-permute-start | bytes 196616 | tf_op jit(solution)/shard_map/z_four/ppermute | solution.py:174
  21.8 1.2 collective-permute-start.9
  23.0 1.6 %copy-done = bf16[1,1,64,128,128]{4,3,2,1,0:T(8,128)(2,1)S(1)} copy-done((bf16[1,1,64,128,128]{4,3,2,1,0:T(8,128)(2,1)S(1)}, bf16[1,1,64,128,128]{4,3,2,1,0:T(8,128)(2,1)}, u32[]{:S(2)}) %copy-start) | copy-done | bytes 2097176
  24.6 3.1 %build_dense.1.dense_ref = bf16[2048,2048]{1,0:T(8,128)(2,1)S(1)} custom-call(s32[129]{0:T(256)S(1)} %pad_add_fusion.refs_0_, s32[129]{0:T(256)S(1)} %collective-permute-done.3.refs_1_, s32[2]{0:T(128)S(1)} %pad_add_fusion.1.refs_2_, bf16[64,128,128]{2,1,0:T(8,128)(2,1)S(1)} %bitcast.11, bf16[64,128,128]{2,1,0:T(8,128)(2,1)S(1)} %collective-permute-done.4.refs_4_), custom_call_target="tpu_custom_call" | custom-call | flops 4194304 | bytes 25165824 | tf_op jit(solution)/shard_map/build_dense/pallas_call | solution.py:66
  27.9 2.6 %head_multiply.3.head_ref = f32[2048,256]{1,0:T(8,128)S(1)} custom-call(bf16[2048,2048]{1,0:T(8,128)(2,1)S(1)} %build_dense.1.dense_ref, bf16[128,256]{1,0:T(8,128)(2,1)S(1)} %convert_element_type.36.refs_0_, bf16[256,256]{1,0:T(8,128)(2,1)S(1)} %collective-permute-done.5.refs_1_, bf16[256,256]{1,0:T(8,128)(2,1)S(1)} %collective-permute-done.6.refs_2_, ...), custom_call_target="tpu_custom_call" | custom-call | flops 1744830464 | bytes 6815744 | tf_op jit(solution)/shard_map/head_multiply/pallas_call | solution.py:117
  30.9 0.6 tail_multiply.7
  31.6 3.1 %collective-permute-start.11 = (bf16[1024,256]{1,0:T(8,128)(2,1)S(1)}, bf16[1024,256]{1,0:T(8,128)(2,1)S(1)}, u32[]{:S(2)}, u32[]{:S(2)}) collective-permute-start(bf16[1024,256]{1,0:T(8,128)(2,1)S(1)} %tail_multiply.7), channel_id=1, source_target_pairs={{0,1},{1,0},{2,3},{3,2},{4,5},{5,4},{6,7},{7,6},{8,9},{9,8},{10,11... | collective-permute-start | bytes 1572872 | tf_op jit(solution)/shard_map/ppermute | solution.py:228
  35.3 0.9 collective-permute-done.11
  36.3 16.5 %all_to_all.15 = bf16[8,128,256]{2,1,0:T(8,128)(2,1)S(1)} all-to-all(bf16[8,128,256]{2,1,0:T(8,128)(2,1)S(1)} %bitcast.12), channel_id=1, replica_groups={{0,2,4,6,8,10,12,14},{1,3,5,7,9,11,13,15},{16,18,20,22,24,26,28,30},{17..., dimensions={0} | all-to-all | bytes 1048576 | tf_op jit(solution)/shard_map/all_to_all | solution.py:231
  52.9 2.6 %collective-permute-start.12 = (bf16[128,256]{1,0:T(8,128)(2,1)S(1)}, bf16[128,256]{1,0:T(8,128)(2,1)S(1)}, u32[]{:S(2)}, u32[]{:S(2)}) collective-permute-start(bf16[128,256]{1,0:T(8,128)(2,1)S(1)} %convert_element_type.40.refs_0_), channel_id=1, source_target_pairs={{0,1},{1,0},{2,3},{3,2},{4,5},{5,4},{6,7},{7,6},{8,9},{9,8},{10,11... | collective-permute-start | bytes 196616 | tf_op jit(solution)/shard_map/ppermute | solution.py:180
  55.4 0.9 collective-permute-done.12
  56.5 2.0 %collective-permute-start.13 = (bf16[256,256]{1,0:T(8,128)(2,1)S(1)}, bf16[256,256]{1,0:T(8,128)(2,1)S(1)}, u32[]{:S(2)}, u32[]{:S(2)}) collective-permute-start(bf16[256,256]{1,0:T(8,128)(2,1)S(1)} %pad_maximum_fusion.4), channel_id=1, source_target_pairs={{0,32},{1,225},{2,34},{3,227},{4,36},{5,229},{6,38},{7,231},{8,40}... | collective-permute-start | bytes 393224 | tf_op jit(solution)/shard_map/z_one/ppermute | solution.py:174
  58.4 3.1 %collective-permute-done.15.refs_4_ = bf16[128,256]{1,0:T(8,128)(2,1)S(1)} collective-permute-done((bf16[128,256]{1,0:T(8,128)(2,1)S(1)}, bf16[128,256]{1,0:T(8,128)(2,1)S(1)}, u32[]{:S(2)}, u32[]{:S(2)}) %collective-permute-start.15) | collective-permute-done | bytes 65568 | tf_op jit(solution)/shard_map/x_own/ppermute | solution.py:178
  61.6 3.2 %collective-permute-start.16 = (bf16[256,256]{1,0:T(8,128)(2,1)S(1)}, bf16[256,256]{1,0:T(8,128)(2,1)S(1)}, u32[]{:S(2)}, u32[]{:S(2)}) collective-permute-start(bf16[256,256]{1,0:T(8,128)(2,1)S(1)} %collective-permute-done.14.refs_2_), channel_id=1, source_target_pairs={{0,32},{1,225},{2,34},{3,227},{4,36},{5,229},{6,38},{7,231},{8,40}... | collective-permute-start | bytes 393224 | tf_op jit(solution)/shard_map/z_three/ppermute | solution.py:174
  65.3 1.4 %collective-permute-done.16 = bf16[256,256]{1,0:T(8,128)(2,1)S(1)} collective-permute-done((bf16[256,256]{1,0:T(8,128)(2,1)S(1)}, bf16[256,256]{1,0:T(8,128)(2,1)S(1)}, u32[]{:S(2)}, u32[]{:S(2)}) %collective-permute-start.16) | collective-permute-done | bytes 131104 | tf_op jit(solution)/shard_map/z_three/ppermute | solution.py:174
  66.7 3.1 %collective-permute-done.17 = bf16[128,256]{1,0:T(8,128)(2,1)S(1)} collective-permute-done((bf16[128,256]{1,0:T(8,128)(2,1)S(1)}, bf16[128,256]{1,0:T(8,128)(2,1)S(1)}, u32[]{:S(2)}, u32[]{:S(2)}) %collective-permute-start.17) | collective-permute-done | bytes 65568 | tf_op jit(solution)/shard_map/z_four/ppermute | solution.py:174
  69.8 0.8 collective-permute-start.19
  70.6 2.6 %head_multiply.4.head_ref = f32[2048,256]{1,0:T(8,128)S(1)} custom-call(bf16[2048,2048]{1,0:T(8,128)(2,1)S(1)} %build_dense.1.dense_ref, bf16[128,256]{1,0:T(8,128)(2,1)S(1)} %convert_element_type.40.refs_0_, bf16[256,256]{1,0:T(8,128)(2,1)S(1)} %collective-permute-done.13.refs_1_, bf16[256,256]{1,0:T(8,128)(2,1)S(1)} %collective-permute-done.14.refs_2_, ...), custom_call_target="tpu_custom_call" | custom-call | flops 1744830464 | bytes 6815744 | tf_op jit(solution)/shard_map/head_multiply/pallas_call | solution.py:117
  73.3 1.7 %collective-permute-done.19.refs_0_ = bf16[384,256]{1,0:T(8,128)(2,1)S(1)} collective-permute-done((bf16[384,256]{1,0:T(8,128)(2,1)S(1)}, bf16[384,256]{1,0:T(8,128)(2,1)S(1)}, u32[]{:S(2)}, u32[]{:S(2)}) %collective-permute-start.19) | collective-permute-done | bytes 196640 | tf_op jit(solution)/shard_map/x_far/ppermute | solution.py:178
  75.6 4.8 %collective-permute-start.20 = (bf16[1024,256]{1,0:T(8,128)(2,1)S(1)}, bf16[1024,256]{1,0:T(8,128)(2,1)S(1)}, u32[]{:S(2)}, u32[]{:S(2)}) collective-permute-start(bf16[1024,256]{1,0:T(8,128)(2,1)S(1)} %tail_multiply.9), channel_id=1, source_target_pairs={{0,1},{1,0},{2,3},{3,2},{4,5},{5,4},{6,7},{7,6},{8,9},{9,8},{10,11... | collective-permute-start | bytes 1572872 | tf_op jit(solution)/shard_map/ppermute | solution.py:228
  80.4 0.6 tail_multiply.8
  81.0 0.9 collective-permute-done.20
  82.0 12.6 %all_to_all.16 = bf16[8,128,256]{2,1,0:T(8,128)(2,1)S(1)} all-to-all(bf16[8,128,256]{2,1,0:T(8,128)(2,1)S(1)} %bitcast.13), channel_id=1, replica_groups={{0,2,4,6,8,10,12,14},{1,3,5,7,9,11,13,15},{16,18,20,22,24,26,28,30},{17..., dimensions={0} | all-to-all | bytes 1048576 | tf_op jit(solution)/shard_map/all_to_all | solution.py:231
  94.7 2.4 %collective-permute-start.21 = (bf16[128,256]{1,0:T(8,128)(2,1)S(1)}, bf16[128,256]{1,0:T(8,128)(2,1)S(1)}, u32[]{:S(2)}, u32[]{:S(2)}) collective-permute-start(bf16[128,256]{1,0:T(8,128)(2,1)S(1)} %convert_element_type.44.refs_0_), channel_id=1, source_target_pairs={{0,1},{1,0},{2,3},{3,2},{4,5},{5,4},{6,7},{7,6},{8,9},{9,8},{10,11... | collective-permute-start | bytes 196616 | tf_op jit(solution)/shard_map/ppermute | solution.py:180
  97.1 0.9 collective-permute-done.21
  98.1 2.0 %collective-permute-start.22 = (bf16[256,256]{1,0:T(8,128)(2,1)S(1)}, bf16[256,256]{1,0:T(8,128)(2,1)S(1)}, u32[]{:S(2)}, u32[]{:S(2)}) collective-permute-start(bf16[256,256]{1,0:T(8,128)(2,1)S(1)} %pad_maximum_fusion.5), channel_id=1, source_target_pairs={{0,32},{1,225},{2,34},{3,227},{4,36},{5,229},{6,38},{7,231},{8,40}... | collective-permute-start | bytes 393224 | tf_op jit(solution)/shard_map/z_one/ppermute | solution.py:174
  100.1 1.5 %collective-permute-start.24 = (bf16[128,256]{1,0:T(8,128)(2,1)S(1)}, bf16[128,256]{1,0:T(8,128)(2,1)S(1)}, u32[]{:S(2)}, u32[]{:S(2)}) collective-permute-start(bf16[128,256]{1,0:T(8,128)(2,1)S(1)} %convert_element_type.44.refs_0_), channel_id=1, source_target_pairs={{0,16},{16,0},{32,48},{48,32},{64,80},{80,64},{96,112},{112,96},{1... | collective-permute-start | bytes 196616 | tf_op jit(solution)/shard_map/x_own/ppermute | solution.py:178
  101.6 2.0 %collective-permute-done.24.refs_4_ = bf16[128,256]{1,0:T(8,128)(2,1)S(1)} collective-permute-done((bf16[128,256]{1,0:T(8,128)(2,1)S(1)}, bf16[128,256]{1,0:T(8,128)(2,1)S(1)}, u32[]{:S(2)}, u32[]{:S(2)}) %collective-permute-start.24) | collective-permute-done | bytes 65568 | tf_op jit(solution)/shard_map/x_own/ppermute | solution.py:178
  104.4 1.7 %collective-permute-start.27 = (bf16[512,256]{1,0:T(8,128)(2,1)S(1)}, bf16[512,256]{1,0:T(8,128)(2,1)S(1)}, u32[]{:S(2)}, u32[]{:S(2)}) collective-permute-start(bf16[512,256]{1,0:T(8,128)(2,1)S(1)} %pad_maximum_fusion.1), channel_id=1, source_target_pairs={{0,16},{16,0},{32,48},{48,32},{64,80},{80,64},{96,112},{112,96},{1... | collective-permute-start | bytes 786440 | tf_op jit(solution)/shard_map/x_near/ppermute | solution.py:178
  106.1 2.2 %collective-permute-start.26 = (bf16[128,256]{1,0:T(8,128)(2,1)S(1)}, bf16[128,256]{1,0:T(8,128)(2,1)S(1)}, u32[]{:S(2)}, u32[]{:S(2)}) collective-permute-start(bf16[128,256]{1,0:T(8,128)(2,1)S(1)} %slice.11), channel_id=1, source_target_pairs={{0,64},{1,193},{2,66},{3,195},{4,68},{5,197},{6,70},{7,199},{8,72}... | collective-permute-start | bytes 196616 | tf_op jit(solution)/shard_map/z_four/ppermute | solution.py:174
  108.4 1.8 %collective-permute-done.26 = bf16[128,256]{1,0:T(8,128)(2,1)S(1)} collective-permute-done((bf16[128,256]{1,0:T(8,128)(2,1)S(1)}, bf16[128,256]{1,0:T(8,128)(2,1)S(1)}, u32[]{:S(2)}, u32[]{:S(2)}) %collective-permute-start.26) | collective-permute-done | bytes 65568 | tf_op jit(solution)/shard_map/z_four/ppermute | solution.py:174
  110.3 2.6 %head_multiply.5.head_ref = f32[2048,256]{1,0:T(8,128)S(1)} custom-call(bf16[2048,2048]{1,0:T(8,128)(2,1)S(1)} %build_dense.1.dense_ref, bf16[128,256]{1,0:T(8,128)(2,1)S(1)} %convert_element_type.44.refs_0_, bf16[256,256]{1,0:T(8,128)(2,1)S(1)} %collective-permute-done.22.refs_1_, bf16[256,256]{1,0:T(8,128)(2,1)S(1)} %collective-permute-done.23.refs_2_, ...), custom_call_target="tpu_custom_call" | custom-call | flops 1744830464 | bytes 6815744 | tf_op jit(solution)/shard_map/head_multiply/pallas_call | solution.py:117
  112.9 1.9 %collective-permute-done.28.refs_0_ = bf16[384,256]{1,0:T(8,128)(2,1)S(1)} collective-permute-done((bf16[384,256]{1,0:T(8,128)(2,1)S(1)}, bf16[384,256]{1,0:T(8,128)(2,1)S(1)}, u32[]{:S(2)}, u32[]{:S(2)}) %collective-permute-start.28) | collective-permute-done | bytes 196640 | tf_op jit(solution)/shard_map/x_far/ppermute | solution.py:178
  114.8 0.6 tail_multiply.11
  115.4 5.6 %collective-permute-start.29 = (bf16[1024,256]{1,0:T(8,128)(2,1)S(1)}, bf16[1024,256]{1,0:T(8,128)(2,1)S(1)}, u32[]{:S(2)}, u32[]{:S(2)}) collective-permute-start(bf16[1024,256]{1,0:T(8,128)(2,1)S(1)} %tail_multiply.11), channel_id=1, source_target_pairs={{0,1},{1,0},{2,3},{3,2},{4,5},{5,4},{6,7},{7,6},{8,9},{9,8},{10,11... | collective-permute-start | bytes 1572872 | tf_op jit(solution)/shard_map/ppermute | solution.py:228
  121.6 0.9 collective-permute-done.29
  122.7 13.0 %all_to_all.17 = bf16[8,128,256]{2,1,0:T(8,128)(2,1)S(1)} all-to-all(bf16[8,128,256]{2,1,0:T(8,128)(2,1)S(1)} %bitcast.14), channel_id=1, replica_groups={{0,2,4,6,8,10,12,14},{1,3,5,7,9,11,13,15},{16,18,20,22,24,26,28,30},{17..., dimensions={0} | all-to-all | bytes 1048576 | tf_op jit(solution)/shard_map/all_to_all | solution.py:231
  135.8 0.7 add_multiply_fusion
  (54 shorter events, 5.6 us)
Async XLA Ops:
  0.9 4.2 %collective-permute-start = (bf16[128,256]{1,0:T(8,128)(2,1)S(1)}, bf16[128,256]{1,0:T(8,128)(2,1)S(1)}, u32[]{:S(2)}, u32[]{:S(2)}) collective-permute-start(bf16[128,256]{1,0:T(8,128)(2,1)S(1)} %convert_element_type.36.refs_0_), channel_id=1, source_target_pairs={{0,1},{1,0},{2,3},{3,2},{4,5},{5,4},{6,7},{7,6},{8,9},{9,8},{10,11... | collective-permute-start | bytes 196616 | tf_op jit(solution)/shard_map/ppermute | solution.py:180
  5.1 17.9 %collective-permute-start.4 = (bf16[64,128,128]{2,1,0:T(8,128)(2,1)}, bf16[64,128,128]{2,1,0:T(8,128)(2,1)S(1)}, u32[]{:S(2)}, u32[]{:S(2)}) collective-permute-start(bf16[64,128,128]{2,1,0:T(8,128)(2,1)} %bitcast.10), channel_id=1, source_target_pairs={{0,1},{1,0},{2,3},{3,2},{4,5},{5,4},{6,7},{7,6},{8,9},{9,8},{10,11... | collective-permute-start | bytes 6291464 | tf_op jit(solution)/shard_map/ppermute | solution.py:220
  5.5 6.3 %collective-permute-start.5 = (bf16[256,256]{1,0:T(8,128)(2,1)S(1)}, bf16[256,256]{1,0:T(8,128)(2,1)S(1)}, u32[]{:S(2)}, u32[]{:S(2)}) collective-permute-start(bf16[256,256]{1,0:T(8,128)(2,1)S(1)} %pad_maximum_fusion.3), channel_id=1, source_target_pairs={{0,32},{1,225},{2,34},{3,227},{4,36},{5,229},{6,38},{7,231},{8,40}... | collective-permute-start | bytes 393224 | tf_op jit(solution)/shard_map/z_one/ppermute | solution.py:174
  9.4 5.1 %collective-permute-start.6 = (bf16[256,256]{1,0:T(8,128)(2,1)S(1)}, bf16[256,256]{1,0:T(8,128)(2,1)S(1)}, u32[]{:S(2)}, u32[]{:S(2)}) collective-permute-start(bf16[256,256]{1,0:T(8,128)(2,1)S(1)} %pad_maximum_fusion.3), channel_id=1, source_target_pairs={{0,64},{1,193},{2,66},{3,195},{4,68},{5,197},{6,70},{7,199},{8,72}... | collective-permute-start | bytes 393224 | tf_op jit(solution)/shard_map/z_two/ppermute | solution.py:174
  11.2 7.3 %collective-permute-start.1 = (bf16[256,256]{1,0:T(8,128)(2,1)S(1)}, bf16[256,256]{1,0:T(8,128)(2,1)S(1)}, u32[]{:S(2)}, u32[]{:S(2)}) collective-permute-start(bf16[256,256]{1,0:T(8,128)(2,1)S(1)} %pad_maximum_fusion.3), channel_id=1, source_target_pairs={{0,96},{1,161},{2,98},{3,163},{4,100},{5,165},{6,102},{7,167},{8,1... | collective-permute-start | bytes 393224 | tf_op jit(solution)/shard_map/z_three/ppermute | solution.py:174
  11.8 16.1 %collective-permute-start.7 = (bf16[384,256]{1,0:T(8,128)(2,1)S(1)}, bf16[384,256]{1,0:T(8,128)(2,1)S(1)}, u32[]{:S(2)}, u32[]{:S(2)}) collective-permute-start(bf16[384,256]{1,0:T(8,128)(2,1)S(1)} %pad_maximum_fusion.2), channel_id=1, source_target_pairs={{0,16},{16,0},{32,48},{48,32},{64,80},{80,64},{96,112},{112,96},{1... | collective-permute-start | bytes 589832 | tf_op jit(solution)/shard_map/x_one/ppermute | solution.py:178
  14.5 13.4 %collective-permute-start.8 = (bf16[256,256]{1,0:T(8,128)(2,1)S(1)}, bf16[256,256]{1,0:T(8,128)(2,1)S(1)}, u32[]{:S(2)}, u32[]{:S(2)}) collective-permute-start(bf16[256,256]{1,0:T(8,128)(2,1)S(1)} %collective-permute-done.6.refs_2_), channel_id=1, source_target_pairs={{0,16},{16,0},{32,48},{48,32},{64,80},{80,64},{96,112},{112,96},{1... | collective-permute-start | bytes 393224 | tf_op jit(solution)/shard_map/x_two/ppermute | solution.py:178
  16.4 5.3 %collective-permute-start.3 = (s32[129]{0:T(256)S(1)}, s32[129]{0:T(256)S(1)}, u32[]{:S(2)}, u32[]{:S(2)}) collective-permute-start(s32[129]{0:T(256)S(1)} %pad_add_fusion.refs_0_), channel_id=1, source_target_pairs={{0,1},{1,0},{2,3},{3,2},{4,5},{5,4},{6,7},{7,6},{8,9},{9,8},{10,11... | collective-permute-start | bytes 1556 | tf_op jit(solution)/shard_map/ppermute | solution.py:216
  18.5 9.2 %collective-permute-start.2 = (bf16[128,256]{1,0:T(8,128)(2,1)S(1)}, bf16[128,256]{1,0:T(8,128)(2,1)S(1)}, u32[]{:S(2)}, u32[]{:S(2)}) collective-permute-start(bf16[128,256]{1,0:T(8,128)(2,1)S(1)} %slice.12), channel_id=1, source_target_pairs={{0,32},{1,225},{2,34},{3,227},{4,36},{5,229},{6,38},{7,231},{8,40}... | collective-permute-start | bytes 196616 | tf_op jit(solution)/shard_map/z_four/ppermute | solution.py:174
  21.8 8.7 %collective-permute-start.9 = (bf16[256,256]{1,0:T(8,128)(2,1)S(1)}, bf16[256,256]{1,0:T(8,128)(2,1)S(1)}, u32[]{:S(2)}, u32[]{:S(2)}) collective-permute-start(bf16[256,256]{1,0:T(8,128)(2,1)S(1)} %collective-permute-done.1.refs_3_), channel_id=1, source_target_pairs={{0,16},{16,0},{32,48},{48,32},{64,80},{80,64},{96,112},{112,96},{1... | collective-permute-start | bytes 393224 | tf_op jit(solution)/shard_map/x_three/ppermute | solution.py:178
  23.0 1.6 %copy-start = (bf16[1,1,64,128,128]{4,3,2,1,0:T(8,128)(2,1)S(1)}, bf16[1,1,64,128,128]{4,3,2,1,0:T(8,128)(2,1)}, u32[]{:S(2)}) copy-start(bf16[1,1,64,128,128]{4,3,2,1,0:T(8,128)(2,1)} %param.6) | copy-start | bytes 6291460
  27.7 3.2 %collective-permute-start.10 = (bf16[128,256]{1,0:T(8,128)(2,1)S(1)}, bf16[128,256]{1,0:T(8,128)(2,1)S(1)}, u32[]{:S(2)}, u32[]{:S(2)}) collective-permute-start(bf16[128,256]{1,0:T(8,128)(2,1)S(1)} %collective-permute-done.2.refs_4_), channel_id=1, source_target_pairs={{0,16},{16,0},{32,48},{48,32},{64,80},{80,64},{96,112},{112,96},{1... | collective-permute-start | bytes 196616 | tf_op jit(solution)/shard_map/x_four/ppermute | solution.py:178
  31.6 4.6 %collective-permute-start.11 = (bf16[1024,256]{1,0:T(8,128)(2,1)S(1)}, bf16[1024,256]{1,0:T(8,128)(2,1)S(1)}, u32[]{:S(2)}, u32[]{:S(2)}) collective-permute-start(bf16[1024,256]{1,0:T(8,128)(2,1)S(1)} %tail_multiply.7), channel_id=1, source_target_pairs={{0,1},{1,0},{2,3},{3,2},{4,5},{5,4},{6,7},{7,6},{8,9},{9,8},{10,11... | collective-permute-start | bytes 1572872 | tf_op jit(solution)/shard_map/ppermute | solution.py:228
  52.9 3.5 %collective-permute-start.12 = (bf16[128,256]{1,0:T(8,128)(2,1)S(1)}, bf16[128,256]{1,0:T(8,128)(2,1)S(1)}, u32[]{:S(2)}, u32[]{:S(2)}) collective-permute-start(bf16[128,256]{1,0:T(8,128)(2,1)S(1)} %convert_element_type.40.refs_0_), channel_id=1, source_target_pairs={{0,1},{1,0},{2,3},{3,2},{4,5},{5,4},{6,7},{7,6},{8,9},{9,8},{10,11... | collective-permute-start | bytes 196616 | tf_op jit(solution)/shard_map/ppermute | solution.py:180
  56.4 5.2 %collective-permute-start.14 = (bf16[256,256]{1,0:T(8,128)(2,1)S(1)}, bf16[256,256]{1,0:T(8,128)(2,1)S(1)}, u32[]{:S(2)}, u32[]{:S(2)}) collective-permute-start(bf16[256,256]{1,0:T(8,128)(2,1)S(1)} %pad_maximum_fusion.4), channel_id=1, source_target_pairs={{0,64},{1,193},{2,66},{3,195},{4,68},{5,197},{6,70},{7,199},{8,72}... | collective-permute-start | bytes 393224 | tf_op jit(solution)/shard_map/z_two/ppermute | solution.py:174
  56.5 8.3 %collective-permute-start.13 = (bf16[256,256]{1,0:T(8,128)(2,1)S(1)}, bf16[256,256]{1,0:T(8,128)(2,1)S(1)}, u32[]{:S(2)}, u32[]{:S(2)}) collective-permute-start(bf16[256,256]{1,0:T(8,128)(2,1)S(1)} %pad_maximum_fusion.4), channel_id=1, source_target_pairs={{0,32},{1,225},{2,34},{3,227},{4,36},{5,229},{6,38},{7,231},{8,40}... | collective-permute-start | bytes 393224 | tf_op jit(solution)/shard_map/z_one/ppermute | solution.py:174
  58.4 3.1 %collective-permute-start.15 = (bf16[128,256]{1,0:T(8,128)(2,1)S(1)}, bf16[128,256]{1,0:T(8,128)(2,1)S(1)}, u32[]{:S(2)}, u32[]{:S(2)}) collective-permute-start(bf16[128,256]{1,0:T(8,128)(2,1)S(1)} %convert_element_type.40.refs_0_), channel_id=1, source_target_pairs={{0,16},{16,0},{32,48},{48,32},{64,80},{80,64},{96,112},{112,96},{1... | collective-permute-start | bytes 196616 | tf_op jit(solution)/shard_map/x_own/ppermute | solution.py:178
  61.6 5.1 %collective-permute-start.16 = (bf16[256,256]{1,0:T(8,128)(2,1)S(1)}, bf16[256,256]{1,0:T(8,128)(2,1)S(1)}, u32[]{:S(2)}, u32[]{:S(2)}) collective-permute-start(bf16[256,256]{1,0:T(8,128)(2,1)S(1)} %collective-permute-done.14.refs_2_), channel_id=1, source_target_pairs={{0,32},{1,225},{2,34},{3,227},{4,36},{5,229},{6,38},{7,231},{8,40}... | collective-permute-start | bytes 393224 | tf_op jit(solution)/shard_map/z_three/ppermute | solution.py:174
  64.7 5.9 %collective-permute-start.18 = (bf16[512,256]{1,0:T(8,128)(2,1)S(1)}, bf16[512,256]{1,0:T(8,128)(2,1)S(1)}, u32[]{:S(2)}, u32[]{:S(2)}) collective-permute-start(bf16[512,256]{1,0:T(8,128)(2,1)S(1)} %pad_maximum_fusion), channel_id=1, source_target_pairs={{0,16},{16,0},{32,48},{48,32},{64,80},{80,64},{96,112},{112,96},{1... | collective-permute-start | bytes 786440 | tf_op jit(solution)/shard_map/x_near/ppermute | solution.py:178
  64.8 4.9 %collective-permute-start.17 = (bf16[128,256]{1,0:T(8,128)(2,1)S(1)}, bf16[128,256]{1,0:T(8,128)(2,1)S(1)}, u32[]{:S(2)}, u32[]{:S(2)}) collective-permute-start(bf16[128,256]{1,0:T(8,128)(2,1)S(1)} %slice.10), channel_id=1, source_target_pairs={{0,64},{1,193},{2,66},{3,195},{4,68},{5,197},{6,70},{7,199},{8,72}... | collective-permute-start | bytes 196616 | tf_op jit(solution)/shard_map/z_four/ppermute | solution.py:174
  69.8 5.2 %collective-permute-start.19 = (bf16[384,256]{1,0:T(8,128)(2,1)S(1)}, bf16[384,256]{1,0:T(8,128)(2,1)S(1)}, u32[]{:S(2)}, u32[]{:S(2)}) collective-permute-start(bf16[384,256]{1,0:T(8,128)(2,1)S(1)} %constant_dynamic-update-slice_fusion.refs_3_), channel_id=1, source_target_pairs={{0,16},{16,0},{32,48},{48,32},{64,80},{80,64},{96,112},{112,96},{1... | collective-permute-start | bytes 589832 | tf_op jit(solution)/shard_map/x_far/ppermute | solution.py:178
  75.6 6.4 %collective-permute-start.20 = (bf16[1024,256]{1,0:T(8,128)(2,1)S(1)}, bf16[1024,256]{1,0:T(8,128)(2,1)S(1)}, u32[]{:S(2)}, u32[]{:S(2)}) collective-permute-start(bf16[1024,256]{1,0:T(8,128)(2,1)S(1)} %tail_multiply.9), channel_id=1, source_target_pairs={{0,1},{1,0},{2,3},{3,2},{4,5},{5,4},{6,7},{7,6},{8,9},{9,8},{10,11... | collective-permute-start | bytes 1572872 | tf_op jit(solution)/shard_map/ppermute | solution.py:228
  94.7 3.3 %collective-permute-start.21 = (bf16[128,256]{1,0:T(8,128)(2,1)S(1)}, bf16[128,256]{1,0:T(8,128)(2,1)S(1)}, u32[]{:S(2)}, u32[]{:S(2)}) collective-permute-start(bf16[128,256]{1,0:T(8,128)(2,1)S(1)} %convert_element_type.44.refs_0_), channel_id=1, source_target_pairs={{0,1},{1,0},{2,3},{3,2},{4,5},{5,4},{6,7},{7,6},{8,9},{9,8},{10,11... | collective-permute-start | bytes 196616 | tf_op jit(solution)/shard_map/ppermute | solution.py:180
  98.0 5.8 %collective-permute-start.23 = (bf16[256,256]{1,0:T(8,128)(2,1)S(1)}, bf16[256,256]{1,0:T(8,128)(2,1)S(1)}, u32[]{:S(2)}, u32[]{:S(2)}) collective-permute-start(bf16[256,256]{1,0:T(8,128)(2,1)S(1)} %pad_maximum_fusion.5), channel_id=1, source_target_pairs={{0,64},{1,193},{2,66},{3,195},{4,68},{5,197},{6,70},{7,199},{8,72}... | collective-permute-start | bytes 393224 | tf_op jit(solution)/shard_map/z_two/ppermute | solution.py:174
  98.1 6.3 %collective-permute-start.22 = (bf16[256,256]{1,0:T(8,128)(2,1)S(1)}, bf16[256,256]{1,0:T(8,128)(2,1)S(1)}, u32[]{:S(2)}, u32[]{:S(2)}) collective-permute-start(bf16[256,256]{1,0:T(8,128)(2,1)S(1)} %pad_maximum_fusion.5), channel_id=1, source_target_pairs={{0,32},{1,225},{2,34},{3,227},{4,36},{5,229},{6,38},{7,231},{8,40}... | collective-permute-start | bytes 393224 | tf_op jit(solution)/shard_map/z_one/ppermute | solution.py:174
  100.1 3.4 %collective-permute-start.24 = (bf16[128,256]{1,0:T(8,128)(2,1)S(1)}, bf16[128,256]{1,0:T(8,128)(2,1)S(1)}, u32[]{:S(2)}, u32[]{:S(2)}) collective-permute-start(bf16[128,256]{1,0:T(8,128)(2,1)S(1)} %convert_element_type.44.refs_0_), channel_id=1, source_target_pairs={{0,16},{16,0},{32,48},{48,32},{64,80},{80,64},{96,112},{112,96},{1... | collective-permute-start | bytes 196616 | tf_op jit(solution)/shard_map/x_own/ppermute | solution.py:178
  103.9 4.5 %collective-permute-start.25 = (bf16[256,256]{1,0:T(8,128)(2,1)S(1)}, bf16[256,256]{1,0:T(8,128)(2,1)S(1)}, u32[]{:S(2)}, u32[]{:S(2)}) collective-permute-start(bf16[256,256]{1,0:T(8,128)(2,1)S(1)} %collective-permute-done.23.refs_2_), channel_id=1, source_target_pairs={{0,32},{1,225},{2,34},{3,227},{4,36},{5,229},{6,38},{7,231},{8,40}... | collective-permute-start | bytes 393224 | tf_op jit(solution)/shard_map/z_three/ppermute | solution.py:174
  104.4 5.8 %collective-permute-start.27 = (bf16[512,256]{1,0:T(8,128)(2,1)S(1)}, bf16[512,256]{1,0:T(8,128)(2,1)S(1)}, u32[]{:S(2)}, u32[]{:S(2)}) collective-permute-start(bf16[512,256]{1,0:T(8,128)(2,1)S(1)} %pad_maximum_fusion.1), channel_id=1, source_target_pairs={{0,16},{16,0},{32,48},{48,32},{64,80},{80,64},{96,112},{112,96},{1... | collective-permute-start | bytes 786440 | tf_op jit(solution)/shard_map/x_near/ppermute | solution.py:178
  106.1 4.1 %collective-permute-start.26 = (bf16[128,256]{1,0:T(8,128)(2,1)S(1)}, bf16[128,256]{1,0:T(8,128)(2,1)S(1)}, u32[]{:S(2)}, u32[]{:S(2)}) collective-permute-start(bf16[128,256]{1,0:T(8,128)(2,1)S(1)} %slice.11), channel_id=1, source_target_pairs={{0,64},{1,193},{2,66},{3,195},{4,68},{5,197},{6,70},{7,199},{8,72}... | collective-permute-start | bytes 196616 | tf_op jit(solution)/shard_map/z_four/ppermute | solution.py:174
  110.2 4.6 %collective-permute-start.28 = (bf16[384,256]{1,0:T(8,128)(2,1)S(1)}, bf16[384,256]{1,0:T(8,128)(2,1)S(1)}, u32[]{:S(2)}, u32[]{:S(2)}) collective-permute-start(bf16[384,256]{1,0:T(8,128)(2,1)S(1)} %constant_dynamic-update-slice_fusion.2.refs_3_), channel_id=1, source_target_pairs={{0,16},{16,0},{32,48},{48,32},{64,80},{80,64},{96,112},{112,96},{1... | collective-permute-start | bytes 589832 | tf_op jit(solution)/shard_map/x_far/ppermute | solution.py:178
  115.4 7.2 %collective-permute-start.29 = (bf16[1024,256]{1,0:T(8,128)(2,1)S(1)}, bf16[1024,256]{1,0:T(8,128)(2,1)S(1)}, u32[]{:S(2)}, u32[]{:S(2)}) collective-permute-start(bf16[1024,256]{1,0:T(8,128)(2,1)S(1)} %tail_multiply.11), channel_id=1, source_target_pairs={{0,1},{1,0},{2,3},{3,2},{4,5},{5,4},{6,7},{7,6},{8,9},{9,8},{10,11... | collective-permute-start | bytes 1572872 | tf_op jit(solution)/shard_map/ppermute | solution.py:228
  121.6 14.1 %copy-start.1 = (f32[128,256]{1,0:T(8,128)S(1)}, f32[128,256]{1,0:T(8,128)}, u32[]{:S(2)}) copy-start(f32[128,256]{1,0:T(8,128)} %param.5) | copy-start | bytes 393220

commit v10 on v9

--- a/solution.py
+++ b/solution.py
@@ -183,25 +183,19 @@
         one = onward(both, 1)
     with jax.named_scope("z_two"):
         two = onward(both, 2)
+    dense = None
     if build is not None:
-        with jax.named_scope("z_three"):
-            three = onward(both, 3)
-        over_one = over(jnp.concatenate([own, one]), "x_one")
-        over_two = over(two, "x_two")
-        with jax.named_scope("z_four"):
-            four = onward(three[:rows], 1)
-        over_three = over(three, "x_three")
-        last, dense = lax.optimization_barrier((four, build(sibling)))
-        over_four = over(last, "x_four")
-        return [own, one, two, three, four, over_one, over_two], [over_three, over_four], dense
-    two, over_own = lax.optimization_barrier((two, over(own, "x_own")))
-    over_near = over(jnp.concatenate([one, two]), "x_near")
+        two, dense = lax.optimization_barrier((two, build(sibling)))
+        over_near = [over(jnp.concatenate([own, one, two]), "x_near")]
+    else:
+        two, over_own = lax.optimization_barrier((two, over(own, "x_own")))
+        over_near = [over_own, over(one, "x_one"), over(two, "x_two")]
     with jax.named_scope("z_three"):
         three = onward(two, 1)
     with jax.named_scope("z_four"):
         four = onward(two[:rows], 2)
     far = jnp.concatenate([three, four])
-    return [own, one, two, far, over_own, over_near], [over(far, "x_far")], None
+    return [own, one, two, far] + over_near, [over(far, "x_far")], dense
 
 
 def per_device(embedding, tiles, tile_rows, tile_cols, counts):

time: 137 us -> 136 us (level)
  starting transfers between devices: 51.3 us -> 43 us
  waiting for transfers between devices: 22.8 us -> 30.3 us
    ppermute x3, starting transfers between devices: 13.5 us -> 8.37 us  [per_device(): arrived = lax.ppermute(theirs, 'col', flip_core)]
    ppermute x12, waiting for transfers between devices: 8.23 us -> 12.5 us  [onward(): return lax.ppermute(piece, ('row', 'col'), pairs)]
    ppermute x12, starting transfers between devices: 19.1 us -> 16.4 us  [onward(): return lax.ppermute(piece, ('row', 'col'), pairs)]
    ppermute x10, waiting for transfers between devices: 9.1 us -> 11.2 us  [over(): return lax.ppermute(piece, 'row', flip_x)]
    ppermute x1, starting transfers between devices: 2.09 us -> 0.02 us  [per_device(): sib_at = lax.ppermute(own_at, 'col', flip_core)]
    ppermute x10, starting transfers between devices: 7.99 us -> 9.46 us  [over(): return lax.ppermute(piece, 'row', flip_x)]
  transfers between devices with their start and end apart: 30 -> 30, of which waited for: 17 -> 21; matrix products, arithmetic and copies ran while one was open for 1% -> 1% of each run, Pallas kernels for 9% -> 9%
where the time goes in v10:
time: 136 us; the launch traced here: 135 us
  starting transfers between devices  43 us (32%)
  blocking collectives  41.7 us (31%)
  waiting for transfers between devices  30.3 us (22%)
  Pallas kernels  14.5 us (11%)
  other arithmetic  3.04 us (2%)
  local copies, waits for them, and re-layouts  1.66 us (1%)
    all_to_all x3, blocking collectives, per_device(): lax.all_to_all(pair.reshape(n_col // 2, per_dev, width), 'col', split_axi...  41.7 us
    ppermute x12, starting transfers between devices, onward(): return lax.ppermute(piece, ('row', 'col'), pairs)  16.4 us
    ppermute x12, waiting for transfers between devices, onward(): return lax.ppermute(piece, ('row', 'col'), pairs)  12.5 us
    ppermute x10, waiting for transfers between devices, over(): return lax.ppermute(piece, 'row', flip_x)  11.2 us
    ppermute x10, starting transfers between devices, over(): return lax.ppermute(piece, 'row', flip_x)  9.46 us
    ppermute x3, starting transfers between devices, gather_pieces(): sibling = lax.ppermute(own, 'col', flip_core)  8.42 us
    ppermute x3, starting transfers between devices, per_device(): arrived = lax.ppermute(theirs, 'col', flip_core)  8.37 us
    pallas_call x3, Pallas kernels, head_multiply(): pl.pallas_call(kernel, out_shape=jax.ShapeDtypeStruct((n_rows, width), jn...  7.92 us
  transfers between devices with their start and end apart: 30, of which 21 were waited for; matrix products, arithmetic and copies ran while one was open for 1% of the time, Pallas kernels for 9%

profile of v10, /device:TPU:1, one launch (start us, length us, event | category | flops | bytes accessed | tf_op | source)
XLA Modules:
  0.0 135.2 jit_solution(15862659462628446466)
XLA Ops:
  0.0 0.9 convert_element_type.36.refs_0_
  0.9 3.3 %collective-permute-start = (bf16[128,256]{1,0:T(8,128)(2,1)S(1)}, bf16[128,256]{1,0:T(8,128)(2,1)S(1)}, u32[]{:S(2)}, u32[]{:S(2)}) collective-permute-start(bf16[128,256]{1,0:T(8,128)(2,1)S(1)} %convert_element_type.36.refs_0_), channel_id=1, source_target_pairs={{0,1},{1,0},{2,3},{3,2},{4,5},{5,4},{6,7},{7,6},{8,9},{9,8},{10,11... | collective-permute-start | bytes 196616 | tf_op jit(solution)/shard_map/ppermute | solution.py:180
  4.2 0.9 collective-permute-done
  6.2 3.9 %collective-permute-start.4 = (bf16[256,256]{1,0:T(8,128)(2,1)S(1)}, bf16[256,256]{1,0:T(8,128)(2,1)S(1)}, u32[]{:S(2)}, u32[]{:S(2)}) collective-permute-start(bf16[256,256]{1,0:T(8,128)(2,1)S(1)} %pad_maximum_fusion.1), channel_id=1, source_target_pairs={{0,32},{1,225},{2,34},{3,227},{4,36},{5,229},{6,38},{7,231},{8,40}... | collective-permute-start | bytes 393224 | tf_op jit(solution)/shard_map/z_one/ppermute | solution.py:174
  10.1 1.2 collective-permute-start.1
  12.1 1.0 collective-permute-done.2.refs_1_
  13.2 1.6 %copy-done = bf16[1,1,64,128,128]{4,3,2,1,0:T(8,128)(2,1)S(1)} copy-done((bf16[1,1,64,128,128]{4,3,2,1,0:T(8,128)(2,1)S(1)}, bf16[1,1,64,128,128]{4,3,2,1,0:T(8,128)(2,1)}, u32[]{:S(2)}) %copy-start) | copy-done | bytes 2097176
  14.7 3.0 %build_dense.1.dense_ref = bf16[2048,2048]{1,0:T(8,128)(2,1)S(1)} custom-call(s32[129]{0:T(256)S(1)} %pad_add_fusion.refs_0_, s32[129]{0:T(256)S(1)} %collective-permute-done.2.refs_1_, s32[2]{0:T(128)S(1)} %pad_add_fusion.1.refs_2_, bf16[64,128,128]{2,1,0:T(8,128)(2,1)S(1)} %bitcast.11, bf16[64,128,128]{2,1,0:T(8,128)(2,1)S(1)} %collective-permute-done.3.refs_4_), custom_call_target="tpu_custom_call" | custom-call | flops 4194304 | bytes 25165824 | tf_op jit(solution)/shard_map/build_dense/pallas_call | solution.py:66
  17.8 1.1 collective-permute-start.5
  19.0 1.9 %collective-permute-start.7 = (bf16[640,256]{1,0:T(8,128)(2,1)S(1)}, bf16[640,256]{1,0:T(8,128)(2,1)S(1)}, u32[]{:S(2)}, u32[]{:S(2)}) collective-permute-start(bf16[640,256]{1,0:T(8,128)(2,1)S(1)} %pad_maximum_fusion), channel_id=1, source_target_pairs={{0,16},{16,0},{32,48},{48,32},{64,80},{80,64},{96,112},{112,96},{1... | collective-permute-start | bytes 983048 | tf_op jit(solution)/shard_map/x_near/ppermute | solution.py:178
  20.9 1.0 collective-permute-start.6
  22.7 2.9 %collective-permute-done.6 = bf16[128,256]{1,0:T(8,128)(2,1)S(1)} collective-permute-done((bf16[128,256]{1,0:T(8,128)(2,1)S(1)}, bf16[128,256]{1,0:T(8,128)(2,1)S(1)}, u32[]{:S(2)}, u32[]{:S(2)}) %collective-permute-start.6) | collective-permute-done | bytes 65568 | tf_op jit(solution)/shard_map/z_four/ppermute | solution.py:174
  26.0 2.4 %collective-permute-done.7.refs_4_ = bf16[640,256]{1,0:T(8,128)(2,1)S(1)} collective-permute-done((bf16[640,256]{1,0:T(8,128)(2,1)S(1)}, bf16[640,256]{1,0:T(8,128)(2,1)S(1)}, u32[]{:S(2)}, u32[]{:S(2)}) %collective-permute-start.7) | collective-permute-done | bytes 327712 | tf_op jit(solution)/shard_map/x_near/ppermute | solution.py:178
  28.4 2.6 %head_multiply.3.head_ref = f32[2048,256]{1,0:T(8,128)S(1)} custom-call(bf16[2048,2048]{1,0:T(8,128)(2,1)S(1)} %build_dense.1.dense_ref, bf16[128,256]{1,0:T(8,128)(2,1)S(1)} %convert_element_type.36.refs_0_, bf16[256,256]{1,0:T(8,128)(2,1)S(1)} %collective-permute-done.4.refs_1_, bf16[256,256]{1,0:T(8,128)(2,1)S(1)} %collective-permute-done.1.refs_2_, ...), custom_call_target="tpu_custom_call" | custom-call | flops 1744830464 | bytes 6815744 | tf_op jit(solution)/shard_map/head_multiply/pallas_call | solution.py:117
  31.0 1.1 collective-permute-done.8.refs_0_
  32.7 1.8 %collective-permute-start.9 = (bf16[1024,256]{1,0:T(8,128)(2,1)S(1)}, bf16[1024,256]{1,0:T(8,128)(2,1)S(1)}, u32[]{:S(2)}, u32[]{:S(2)}) collective-permute-start(bf16[1024,256]{1,0:T(8,128)(2,1)S(1)} %tail_multiply.7), channel_id=1, source_target_pairs={{0,1},{1,0},{2,3},{3,2},{4,5},{5,4},{6,7},{7,6},{8,9},{9,8},{10,11... | collective-permute-start | bytes 1572872 | tf_op jit(solution)/shard_map/ppermute | solution.py:222
  35.1 0.9 collective-permute-done.9
  36.1 16.5 %all_to_all.15 = bf16[8,128,256]{2,1,0:T(8,128)(2,1)S(1)} all-to-all(bf16[8,128,256]{2,1,0:T(8,128)(2,1)S(1)} %bitcast.12), channel_id=1, replica_groups={{0,2,4,6,8,10,12,14},{1,3,5,7,9,11,13,15},{16,18,20,22,24,26,28,30},{17..., dimensions={0} | all-to-all | bytes 1048576 | tf_op jit(solution)/shard_map/all_to_all | solution.py:225
  52.7 2.6 %collective-permute-start.10 = (bf16[128,256]{1,0:T(8,128)(2,1)S(1)}, bf16[128,256]{1,0:T(8,128)(2,1)S(1)}, u32[]{:S(2)}, u32[]{:S(2)}) collective-permute-start(bf16[128,256]{1,0:T(8,128)(2,1)S(1)} %convert_element_type.40.refs_0_), channel_id=1, source_target_pairs={{0,1},{1,0},{2,3},{3,2},{4,5},{5,4},{6,7},{7,6},{8,9},{9,8},{10,11... | collective-permute-start | bytes 196616 | tf_op jit(solution)/shard_map/ppermute | solution.py:180
  55.2 0.9 collective-permute-done.10
  56.2 1.9 %collective-permute-start.12 = (bf16[256,256]{1,0:T(8,128)(2,1)S(1)}, bf16[256,256]{1,0:T(8,128)(2,1)S(1)}, u32[]{:S(2)}, u32[]{:S(2)}) collective-permute-start(bf16[256,256]{1,0:T(8,128)(2,1)S(1)} %pad_maximum_fusion.2), channel_id=1, source_target_pairs={{0,64},{1,193},{2,66},{3,195},{4,68},{5,197},{6,70},{7,199},{8,72}... | collective-permute-start | bytes 393224 | tf_op jit(solution)/shard_map/z_two/ppermute | solution.py:174
  58.0 1.0 collective-permute-start.11
  59.0 2.1 %collective-permute-done.13.refs_4_ = bf16[128,256]{1,0:T(8,128)(2,1)S(1)} collective-permute-done((bf16[128,256]{1,0:T(8,128)(2,1)S(1)}, bf16[128,256]{1,0:T(8,128)(2,1)S(1)}, u32[]{:S(2)}, u32[]{:S(2)}) %collective-permute-start.13) | collective-permute-done | bytes 65568 | tf_op jit(solution)/shard_map/x_own/ppermute | solution.py:178
  61.1 1.7 %collective-permute-done.12.refs_2_ = bf16[256,256]{1,0:T(8,128)(2,1)S(1)} collective-permute-done((bf16[256,256]{1,0:T(8,128)(2,1)S(1)}, bf16[256,256]{1,0:T(8,128)(2,1)S(1)}, u32[]{:S(2)}, u32[]{:S(2)}) %collective-permute-start.12) | collective-permute-done | bytes 131104 | tf_op jit(solution)/shard_map/z_two/ppermute | solution.py:174
  62.9 1.5 %collective-permute-start.14 = (bf16[256,256]{1,0:T(8,128)(2,1)S(1)}, bf16[256,256]{1,0:T(8,128)(2,1)S(1)}, u32[]{:S(2)}, u32[]{:S(2)}) collective-permute-start(bf16[256,256]{1,0:T(8,128)(2,1)S(1)} %collective-permute-done.12.refs_2_), channel_id=1, source_target_pairs={{0,32},{1,225},{2,34},{3,227},{4,36},{5,229},{6,38},{7,231},{8,40}... | collective-permute-start | bytes 393224 | tf_op jit(solution)/shard_map/z_three/ppermute | solution.py:174
  64.4 1.3 collective-permute-start.17
  65.7 1.2 collective-permute-start.16
  67.0 3.5 %collective-permute-done.15 = bf16[128,256]{1,0:T(8,128)(2,1)S(1)} collective-permute-done((bf16[128,256]{1,0:T(8,128)(2,1)S(1)}, bf16[128,256]{1,0:T(8,128)(2,1)S(1)}, u32[]{:S(2)}, u32[]{:S(2)}) %collective-permute-start.15) | collective-permute-done | bytes 65568 | tf_op jit(solution)/shard_map/z_four/ppermute | solution.py:174
  70.9 2.6 %head_multiply.4.head_ref = f32[2048,256]{1,0:T(8,128)S(1)} custom-call(bf16[2048,2048]{1,0:T(8,128)(2,1)S(1)} %build_dense.1.dense_ref, bf16[128,256]{1,0:T(8,128)(2,1)S(1)} %convert_element_type.40.refs_0_, bf16[256,256]{1,0:T(8,128)(2,1)S(1)} %collective-permute-done.11.refs_1_, bf16[256,256]{1,0:T(8,128)(2,1)S(1)} %collective-permute-done.12.refs_2_, ...), custom_call_target="tpu_custom_call" | custom-call | flops 1744830464 | bytes 6815744 | tf_op jit(solution)/shard_map/head_multiply/pallas_call | solution.py:117
  73.5 1.4 %collective-permute-done.18.refs_0_ = bf16[384,256]{1,0:T(8,128)(2,1)S(1)} collective-permute-done((bf16[384,256]{1,0:T(8,128)(2,1)S(1)}, bf16[384,256]{1,0:T(8,128)(2,1)S(1)}, u32[]{:S(2)}, u32[]{:S(2)}) %collective-permute-start.18) | collective-permute-done | bytes 196640 | tf_op jit(solution)/shard_map/x_far/ppermute | solution.py:178
  75.6 4.1 %collective-permute-start.19 = (bf16[1024,256]{1,0:T(8,128)(2,1)S(1)}, bf16[1024,256]{1,0:T(8,128)(2,1)S(1)}, u32[]{:S(2)}, u32[]{:S(2)}) collective-permute-start(bf16[1024,256]{1,0:T(8,128)(2,1)S(1)} %tail_multiply.9), channel_id=1, source_target_pairs={{0,1},{1,0},{2,3},{3,2},{4,5},{5,4},{6,7},{7,6},{8,9},{9,8},{10,11... | collective-permute-start | bytes 1572872 | tf_op jit(solution)/shard_map/ppermute | solution.py:222
  80.3 0.9 collective-permute-done.19
  81.4 12.5 %all_to_all.16 = bf16[8,128,256]{2,1,0:T(8,128)(2,1)S(1)} all-to-all(bf16[8,128,256]{2,1,0:T(8,128)(2,1)S(1)} %bitcast.13), channel_id=1, replica_groups={{0,2,4,6,8,10,12,14},{1,3,5,7,9,11,13,15},{16,18,20,22,24,26,28,30},{17..., dimensions={0} | all-to-all | bytes 1048576 | tf_op jit(solution)/shard_map/all_to_all | solution.py:225
  94.0 2.6 %collective-permute-start.20 = (bf16[128,256]{1,0:T(8,128)(2,1)S(1)}, bf16[128,256]{1,0:T(8,128)(2,1)S(1)}, u32[]{:S(2)}, u32[]{:S(2)}) collective-permute-start(bf16[128,256]{1,0:T(8,128)(2,1)S(1)} %convert_element_type.44.refs_0_), channel_id=1, source_target_pairs={{0,1},{1,0},{2,3},{3,2},{4,5},{5,4},{6,7},{7,6},{8,9},{9,8},{10,11... | collective-permute-start | bytes 196616 | tf_op jit(solution)/shard_map/ppermute | solution.py:180
  96.5 0.9 collective-permute-done.20
  97.4 0.9 collective-permute-start.22
  98.4 1.4 %collective-permute-start.23 = (bf16[128,256]{1,0:T(8,128)(2,1)S(1)}, bf16[128,256]{1,0:T(8,128)(2,1)S(1)}, u32[]{:S(2)}, u32[]{:S(2)}) collective-permute-start(bf16[128,256]{1,0:T(8,128)(2,1)S(1)} %convert_element_type.44.refs_0_), channel_id=1, source_target_pairs={{0,16},{16,0},{32,48},{48,32},{64,80},{80,64},{96,112},{112,96},{1... | collective-permute-start | bytes 196616 | tf_op jit(solution)/shard_map/x_own/ppermute | solution.py:178
  100.2 2.1 %collective-permute-done.23.refs_4_ = bf16[128,256]{1,0:T(8,128)(2,1)S(1)} collective-permute-done((bf16[128,256]{1,0:T(8,128)(2,1)S(1)}, bf16[128,256]{1,0:T(8,128)(2,1)S(1)}, u32[]{:S(2)}, u32[]{:S(2)}) %collective-permute-start.23) | collective-permute-done | bytes 65568 | tf_op jit(solution)/shard_map/x_own/ppermute | solution.py:178
  102.3 1.1 collective-permute-done.22.refs_2_
  103.5 2.9 %collective-permute-start.24 = (bf16[256,256]{1,0:T(8,128)(2,1)S(1)}, bf16[256,256]{1,0:T(8,128)(2,1)S(1)}, u32[]{:S(2)}, u32[]{:S(2)}) collective-permute-start(bf16[256,256]{1,0:T(8,128)(2,1)S(1)} %collective-permute-done.22.refs_2_), channel_id=1, source_target_pairs={{0,32},{1,225},{2,34},{3,227},{4,36},{5,229},{6,38},{7,231},{8,40}... | collective-permute-start | bytes 393224 | tf_op jit(solution)/shard_map/z_three/ppermute | solution.py:174
  106.9 1.2 collective-permute-start.26
  108.3 2.2 %collective-permute-done.25 = bf16[128,256]{1,0:T(8,128)(2,1)S(1)} collective-permute-done((bf16[128,256]{1,0:T(8,128)(2,1)S(1)}, bf16[128,256]{1,0:T(8,128)(2,1)S(1)}, u32[]{:S(2)}, u32[]{:S(2)}) %collective-permute-start.25) | collective-permute-done | bytes 65568 | tf_op jit(solution)/shard_map/z_four/ppermute | solution.py:174
  110.6 1.6 %collective-permute-start.28 = (bf16[384,256]{1,0:T(8,128)(2,1)S(1)}, bf16[384,256]{1,0:T(8,128)(2,1)S(1)}, u32[]{:S(2)}, u32[]{:S(2)}) collective-permute-start(bf16[384,256]{1,0:T(8,128)(2,1)S(1)} %constant_dynamic-update-slice_fusion.4.refs_3_), channel_id=1, source_target_pairs={{0,16},{16,0},{32,48},{48,32},{64,80},{80,64},{96,112},{112,96},{1... | collective-permute-start | bytes 589832 | tf_op jit(solution)/shard_map/x_far/ppermute | solution.py:178
  112.2 2.0 %collective-permute-done.26.refs_5_ = bf16[256,256]{1,0:T(8,128)(2,1)S(1)} collective-permute-done((bf16[256,256]{1,0:T(8,128)(2,1)S(1)}, bf16[256,256]{1,0:T(8,128)(2,1)S(1)}, u32[]{:S(2)}, u32[]{:S(2)}) %collective-permute-start.26) | collective-permute-done | bytes 131104 | tf_op jit(solution)/shard_map/x_one/ppermute | solution.py:178
  114.1 2.6 %head_multiply.5.head_ref = f32[2048,256]{1,0:T(8,128)S(1)} custom-call(bf16[2048,2048]{1,0:T(8,128)(2,1)S(1)} %build_dense.1.dense_ref, bf16[128,256]{1,0:T(8,128)(2,1)S(1)} %convert_element_type.44.refs_0_, bf16[256,256]{1,0:T(8,128)(2,1)S(1)} %collective-permute-done.21.refs_1_, bf16[256,256]{1,0:T(8,128)(2,1)S(1)} %collective-permute-done.22.refs_2_, ...), custom_call_target="tpu_custom_call" | custom-call | flops 1744830464 | bytes 6815744 | tf_op jit(solution)/shard_map/head_multiply/pallas_call | solution.py:117
  117.5 2.5 %collective-permute-start.29 = (bf16[1024,256]{1,0:T(8,128)(2,1)S(1)}, bf16[1024,256]{1,0:T(8,128)(2,1)S(1)}, u32[]{:S(2)}, u32[]{:S(2)}) collective-permute-start(bf16[1024,256]{1,0:T(8,128)(2,1)S(1)} %tail_multiply.11), channel_id=1, source_target_pairs={{0,1},{1,0},{2,3},{3,2},{4,5},{5,4},{6,7},{7,6},{8,9},{9,8},{10,11... | collective-permute-start | bytes 1572872 | tf_op jit(solution)/shard_map/ppermute | solution.py:222
  120.6 0.9 collective-permute-done.29
  121.7 12.7 %all_to_all.17 = bf16[8,128,256]{2,1,0:T(8,128)(2,1)S(1)} all-to-all(bf16[8,128,256]{2,1,0:T(8,128)(2,1)S(1)} %bitcast.14), channel_id=1, replica_groups={{0,2,4,6,8,10,12,14},{1,3,5,7,9,11,13,15},{16,18,20,22,24,26,28,30},{17..., dimensions={0} | all-to-all | bytes 1048576 | tf_op jit(solution)/shard_map/all_to_all | solution.py:225
  (54 shorter events, 9.1 us)
Async XLA Ops:
  0.9 4.2 %collective-permute-start = (bf16[128,256]{1,0:T(8,128)(2,1)S(1)}, bf16[128,256]{1,0:T(8,128)(2,1)S(1)}, u32[]{:S(2)}, u32[]{:S(2)}) collective-permute-start(bf16[128,256]{1,0:T(8,128)(2,1)S(1)} %convert_element_type.36.refs_0_), channel_id=1, source_target_pairs={{0,1},{1,0},{2,3},{3,2},{4,5},{5,4},{6,7},{7,6},{8,9},{9,8},{10,11... | collective-permute-start | bytes 196616 | tf_op jit(solution)/shard_map/ppermute | solution.py:180
  5.1 8.0 %collective-permute-start.3 = (bf16[64,128,128]{2,1,0:T(8,128)(2,1)}, bf16[64,128,128]{2,1,0:T(8,128)(2,1)S(1)}, u32[]{:S(2)}, u32[]{:S(2)}) collective-permute-start(bf16[64,128,128]{2,1,0:T(8,128)(2,1)} %bitcast.10), channel_id=1, source_target_pairs={{0,1},{1,0},{2,3},{3,2},{4,5},{5,4},{6,7},{7,6},{8,9},{9,8},{10,11... | collective-permute-start | bytes 6291464 | tf_op jit(solution)/shard_map/ppermute | solution.py:214
  6.2 12.8 %collective-permute-start.4 = (bf16[256,256]{1,0:T(8,128)(2,1)S(1)}, bf16[256,256]{1,0:T(8,128)(2,1)S(1)}, u32[]{:S(2)}, u32[]{:S(2)}) collective-permute-start(bf16[256,256]{1,0:T(8,128)(2,1)S(1)} %pad_maximum_fusion.1), channel_id=1, source_target_pairs={{0,32},{1,225},{2,34},{3,227},{4,36},{5,229},{6,38},{7,231},{8,40}... | collective-permute-start | bytes 393224 | tf_op jit(solution)/shard_map/z_one/ppermute | solution.py:174
  10.1 7.7 %collective-permute-start.1 = (bf16[256,256]{1,0:T(8,128)(2,1)S(1)}, bf16[256,256]{1,0:T(8,128)(2,1)S(1)}, u32[]{:S(2)}, u32[]{:S(2)}) collective-permute-start(bf16[256,256]{1,0:T(8,128)(2,1)S(1)} %pad_maximum_fusion.1), channel_id=1, source_target_pairs={{0,64},{1,193},{2,66},{3,195},{4,68},{5,197},{6,70},{7,199},{8,72}... | collective-permute-start | bytes 393224 | tf_op jit(solution)/shard_map/z_two/ppermute | solution.py:174
  12.0 1.1 collective-permute-start.2
  13.2 1.6 %copy-start = (bf16[1,1,64,128,128]{4,3,2,1,0:T(8,128)(2,1)S(1)}, bf16[1,1,64,128,128]{4,3,2,1,0:T(8,128)(2,1)}, u32[]{:S(2)}) copy-start(bf16[1,1,64,128,128]{4,3,2,1,0:T(8,128)(2,1)} %param.6) | copy-start | bytes 6291460
  17.8 4.8 %collective-permute-start.5 = (bf16[256,256]{1,0:T(8,128)(2,1)S(1)}, bf16[256,256]{1,0:T(8,128)(2,1)S(1)}, u32[]{:S(2)}, u32[]{:S(2)}) collective-permute-start(bf16[256,256]{1,0:T(8,128)(2,1)S(1)} %collective-permute-done.1.refs_2_), channel_id=1, source_target_pairs={{0,32},{1,225},{2,34},{3,227},{4,36},{5,229},{6,38},{7,231},{8,40}... | collective-permute-start | bytes 393224 | tf_op jit(solution)/shard_map/z_three/ppermute | solution.py:174
  19.0 9.4 %collective-permute-start.7 = (bf16[640,256]{1,0:T(8,128)(2,1)S(1)}, bf16[640,256]{1,0:T(8,128)(2,1)S(1)}, u32[]{:S(2)}, u32[]{:S(2)}) collective-permute-start(bf16[640,256]{1,0:T(8,128)(2,1)S(1)} %pad_maximum_fusion), channel_id=1, source_target_pairs={{0,16},{16,0},{32,48},{48,32},{64,80},{80,64},{96,112},{112,96},{1... | collective-permute-start | bytes 983048 | tf_op jit(solution)/shard_map/x_near/ppermute | solution.py:178
  20.9 4.7 %collective-permute-start.6 = (bf16[128,256]{1,0:T(8,128)(2,1)S(1)}, bf16[128,256]{1,0:T(8,128)(2,1)S(1)}, u32[]{:S(2)}, u32[]{:S(2)}) collective-permute-start(bf16[128,256]{1,0:T(8,128)(2,1)S(1)} %slice.9), channel_id=1, source_target_pairs={{0,64},{1,193},{2,66},{3,195},{4,68},{5,197},{6,70},{7,199},{8,72}... | collective-permute-start | bytes 196616 | tf_op jit(solution)/shard_map/z_four/ppermute | solution.py:174
  25.6 6.5 %collective-permute-start.8 = (bf16[384,256]{1,0:T(8,128)(2,1)S(1)}, bf16[384,256]{1,0:T(8,128)(2,1)S(1)}, u32[]{:S(2)}, u32[]{:S(2)}) collective-permute-start(bf16[384,256]{1,0:T(8,128)(2,1)S(1)} %constant_dynamic-update-slice_fusion.refs_3_), channel_id=1, source_target_pairs={{0,16},{16,0},{32,48},{48,32},{64,80},{80,64},{96,112},{112,96},{1... | collective-permute-start | bytes 589832 | tf_op jit(solution)/shard_map/x_far/ppermute | solution.py:178
  32.7 3.3 %collective-permute-start.9 = (bf16[1024,256]{1,0:T(8,128)(2,1)S(1)}, bf16[1024,256]{1,0:T(8,128)(2,1)S(1)}, u32[]{:S(2)}, u32[]{:S(2)}) collective-permute-start(bf16[1024,256]{1,0:T(8,128)(2,1)S(1)} %tail_multiply.7), channel_id=1, source_target_pairs={{0,1},{1,0},{2,3},{3,2},{4,5},{5,4},{6,7},{7,6},{8,9},{9,8},{10,11... | collective-permute-start | bytes 1572872 | tf_op jit(solution)/shard_map/ppermute | solution.py:222
  52.7 3.5 %collective-permute-start.10 = (bf16[128,256]{1,0:T(8,128)(2,1)S(1)}, bf16[128,256]{1,0:T(8,128)(2,1)S(1)}, u32[]{:S(2)}, u32[]{:S(2)}) collective-permute-start(bf16[128,256]{1,0:T(8,128)(2,1)S(1)} %convert_element_type.40.refs_0_), channel_id=1, source_target_pairs={{0,1},{1,0},{2,3},{3,2},{4,5},{5,4},{6,7},{7,6},{8,9},{9,8},{10,11... | collective-permute-start | bytes 196616 | tf_op jit(solution)/shard_map/ppermute | solution.py:180
  56.2 6.7 %collective-permute-start.12 = (bf16[256,256]{1,0:T(8,128)(2,1)S(1)}, bf16[256,256]{1,0:T(8,128)(2,1)S(1)}, u32[]{:S(2)}, u32[]{:S(2)}) collective-permute-start(bf16[256,256]{1,0:T(8,128)(2,1)S(1)} %pad_maximum_fusion.2), channel_id=1, source_target_pairs={{0,64},{1,193},{2,66},{3,195},{4,68},{5,197},{6,70},{7,199},{8,72}... | collective-permute-start | bytes 393224 | tf_op jit(solution)/shard_map/z_two/ppermute | solution.py:174
  58.0 3.1 %collective-permute-start.13 = (bf16[128,256]{1,0:T(8,128)(2,1)S(1)}, bf16[128,256]{1,0:T(8,128)(2,1)S(1)}, u32[]{:S(2)}, u32[]{:S(2)}) collective-permute-start(bf16[128,256]{1,0:T(8,128)(2,1)S(1)} %convert_element_type.40.refs_0_), channel_id=1, source_target_pairs={{0,16},{16,0},{32,48},{48,32},{64,80},{80,64},{96,112},{112,96},{1... | collective-permute-start | bytes 196616 | tf_op jit(solution)/shard_map/x_own/ppermute | solution.py:178
  58.0 7.7 %collective-permute-start.11 = (bf16[256,256]{1,0:T(8,128)(2,1)S(1)}, bf16[256,256]{1,0:T(8,128)(2,1)S(1)}, u32[]{:S(2)}, u32[]{:S(2)}) collective-permute-start(bf16[256,256]{1,0:T(8,128)(2,1)S(1)} %pad_maximum_fusion.2), channel_id=1, source_target_pairs={{0,32},{1,225},{2,34},{3,227},{4,36},{5,229},{6,38},{7,231},{8,40}... | collective-permute-start | bytes 393224 | tf_op jit(solution)/shard_map/z_one/ppermute | solution.py:174
  62.9 4.1 %collective-permute-start.14 = (bf16[256,256]{1,0:T(8,128)(2,1)S(1)}, bf16[256,256]{1,0:T(8,128)(2,1)S(1)}, u32[]{:S(2)}, u32[]{:S(2)}) collective-permute-start(bf16[256,256]{1,0:T(8,128)(2,1)S(1)} %collective-permute-done.12.refs_2_), channel_id=1, source_target_pairs={{0,32},{1,225},{2,34},{3,227},{4,36},{5,229},{6,38},{7,231},{8,40}... | collective-permute-start | bytes 393224 | tf_op jit(solution)/shard_map/z_three/ppermute | solution.py:174
  64.4 6.5 %collective-permute-start.17 = (bf16[256,256]{1,0:T(8,128)(2,1)S(1)}, bf16[256,256]{1,0:T(8,128)(2,1)S(1)}, u32[]{:S(2)}, u32[]{:S(2)}) collective-permute-start(bf16[256,256]{1,0:T(8,128)(2,1)S(1)} %collective-permute-done.12.refs_2_), channel_id=1, source_target_pairs={{0,16},{16,0},{32,48},{48,32},{64,80},{80,64},{96,112},{112,96},{1... | collective-permute-start | bytes 393224 | tf_op jit(solution)/shard_map/x_two/ppermute | solution.py:178
  65.7 4.7 %collective-permute-start.15 = (bf16[128,256]{1,0:T(8,128)(2,1)S(1)}, bf16[128,256]{1,0:T(8,128)(2,1)S(1)}, u32[]{:S(2)}, u32[]{:S(2)}) collective-permute-start(bf16[128,256]{1,0:T(8,128)(2,1)S(1)} %slice.10), channel_id=1, source_target_pairs={{0,64},{1,193},{2,66},{3,195},{4,68},{5,197},{6,70},{7,199},{8,72}... | collective-permute-start | bytes 196616 | tf_op jit(solution)/shard_map/z_four/ppermute | solution.py:174
  65.7 5.1 %collective-permute-start.16 = (bf16[256,256]{1,0:T(8,128)(2,1)S(1)}, bf16[256,256]{1,0:T(8,128)(2,1)S(1)}, u32[]{:S(2)}, u32[]{:S(2)}) collective-permute-start(bf16[256,256]{1,0:T(8,128)(2,1)S(1)} %collective-permute-done.11.refs_1_), channel_id=1, source_target_pairs={{0,16},{16,0},{32,48},{48,32},{64,80},{80,64},{96,112},{112,96},{1... | collective-permute-start | bytes 393224 | tf_op jit(solution)/shard_map/x_one/ppermute | solution.py:178
  70.4 4.5 %collective-permute-start.18 = (bf16[384,256]{1,0:T(8,128)(2,1)S(1)}, bf16[384,256]{1,0:T(8,128)(2,1)S(1)}, u32[]{:S(2)}, u32[]{:S(2)}) collective-permute-start(bf16[384,256]{1,0:T(8,128)(2,1)S(1)} %constant_dynamic-update-slice_fusion.2.refs_3_), channel_id=1, source_target_pairs={{0,16},{16,0},{32,48},{48,32},{64,80},{80,64},{96,112},{112,96},{1... | collective-permute-start | bytes 589832 | tf_op jit(solution)/shard_map/x_far/ppermute | solution.py:178
  75.6 5.7 %collective-permute-start.19 = (bf16[1024,256]{1,0:T(8,128)(2,1)S(1)}, bf16[1024,256]{1,0:T(8,128)(2,1)S(1)}, u32[]{:S(2)}, u32[]{:S(2)}) collective-permute-start(bf16[1024,256]{1,0:T(8,128)(2,1)S(1)} %tail_multiply.9), channel_id=1, source_target_pairs={{0,1},{1,0},{2,3},{3,2},{4,5},{5,4},{6,7},{7,6},{8,9},{9,8},{10,11... | collective-permute-start | bytes 1572872 | tf_op jit(solution)/shard_map/ppermute | solution.py:222
  94.0 3.5 %collective-permute-start.20 = (bf16[128,256]{1,0:T(8,128)(2,1)S(1)}, bf16[128,256]{1,0:T(8,128)(2,1)S(1)}, u32[]{:S(2)}, u32[]{:S(2)}) collective-permute-start(bf16[128,256]{1,0:T(8,128)(2,1)S(1)} %convert_element_type.44.refs_0_), channel_id=1, source_target_pairs={{0,1},{1,0},{2,3},{3,2},{4,5},{5,4},{6,7},{7,6},{8,9},{9,8},{10,11... | collective-permute-start | bytes 196616 | tf_op jit(solution)/shard_map/ppermute | solution.py:180
  97.4 6.1 %collective-permute-start.22 = (bf16[256,256]{1,0:T(8,128)(2,1)S(1)}, bf16[256,256]{1,0:T(8,128)(2,1)S(1)}, u32[]{:S(2)}, u32[]{:S(2)}) collective-permute-start(bf16[256,256]{1,0:T(8,128)(2,1)S(1)} %pad_maximum_fusion.3), channel_id=1, source_target_pairs={{0,64},{1,193},{2,66},{3,195},{4,68},{5,197},{6,70},{7,199},{8,72}... | collective-permute-start | bytes 393224 | tf_op jit(solution)/shard_map/z_two/ppermute | solution.py:174
  98.4 4.0 %collective-permute-start.23 = (bf16[128,256]{1,0:T(8,128)(2,1)S(1)}, bf16[128,256]{1,0:T(8,128)(2,1)S(1)}, u32[]{:S(2)}, u32[]{:S(2)}) collective-permute-start(bf16[128,256]{1,0:T(8,128)(2,1)S(1)} %convert_element_type.44.refs_0_), channel_id=1, source_target_pairs={{0,16},{16,0},{32,48},{48,32},{64,80},{80,64},{96,112},{112,96},{1... | collective-permute-start | bytes 196616 | tf_op jit(solution)/shard_map/x_own/ppermute | solution.py:178
  99.8 7.2 %collective-permute-start.21 = (bf16[256,256]{1,0:T(8,128)(2,1)S(1)}, bf16[256,256]{1,0:T(8,128)(2,1)S(1)}, u32[]{:S(2)}, u32[]{:S(2)}) collective-permute-start(bf16[256,256]{1,0:T(8,128)(2,1)S(1)} %pad_maximum_fusion.3), channel_id=1, source_target_pairs={{0,32},{1,225},{2,34},{3,227},{4,36},{5,229},{6,38},{7,231},{8,40}... | collective-permute-start | bytes 393224 | tf_op jit(solution)/shard_map/z_one/ppermute | solution.py:174
  103.5 4.8 %collective-permute-start.24 = (bf16[256,256]{1,0:T(8,128)(2,1)S(1)}, bf16[256,256]{1,0:T(8,128)(2,1)S(1)}, u32[]{:S(2)}, u32[]{:S(2)}) collective-permute-start(bf16[256,256]{1,0:T(8,128)(2,1)S(1)} %collective-permute-done.22.refs_2_), channel_id=1, source_target_pairs={{0,32},{1,225},{2,34},{3,227},{4,36},{5,229},{6,38},{7,231},{8,40}... | collective-permute-start | bytes 393224 | tf_op jit(solution)/shard_map/z_three/ppermute | solution.py:174
  106.4 5.8 %collective-permute-start.27 = (bf16[256,256]{1,0:T(8,128)(2,1)S(1)}, bf16[256,256]{1,0:T(8,128)(2,1)S(1)}, u32[]{:S(2)}, u32[]{:S(2)}) collective-permute-start(bf16[256,256]{1,0:T(8,128)(2,1)S(1)} %collective-permute-done.22.refs_2_), channel_id=1, source_target_pairs={{0,16},{16,0},{32,48},{48,32},{64,80},{80,64},{96,112},{112,96},{1... | collective-permute-start | bytes 393224 | tf_op jit(solution)/shard_map/x_two/ppermute | solution.py:178
  106.4 4.2 %collective-permute-start.25 = (bf16[128,256]{1,0:T(8,128)(2,1)S(1)}, bf16[128,256]{1,0:T(8,128)(2,1)S(1)}, u32[]{:S(2)}, u32[]{:S(2)}) collective-permute-start(bf16[128,256]{1,0:T(8,128)(2,1)S(1)} %slice.11), channel_id=1, source_target_pairs={{0,64},{1,193},{2,66},{3,195},{4,68},{5,197},{6,70},{7,199},{8,72}... | collective-permute-start | bytes 196616 | tf_op jit(solution)/shard_map/z_four/ppermute | solution.py:174
  106.9 7.2 %collective-permute-start.26 = (bf16[256,256]{1,0:T(8,128)(2,1)S(1)}, bf16[256,256]{1,0:T(8,128)(2,1)S(1)}, u32[]{:S(2)}, u32[]{:S(2)}) collective-permute-start(bf16[256,256]{1,0:T(8,128)(2,1)S(1)} %collective-permute-done.21.refs_1_), channel_id=1, source_target_pairs={{0,16},{16,0},{32,48},{48,32},{64,80},{80,64},{96,112},{112,96},{1... | collective-permute-start | bytes 393224 | tf_op jit(solution)/shard_map/x_one/ppermute | solution.py:178
  110.6 6.3 %collective-permute-start.28 = (bf16[384,256]{1,0:T(8,128)(2,1)S(1)}, bf16[384,256]{1,0:T(8,128)(2,1)S(1)}, u32[]{:S(2)}, u32[]{:S(2)}) collective-permute-start(bf16[384,256]{1,0:T(8,128)(2,1)S(1)} %constant_dynamic-update-slice_fusion.4.refs_3_), channel_id=1, source_target_pairs={{0,16},{16,0},{32,48},{48,32},{64,80},{80,64},{96,112},{112,96},{1... | collective-permute-start | bytes 589832 | tf_op jit(solution)/shard_map/x_far/ppermute | solution.py:178
  117.5 4.0 %collective-permute-start.29 = (bf16[1024,256]{1,0:T(8,128)(2,1)S(1)}, bf16[1024,256]{1,0:T(8,128)(2,1)S(1)}, u32[]{:S(2)}, u32[]{:S(2)}) collective-permute-start(bf16[1024,256]{1,0:T(8,128)(2,1)S(1)} %tail_multiply.11), channel_id=1, source_target_pairs={{0,1},{1,0},{2,3},{3,2},{4,5},{5,4},{6,7},{7,6},{8,9},{9,8},{10,11... | collective-permute-start | bytes 1572872 | tf_op jit(solution)/shard_map/ppermute | solution.py:222
  120.6 13.8 %copy-start.1 = (f32[128,256]{1,0:T(8,128)S(1)}, f32[128,256]{1,0:T(8,128)}, u32[]{:S(2)}) copy-start(f32[128,256]{1,0:T(8,128)} %param.5) | copy-start | bytes 393220
